TPU v7x, 32 devices: a whole 2x2x4 slice. The times are simulated.
32 devices in a mesh: dp: 8 (over z, core), seq: 4 (over y, x).
Axes of the slice: x: 2, y: 2, z: 4, core: 2. Of those that a mesh axis runs over, the one named last changes fastest.
Arguments:
- query_in: bfloat16 [8, 512, 2048], P('dp', 'seq'), may hold values from -6 to 6
- key_in: bfloat16 [8, 512, 2048], P('dp', 'seq'), may hold values from -6 to 6
- value_in: bfloat16 [8, 512, 2048], P('dp', 'seq'), may hold values from -6 to 6
- grad_out: bfloat16 [8, 512, 2048], P('dp', 'seq'), may hold values from -6 to 6
- w_query: bfloat16 [2048, 128], replicated, may hold values from -0.5 to 0.5
- w_key: bfloat16 [2048, 128], replicated, may hold values from -0.5 to 0.5
- norm_gain: float32 [2048], replicated, may hold values from 0.1 to 1.9
Outputs:
- grad_query: bfloat16 [8, 512, 2048], P('dp', 'seq')
- grad_key: bfloat16 [8, 512, 2048], P('dp', 'seq')
- grad_value: bfloat16 [8, 512, 2048], P('dp', 'seq')
- grad_w_query: float32 [2048, 128], P('dp')
- grad_w_key: float32 [2048, 128], P('dp')
- grad_gain: float32 [2048], P('dp')
All inputs are finite; a program needn't handle non-finite values.
Results may differ from a plain program's by a relative error of at most 0.0077.
Values sent between devices are 32-bit elements; how exact they have to be, the bound alone decides.
No kernel may reach another device: no remote copies, remote signals or barrier semaphores. Data moves between devices by JAX's collectives and lax.ppermute only.
A program may use at most 128 MiB of HBM per device.

v0:
```python
import jax
import jax.numpy as jnp
from jax import lax
from jax.sharding import PartitionSpec as P

HEAD = 128


norm_eps = 1e-05
highest = lax.Precision.HIGHEST


def entering(value, axis, combine, identity, reverse):
    peers, mine = (lax.axis_size(axis), lax.axis_index(axis))
    everything = lax.all_gather(value, axis)
    start = jnp.broadcast_to(jnp.asarray(identity, value.dtype), value.shape)

    def turn(k, before):
        at = peers - 1 - k if reverse else k
        reached = at > mine if reverse else at < mine
        new = combine(before, everything[at])
        return jnp.where(reached, new, before)

    return lax.fori_loop(0, peers, turn, start)


def add_states(earlier, later):
    return earlier + later


def per_device(query_in, key_in, value_in, grad_out, w_query, w_key, norm_gain):
    seq_count, tok_rows, width_all = query_in.shape
    head_count = width_all // HEAD

    def split_heads(tensor):
        return tensor.reshape(seq_count, tok_rows, head_count, HEAD)

    query_h = split_heads(query_in)
    key_h = split_heads(key_in)
    value_h = split_heads(value_in)
    grad_h = split_heads(grad_out)
    map_query = w_query.reshape(head_count, HEAD, HEAD)
    map_key = w_key.reshape(head_count, HEAD, HEAD)
    pre_query = jnp.einsum("bthd,hde->bthe", query_h, map_query, preferred_element_type=jnp.float32)
    pre_key = jnp.einsum("bthd,hde->bthe", key_h, map_key, preferred_element_type=jnp.float32)
    feat_query = (jax.nn.elu(pre_query) + 1.0).astype(jnp.bfloat16)
    feat_key = (jax.nn.elu(pre_key) + 1.0).astype(jnp.bfloat16)
    position = lax.broadcasted_iota(jnp.int32, (tok_rows, tok_rows), 0)
    column = lax.broadcasted_iota(jnp.int32, (tok_rows, tok_rows), 1)
    causal = position >= column
    local_state = jnp.einsum(
        "bthf,bthe->bhfe", feat_key, value_h, preferred_element_type=jnp.float32
    )
    zero_state = jnp.zeros_like(local_state)
    scores = jnp.einsum("bthf,bshf->bhts", feat_query, feat_key, preferred_element_type=jnp.float32)
    attn_weights = jnp.where(causal, scores, 0.0).astype(jnp.bfloat16)
    inner_sum = jnp.einsum(
        "bhts,bshe->bthe", attn_weights, value_h, preferred_element_type=jnp.float32
    )
    prior_state = entering(local_state, "seq", add_states, zero_state, False)
    query_wide = feat_query.astype(jnp.float32)
    numerator = inner_sum + jnp.einsum(
        "bthf,bhfe->bthe", query_wide, prior_state, precision=highest
    )
    inv_rms = lax.rsqrt(jnp.mean(numerator * numerator, axis=-1, keepdims=True) + norm_eps)
    normed = numerator * inv_rms
    gain_h = norm_gain.reshape(head_count, HEAD)
    grad_f = grad_h.astype(jnp.float32)
    grad_normed = grad_f * gain_h
    grad_numer = inv_rms * (
        grad_normed - normed * jnp.mean(grad_normed * normed, axis=-1, keepdims=True)
    )
    grad_gain = jnp.sum(normed * grad_f, axis=(0, 1)).reshape(width_all)
    numer_low = grad_numer.astype(jnp.bfloat16)
    local_adjoint = jnp.einsum(
        "bthf,bthe->bhfe", feat_query, numer_low, preferred_element_type=jnp.float32
    )
    mixed = jnp.einsum("bthe,bshe->bhts", numer_low, value_h, preferred_element_type=jnp.float32)
    mixed_low = jnp.where(causal, mixed, 0.0).astype(jnp.bfloat16)
    grad_fq = jnp.einsum("bhts,bshf->bthf", mixed_low, feat_key, preferred_element_type=jnp.float32)
    grad_fq = grad_fq + jnp.einsum("bthe,bhfe->bthf", grad_numer, prior_state, precision=highest)
    slope_query = jnp.minimum(jnp.exp(pre_query), 1.0)
    pre_grad_q = (grad_fq * slope_query).astype(jnp.bfloat16)
    grad_query = jnp.einsum(
        "bthe,hde->bthd", pre_grad_q, map_query, preferred_element_type=jnp.float32
    )
    sum_wq = jnp.einsum("bthd,bthe->hde", query_h, pre_grad_q, preferred_element_type=jnp.float32)
    later_state = entering(local_adjoint, "seq", add_states, zero_state, True)
    grad_fk = jnp.einsum(
        "bhts,bthf->bshf", mixed_low, feat_query, preferred_element_type=jnp.float32
    )
    grad_fk = grad_fk + jnp.einsum(
        "bshe,bhfe->bshf", value_h.astype(jnp.float32), later_state, precision=highest
    )
    grad_v = jnp.einsum(
        "bhts,bthe->bshe", attn_weights, numer_low, preferred_element_type=jnp.float32
    )
    grad_v = grad_v + jnp.einsum(
        "bshf,bhfe->bshe", feat_key.astype(jnp.float32), later_state, precision=highest
    )
    slope_key = jnp.minimum(jnp.exp(pre_key), 1.0)
    pre_grad_k = (grad_fk * slope_key).astype(jnp.bfloat16)
    grad_key = jnp.einsum("bthe,hde->bthd", pre_grad_k, map_key, preferred_element_type=jnp.float32)
    sum_wk = jnp.einsum("bthd,bthe->hde", key_h, pre_grad_k, preferred_element_type=jnp.float32)
    sum_wq = sum_wq.reshape(width_all, HEAD)
    sum_wk = sum_wk.reshape(width_all, HEAD)
    owned = (
        lax.psum_scatter(sum_wq, "dp", scatter_dimension=0, tiled=True),
        lax.psum_scatter(sum_wk, "dp", scatter_dimension=0, tiled=True),
        lax.psum_scatter(grad_gain, "dp", scatter_dimension=0, tiled=True),
    )
    total_wq, total_wk, total_gain = lax.psum((owned[0], owned[1], owned[2]), "seq")
    out_shape = (seq_count, tok_rows, width_all)
    return (
        grad_query.astype(jnp.bfloat16).reshape(out_shape),
        grad_key.astype(jnp.bfloat16).reshape(out_shape),
        grad_v.astype(jnp.bfloat16).reshape(out_shape),
        total_wq,
        total_wk,
        total_gain,
    )


def solution(mesh):
    in_specs = (
        P("dp", "seq", None),
        P("dp", "seq", None),
        P("dp", "seq", None),
        P("dp", "seq", None),
        P(),
        P(),
        P(),
    )
    out_specs = (
        P("dp", "seq", None),
        P("dp", "seq", None),
        P("dp", "seq", None),
        P("dp", None),
        P("dp", None),
        P("dp"),
    )
    return jax.shard_map(
        per_device, mesh=mesh, in_specs=in_specs, out_specs=out_specs, check_vma=False
    )
```

profile of v0, /device:TPU:0, one launch (start us, length us, event | category | flops | bytes accessed | tf_op | source)
XLA Modules:
  0.0 257.0 jit_solution(16946345542521992046)
XLA Ops:
  7.2 1.4 copy.87
  8.6 1.5 copy.86
  10.2 1.3 copy.88
  12.3 0.6 copy-done.7
  12.9 0.9 fusion.23
  13.8 1.3 fusion.33
  15.1 2.3 copy.53
  17.8 0.8 copy-done.11
  18.6 1.6 convolution_bitcast_fusion
  20.2 50.4 %all-gather.5.cloned.1.call-done = f32[64,128,128]{2,1,0:T(8,128)} async-done(((f32[16,128,128]{2,1,0:T(8,128)}), f32[64,128,128]{2,1,0:T(8,128)}) %all-gather.5.cloned.1.call-update) | async-done | bytes 4194320 | tf_op jit(solution)/shard_map/all_gather | solution.py:15
  70.6 6.4 %while.30 = (s32[]{:T(128)}, f32[1,16,128,128]{3,2,1,0:T(8,128)S(1)}, s32[]{:T(128)}, f32[4,1,16,128,128]{4,3,2,1,0:T(8,128)}, s32[]{:T(128)}, /*index=5*/s32[]{:T(128)}) while((s32[]{:T(128)}, f32[1,16,128,128]{3,2,1,0:T(8,128)S(1)}, s32[]{:T(128)}, f32[4,1,16,128,128]{4,3,2,1,0:T(8,128)}, s32[]{:T(128)}, ...), condition=%wide.region_1.2_spmd.clone, body=%wide.region_0.1_spmd.clone.sunk | while | flops 786436 | bytes 3145829 | solution.py:24
  70.6 1.6 add_select_fusion.4
  72.2 1.6 add_select_fusion.4
  73.9 1.6 add_select_fusion.4
  75.5 1.6 add_select_fusion.4
  77.1 2.3 multiply_reduce_fusion.2
  79.4 0.8 multiply_reduce_fusion
  80.2 0.4 fusion.35
  80.6 0.8 copy-done.13
  81.4 1.5 fusion.27
  82.9 1.9 fusion.7
  84.8 0.8 copy-done.22
  85.6 1.6 fusion.36
  87.2 1.5 fusion.10
  88.8 1.5 fusion.38
  90.3 2.5 fusion.37
  92.8 42.9 %all-gather.7.cloned.1.call-done = f32[64,128,128]{2,1,0:T(8,128)} async-done(((f32[16,128,128]{2,1,0:T(8,128)}), f32[64,128,128]{2,1,0:T(8,128)}) %all-gather.7.cloned.1.call-update) | async-done | bytes 4194320 | tf_op jit(solution)/shard_map/all_gather | solution.py:15
  135.7 6.6 %while.31 = (s32[]{:T(128)}, f32[1,16,128,128]{3,2,1,0:T(8,128)S(1)}, s32[]{:T(128)}, f32[4,1,16,128,128]{4,3,2,1,0:T(8,128)}, s32[]{:T(128)}, /*index=5*/s32[]{:T(128)}, s32[]{:T(128)}, s32[]{:T(128)}) while((s32[]{:T(128)}, f32[1,16,128,128]{3,2,1,0:T(8,128)S(1)}, s32[]{:T(128)}, f32[4,1,16,128,128]{4,3,2,1,0:T(8,128)}, ...), condition=%wide.region_5.6_spmd.clone, body=%wide.region_4.5_spmd.clone.sunk | while | flops 786440 | bytes 3145891 | solution.py:24
  135.7 1.7 add_select_fusion.5
  137.5 1.6 add_select_fusion.5
  139.1 1.6 add_select_fusion.5
  140.7 1.6 add_select_fusion.5
  142.3 2.5 fusion.11
  144.9 1.5 fusion.39
  146.5 0.6 dynamic-slice
  147.8 2.1 convolution_convert_fusion.1
  149.9 2.0 copy.68
  151.9 16.7 %all-reduce = f32[2048]{0:T(1024)S(1)} all-reduce(f32[2048]{0:T(1024)S(1)} %bitcast.164), channel_id=6, replica_groups=mesh['dp'=8,'seq'=4] {'dp'}, use_global_device_ids=true, to_apply=%region_11.12.clone | all-reduce | flops 2048 | bytes 16384
  168.8 9.6 %psum.23 = f32[256]{0:T(256)} all-reduce(f32[256]{0:T(256)S(1)} %dynamic-slice.1), channel_id=1, replica_groups=mesh['dp'=8,'seq'=4] {'seq'}, use_global_device_ids=true, to_apply=%region_12.13 | all-reduce | flops 256 | bytes 2048 | tf_op jit(solution)/shard_map/psum | solution.py:112
  178.3 1.3 fusion.25
  179.6 1.5 convolution_convert_fusion
  181.1 1.0 copy.69
  182.1 21.3 %reduce-scatter.5.cloned.1.call-done = f32[256,128]{1,0:T(8,128)} async-done(((f32[2048,128]{1,0:T(8,128)}), f32[256,128]{1,0:T(8,128)}) %reduce-scatter.5.cloned.1.call-update) | async-done | bytes 131088 | tf_op jit(solution)/shard_map/reduce_scatter | solution.py:109
  203.4 2.2 fusion.5
  205.6 1.0 copy.70
  206.6 40.7 %all-reduce.4.cloned.1.call-done = (f32[256,128]{1,0:T(8,128)}, f32[256,128]{1,0:T(8,128)}) async-done(((f32[256,128]{1,0:T(8,128)}, f32[256,128]{1,0:T(8,128)}), (f32[256,128]{1,0:T(8,128)}, f32[256,128]{1,0:T(8,128)})) %all-reduce.4.cloned.1.call-update) | async-done | bytes 262160 | tf_op jit(solution)/shard_map/psum | solution.py:112
  247.3 1.6 copy.111
  248.9 1.6 copy.112
  (66 shorter events, 1.6 us)
Async XLA Ops:
  7.2 4.3 %copy-start = (bf16[2048,128]{1,0:T(8,128)(2,1)S(1)}, bf16[2048,128]{1,0:T(8,128)(2,1)}, u32[]{:S(2)}) copy-start(bf16[2048,128]{1,0:T(8,128)(2,1)} %param.15) | copy-start | bytes 1572868
  7.2 4.7 %copy-start.21 = (bf16[2048,128]{1,0:T(8,128)(2,1)S(1)}, bf16[2048,128]{1,0:T(8,128)(2,1)}, u32[]{:S(2)}) copy-start(bf16[2048,128]{1,0:T(8,128)(2,1)} %param.16) | copy-start | bytes 1572868
  7.2 63.4 %all-gather.5.cloned.1.call-start = ((), (), s32[]{:S(2)}) async-start(), calls=%async_computation.4 | async-start | bytes 5242880 | tf_op jit(solution)/shard_map/all_gather | solution.py:15
  8.6 3.3 %copy-start.17 = (bf16[1,128,2048]{1,2,0:T(8,128)(2,1)}, bf16[1,128,2048]{1,2,0:T(8,128)(2,1)S(1)}, u32[]{:S(2)}) copy-start(bf16[1,128,2048]{1,2,0:T(8,128)(2,1)S(1)} %copy.87) | copy-start | bytes 1572868
  10.1 1.8 copy-start.15
  11.5 6.3 %copy-start.9 = (bf16[16,8,16,128]{3,2,1,0:T(8,128)(2,1)}, bf16[16,8,16,128]{3,2,1,0:T(8,128)(2,1)S(1)}, u32[]{:S(2)}) copy-start(bf16[16,8,16,128]{3,2,1,0:T(8,128)(2,1)S(1)} %copy.88) | copy-start | bytes 1572868
  11.9 1.0 copy-start.7
  12.9 2.2 copy-start.5
  13.8 6.4 %copy-start.3 = (bf16[128,16,128]{0,2,1:T(8,128)(2,1)}, bf16[128,16,128]{0,2,1:T(8,128)(2,1)S(1)}, u32[]{:S(2)}) copy-start(bf16[128,16,128]{0,2,1:T(8,128)(2,1)S(1)} %get-tuple-element.278) | copy-start | bytes 1572868
  15.1 120.7 %all-gather.7.cloned.1.call-start = ((), (), s32[]{:S(2)}) async-start(), calls=%async_computation.5 | async-start | bytes 5242880 | tf_op jit(solution)/shard_map/all_gather | solution.py:15
  17.8 0.8 copy-start.11
  70.6 8.8 %copy-start.23 = (f32[2048]{0:T(1024)S(1)}, f32[2048]{0:T(1024)}, u32[]{:S(2)}) copy-start(f32[2048]{0:T(1024)} %param.17) | copy-start | bytes 24580
  77.1 2.4 copy-start.1
  80.6 0.8 copy-start.13
  82.9 99.3 %reduce-scatter.3.cloned.1.call-start = ((), (), s32[]{:S(2)}) async-start(), calls=%async_computation.2 | async-start | bytes 1179648 | tf_op jit(solution)/shard_map/reduce_scatter | solution.py:108
  82.9 4.3 %copy-start.2 = (f32[1,128,2048]{1,2,0:T(8,128)S(1)}, f32[1,128,2048]{1,2,0:T(8,128)}, u32[]{:S(2)}) copy-start(f32[1,128,2048]{1,2,0:T(8,128)} %copy.53) | copy-start | bytes 3145732
  82.9 4.3 %copy-start.8 = (f32[1,128,16,128]{1,3,2,0:T(8,128)S(1)}, f32[1,128,16,128]{1,3,2,0:T(8,128)}, u32[]{:S(2)}) copy-start(f32[1,128,16,128]{1,3,2,0:T(8,128)} %copy-done.7) | copy-start | bytes 3145732
  84.8 0.8 copy-start.22
  85.6 3.1 %copy-start.18 = (bf16[1,128,2048]{1,2,0:T(8,128)(2,1)S(1)}, bf16[1,128,2048]{1,2,0:T(8,128)(2,1)}, u32[]{:S(2)}) copy-start(bf16[1,128,2048]{1,2,0:T(8,128)(2,1)} %copy-done.17) | copy-start | bytes 1572868
  88.7 1.5 copy-start.19
  90.3 113.1 %reduce-scatter.5.cloned.1.call-start = ((), (), s32[]{:S(2)}) async-start(), calls=%async_computation.3 | async-start | bytes 1179648 | tf_op jit(solution)/shard_map/reduce_scatter | solution.py:109
  135.7 6.6 %copy-start.6 = (f32[1,128,16,128]{1,3,2,0:T(8,128)S(1)}, f32[1,128,16,128]{1,3,2,0:T(8,128)}, u32[]{:S(2)}) copy-start(f32[1,128,16,128]{1,3,2,0:T(8,128)} %copy-done.5) | copy-start | bytes 3145732
  135.7 6.6 %copy-start.10 = (bf16[16,8,16,128]{3,2,1,0:T(8,128)(2,1)S(1)}, bf16[16,8,16,128]{3,2,1,0:T(8,128)(2,1)}, u32[]{:S(2)}) copy-start(bf16[16,8,16,128]{3,2,1,0:T(8,128)(2,1)} %copy-done.9) | copy-start | bytes 1572868
  142.3 2.6 %copy-start.16 = (bf16[1,128,2048]{1,2,0:T(8,128)(2,1)S(1)}, bf16[1,128,2048]{1,2,0:T(8,128)(2,1)}, u32[]{:S(2)}) copy-start(bf16[1,128,2048]{1,2,0:T(8,128)(2,1)} %copy-done.15) | copy-start | bytes 1572868
  142.3 4.2 %copy-start.24 = (u32[32]{0:T(128)S(1)}, u32[32]{0:T(128)}, u32[]{:S(2)}) copy-start(u32[32]{0:T(128)} %constant.93) | copy-start | bytes 388
  144.9 1.5 copy-start.20
  144.9 33.4 %copy-start.12 = (bf16[16,128,128]{2,1,0:T(8,128)(2,1)S(1)}, bf16[16,128,128]{2,1,0:T(8,128)(2,1)}, u32[]{:S(2)}) copy-start(bf16[16,128,128]{2,1,0:T(8,128)(2,1)} %copy-done.11) | copy-start | bytes 1572868
  144.9 33.4 %copy-start.14 = (bf16[1,128,16,128]{1,3,2,0:T(8,128)(2,1)S(1)}, bf16[1,128,16,128]{1,3,2,0:T(8,128)(2,1)}, u32[]{:S(2)}) copy-start(bf16[1,128,16,128]{1,3,2,0:T(8,128)(2,1)} %copy-done.13) | copy-start | bytes 1572868
  146.4 57.0 %copy-start.4 = (bf16[128,16,128]{0,2,1:T(8,128)(2,1)S(1)}, bf16[128,16,128]{0,2,1:T(8,128)(2,1)}, u32[]{:S(2)}) copy-start(bf16[128,16,128]{0,2,1:T(8,128)(2,1)} %copy-done.3) | copy-start | bytes 1572868
  146.5 100.8 %all-reduce.4.cloned.1.call-start = ((), (), s32[]{:S(2)}) async-start(), calls=%async_computation.6 | async-start | bytes 524288 | tf_op jit(solution)/shard_map/psum | solution.py:112
Sparse Core Ops, SparseCore 0:
  15.2 55.3 all-gather.4
  83.0 52.6 all-gather.6
  138.0 32.5 reduce-scatter.2
  172.7 30.5 reduce-scatter.4
  206.1 41.1 all-reduce.3
where the time goes:
time: 258 us; the launch traced here: 257 us
  waiting for transfers between devices  155 us (60%)
  matrix products  27.7 us (11%)
  blocking collectives  26.3 us (10%)
  local copies, waits for them, and re-layouts  17.5 us (7%)
  other arithmetic  14.9 us (6%)
  between operations  14.9 us (6%)
    all_gather x2, waiting for transfers between devices, entering(): everything = lax.all_gather(value, axis)  93.4 us
    psum x1, waiting for transfers between devices, per_device(): lax.psum((owned[0], owned[1], owned[2]), 'seq')  40.7 us
    reduce_scatter x1, waiting for transfers between devices, per_device(): lax.psum_scatter(sum_wk, 'dp', scatter_dimension=0, tiled=True)  21.3 us
    unnamed x1, blocking collectives  16.7 us
    select_n x8, other arithmetic, turn(): return jnp.where(reached, new, before)  12.8 us
    unnamed x58, local copies, waits for them, and re-layouts  12.3 us
    psum x1, blocking collectives, per_device(): lax.psum((owned[0], owned[1], owned[2]), 'seq')  9.59 us
  transfers between devices with their start and end apart: 5, of which 4 were waited for; matrix products, arithmetic and copies ran while one was open for 14% of the time, Pallas kernels for 0%

commit v1 on v0

v1 whole, which is shorter than its diff:
```python
import functools

import jax
import jax.numpy as jnp
from jax import lax
from jax.experimental import pallas as pl
from jax.experimental.pallas import tpu as pltpu
from jax.sharding import PartitionSpec as P

HEAD = 128
GROUP = 4
NORM_EPS = 1e-05
F32 = jnp.float32
BF16 = jnp.bfloat16


def dot(a, b, ca=1, cb=0):
    return lax.dot_general(a, b, (((ca,), (cb,)), ((), ())), preferred_element_type=F32)


def feature(pre):
    return jnp.where(pre > 0.0, pre + 1.0, jnp.exp(jnp.minimum(pre, 0.0)))


def split_low(value):
    high = value.astype(BF16)
    return high, (value - high.astype(F32)).astype(BF16)


def tril(rows):
    return lax.broadcasted_iota(jnp.int32, (rows, rows), 0) >= lax.broadcasted_iota(
        jnp.int32, (rows, rows), 1
    )


def columns(offset, i):
    at = (2 * i + offset) * HEAD
    return slice(at, at + HEAD)


def key_kernel(offset, key, value, w_key, feat_key, slope, state):
    for i in range(GROUP):
        at = columns(offset, i)
        feat = feature(dot(key[:, at], w_key[at, :]))
        low = feat.astype(BF16)
        feat_key[i] = low
        slope[i] = jnp.minimum(feat, 1.0)
        state[i] = dot(low, value[:, at], 0, 0)


def query_kernel(offset, query, value, w_query, feat_key, feat_query, slope, attn, inner):
    causal = tril(query.shape[0])
    for i in range(GROUP):
        at = columns(offset, i)
        feat = feature(dot(query[:, at], w_query[at, :]))
        low = feat.astype(BF16)
        feat_query[i] = low
        slope[i] = jnp.minimum(feat, 1.0)
        weights = jnp.where(causal, dot(low, feat_key[i], 1, 1), 0.0).astype(BF16)
        attn[i] = weights
        inner[i] = dot(weights, value[:, at])


def numer_kernel(offset, keep, first, second, feat_query, inner, grad, gain, adjoint, low_out, rest_out, ph_out, pl_out, gain_out):
    keep_first = keep[0] > 0
    keep_second = keep[1] > 0
    for i in range(GROUP):
        at = columns(offset, i)
        prior = jnp.where(keep_first, first[i], 0.0) + jnp.where(keep_second, second[i], 0.0)
        high, low = split_low(prior)
        ph_out[i] = high
        pl_out[i] = low
        feat = feat_query[i]
        numer = inner[i] + dot(feat, high) + dot(feat, low)
        inv = lax.rsqrt(jnp.mean(numer * numer, axis=-1, keepdims=True) + NORM_EPS)
        normed = numer * inv
        grad_f = grad[:, at].astype(F32)
        scaled = grad_f * gain[:, at]
        grad_numer = inv * (scaled - normed * jnp.mean(scaled * normed, axis=-1, keepdims=True))
        gain_out[i] = jnp.broadcast_to(jnp.sum(normed * grad_f, axis=0, keepdims=True), (8, HEAD))
        numer_low, rest = split_low(grad_numer)
        low_out[i] = numer_low
        rest_out[i] = rest
        adjoint[i] = dot(feat, numer_low, 0, 0)


def query_grad_kernel(offset, numer_low, rest, high, low, feat_key, slope, query, value, gain, mixed_out, pre_out, weight):
    causal = tril(query.shape[0])
    rows = HEAD
    for i in range(GROUP):
        at = columns(offset, i)
        grad_low = numer_low[i]
        mixed = jnp.where(causal, dot(grad_low, value[:, at], 1, 1), 0.0).astype(BF16)
        mixed_out[i] = mixed
        grad_fq = (
            dot(mixed, feat_key[i])
            + dot(grad_low, high[i], 1, 1)
            + dot(grad_low, low[i], 1, 1)
            + dot(rest[i], high[i], 1, 1)
        )
        pre = (grad_fq * slope[i]).astype(BF16)
        pre_out[i] = pre
        weight[i, :rows, :] = dot(query[:, at], pre, 0, 0)
        weight[i, rows:, :] = gain[i]


def key_grad_kernel(offset, keep, first, second, mixed, feat_query, slope, key, value, pre_out, lh_out, ll_out, weight):
    keep_first = keep[2] > 0
    keep_second = keep[3] > 0
    for i in range(GROUP):
        at = columns(offset, i)
        later = jnp.where(keep_first, first[i], 0.0) + jnp.where(keep_second, second[i], 0.0)
        high, low = split_low(later)
        lh_out[i] = high
        ll_out[i] = low
        val = value[:, at]
        grad_fk = dot(mixed[i], feat_query[i], 0, 0) + dot(val, high, 1, 1) + dot(val, low, 1, 1)
        pre = (grad_fk * slope[i]).astype(BF16)
        pre_out[i] = pre
        weight[i] = dot(key[:, at], pre, 0, 0)


def back_kernel(groups, *refs):
    pre, w, out = refs[:groups], refs[groups], refs[groups + 1]
    for g in range(groups):
        for i in range(GROUP):
            at = place(g, i, groups)
            out[:, at] = dot(pre[g][i], w[at, :], 1, 1).astype(BF16)


def value_grad_kernel(groups, *refs):
    attn, numer_low, feat_key, high, low = (refs[k * groups : (k + 1) * groups] for k in range(5))
    out = refs[5 * groups]
    for g in range(groups):
        for i in range(GROUP):
            feat = feat_key[g][i]
            grad = dot(attn[g][i], numer_low[g][i], 0, 0) + dot(feat, high[g][i]) + dot(feat, low[g][i])
            out[:, place(g, i, groups)] = grad.astype(BF16)


def head_of(g, i, groups):
    half = groups // 2
    return (g % half) * 2 * GROUP + 2 * i + g // half


def place(g, i, groups):
    at = head_of(g, i, groups) * HEAD
    return slice(at, at + HEAD)


def call(body, ins, outs, name, flops):
    bytes_all = sum(x.size * x.dtype.itemsize for x, _ in ins if x.dtype != jnp.int32)
    return pl.pallas_call(
        body,
        grid=(1,),
        in_specs=[spec for _, spec in ins],
        out_specs=[pl.BlockSpec(shape, lambda _, n=len(shape): (0,) * n) for shape, _ in outs],
        out_shape=[jax.ShapeDtypeStruct(shape, kind) for shape, kind in outs],
        compiler_params=pltpu.CompilerParams(vmem_limit_bytes=48 * 1024 * 1024),
        cost_estimate=pl.CostEstimate(flops=flops, bytes_accessed=bytes_all, transcendentals=0),
        name=name,
    )(*[x for x, _ in ins])


def whole(x):
    return (x, pl.BlockSpec(x.shape, lambda _, n=x.ndim: (0,) * n))


def scan_generic(value, reverse):
    peers, mine = lax.axis_size("seq"), lax.axis_index("seq")
    everything = lax.all_gather(value, "seq")

    def turn(k, before):
        reached = k > mine if reverse else k < mine
        return before + jnp.where(reached, everything[k], 0.0)

    return lax.fori_loop(0, peers, turn, jnp.zeros_like(value))


def swap(value, axis, bit):
    return lax.ppermute(value, axis, [(i, i ^ bit) for i in range(lax.axis_size(axis))])


def pick(value, axis, index):
    first = index == 0
    return jnp.where(first, value[0], value[1]), jnp.where(first, value[1], value[0])


def owned_sum(weights):
    dp = lax.axis_index("dp")
    core, near, far = dp % 2, (dp // 2) % 2, dp // 4
    rows = weights.shape[1]
    by = weights.reshape(4, 2, rows, HEAD)
    kept, sent = pick(by.transpose(1, 0, 2, 3), 0, core)
    part = kept + swap(sent, "dp", 1)
    kept, sent = pick(part.reshape(2, 2, rows, HEAD).transpose(1, 0, 2, 3), 0, near)
    part = kept + swap(sent, "dp", 2)
    kept, sent = pick(part, 0, far)
    return kept + swap(sent, "dp", 4)


def square_sum(value):
    value = value + swap(value, "seq", 1)
    return value + swap(value, "seq", 2)


def per_device(query_in, key_in, value_in, grad_out, w_query, w_key, norm_gain):
    _, rows, width = query_in.shape
    heads = width // HEAD
    groups = heads // GROUP
    half = groups // 2
    tuned = lax.axis_size("seq") == 4 and lax.axis_size("dp") == 8 and heads == 16
    query, key, value, grad = (x.reshape(rows, width) for x in (query_in, key_in, value_in, grad_out))
    gain = norm_gain.reshape(1, width)
    wide = 2 * GROUP * HEAD

    def cols(x, g):
        return (x, pl.BlockSpec((x.shape[0], wide), lambda _: (0, g % half)))

    def wrows(x, g):
        return (x, pl.BlockSpec((wide, HEAD), lambda _: (g % half, 0)))

    mine = lax.axis_index("seq")
    at_x, at_y = mine % 2, mine // 2
    if tuned:
        keep = jnp.stack([at_x, at_y, 1 - at_x, 1 - at_y]).astype(jnp.int32)
    else:
        keep = jnp.array([1, 0, 1, 0], jnp.int32)
    flags = (keep, pl.BlockSpec(memory_space=pltpu.SMEM))

    def tok(kind):
        return ((GROUP, rows, HEAD), kind)

    def sq(kind):
        return ((GROUP, HEAD, HEAD), kind)

    unit = 2 * rows * HEAD * HEAD * GROUP

    def around(states, reverse):
        if not tuned:
            total = scan_generic(states, reverse)
            return total, total
        first = swap(states, "seq", 1)
        return first, swap(states + first, "seq", 2)

    feat_k, slope_k, state = [], [], []
    for g in range(groups):
        f, s, m = call(
            functools.partial(key_kernel, g // half),
            [cols(key, g), cols(value, g), wrows(w_key, g)],
            [tok(BF16), tok(F32), sq(F32)],
            f"key_state_{g}",
            2 * unit,
        )
        feat_k.append(f)
        slope_k.append(s)
        state.append(m)
    prior = [around(m, False) for m in state]
    feat_q, slope_q, attn, inner = [], [], [], []
    for g in range(groups):
        f, s, a, n = call(
            functools.partial(query_kernel, g // half),
            [cols(query, g), cols(value, g), wrows(w_query, g), whole(feat_k[g])],
            [tok(BF16), tok(F32), ((GROUP, rows, rows), BF16), tok(F32)],
            f"query_attn_{g}",
            3 * unit,
        )
        feat_q.append(f)
        slope_q.append(s)
        attn.append(a)
        inner.append(n)
    numer = []
    later = []
    for g in range(groups):
        out = call(
            functools.partial(numer_kernel, g // half),
            [flags, whole(prior[g][0]), whole(prior[g][1]), whole(feat_q[g]), whole(inner[g]), cols(grad, g), cols(gain, g)],
            [sq(F32), tok(BF16), tok(BF16), sq(BF16), sq(BF16), ((GROUP, 8, HEAD), F32)],
            f"numer_{g}",
            3 * unit,
        )
        numer.append(out)
        later.append(around(out[0], True))
    mixed, pre_q, sum_q = [], [], []
    for g in range(groups):
        _, low, rest, ph, pl_, gains = numer[g]
        m, p, w = call(
            functools.partial(query_grad_kernel, g // half),
            [whole(x) for x in (low, rest, ph, pl_, feat_k[g], slope_q[g])] + [cols(query, g), cols(value, g), whole(gains)],
            [((GROUP, rows, rows), BF16), tok(BF16), ((GROUP, HEAD + 8, HEAD), F32)],
            f"query_grad_{g}",
            6 * unit,
        )
        mixed.append(m)
        pre_q.append(p)
        sum_q.append(w)
    pre_k, late_h, late_l, sum_k = [], [], [], []
    for g in range(groups):
        p, h, l, w = call(
            functools.partial(key_grad_kernel, g // half),
            [flags, whole(later[g][0]), whole(later[g][1]), whole(mixed[g]), whole(feat_q[g]), whole(slope_k[g]), cols(key, g), cols(value, g)],
            [tok(BF16), sq(BF16), sq(BF16), sq(F32)],
            f"key_grad_{g}",
            4 * unit,
        )
        pre_k.append(p)
        late_h.append(h)
        late_l.append(l)
        sum_k.append(w)

    full = [((rows, width), BF16)]
    (grad_query,) = call(
        functools.partial(back_kernel, groups), [whole(x) for x in pre_q] + [whole(w_query)], full, "grad_query", groups * unit
    )
    (grad_key,) = call(
        functools.partial(back_kernel, groups), [whole(x) for x in pre_k] + [whole(w_key)], full, "grad_key", groups * unit
    )
    (grad_value,) = call(
        functools.partial(value_grad_kernel, groups),
        [whole(x) for x in attn + [n[1] for n in numer] + feat_k + late_h + late_l],
        full,
        "grad_value",
        3 * groups * unit,
    )

    if tuned:
        halves = [jnp.concatenate(sum_q[b * half : (b + 1) * half], axis=0) for b in range(2)]
        part_q = owned_sum(jnp.concatenate(halves, axis=1))
        part_k = [
            owned_sum(jnp.concatenate(sum_k[b * half : (b + 1) * half], axis=0)) for b in range(2)
        ]
        early = square_sum(jnp.concatenate([part_q, part_k[0]], axis=0))
        last = square_sum(part_k[1])
        step = HEAD + 8
        total_q = jnp.concatenate([early[:HEAD], early[step : step + HEAD]], axis=0)
        total_gain = jnp.concatenate([early[HEAD], early[step + HEAD]], axis=0)
        total_k = jnp.concatenate([early[2 * step :], last], axis=0)
    else:

        def in_order(parts):
            spread = [None] * heads
            for g in range(groups):
                for i in range(GROUP):
                    spread[head_of(g, i, groups)] = parts[g][i]
            return jnp.stack(spread)

        both = in_order(sum_q)
        owned = (
            lax.psum_scatter(both[:, :HEAD].reshape(width, HEAD), "dp", scatter_dimension=0, tiled=True),
            lax.psum_scatter(in_order(sum_k).reshape(width, HEAD), "dp", scatter_dimension=0, tiled=True),
            lax.psum_scatter(both[:, HEAD].reshape(width), "dp", scatter_dimension=0, tiled=True),
        )
        total_q, total_k, total_gain = lax.psum(owned, "seq")
    shape = query_in.shape
    return (
        grad_query.reshape(shape),
        grad_key.reshape(shape),
        grad_value.reshape(shape),
        total_q,
        total_k,
        total_gain,
    )


def solution(mesh):
    split = P("dp", "seq", None)
    return jax.shard_map(
        per_device,
        mesh=mesh,
        in_specs=(split, split, split, split, P(), P(), P()),
        out_specs=(split, split, split, P("dp", None), P("dp", None), P("dp")),
        check_vma=False,
    )
```

time: 258 us -> 136 us (0.53)
  waiting for transfers between devices: 155 us -> 41.6 us
  Pallas kernels: 0 us -> 35.1 us
  starting transfers between devices: 0.21 us -> 34.9 us
  matrix products: 27.7 us -> 0 us
  blocking collectives: 26.3 us -> 0 us
  between operations: 14.9 us -> 1.36 us
  other arithmetic: 14.9 us -> 8.72 us
  local copies, waits for them, and re-layouts: 17.5 us -> 13.4 us
    all_gather x2 -> x0, waiting for transfers between devices: 93.4 us -> none  [entering(): everything = lax.all_gather(value, axis)]
    ppermute x0 -> x29, waiting for transfers between devices: none -> 41.6 us  [swap(): lax.ppermute(value, axis, [(i, i ^ bit) for i in range(lax.axis_size(axis...]
    psum x1 -> x0, waiting for transfers between devices: 40.7 us -> none  [per_device(): lax.psum((owned[0], owned[1], owned[2]), 'seq')]
    pallas_call x0 -> x23, Pallas kernels: none -> 35.1 us  [call(): pl.pallas_call(body, grid=(1,), in_specs=[spec for _, spec in ins], out_s...]
    ppermute x0 -> x29, starting transfers between devices: none -> 34.9 us  [swap(): lax.ppermute(value, axis, [(i, i ^ bit) for i in range(lax.axis_size(axis...]
    dot_general x18 -> x0, matrix products: 27.7 us -> none  [the longest x1 2.55 us: per_device(): jnp.einsum('bshe,bhfe->bshf', value_h.astype(jnp.float32), later_state, p...]
    reduce_scatter x2 -> x0, waiting for transfers between devices: 21.3 us -> none  [the longest x1 21.3 us: per_device(): lax.psum_scatter(sum_wk, 'dp', scatter_dimension=0, tiled=True)]
    unnamed x1 -> x0, blocking collectives: 16.7 us -> none
  transfers between devices with their start and end apart: 5 -> 29, of which waited for: 4 -> 15; matrix products, arithmetic and copies ran while one was open for 14% -> 5% of each run, Pallas kernels for 0% -> 26%
where the time goes in v1:
time: 136 us; the launch traced here: 135 us
  waiting for transfers between devices  41.6 us (31%)
  Pallas kernels  35.1 us (26%)
  starting transfers between devices  34.9 us (26%)
  local copies, waits for them, and re-layouts  13.4 us (10%)
  other arithmetic  8.72 us (6%)
  between operations  1.36 us (1%)
    ppermute x29, waiting for transfers between devices, swap(): lax.ppermute(value, axis, [(i, i ^ bit) for i in range(lax.axis_size(axis...  41.6 us
    pallas_call x23, Pallas kernels, call(): pl.pallas_call(body, grid=(1,), in_specs=[spec for _, spec in ins], out_s...  35.1 us
    ppermute x29, starting transfers between devices, swap(): lax.ppermute(value, axis, [(i, i ^ bit) for i in range(lax.axis_size(axis...  34.9 us
    unnamed x100, local copies, waits for them, and re-layouts  13.2 us
    add x8, other arithmetic, around(): return (first, swap(states + first, 'seq', 2))  5.98 us
  transfers between devices with their start and end apart: 29, of which 15 were waited for; matrix products, arithmetic and copies ran while one was open for 5% of the time, Pallas kernels for 26%

profile of v1, /device:TPU:0, one launch (start us, length us, event | category | flops | bytes accessed | tf_op | source)
XLA Modules:
  0.0 135.0 jit_solution(5636171891142816786)
XLA Ops:
  4.2 3.0 %collective-permute-start = (f32[4,128,128]{2,1,0:T(8,128)S(1)}, f32[4,128,128]{2,1,0:T(8,128)S(1)}, u32[]{:S(2)}, u32[]{:S(2)}) collective-permute-start(f32[4,128,128]{2,1,0:T(8,128)S(1)} %get-tuple-element.86), channel_id=1, source_target_pairs={{0,1},{1,0},{2,3},{3,2},{4,5},{5,4},{6,7},{7,6},{8,9},{9,8},{10,11... | collective-permute-start | bytes 786440 | tf_op jit(solution)/shard_map/ppermute | solution.py:181
  10.1 2.0 %collective-permute-start.6 = (f32[4,128,128]{2,1,0:T(8,128)}, f32[4,128,128]{2,1,0:T(8,128)S(1)}, u32[]{:S(2)}, u32[]{:S(2)}) collective-permute-start(f32[4,128,128]{2,1,0:T(8,128)} %get-tuple-element.119), channel_id=1, source_target_pairs={{0,1},{1,0},{2,3},{3,2},{4,5},{5,4},{6,7},{7,6},{8,9},{9,8},{10,11... | collective-permute-start | bytes 786440 | tf_op jit(solution)/shard_map/ppermute | solution.py:181
  12.6 1.7 %collective-permute-done.first = f32[4,128,128]{2,1,0:T(8,128)S(1)} collective-permute-done((f32[4,128,128]{2,1,0:T(8,128)S(1)}, f32[4,128,128]{2,1,0:T(8,128)S(1)}, u32[]{:S(2)}, u32[]{:S(2)}) %collective-permute-start) | collective-permute-done | bytes 262176 | tf_op jit(solution)/shard_map/ppermute | solution.py:181
  15.0 2.1 %collective-permute-start.1 = (f32[4,128,128]{2,1,0:T(8,128)}, f32[4,128,128]{2,1,0:T(8,128)}, u32[]{:S(2)}, u32[]{:S(2)}) collective-permute-start(f32[4,128,128]{2,1,0:T(8,128)} %add.81), channel_id=1, source_target_pairs={{0,2},{1,3},{2,0},{3,1},{4,6},{5,7},{6,4},{7,5},{8,10},{9,11},{10,... | collective-permute-start | bytes 786440 | tf_op jit(solution)/shard_map/ppermute | solution.py:181
  17.1 2.8 %collective-permute-done.2.first = f32[4,128,128]{2,1,0:T(8,128)S(1)} collective-permute-done((f32[4,128,128]{2,1,0:T(8,128)S(1)}, f32[4,128,128]{2,1,0:T(8,128)S(1)}, u32[]{:S(2)}, u32[]{:S(2)}) %collective-permute-start.2) | collective-permute-done | bytes 262176 | tf_op jit(solution)/shard_map/ppermute | solution.py:181
  20.7 2.1 %collective-permute-start.3 = (f32[4,128,128]{2,1,0:T(8,128)}, f32[4,128,128]{2,1,0:T(8,128)}, u32[]{:S(2)}, u32[]{:S(2)}) collective-permute-start(f32[4,128,128]{2,1,0:T(8,128)} %add.82), channel_id=1, source_target_pairs={{0,2},{1,3},{2,0},{3,1},{4,6},{5,7},{6,4},{7,5},{8,10},{9,11},{10,... | collective-permute-start | bytes 786440 | tf_op jit(solution)/shard_map/ppermute | solution.py:181
  22.7 2.8 %collective-permute-done.6.first = f32[4,128,128]{2,1,0:T(8,128)S(1)} collective-permute-done((f32[4,128,128]{2,1,0:T(8,128)}, f32[4,128,128]{2,1,0:T(8,128)S(1)}, u32[]{:S(2)}, u32[]{:S(2)}) %collective-permute-start.6) | collective-permute-done | bytes 262176 | tf_op jit(solution)/shard_map/ppermute | solution.py:181
  25.5 1.7 %add.84 = f32[4,128,128]{2,1,0:T(8,128)} add(f32[4,128,128]{2,1,0:T(8,128)} %get-tuple-element.119, f32[4,128,128]{2,1,0:T(8,128)S(1)} %collective-permute-done.6.first) | non-fusion elementwise | flops 65536 | bytes 786432 | tf_op jit(solution)/shard_map/add | solution.py:244
  27.2 2.1 %collective-permute-start.7 = (f32[4,128,128]{2,1,0:T(8,128)}, f32[4,128,128]{2,1,0:T(8,128)}, u32[]{:S(2)}, u32[]{:S(2)}) collective-permute-start(f32[4,128,128]{2,1,0:T(8,128)} %add.84), channel_id=1, source_target_pairs={{0,2},{1,3},{2,0},{3,1},{4,6},{5,7},{6,4},{7,5},{8,10},{9,11},{10,... | collective-permute-start | bytes 786440 | tf_op jit(solution)/shard_map/ppermute | solution.py:181
  31.1 1.8 %collective-permute-start.5 = (f32[4,128,128]{2,1,0:T(8,128)}, f32[4,128,128]{2,1,0:T(8,128)}, u32[]{:S(2)}, u32[]{:S(2)}) collective-permute-start(f32[4,128,128]{2,1,0:T(8,128)} %add.83), channel_id=1, source_target_pairs={{0,2},{1,3},{2,0},{3,1},{4,6},{5,7},{6,4},{7,5},{8,10},{9,11},{10,... | collective-permute-start | bytes 786440 | tf_op jit(solution)/shard_map/ppermute | solution.py:181
  33.0 1.2 query_attn_0.1
  35.5 1.2 query_attn_1.1
  38.1 3.2 %numer_0.1 = (f32[4,128,128]{2,1,0:T(8,128)}, bf16[4,128,128]{2,1,0:T(8,128)(2,1)S(1)}, bf16[4,128,128]{2,1,0:T(8,128)(2,1)S(1)}, bf16[4,128,128]{2,1,0:T(8,128)...) custom-call(s32[4]{0:T(128)S(1)} %pad_add_fusion.keep, ...), custom_call_target="tpu_custom_call" | custom-call | flops 50331648 | bytes 1449984 | tf_op jit(solution)/shard_map/numer_0/pallas_call | solution.py:153
  43.9 1.5 %collective-permute-start.8 = (f32[4,128,128]{2,1,0:T(8,128)}, f32[4,128,128]{2,1,0:T(8,128)S(1)}, u32[]{:S(2)}, u32[]{:S(2)}) collective-permute-start(f32[4,128,128]{2,1,0:T(8,128)} %get-tuple-element.130), channel_id=1, source_target_pairs={{0,1},{1,0},{2,3},{3,2},{4,5},{5,4},{6,7},{7,6},{8,9},{9,8},{10,11... | collective-permute-start | bytes 786440 | tf_op jit(solution)/shard_map/ppermute | solution.py:181
  45.4 3.2 %numer_1.1 = (f32[4,128,128]{2,1,0:T(8,128)}, bf16[4,128,128]{2,1,0:T(8,128)(2,1)S(1)}, bf16[4,128,128]{2,1,0:T(8,128)(2,1)S(1)}, bf16[4,128,128]{2,1,0:T(8,128)...) custom-call(s32[4]{0:T(128)S(1)} %pad_add_fusion.keep, ...), custom_call_target="tpu_custom_call" | custom-call | flops 50331648 | bytes 1449984 | tf_op jit(solution)/shard_map/numer_1/pallas_call | solution.py:153
  52.4 1.2 query_attn_2.1
  53.6 1.2 query_attn_3.1
  54.8 2.5 %numer_2.1 = (f32[4,128,128]{2,1,0:T(8,128)S(1)}, bf16[4,128,128]{2,1,0:T(8,128)(2,1)S(1)}, bf16[4,128,128]{2,1,0:T(8,128)(2,1)S(1)}, bf16[4,128,128]{2,1,0:T(8,...) custom-call(s32[4]{0:T(128)S(1)} %pad_add_fusion.keep, f32[4,128,128]{2,1,0:T(8,128)S(1)} %copy-done.10, ...), custom_call_target="tpu_custom_call" | custom-call | flops 50331648 | bytes 1449984 | tf_op jit(solution)/shard_map/numer_2/pallas_call | solution.py:153
  57.4 1.6 %collective-permute-start.12 = (f32[4,128,128]{2,1,0:T(8,128)S(1)}, f32[4,128,128]{2,1,0:T(8,128)S(1)}, u32[]{:S(2)}, u32[]{:S(2)}) collective-permute-start(f32[4,128,128]{2,1,0:T(8,128)S(1)} %get-tuple-element.138), channel_id=1, source_target_pairs={{0,1},{1,0},{2,3},{3,2},{4,5},{5,4},{6,7},{7,6},{8,9},{9,8},{10,11... | collective-permute-start | bytes 786440 | tf_op jit(solution)/shard_map/ppermute | solution.py:181
  59.0 2.5 %numer_3.1 = (f32[4,128,128]{2,1,0:T(8,128)S(1)}, bf16[4,128,128]{2,1,0:T(8,128)(2,1)S(1)}, bf16[4,128,128]{2,1,0:T(8,128)(2,1)S(1)}, bf16[4,128,128]{2,1,0:T(8,...) custom-call(s32[4]{0:T(128)S(1)} %pad_add_fusion.keep, ...), custom_call_target="tpu_custom_call" | custom-call | flops 50331648 | bytes 1449984 | tf_op jit(solution)/shard_map/numer_3/pallas_call | solution.py:153
  62.1 1.6 %query_grad_0.1 = (bf16[4,128,128]{2,1,0:T(8,128)(2,1)S(1)}, bf16[4,128,128]{2,1,0:T(8,128)(2,1)S(1)}, f32[4,136,128]{2,1,0:T(8,128)S(1)}) custom-call(bf16[4,128,128]{2,1,0:T(8,128)(2,1)S(1)} %copy-done.14, bf16[4,128,128]{2,1,0:T(8,128)(2,1)S(1)} %copy-done.35, bf16[4,128,128]{2,1,0:T(8,128)(2,1)S(1)} %copy-done.37, bf16[4,128,128]{2,1,0:T(8,128)(2,1)S(1)} %copy-done.39, ...), custom_call_target="tpu_custom_call" | custom-call | flops 100663296 | bytes 1982464 | tf_op jit(solution)/shard_map/query_grad_0/pallas_call | solution.py:153
  63.8 1.6 %query_grad_1.1 = (bf16[4,128,128]{2,1,0:T(8,128)(2,1)S(1)}, bf16[4,128,128]{2,1,0:T(8,128)(2,1)S(1)}, f32[4,136,128]{2,1,0:T(8,128)S(1)}) custom-call(bf16[4,128,128]{2,1,0:T(8,128)(2,1)S(1)} %copy-done.16, bf16[4,128,128]{2,1,0:T(8,128)(2,1)S(1)} %copy-done.41, bf16[4,128,128]{2,1,0:T(8,128)(2,1)S(1)} %copy-done.43, bf16[4,128,128]{2,1,0:T(8,128)(2,1)S(1)} %copy-done.45, ...), custom_call_target="tpu_custom_call" | custom-call | flops 100663296 | bytes 1982464 | tf_op jit(solution)/shard_map/query_grad_1/pallas_call | solution.py:153
  65.4 1.6 %query_grad_2.1 = (bf16[4,128,128]{2,1,0:T(8,128)(2,1)S(1)}, bf16[4,128,128]{2,1,0:T(8,128)(2,1)S(1)}, f32[4,136,128]{2,1,0:T(8,128)S(1)}) custom-call(bf16[4,128,128]{2,1,0:T(8,128)(2,1)S(1)} %get-tuple-element.112.numer_low.refs_6_, bf16[4,128,128]{2,1,0:T(8,128)(2,1)S(1)} %get-tuple-element.113.rest, bf16[4,128,128]{2,1,0:T(8,128)(2,1)S(1)} %get-tuple-element.114.high, ...), custom_call_target="tpu_custom_call" | custom-call | flops 100663296 | bytes 1982464 | tf_op jit(solution)/shard_map/query_grad_2/pallas_call | solution.py:153
  67.0 1.6 %query_grad_3.1 = (bf16[4,128,128]{2,1,0:T(8,128)(2,1)S(1)}, bf16[4,128,128]{2,1,0:T(8,128)(2,1)S(1)}, f32[4,136,128]{2,1,0:T(8,128)S(1)}) custom-call(bf16[4,128,128]{2,1,0:T(8,128)(2,1)S(1)} %get-tuple-element.123.numer_low.refs_7_, bf16[4,128,128]{2,1,0:T(8,128)(2,1)S(1)} %get-tuple-element.124.rest, bf16[4,128,128]{2,1,0:T(8,128)(2,1)S(1)} %get-tuple-element.125.high, ...), custom_call_target="tpu_custom_call" | custom-call | flops 100663296 | bytes 1982464 | tf_op jit(solution)/shard_map/query_grad_3/pallas_call | solution.py:153
  70.9 1.8 %collective-permute-start.11 = (f32[4,128,128]{2,1,0:T(8,128)S(1)}, f32[4,128,128]{2,1,0:T(8,128)S(1)}, u32[]{:S(2)}, u32[]{:S(2)}) collective-permute-start(f32[4,128,128]{2,1,0:T(8,128)S(1)} %add.86), channel_id=1, source_target_pairs={{0,2},{1,3},{2,0},{3,1},{4,6},{5,7},{6,4},{7,5},{8,10},{9,11},{10,... | collective-permute-start | bytes 786440 | tf_op jit(solution)/shard_map/ppermute | solution.py:181
  73.5 1.8 %collective-permute-start.15 = (f32[4,128,128]{2,1,0:T(8,128)S(1)}, f32[4,128,128]{2,1,0:T(8,128)S(1)}, u32[]{:S(2)}, u32[]{:S(2)}) collective-permute-start(f32[4,128,128]{2,1,0:T(8,128)S(1)} %add.88), channel_id=1, source_target_pairs={{0,2},{1,3},{2,0},{3,1},{4,6},{5,7},{6,4},{7,5},{8,10},{9,11},{10,... | collective-permute-start | bytes 786440 | tf_op jit(solution)/shard_map/ppermute | solution.py:181
  75.3 3.6 %collective-permute-done.9.second = f32[4,128,128]{2,1,0:T(8,128)S(1)} collective-permute-done((f32[4,128,128]{2,1,0:T(8,128)S(1)}, f32[4,128,128]{2,1,0:T(8,128)S(1)}, u32[]{:S(2)}, u32[]{:S(2)}) %collective-permute-start.9) | collective-permute-done | bytes 262176 | tf_op jit(solution)/shard_map/ppermute | solution.py:181
  78.9 1.6 %key_grad_0.1 = (bf16[4,128,128]{2,1,0:T(8,128)(2,1)S(1)}, bf16[4,128,128]{2,1,0:T(8,128)(2,1)S(1)}, bf16[4,128,128]{2,1,0:T(8,128)(2,1)S(1)}, f32[4,128,128]{2,1,0:T(8,128)S(1)}) custom-call(s32[4]{0:T(128)S(1)} %pad_add_fusion.keep, f32[4,128,128]{2,1,0:T(8,128)S(1)} %collective-permute-done.8.first, f32[4,128,128]{2,1,0:T(8,128)S(1)} %collective-permute-done.9.second, ...), custom_call_target="tpu_custom_call" | custom-call | flops 67108864 | bytes 2097152 | tf_op jit(solution)/shard_map/key_grad_0/pallas_call | solution.py:153
  80.5 4.0 %collective-permute-done.11.second = f32[4,128,128]{2,1,0:T(8,128)S(1)} collective-permute-done((f32[4,128,128]{2,1,0:T(8,128)S(1)}, f32[4,128,128]{2,1,0:T(8,128)S(1)}, u32[]{:S(2)}, u32[]{:S(2)}) %collective-permute-start.11) | collective-permute-done | bytes 262176 | tf_op jit(solution)/shard_map/ppermute | solution.py:181
  84.5 1.6 %key_grad_1.1 = (bf16[4,128,128]{2,1,0:T(8,128)(2,1)S(1)}, bf16[4,128,128]{2,1,0:T(8,128)(2,1)S(1)}, bf16[4,128,128]{2,1,0:T(8,128)(2,1)S(1)}, f32[4,128,128]{2,1,0:T(8,128)S(1)}) custom-call(s32[4]{0:T(128)S(1)} %pad_add_fusion.keep, f32[4,128,128]{2,1,0:T(8,128)S(1)} %collective-permute-done.10.first, f32[4,128,128]{2,1,0:T(8,128)S(1)} %collective-permute-done.11.second, ...), custom_call_target="tpu_custom_call" | custom-call | flops 67108864 | bytes 2097152 | tf_op jit(solution)/shard_map/key_grad_1/pallas_call | solution.py:153
  86.4 3.1 %collective-permute-done.13.second = f32[4,128,128]{2,1,0:T(8,128)S(1)} collective-permute-done((f32[4,128,128]{2,1,0:T(8,128)S(1)}, f32[4,128,128]{2,1,0:T(8,128)S(1)}, u32[]{:S(2)}, u32[]{:S(2)}) %collective-permute-start.13) | collective-permute-done | bytes 262176 | tf_op jit(solution)/shard_map/ppermute | solution.py:181
  89.5 1.6 %key_grad_2.1 = (bf16[4,128,128]{2,1,0:T(8,128)(2,1)S(1)}, bf16[4,128,128]{2,1,0:T(8,128)(2,1)S(1)}, bf16[4,128,128]{2,1,0:T(8,128)(2,1)S(1)}, f32[4,128,128]{2,1,0:T(8,128)S(1)}) custom-call(s32[4]{0:T(128)S(1)} %pad_add_fusion.keep, f32[4,128,128]{2,1,0:T(8,128)S(1)} %collective-permute-done.12.first, f32[4,128,128]{2,1,0:T(8,128)S(1)} %collective-permute-done.13.second, ...), custom_call_target="tpu_custom_call" | custom-call | flops 67108864 | bytes 2097152 | tf_op jit(solution)/shard_map/key_grad_2/pallas_call | solution.py:153
  91.1 1.2 collective-permute-done.15.second
  92.3 1.6 %key_grad_3.1 = (bf16[4,128,128]{2,1,0:T(8,128)(2,1)S(1)}, bf16[4,128,128]{2,1,0:T(8,128)(2,1)S(1)}, bf16[4,128,128]{2,1,0:T(8,128)(2,1)S(1)}, f32[4,128,128]{2,1,0:T(8,128)S(1)}) custom-call(s32[4]{0:T(128)S(1)} %pad_add_fusion.keep, f32[4,128,128]{2,1,0:T(8,128)S(1)} %collective-permute-done.14.first, f32[4,128,128]{2,1,0:T(8,128)S(1)} %collective-permute-done.15.second, ...), custom_call_target="tpu_custom_call" | custom-call | flops 67108864 | bytes 2097152 | tf_op jit(solution)/shard_map/key_grad_3/pallas_call | solution.py:153
  94.2 1.6 %collective-permute-start.17 = (f32[2,272,128]{2,1,0:T(8,128)S(1)}, f32[2,272,128]{2,1,0:T(8,128)S(1)}, u32[]{:S(2)}, u32[]{:S(2)}) collective-permute-start(f32[2,272,128]{2,1,0:T(8,128)S(1)} %select_bitcast_fusion.1), channel_id=1, source_target_pairs={{0,8},{4,12},{8,0},{12,4},{16,24},{20,28},{24,16},{28,20},{1,9},{5... | collective-permute-start | bytes 835592 | tf_op jit(solution)/shard_map/ppermute | solution.py:181
  96.6 1.6 %collective-permute-start.25 = (f32[2,128,128]{2,1,0:T(8,128)S(1)}, f32[2,128,128]{2,1,0:T(8,128)S(1)}, u32[]{:S(2)}, u32[]{:S(2)}) collective-permute-start(f32[2,128,128]{2,1,0:T(8,128)S(1)} %select_bitcast_fusion.5), channel_id=1, source_target_pairs={{0,8},{4,12},{8,0},{12,4},{16,24},{20,28},{24,16},{28,20},{1,9},{5... | collective-permute-start | bytes 393224 | tf_op jit(solution)/shard_map/ppermute | solution.py:181
  98.2 5.5 %collective-permute-done.17 = f32[2,272,128]{2,1,0:T(8,128)S(1)} collective-permute-done((f32[2,272,128]{2,1,0:T(8,128)S(1)}, f32[2,272,128]{2,1,0:T(8,128)S(1)}, u32[]{:S(2)}, u32[]{:S(2)}) %collective-permute-start.17) | collective-permute-done | bytes 278560 | tf_op jit(solution)/shard_map/ppermute | solution.py:181
  103.8 2.7 %collective-permute-start.18 = (f32[272,128]{1,0:T(8,128)S(1)}, f32[272,128]{1,0:T(8,128)S(1)}, u32[]{:S(2)}, u32[]{:S(2)}) collective-permute-start(f32[272,128]{1,0:T(8,128)S(1)} %select_bitcast_fusion.4), channel_id=1, source_target_pairs={{0,16},{4,20},{8,24},{12,28},{16,0},{20,4},{24,8},{28,12},{1,17},{... | collective-permute-start | bytes 417800 | tf_op jit(solution)/shard_map/ppermute | solution.py:181
  106.6 2.7 %collective-permute-start.21 = (f32[128,128]{1,0:T(8,128)S(1)}, f32[128,128]{1,0:T(8,128)S(1)}, u32[]{:S(2)}, u32[]{:S(2)}) collective-permute-start(f32[128,128]{1,0:T(8,128)S(1)} %select_bitcast_fusion.8), channel_id=1, source_target_pairs={{0,16},{4,20},{8,24},{12,28},{16,0},{20,4},{24,8},{28,12},{1,17},{... | collective-permute-start | bytes 196616 | tf_op jit(solution)/shard_map/ppermute | solution.py:181
  109.3 3.6 %collective-permute-done.25 = f32[2,128,128]{2,1,0:T(8,128)S(1)} collective-permute-done((f32[2,128,128]{2,1,0:T(8,128)S(1)}, f32[2,128,128]{2,1,0:T(8,128)S(1)}, u32[]{:S(2)}, u32[]{:S(2)}) %collective-permute-start.25) | collective-permute-done | bytes 131104 | tf_op jit(solution)/shard_map/ppermute | solution.py:181
  113.0 3.0 %collective-permute-done.21 = f32[128,128]{1,0:T(8,128)S(1)} collective-permute-done((f32[128,128]{1,0:T(8,128)S(1)}, f32[128,128]{1,0:T(8,128)S(1)}, u32[]{:S(2)}, u32[]{:S(2)}) %collective-permute-start.21) | collective-permute-done | bytes 65568 | tf_op jit(solution)/shard_map/ppermute | solution.py:181
  116.0 1.6 %collective-permute-start.22 = (f32[400,128]{1,0:T(8,128)S(1)}, f32[400,128]{1,0:T(8,128)S(1)}, u32[]{:S(2)}, u32[]{:S(2)}) collective-permute-start(f32[400,128]{1,0:T(8,128)S(1)} %pad_maximum_fusion.2), channel_id=1, source_target_pairs={{0,1},{1,0},{2,3},{3,2},{4,5},{5,4},{6,7},{7,6},{8,9},{9,8},{10,11... | collective-permute-start | bytes 614408 | tf_op jit(solution)/shard_map/ppermute | solution.py:181
  117.6 4.9 %collective-permute-done.22 = f32[400,128]{1,0:T(8,128)S(1)} collective-permute-done((f32[400,128]{1,0:T(8,128)S(1)}, f32[400,128]{1,0:T(8,128)S(1)}, u32[]{:S(2)}, u32[]{:S(2)}) %collective-permute-start.22) | collective-permute-done | bytes 204832 | tf_op jit(solution)/shard_map/ppermute | solution.py:181
  124.3 3.5 %collective-permute-done.27 = f32[128,128]{1,0:T(8,128)S(1)} collective-permute-done((f32[128,128]{1,0:T(8,128)S(1)}, f32[128,128]{1,0:T(8,128)S(1)}, u32[]{:S(2)}, u32[]{:S(2)}) %collective-permute-start.27) | collective-permute-done | bytes 65568 | tf_op jit(solution)/shard_map/ppermute | solution.py:181
  127.9 1.2 collective-permute-start.28
  129.1 1.3 grad_query.1
  130.4 1.3 grad_key.1
  131.7 1.4 %grad_value.1 = bf16[128,2048]{1,0:T(8,128)(2,1)} custom-call(bf16[4,128,128]{2,1,0:T(8,128)(2,1)S(1)} %copy-done.31, bf16[4,128,128]{2,1,0:T(8,128)(2,1)S(1)} %copy-done.33, bf16[4,128,128]{2,1,0:T(8,128)(2,1)S(1)} %get-tuple-element.148.refs_2_, bf16[4,128,128]{2,1,0:T(8,128)(2,1)S(1)} %get-tuple-element.149.refs_3_, bf16[4,128,128]{2,1,0:T(8,128)(2,1)S(1)} %copy-done.14, ...), custom_call_target="tpu_custom_call" | custom-call | flops 201326592 | bytes 2621440 | tf_op jit(solution)/shard_map/grad_value/pallas_call | solution.py:153
  (178 shorter events, 28.3 us)
Async XLA Ops:
  4.2 4.1 %copy-start.23 = (f32[4,128,128]{2,1,0:T(8,128)}, f32[4,128,128]{2,1,0:T(8,128)S(1)}, u32[]{:S(2)}) copy-start(f32[4,128,128]{2,1,0:T(8,128)S(1)} %get-tuple-element.132.slope) | copy-start | bytes 786436
  4.2 10.1 %collective-permute-start = (f32[4,128,128]{2,1,0:T(8,128)S(1)}, f32[4,128,128]{2,1,0:T(8,128)S(1)}, u32[]{:S(2)}, u32[]{:S(2)}) collective-permute-start(f32[4,128,128]{2,1,0:T(8,128)S(1)} %get-tuple-element.86), channel_id=1, source_target_pairs={{0,1},{1,0},{2,3},{3,2},{4,5},{5,4},{6,7},{7,6},{8,9},{9,8},{10,11... | collective-permute-start | bytes 786440 | tf_op jit(solution)/shard_map/ppermute | solution.py:181
  8.3 11.6 %collective-permute-start.2 = (f32[4,128,128]{2,1,0:T(8,128)S(1)}, f32[4,128,128]{2,1,0:T(8,128)S(1)}, u32[]{:S(2)}, u32[]{:S(2)}) collective-permute-start(f32[4,128,128]{2,1,0:T(8,128)S(1)} %get-tuple-element.97), channel_id=1, source_target_pairs={{0,1},{1,0},{2,3},{3,2},{4,5},{5,4},{6,7},{7,6},{8,9},{9,8},{10,11... | collective-permute-start | bytes 786440 | tf_op jit(solution)/shard_map/ppermute | solution.py:181
  10.1 15.4 %collective-permute-start.6 = (f32[4,128,128]{2,1,0:T(8,128)}, f32[4,128,128]{2,1,0:T(8,128)S(1)}, u32[]{:S(2)}, u32[]{:S(2)}) collective-permute-start(f32[4,128,128]{2,1,0:T(8,128)} %get-tuple-element.119), channel_id=1, source_target_pairs={{0,1},{1,0},{2,3},{3,2},{4,5},{5,4},{6,7},{7,6},{8,9},{9,8},{10,11... | collective-permute-start | bytes 786440 | tf_op jit(solution)/shard_map/ppermute | solution.py:181
  12.5 7.4 %copy-start.19 = (f32[4,128,128]{2,1,0:T(8,128)}, f32[4,128,128]{2,1,0:T(8,128)S(1)}, u32[]{:S(2)}) copy-start(f32[4,128,128]{2,1,0:T(8,128)S(1)} %get-tuple-element.140.slope) | copy-start | bytes 786436
  12.5 17.8 %collective-permute-start.4 = (f32[4,128,128]{2,1,0:T(8,128)S(1)}, f32[4,128,128]{2,1,0:T(8,128)S(1)}, u32[]{:S(2)}, u32[]{:S(2)}) collective-permute-start(f32[4,128,128]{2,1,0:T(8,128)S(1)} %get-tuple-element.108), channel_id=1, source_target_pairs={{0,1},{1,0},{2,3},{3,2},{4,5},{5,4},{6,7},{7,6},{8,9},{9,8},{10,11... | collective-permute-start | bytes 786440 | tf_op jit(solution)/shard_map/ppermute | solution.py:181
  15.0 18.0 %copy-start.1 = (bf16[1,128,2048]{2,1,0:T(8,128)(2,1)S(1)}, bf16[1,128,2048]{2,1,0:T(8,128)(2,1)}, u32[]{:S(2)}) copy-start(bf16[1,128,2048]{2,1,0:T(8,128)(2,1)} %param.9) | copy-start | bytes 1572868
  15.0 18.0 %copy-start.4 = (bf16[1,128,2048]{2,1,0:T(8,128)(2,1)S(1)}, bf16[1,128,2048]{2,1,0:T(8,128)(2,1)}, u32[]{:S(2)}) copy-start(bf16[1,128,2048]{2,1,0:T(8,128)(2,1)} %param.7) | copy-start | bytes 1572868
  15.0 18.0 %copy-start.7 = (bf16[2048,128]{1,0:T(8,128)(2,1)S(1)}, bf16[2048,128]{1,0:T(8,128)(2,1)}, u32[]{:S(2)}) copy-start(bf16[2048,128]{1,0:T(8,128)(2,1)} %refs_4_.2) | copy-start | bytes 1572868
  15.0 23.1 %collective-permute-start.1 = (f32[4,128,128]{2,1,0:T(8,128)}, f32[4,128,128]{2,1,0:T(8,128)}, u32[]{:S(2)}, u32[]{:S(2)}) collective-permute-start(f32[4,128,128]{2,1,0:T(8,128)} %add.81), channel_id=1, source_target_pairs={{0,2},{1,3},{2,0},{3,1},{4,6},{5,7},{6,4},{7,5},{8,10},{9,11},{10,... | collective-permute-start | bytes 786440 | tf_op jit(solution)/shard_map/ppermute | solution.py:181
  20.7 24.8 %collective-permute-start.3 = (f32[4,128,128]{2,1,0:T(8,128)}, f32[4,128,128]{2,1,0:T(8,128)}, u32[]{:S(2)}, u32[]{:S(2)}) collective-permute-start(f32[4,128,128]{2,1,0:T(8,128)} %add.82), channel_id=1, source_target_pairs={{0,2},{1,3},{2,0},{3,1},{4,6},{5,7},{6,4},{7,5},{8,10},{9,11},{10,... | collective-permute-start | bytes 786440 | tf_op jit(solution)/shard_map/ppermute | solution.py:181
  27.2 31.7 %collective-permute-start.7 = (f32[4,128,128]{2,1,0:T(8,128)}, f32[4,128,128]{2,1,0:T(8,128)}, u32[]{:S(2)}, u32[]{:S(2)}) collective-permute-start(f32[4,128,128]{2,1,0:T(8,128)} %add.84), channel_id=1, source_target_pairs={{0,2},{1,3},{2,0},{3,1},{4,6},{5,7},{6,4},{7,5},{8,10},{9,11},{10,... | collective-permute-start | bytes 786440 | tf_op jit(solution)/shard_map/ppermute | solution.py:181
  31.1 23.6 %collective-permute-start.5 = (f32[4,128,128]{2,1,0:T(8,128)}, f32[4,128,128]{2,1,0:T(8,128)}, u32[]{:S(2)}, u32[]{:S(2)}) collective-permute-start(f32[4,128,128]{2,1,0:T(8,128)} %add.83), channel_id=1, source_target_pairs={{0,2},{1,3},{2,0},{3,1},{4,6},{5,7},{6,4},{7,5},{8,10},{9,11},{10,... | collective-permute-start | bytes 786440 | tf_op jit(solution)/shard_map/ppermute | solution.py:181
  35.5 5.8 %copy-start.11 = (bf16[4,128,128]{2,1,0:T(8,128)(2,1)}, bf16[4,128,128]{2,1,0:T(8,128)(2,1)S(1)}, u32[]{:S(2)}) copy-start(bf16[4,128,128]{2,1,0:T(8,128)(2,1)S(1)} %get-tuple-element.88.feat_query) | copy-start | bytes 393220
  43.9 4.7 %copy-start.46 = (f32[4,8,128]{2,1,0:T(8,128)}, f32[4,8,128]{2,1,0:T(8,128)S(1)}, u32[]{:S(2)}) copy-start(f32[4,8,128]{2,1,0:T(8,128)S(1)} %get-tuple-element.95.gain) | copy-start | bytes 49156
  43.9 24.7 %collective-permute-start.8 = (f32[4,128,128]{2,1,0:T(8,128)}, f32[4,128,128]{2,1,0:T(8,128)S(1)}, u32[]{:S(2)}, u32[]{:S(2)}) collective-permute-start(f32[4,128,128]{2,1,0:T(8,128)} %get-tuple-element.130), channel_id=1, source_target_pairs={{0,1},{1,0},{2,3},{3,2},{4,5},{5,4},{6,7},{7,6},{8,9},{9,8},{10,11... | collective-permute-start | bytes 786440 | tf_op jit(solution)/shard_map/ppermute | solution.py:181
  51.8 18.1 %collective-permute-start.10 = (f32[4,128,128]{2,1,0:T(8,128)}, f32[4,128,128]{2,1,0:T(8,128)S(1)}, u32[]{:S(2)}, u32[]{:S(2)}) collective-permute-start(f32[4,128,128]{2,1,0:T(8,128)} %get-tuple-element.134), channel_id=1, source_target_pairs={{0,1},{1,0},{2,3},{3,2},{4,5},{5,4},{6,7},{7,6},{8,9},{9,8},{10,11... | collective-permute-start | bytes 786440 | tf_op jit(solution)/shard_map/ppermute | solution.py:181
  54.8 7.3 %copy-start.14 = (bf16[4,128,128]{2,1,0:T(8,128)(2,1)S(1)}, bf16[4,128,128]{2,1,0:T(8,128)(2,1)}, u32[]{:S(2)}) copy-start(bf16[4,128,128]{2,1,0:T(8,128)(2,1)} %copy-done.13) | copy-start | bytes 393220
  54.8 7.3 %copy-start.28 = (f32[4,128,128]{2,1,0:T(8,128)S(1)}, f32[4,128,128]{2,1,0:T(8,128)}, u32[]{:S(2)}) copy-start(f32[4,128,128]{2,1,0:T(8,128)} %copy-done.27) | copy-start | bytes 786436
  54.8 7.3 %copy-start.35 = (bf16[4,128,128]{2,1,0:T(8,128)(2,1)S(1)}, bf16[4,128,128]{2,1,0:T(8,128)(2,1)}, u32[]{:S(2)}) copy-start(bf16[4,128,128]{2,1,0:T(8,128)(2,1)} %copy-done.34) | copy-start | bytes 393220
  54.8 7.3 %copy-start.37 = (bf16[4,128,128]{2,1,0:T(8,128)(2,1)S(1)}, bf16[4,128,128]{2,1,0:T(8,128)(2,1)}, u32[]{:S(2)}) copy-start(bf16[4,128,128]{2,1,0:T(8,128)(2,1)} %copy-done.36) | copy-start | bytes 393220
  54.8 7.3 %copy-start.39 = (bf16[4,128,128]{2,1,0:T(8,128)(2,1)S(1)}, bf16[4,128,128]{2,1,0:T(8,128)(2,1)}, u32[]{:S(2)}) copy-start(bf16[4,128,128]{2,1,0:T(8,128)(2,1)} %copy-done.38) | copy-start | bytes 393220
  54.8 7.3 %copy-start.47 = (f32[4,8,128]{2,1,0:T(8,128)S(1)}, f32[4,8,128]{2,1,0:T(8,128)}, u32[]{:S(2)}) copy-start(f32[4,8,128]{2,1,0:T(8,128)} %copy-done.46) | copy-start | bytes 49156
  57.4 15.7 %collective-permute-start.12 = (f32[4,128,128]{2,1,0:T(8,128)S(1)}, f32[4,128,128]{2,1,0:T(8,128)S(1)}, u32[]{:S(2)}, u32[]{:S(2)}) collective-permute-start(f32[4,128,128]{2,1,0:T(8,128)S(1)} %get-tuple-element.138), channel_id=1, source_target_pairs={{0,1},{1,0},{2,3},{3,2},{4,5},{5,4},{6,7},{7,6},{8,9},{9,8},{10,11... | collective-permute-start | bytes 786440 | tf_op jit(solution)/shard_map/ppermute | solution.py:181
  61.5 12.0 %collective-permute-start.14 = (f32[4,128,128]{2,1,0:T(8,128)S(1)}, f32[4,128,128]{2,1,0:T(8,128)S(1)}, u32[]{:S(2)}, u32[]{:S(2)}) collective-permute-start(f32[4,128,128]{2,1,0:T(8,128)S(1)} %get-tuple-element.142), channel_id=1, source_target_pairs={{0,1},{1,0},{2,3},{3,2},{4,5},{5,4},{6,7},{7,6},{8,9},{9,8},{10,11... | collective-permute-start | bytes 786440 | tf_op jit(solution)/shard_map/ppermute | solution.py:181
  69.6 9.3 %collective-permute-start.9 = (f32[4,128,128]{2,1,0:T(8,128)S(1)}, f32[4,128,128]{2,1,0:T(8,128)S(1)}, u32[]{:S(2)}, u32[]{:S(2)}) collective-permute-start(f32[4,128,128]{2,1,0:T(8,128)S(1)} %add.85), channel_id=1, source_target_pairs={{0,2},{1,3},{2,0},{3,1},{4,6},{5,7},{6,4},{7,5},{8,10},{9,11},{10,... | collective-permute-start | bytes 786440 | tf_op jit(solution)/shard_map/ppermute | solution.py:181
  70.9 13.6 %collective-permute-start.11 = (f32[4,128,128]{2,1,0:T(8,128)S(1)}, f32[4,128,128]{2,1,0:T(8,128)S(1)}, u32[]{:S(2)}, u32[]{:S(2)}) collective-permute-start(f32[4,128,128]{2,1,0:T(8,128)S(1)} %add.86), channel_id=1, source_target_pairs={{0,2},{1,3},{2,0},{3,1},{4,6},{5,7},{6,4},{7,5},{8,10},{9,11},{10,... | collective-permute-start | bytes 786440 | tf_op jit(solution)/shard_map/ppermute | solution.py:181
  73.0 5.9 %copy-start.3 = (bf16[1,128,2048]{2,1,0:T(8,128)(2,1)S(1)}, bf16[1,128,2048]{2,1,0:T(8,128)(2,1)}, u32[]{:S(2)}) copy-start(bf16[1,128,2048]{2,1,0:T(8,128)(2,1)} %param.8) | copy-start | bytes 1572868
  73.0 5.9 %copy-start.12 = (bf16[4,128,128]{2,1,0:T(8,128)(2,1)S(1)}, bf16[4,128,128]{2,1,0:T(8,128)(2,1)}, u32[]{:S(2)}) copy-start(bf16[4,128,128]{2,1,0:T(8,128)(2,1)} %copy-done.11) | copy-start | bytes 393220
  73.0 5.9 %copy-start.24 = (f32[4,128,128]{2,1,0:T(8,128)S(1)}, f32[4,128,128]{2,1,0:T(8,128)}, u32[]{:S(2)}) copy-start(f32[4,128,128]{2,1,0:T(8,128)} %copy-done.23) | copy-start | bytes 786436
  73.0 21.1 %collective-permute-start.16 = (f32[4,272,128]{2,1,0:T(8,128)S(1)}, f32[4,272,128]{2,1,0:T(8,128)S(1)}, u32[]{:S(2)}, u32[]{:S(2)}) collective-permute-start(f32[4,272,128]{2,1,0:T(8,128)S(1)} %select_bitcast_fusion), channel_id=1, source_target_pairs={{0,4},{4,0},{8,12},{12,8},{16,20},{20,16},{24,28},{28,24},{1,5},{5... | collective-permute-start | bytes 1671176 | tf_op jit(solution)/shard_map/ppermute | solution.py:181
  73.1 16.4 %collective-permute-start.13 = (f32[4,128,128]{2,1,0:T(8,128)S(1)}, f32[4,128,128]{2,1,0:T(8,128)S(1)}, u32[]{:S(2)}, u32[]{:S(2)}) collective-permute-start(f32[4,128,128]{2,1,0:T(8,128)S(1)} %add.87), channel_id=1, source_target_pairs={{0,2},{1,3},{2,0},{3,1},{4,6},{5,7},{6,4},{7,5},{8,10},{9,11},{10,... | collective-permute-start | bytes 786440 | tf_op jit(solution)/shard_map/ppermute | solution.py:181
  73.5 11.0 %copy-start.22 = (f32[4,128,128]{2,1,0:T(8,128)S(1)}, f32[4,128,128]{2,1,0:T(8,128)}, u32[]{:S(2)}) copy-start(f32[4,128,128]{2,1,0:T(8,128)} %copy-done.21) | copy-start | bytes 786436
  73.5 18.8 %collective-permute-start.15 = (f32[4,128,128]{2,1,0:T(8,128)S(1)}, f32[4,128,128]{2,1,0:T(8,128)S(1)}, u32[]{:S(2)}, u32[]{:S(2)}) collective-permute-start(f32[4,128,128]{2,1,0:T(8,128)S(1)} %add.88), channel_id=1, source_target_pairs={{0,2},{1,3},{2,0},{3,1},{4,6},{5,7},{6,4},{7,5},{8,10},{9,11},{10,... | collective-permute-start | bytes 786440 | tf_op jit(solution)/shard_map/ppermute | solution.py:181
  86.3 6.0 %copy-start.18 = (f32[4,128,128]{2,1,0:T(8,128)S(1)}, f32[4,128,128]{2,1,0:T(8,128)}, u32[]{:S(2)}) copy-start(f32[4,128,128]{2,1,0:T(8,128)} %copy-done.17) | copy-start | bytes 786436
  86.3 9.6 %collective-permute-start.19 = (f32[4,128,128]{2,1,0:T(8,128)S(1)}, f32[4,128,128]{2,1,0:T(8,128)S(1)}, u32[]{:S(2)}, u32[]{:S(2)}) collective-permute-start(f32[4,128,128]{2,1,0:T(8,128)S(1)} %select_bitcast_fusion.3), channel_id=1, source_target_pairs={{0,4},{4,0},{8,12},{12,8},{16,20},{20,16},{24,28},{28,24},{1,5},{5... | collective-permute-start | bytes 786440 | tf_op jit(solution)/shard_map/ppermute | solution.py:181
  94.0 2.5 %collective-permute-start.24 = (f32[4,128,128]{2,1,0:T(8,128)S(1)}, f32[4,128,128]{2,1,0:T(8,128)S(1)}, u32[]{:S(2)}, u32[]{:S(2)}) collective-permute-start(f32[4,128,128]{2,1,0:T(8,128)S(1)} %select_bitcast_fusion.2), channel_id=1, source_target_pairs={{0,4},{4,0},{8,12},{12,8},{16,20},{20,16},{24,28},{28,24},{1,5},{5... | collective-permute-start | bytes 786440 | tf_op jit(solution)/shard_map/ppermute | solution.py:181
  94.2 9.5 %collective-permute-start.17 = (f32[2,272,128]{2,1,0:T(8,128)S(1)}, f32[2,272,128]{2,1,0:T(8,128)S(1)}, u32[]{:S(2)}, u32[]{:S(2)}) collective-permute-start(f32[2,272,128]{2,1,0:T(8,128)S(1)} %select_bitcast_fusion.1), channel_id=1, source_target_pairs={{0,8},{4,12},{8,0},{12,4},{16,24},{20,28},{24,16},{28,20},{1,9},{5... | collective-permute-start | bytes 835592 | tf_op jit(solution)/shard_map/ppermute | solution.py:181
  96.0 10.6 %collective-permute-start.20 = (f32[2,128,128]{2,1,0:T(8,128)S(1)}, f32[2,128,128]{2,1,0:T(8,128)S(1)}, u32[]{:S(2)}, u32[]{:S(2)}) collective-permute-start(f32[2,128,128]{2,1,0:T(8,128)S(1)} %select_bitcast_fusion.6), channel_id=1, source_target_pairs={{0,8},{4,12},{8,0},{12,4},{16,24},{20,28},{24,16},{28,20},{1,9},{5... | collective-permute-start | bytes 393224 | tf_op jit(solution)/shard_map/ppermute | solution.py:181
  96.6 16.3 %collective-permute-start.25 = (f32[2,128,128]{2,1,0:T(8,128)S(1)}, f32[2,128,128]{2,1,0:T(8,128)S(1)}, u32[]{:S(2)}, u32[]{:S(2)}) collective-permute-start(f32[2,128,128]{2,1,0:T(8,128)S(1)} %select_bitcast_fusion.5), channel_id=1, source_target_pairs={{0,8},{4,12},{8,0},{12,4},{16,24},{20,28},{24,16},{28,20},{1,9},{5... | collective-permute-start | bytes 393224 | tf_op jit(solution)/shard_map/ppermute | solution.py:181
  103.8 9.1 %collective-permute-start.18 = (f32[272,128]{1,0:T(8,128)S(1)}, f32[272,128]{1,0:T(8,128)S(1)}, u32[]{:S(2)}, u32[]{:S(2)}) collective-permute-start(f32[272,128]{1,0:T(8,128)S(1)} %select_bitcast_fusion.4), channel_id=1, source_target_pairs={{0,16},{4,20},{8,24},{12,28},{16,0},{20,4},{24,8},{28,12},{1,17},{... | collective-permute-start | bytes 417800 | tf_op jit(solution)/shard_map/ppermute | solution.py:181
  106.6 9.3 %collective-permute-start.21 = (f32[128,128]{1,0:T(8,128)S(1)}, f32[128,128]{1,0:T(8,128)S(1)}, u32[]{:S(2)}, u32[]{:S(2)}) collective-permute-start(f32[128,128]{1,0:T(8,128)S(1)} %select_bitcast_fusion.8), channel_id=1, source_target_pairs={{0,16},{4,20},{8,24},{12,28},{16,0},{20,4},{24,8},{28,12},{1,17},{... | collective-permute-start | bytes 196616 | tf_op jit(solution)/shard_map/ppermute | solution.py:181
  116.0 6.5 %collective-permute-start.22 = (f32[400,128]{1,0:T(8,128)S(1)}, f32[400,128]{1,0:T(8,128)S(1)}, u32[]{:S(2)}, u32[]{:S(2)}) collective-permute-start(f32[400,128]{1,0:T(8,128)S(1)} %pad_maximum_fusion.2), channel_id=1, source_target_pairs={{0,1},{1,0},{2,3},{3,2},{4,5},{5,4},{6,7},{7,6},{8,9},{9,8},{10,11... | collective-permute-start | bytes 614408 | tf_op jit(solution)/shard_map/ppermute | solution.py:181
  117.6 5.9 %collective-permute-start.26 = (f32[128,128]{1,0:T(8,128)S(1)}, f32[128,128]{1,0:T(8,128)S(1)}, u32[]{:S(2)}, u32[]{:S(2)}) collective-permute-start(f32[128,128]{1,0:T(8,128)S(1)} %select_bitcast_fusion.7), channel_id=1, source_target_pairs={{0,16},{4,20},{8,24},{12,28},{16,0},{20,4},{24,8},{28,12},{1,17},{... | collective-permute-start | bytes 196616 | tf_op jit(solution)/shard_map/ppermute | solution.py:181
  122.6 7.8 %copy-start.6 = (bf16[2048,128]{1,0:T(8,128)(2,1)S(1)}, bf16[2048,128]{1,0:T(8,128)(2,1)}, u32[]{:S(2)}) copy-start(bf16[2048,128]{1,0:T(8,128)(2,1)} %refs_4_.3) | copy-start | bytes 1572868
  122.6 10.5 %collective-permute-start.23 = (f32[400,128]{1,0:T(8,128)S(1)}, f32[400,128]{1,0:T(8,128)S(1)}, u32[]{:S(2)}, u32[]{:S(2)}) collective-permute-start(f32[400,128]{1,0:T(8,128)S(1)} %fusion.2), channel_id=1, source_target_pairs={{0,2},{1,3},{2,0},{3,1},{4,6},{5,7},{6,4},{7,5},{8,10},{9,11},{10,... | collective-permute-start | bytes 614408 | tf_op jit(solution)/shard_map/ppermute | solution.py:181
  123.5 4.3 %collective-permute-start.27 = (f32[128,128]{1,0:T(8,128)S(1)}, f32[128,128]{1,0:T(8,128)S(1)}, u32[]{:S(2)}, u32[]{:S(2)}) collective-permute-start(f32[128,128]{1,0:T(8,128)S(1)} %bitcast_add_fusion.6), channel_id=1, source_target_pairs={{0,1},{1,0},{2,3},{3,2},{4,5},{5,4},{6,7},{7,6},{8,9},{9,8},{10,11... | collective-permute-start | bytes 196616 | tf_op jit(solution)/shard_map/ppermute | solution.py:181
  127.9 5.2 %collective-permute-start.28 = (f32[128,128]{1,0:T(8,128)S(1)}, f32[128,128]{1,0:T(8,128)S(1)}, u32[]{:S(2)}, u32[]{:S(2)}) collective-permute-start(f32[128,128]{1,0:T(8,128)S(1)} %add.102), channel_id=1, source_target_pairs={{0,2},{1,3},{2,0},{3,1},{4,6},{5,7},{6,4},{7,5},{8,10},{9,11},{10,... | collective-permute-start | bytes 196616 | tf_op jit(solution)/shard_map/ppermute | solution.py:181
  (31 other events, 41.8 us)

commit v2 on v0

v2 whole, which is shorter than its diff:
```python
import functools

import jax
import jax.numpy as jnp
from jax import lax
from jax.experimental import pallas as pl
from jax.experimental.pallas import tpu as pltpu
from jax.sharding import PartitionSpec as P

HEAD = 128
GROUP = 4
FIRST_VMEM = 64 * 1024 - 1600
NORM_EPS = 1e-05
F32 = jnp.float32
BF16 = jnp.bfloat16


def dot(a, b, ca=1, cb=0):
    return lax.dot_general(a, b, (((ca,), (cb,)), ((), ())), preferred_element_type=F32)


def feature(pre):
    return jnp.where(pre > 0.0, pre + 1.0, jnp.exp(jnp.minimum(pre, 0.0)))


def split_low(value):
    high = value.astype(BF16)
    return high, (value - high.astype(F32)).astype(BF16)


def tril(rows):
    return lax.broadcasted_iota(jnp.int32, (rows, rows), 0) >= lax.broadcasted_iota(
        jnp.int32, (rows, rows), 1
    )


def columns(offset, i):
    at = (2 * i + offset) * HEAD
    return slice(at, at + HEAD)


def place_in_square():
    mine = lax.axis_index("seq")
    return lax.rem(mine, 2), lax.div(mine, 2)


def summed(order, later, first, second):
    if order == "all":
        return [first[i] for i in range(GROUP)]
    at_x, at_y = place_in_square()
    if order == "xy":
        keep_first, keep_second = at_x != later, at_y != later
        return [
            jnp.where(keep_first, first[i], 0.0) + jnp.where(keep_second, second[i], 0.0) for i in range(GROUP)
        ]
    keep_first = at_y != later
    return [jnp.where(keep_first, first[i], 0.0) + second[i] for i in range(GROUP)]


def turn_kernel(later, own, first, out):
    at_x, at_y = place_in_square()
    out[...] = jnp.where(at_y != later, first[...], 0.0) + jnp.where(at_x == later, own[...], 0.0)


def bit_clear(bit):
    return lax.rem(lax.div(lax.axis_index("dp"), bit), 2) == 0


def key_features(key, w_key):
    return [
        [feature(dot(key[:, c], w_key[c, :])).astype(BF16) for c in (columns(offset, i) for i in range(GROUP))]
        for offset in range(2)
    ]


def key_states(low, value, outs):
    for offset in range(2):
        feat_key, state = outs[2 * offset : 2 * offset + 2]
        states = [dot(low[offset][i], value[:, columns(offset, i)], 0, 0) for i in range(GROUP)]
        for i in range(GROUP):
            state[i] = states[i]
            feat_key[i] = low[offset][i]


def key_kernel(key, value, w_key, *outs):
    key_states(key_features(key, w_key), value, outs)


def first_kernel(key, value, w_key, *refs):
    outs, (key_buf, value_buf, w_buf, sems) = refs[:4], refs[4:]
    span = pl.ds(0, key_buf.shape[1])
    copies = [
        pltpu.make_async_copy(key.at[:, span], key_buf, sems.at[0]),
        pltpu.make_async_copy(w_key.at[span, :], w_buf, sems.at[1]),
        pltpu.make_async_copy(value.at[:, span], value_buf, sems.at[2]),
    ]
    for copy in copies:
        copy.start()
    copies[0].wait()
    copies[1].wait()
    low = key_features(key_buf, w_buf)
    copies[2].wait()
    key_states(low, value_buf, outs)


def query_kernel(offset, query, w_query, feat_key, feat_query, attn):
    causal = tril(query.shape[0])
    at = [columns(offset, i) for i in range(GROUP)]
    low = [feature(dot(query[:, c], w_query[c, :])).astype(BF16) for c in at]
    scores = [dot(low[i], feat_key[i], 1, 1) for i in range(GROUP)]
    for i in range(GROUP):
        feat_query[i] = low[i]
        attn[i] = jnp.where(causal, scores[i], 0.0).astype(BF16)


def numer_kernel(offset, order, first, second, feat_query, attn, value, grad, gain, adjoint, low_out, rest_out, ph_out, pl_out, gain_out):
    every = range(GROUP)
    at = [columns(offset, i) for i in every]
    inner = [dot(attn[i], value[:, at[i]]) for i in every]
    prior = summed(order, 0, first, second)
    parts = [split_low(p) for p in prior]
    feat = [feat_query[i] for i in every]
    numer = [inner[i] + dot(feat[i], parts[i][0]) + dot(feat[i], parts[i][1]) for i in every]
    inv = [lax.rsqrt(jnp.mean(n * n, axis=-1, keepdims=True) + NORM_EPS) for n in numer]
    normed = [n * r for n, r in zip(numer, inv)]
    grad_f = [grad[:, c].astype(F32) for c in at]
    scaled = [x * gain[:, c] for x, c in zip(grad_f, at)]
    means = [jnp.mean(x * n, axis=-1, keepdims=True) for x, n in zip(scaled, normed)]
    grads = [split_low(inv[i] * (scaled[i] - normed[i] * means[i])) for i in every]
    states = [dot(feat[i], grads[i][0], 0, 0) for i in every]
    for i in every:
        adjoint[i] = states[i]
        low_out[i], rest_out[i] = grads[i]
        ph_out[i], pl_out[i] = parts[i]
        gain_out[i] = jnp.broadcast_to(jnp.sum(normed[i] * grad_f[i], axis=0, keepdims=True), (8, HEAD))


def query_grad_kernel(offset, numer_low, rest, high, low, feat_key, query, value, w_query, gain, mixed_out, grad_out, weight):
    causal = tril(query.shape[0])
    every = range(GROUP)
    at = [columns(offset, i) for i in every]
    grad_low = [numer_low[i] for i in every]
    slope = [jnp.minimum(feature(dot(query[:, c], w_query[c, :])), 1.0) for c in at]
    raw = [dot(grad_low[i], value[:, at[i]], 1, 1) for i in every]
    mixed = [jnp.where(causal, x, 0.0).astype(BF16) for x in raw]
    grad_fq = [
        dot(mixed[i], feat_key[i])
        + dot(grad_low[i], high[i], 1, 1)
        + dot(grad_low[i], low[i], 1, 1)
        + dot(rest[i], high[i], 1, 1)
        for i in every
    ]
    pre = [(grad_fq[i] * slope[i]).astype(BF16) for i in every]
    sums = [dot(query[:, at[i]], pre[i], 0, 0) for i in every]
    back = [dot(pre[i], w_query[at[i], :], 1, 1) for i in every]
    for i in every:
        mixed_out[i] = mixed[i]
        grad_out[i] = back[i].astype(BF16)
        weight[i, :HEAD, :] = sums[i]
        weight[i, HEAD:, :] = gain[i]


def key_grad_kernel(offset, order, first, second, mixed, feat_query, key, value, w_key, pre_out, lh_out, ll_out, weight):
    every = range(GROUP)
    at = [columns(offset, i) for i in every]
    slope = [jnp.minimum(feature(dot(key[:, c], w_key[c, :])), 1.0) for c in at]
    later = summed(order, 1, first, second)
    parts = [split_low(x) for x in later]
    val = [value[:, c] for c in at]
    grad_fk = [
        dot(mixed[i], feat_query[i], 0, 0) + dot(val[i], parts[i][0], 1, 1) + dot(val[i], parts[i][1], 1, 1)
        for i in every
    ]
    pre = [(grad_fk[i] * slope[i]).astype(BF16) for i in every]
    sums = [dot(key[:, at[i]], pre[i], 0, 0) for i in every]
    for i in every:
        weight[i] = sums[i]
        pre_out[i] = pre[i]
        lh_out[i], ll_out[i] = parts[i]


def value_grad_kernel(offset, attn, numer_low, feat_key, high, low, pre, w_key, key_out, value_out):
    every = range(GROUP)
    feat = [feat_key[i] for i in every]
    grads = [
        dot(attn[i], numer_low[i], 0, 0) + dot(feat[i], high[i]) + dot(feat[i], low[i]) for i in every
    ]
    back = [dot(pre[i], w_key[columns(offset, i), :], 1, 1) for i in every]
    for i in every:
        value_out[i] = grads[i].astype(BF16)
        key_out[i] = back[i].astype(BF16)


def lay_kernel(groups, *refs):
    out, laid, sem = refs[groups:]
    for g in range(groups):
        for i in range(GROUP):
            laid[:, place(g, i)] = refs[g][i]
    copy = pltpu.make_async_copy(laid, out, sem)
    copy.start()
    copy.wait()


def pair_kernel(one, two, out):
    out[...] = one[...] + two[...]


def core_kernel(even, odd, kept, sent):
    first = bit_clear(1)
    for m in range(2):
        for b, part in enumerate((even, odd)):
            one, two = part[2 * m], part[2 * m + 1]
            kept[m, b] = jnp.where(first, one, two)
            sent[m, b] = jnp.where(first, two, one)


def near_kernel(*refs):
    parts, (kept, sent) = refs[:-2], refs[-2:]
    first = bit_clear(2)
    for block in range(2):
        own, theirs = parts[2 * block : 2 * block + 2]
        one, two = own[0] + theirs[0], own[1] + theirs[1]
        kept[block] = jnp.where(first, one, two)
        sent[block] = jnp.where(first, two, one)


def far_kernel(mine, theirs, kept, sent):
    first = bit_clear(4)
    one, two = mine[0] + theirs[0], mine[1] + theirs[1]
    kept[...] = jnp.where(first, one, two)
    sent[...] = jnp.where(first, two, one)


def spread_kernel(*refs):
    (low_own, low_theirs, high_own, high_theirs), outs = refs[:4], refs[4:]
    near, far = bit_clear(2), bit_clear(4)
    for m in range(2):
        low = low_own[m] + low_theirs[m]
        high = high_own[m] + high_theirs[m]
        here, there = jnp.where(far, low, high), jnp.where(far, high, low)
        same = near if m == 0 else jnp.logical_not(near)

        @pl.when(same)
        def _():
            outs[0][...] = here
            outs[2][...] = there

        @pl.when(jnp.logical_not(same))
        def _():
            outs[1][...] = here
            outs[3][...] = there


def gather_kernel(own, near, far, both, out):
    out[...] = (own[...] + near[...]) + (far[...] + both[...])


def halves_kernel(one, two, even, odd):
    even[...] = one[0] + two[0]
    odd[...] = one[1] + two[1]


def both_pairs_kernel(even, even_other, odd, odd_other, even_out, odd_out):
    even_out[...] = even[...] + even_other[...]
    odd_out[...] = odd[...] + odd_other[...]


def total_kernel(*refs):
    query, (key, key_x, key_y, key_d), (out_q, out_k, out_gain) = refs[:4], refs[4:8], refs[8:]
    total_k = (key[...] + key_x[...]) + (key_y[...] + key_d[...])
    for b in range(2):
        total_q = query[2 * b][...] + query[2 * b + 1][...]
        out_q[b * HEAD : (b + 1) * HEAD, :] = total_q[:HEAD, :]
        out_gain[b : b + 1, :] = total_q[HEAD : HEAD + 1, :]
        out_k[b * HEAD : (b + 1) * HEAD, :] = total_k[b]


def head_of(g, i):
    return (g // 2) * 2 * GROUP + 2 * i + g % 2


def place(g, i):
    at = head_of(g, i) * HEAD
    return slice(at, at + HEAD)


class Order:
    def __init__(self):
        self.last = None

    def __call__(self, body, ins, outs, name, scratch=(), to_hbm=False, chain=True, vmem=12 * 1024):
        at = len(ins)
        after = chain and self.last is not None
        if after:
            ins = ins + [(self.last, pl.BlockSpec(memory_space=pl.ANY))]
        inputs, results = len(ins), len(outs)

        def ordered(*refs):
            body(*refs[:at], *refs[inputs : inputs + results], *refs[inputs + results + chain :])
            if chain:
                token = refs[inputs + results]
                token[...] = jnp.zeros_like(token)

        out_specs = [
            pl.BlockSpec(memory_space=pltpu.HBM) if to_hbm else pl.BlockSpec(shape, lambda _, n=len(shape): (0,) * n)
            for shape, _ in outs
        ]
        out_shape = [jax.ShapeDtypeStruct(shape, kind) for shape, kind in outs]
        if chain:
            out_specs.append(pl.BlockSpec((8, HEAD), lambda _: (0, 0)))
            out_shape.append(jax.ShapeDtypeStruct((8, HEAD), F32))
        result = pl.pallas_call(
            ordered,
            grid=(1,),
            in_specs=[spec for _, spec in ins],
            out_specs=out_specs,
            out_shape=out_shape,
            scratch_shapes=list(scratch),
            compiler_params=pltpu.CompilerParams(vmem_limit_bytes=vmem * 1024),
            cost_estimate=pl.CostEstimate(flops=200000000, bytes_accessed=0, transcendentals=0),
            name=name,
        )(*[x for x, _ in ins])
        if chain:
            self.last = result[-1]
            return result[:-1]
        return result


def whole(x):
    return (x, pl.BlockSpec(x.shape, lambda _, n=x.ndim: (0,) * n))


def in_hbm(x):
    return (x, pl.BlockSpec(memory_space=pltpu.HBM))


def scan_generic(value, reverse):
    peers, mine = lax.axis_size("seq"), lax.axis_index("seq")
    everything = lax.all_gather(value, "seq")

    def turn(k, before):
        reached = k > mine if reverse else k < mine
        return before + jnp.where(reached, everything[k], 0.0)

    return lax.fori_loop(0, peers, turn, jnp.zeros_like(value))


def swap(value, axis, bit):
    return lax.ppermute(value, axis, [(i, i ^ bit) for i in range(lax.axis_size(axis))])


def per_device(query_in, key_in, value_in, grad_out, w_query, w_key, norm_gain):
    _, rows, width = query_in.shape
    heads = width // HEAD
    groups = heads // GROUP
    tuned = lax.axis_size("seq") == 4 and lax.axis_size("dp") == 8 and heads == 16
    query, key, value, grad = (x.reshape(rows, width) for x in (query_in, key_in, value_in, grad_out))
    gain = norm_gain.reshape(1, width)
    wide = 2 * GROUP * HEAD

    def cols(x, g):
        return (x, pl.BlockSpec((x.shape[0], wide), lambda _: (0, g // 2)))

    def wrows(x, g):
        return (x, pl.BlockSpec((wide, HEAD), lambda _: (g // 2, 0)))

    def tok(kind):
        return ((GROUP, rows, HEAD), kind)

    def sq(kind):
        return ((GROUP, HEAD, HEAD), kind)

    call = Order()

    def pair(one, two, name):
        (out,) = call(pair_kernel, [whole(one), whole(two)], [(one.shape, F32)], name)
        return out

    feat_k, state, feat_q, attn = {}, {}, {}, {}
    numer, mixed, back_q, sum_q = {}, {}, {}, {}
    pre_k, late_h, late_l, sum_k, back_k, back_v = {}, {}, {}, {}, {}, {}
    first, second, first_back, second_back = {}, {}, {}, {}

    def order_of(g):
        if not tuned:
            return "all"
        return ("xy", "yx")[g % 2]

    def hop_one(value, g, later):
        if not tuned:
            return scan_generic(value, later == 1)
        return swap(value, "seq", 1 if order_of(g) == "xy" else 2)

    def hop_two(value, brought, g, later):
        if not tuned:
            return brought
        if order_of(g) == "xy":
            return swap(pair(value, brought, f"pair_{later}_{g}"), "seq", 2)
        body = functools.partial(turn_kernel, later)
        (out,) = call(body, [whole(value), whole(brought)], [(value.shape, F32)], f"turn_{later}_{g}")
        return swap(out, "seq", 1)

    def key_state(g):
        outs = [tok(BF16), sq(F32)] * 2
        if g == 0:
            scratch = [
                pltpu.VMEM((rows, wide), BF16),
                pltpu.VMEM((rows, wide), BF16),
                pltpu.VMEM((wide, HEAD), BF16),
                pltpu.SemaphoreType.DMA((3,)),
            ]
            inputs = [in_hbm(key), in_hbm(value), in_hbm(w_key)]
            result = call(first_kernel, inputs, outs, "key_state_0", scratch, vmem=FIRST_VMEM)
        else:
            result = call(key_kernel, [cols(key, g), cols(value, g), wrows(w_key, g)], outs, f"key_state_{g}")
        feat_k[g], state[g], feat_k[g + 1], state[g + 1] = result
        for k in (g, g + 1):
            first[k] = hop_one(state[k], k, 0)

    def prior_hop(g):
        second[g] = hop_two(state[g], first[g], g, 0)

    def query_attn(g):
        feat_q[g], attn[g] = call(
            functools.partial(query_kernel, g % 2),
            [cols(query, g), wrows(w_query, g), whole(feat_k[g])],
            [tok(BF16), ((GROUP, rows, rows), BF16)],
            f"query_attn_{g}",
        )

    def numer_state(g):
        numer[g] = call(
            functools.partial(numer_kernel, g % 2, order_of(g)),
            [whole(first[g]), whole(second[g]), whole(feat_q[g]), whole(attn[g]), cols(value, g), cols(grad, g), cols(gain, g)],
            [sq(F32), tok(BF16), tok(BF16), sq(BF16), sq(BF16), ((GROUP, 8, HEAD), F32)],
            f"numer_{g}",
        )
        first_back[g] = hop_one(numer[g][0], g, 1)

    def later_hop(g):
        second_back[g] = hop_two(numer[g][0], first_back[g], g, 1)

    def query_grad(g):
        _, low, rest, ph, pl_, gains = numer[g]
        mixed[g], back_q[g], sum_q[g] = call(
            functools.partial(query_grad_kernel, g % 2),
            [whole(x) for x in (low, rest, ph, pl_, feat_k[g])]
            + [cols(query, g), cols(value, g), wrows(w_query, g), whole(gains)],
            [((GROUP, rows, rows), BF16), tok(BF16), ((GROUP, HEAD + 8, HEAD), F32)],
            f"query_grad_{g}",
        )

    def key_grad(g):
        pre_k[g], late_h[g], late_l[g], sum_k[g] = call(
            functools.partial(key_grad_kernel, g % 2, order_of(g)),
            [whole(first_back[g]), whole(second_back[g]), whole(mixed[g]), whole(feat_q[g])]
            + [cols(key, g), cols(value, g), wrows(w_key, g)],
            [tok(BF16), sq(BF16), sq(BF16), sq(F32)],
            f"key_grad_{g}",
        )

    def value_grad(g):
        back_k[g], back_v[g] = call(
            functools.partial(value_grad_kernel, g % 2),
            [whole(x) for x in (attn[g], numer[g][1], feat_k[g], late_h[g], late_l[g], pre_k[g])] + [wrows(w_key, g)],
            [tok(BF16), tok(BF16)],
            f"value_grad_{g}",
        )

    hops = {}

    def core_hop(b):
        parts = sum_q if b > 1 else sum_k
        parts = [whole(parts[2 * (b % 2)]), whole(parts[2 * (b % 2) + 1])]
        shape = (2, 2) + parts[0][0].shape[1:]
        kept, sent = call(core_kernel, parts, [(shape, F32)] * 2, f"core_{b}")
        hops[b] = (kept, swap(sent, "dp", 1))

    def near_hop(b):
        inputs = [whole(x) for x in hops[2] + hops[3]]
        kept, sent = call(near_kernel, inputs, [(hops[2][0].shape, F32)] * 2, "near")
        hops[2] = (kept, swap(sent, "dp", 2))

    def far_hop(b):
        kept, sent = call(far_kernel, [whole(x) for x in hops[2]], [(hops[2][0].shape[1:], F32)] * 2, "far")
        hops[2] = (kept, swap(sent, "dp", 4))

    def z_hop(b):
        inputs = hops[0] + hops[1]
        own, *sent = call(spread_kernel, [whole(x) for x in inputs], [(inputs[1].shape[1:], F32)] * 4, "spread")
        hops[0] = (own,) + tuple(swap(x, "dp", 2 * bits) for bits, x in enumerate(sent, 1))

    totals = {}

    def square(part):
        return (part,) + tuple(swap(part, "seq", bits) for bits in (1, 2, 3))

    def query_first(_):
        parts = call(halves_kernel, [whole(x) for x in hops[2]], [(hops[2][0].shape[1:], F32)] * 2, "query_sum")
        totals["query"] = [(x, swap(x, "seq", bit)) for bit, x in enumerate(parts, 1)]

    def query_second(_):
        parts = call(
            both_pairs_kernel, [whole(x) for x in sum(totals["query"], ())], [(totals["query"][0][0].shape, F32)] * 2, "query_turn"
        )
        totals["query"] = [(x, swap(x, "seq", 2 - bit)) for bit, x in enumerate(parts)]

    def key_square(_):
        (part,) = call(gather_kernel, [whole(x) for x in hops[0]], [(hops[0][0].shape, F32)], "key_sum")
        totals["key"] = square(part)

    def total(_):
        rows_out = ((2 * HEAD, HEAD), F32)
        totals["q"], totals["k"], totals["gain"] = call(
            total_kernel,
            [whole(x) for x in sum(totals["query"], ()) + totals["key"]],
            [rows_out, rows_out, ((2, HEAD), F32)],
            "total",
        )

    def listed(by_group):
        return [by_group[g] for g in range(groups)]

    laid = {}

    def lay(k):
        parts = (back_q, back_k, back_v)[k]
        (laid[k],) = call(
            functools.partial(lay_kernel, groups),
            [whole(x) for x in listed(parts)],
            [((rows, width), BF16)],
            f"lay_{k}",
            [pltpu.VMEM((rows, width), BF16), pltpu.SemaphoreType.DMA(())],
            True,
        )

    if tuned:
        steps = (
            "K0K2Q0Q1p0p1Q2Q3p2p3N0N1G0G1N2N3a2G2G3",
            "l0l1a3l2l3B2H0H1a0V0V1H2H3a1c2V2V3Z0E0L0L1C0F0L2T0",
        )
        steps = "".join(steps)
    else:
        steps = "".join(f"K{g}" for g in range(0, groups, 2))
        steps += "".join(f"{kind}{g}" for kind in "pQNlGHV" for g in range(groups)) + "L0L1L2"
    does = {
        "K": key_state,
        "p": prior_hop,
        "Q": query_attn,
        "N": numer_state,
        "l": later_hop,
        "G": query_grad,
        "H": key_grad,
        "V": value_grad,
        "L": lay,
        "a": core_hop,
        "B": near_hop,
        "c": far_hop,
        "Z": z_hop,
        "E": query_first,
        "F": query_second,
        "C": key_square,
        "T": total,
    }
    for k in range(0, len(steps), 2):
        does[steps[k]](int(steps[k + 1]))
    if tuned:
        total_q, total_k, total_gain = totals["q"], totals["k"], totals["gain"].reshape(2 * HEAD)
    else:

        def in_order(parts):
            spread = [None] * heads
            for g in range(groups):
                for i in range(GROUP):
                    spread[head_of(g, i)] = parts[g][i]
            return jnp.stack(spread)

        both = in_order(sum_q)
        owned = (
            lax.psum_scatter(both[:, :HEAD].reshape(width, HEAD), "dp", scatter_dimension=0, tiled=True),
            lax.psum_scatter(in_order(sum_k).reshape(width, HEAD), "dp", scatter_dimension=0, tiled=True),
            lax.psum_scatter(both[:, HEAD].reshape(width), "dp", scatter_dimension=0, tiled=True),
        )
        total_q, total_k, total_gain = lax.psum(owned, "seq")
    shape = query_in.shape
    return (
        laid[0].reshape(shape),
        laid[1].reshape(shape),
        laid[2].reshape(shape),
        total_q,
        total_k,
        total_gain,
    )


def solution(mesh):
    split = P("dp", "seq", None)
    return jax.shard_map(
        per_device,
        mesh=mesh,
        in_specs=(split, split, split, split, P(), P(), P()),
        out_specs=(split, split, split, P("dp", None), P("dp", None), P("dp")),
        check_vma=False,
    )
```

time: 258 us -> 86.6 us (0.34)
  the two profiles are of different devices: /device:TPU:0 before, /device:TPU:21 now
where the time goes in v2:
time: 86.6 us; the launch traced here: 86.4 us
  waiting for transfers between devices  40.8 us (47%)
  starting transfers between devices  25.8 us (30%)
  Pallas kernels  18.1 us (21%)
  between operations  1.03 us (1%)
    ppermute x32, waiting for transfers between devices, swap(): lax.ppermute(value, axis, [(i, i ^ bit) for i in range(lax.axis_size(axis...  40.8 us
    ppermute x32, starting transfers between devices, swap(): lax.ppermute(value, axis, [(i, i ^ bit) for i in range(lax.axis_size(axis...  25.8 us
    pallas_call x44, Pallas kernels, __call__(): pl.pallas_call(ordered, grid=(1,), in_specs=[spec for _, spec in ins], ou...  18.1 us
  transfers between devices with their start and end apart: 32, of which 17 were waited for; matrix products, arithmetic and copies ran while one was open for 0% of the time, Pallas kernels for 17%

profile of v2, /device:TPU:21, one launch (start us, length us, event | category | flops | bytes accessed | tf_op | source)
XLA Modules:
  0.0 86.4 jit_solution(13727596799543045120)
XLA Ops:
  0.7 2.5 %key_state_0.1 = (bf16[4,128,128]{2,1,0:T(8,128)(2,1)}, f32[4,128,128]{2,1,0:T(8,128)}, bf16[4,128,128]{2,1,0:T(8,128)(2,1)}, f32[4,128,128]{2,1,0:T(8,128)}, f32[8,128]{1,0:T(8,128)}) custom-call(bf16[128,2048]{1,0:T(8,128)(2,1)} %bitcast.31, bf16[128,2048]{1,0:T(8,128)(2,1)} %bitcast.9, bf16[2048,128]{1,0:T(8,128)(2,1)} %refs_6_.15), custom_call_target="tpu_custom_call" | custom-call | flops 200000000 | tf_op jit(solution)/shard_map/key_state_0/pallas_call | solution.py:312
  3.2 1.3 %collective-permute-start = (f32[4,128,128]{2,1,0:T(8,128)}, f32[4,128,128]{2,1,0:T(8,128)S(1)}, u32[]{:S(2)}, u32[]{:S(2)}) collective-permute-start(f32[4,128,128]{2,1,0:T(8,128)} %get-tuple-element.160.refs_0_), channel_id=1, source_target_pairs={{0,1},{1,0},{2,3},{3,2},{4,5},{5,4},{6,7},{7,6},{8,9},{9,8},{10,11... | collective-permute-start | bytes 786440 | tf_op jit(solution)/shard_map/ppermute | solution.py:349
  5.6 1.2 %collective-permute-start.2 = (f32[4,128,128]{2,1,0:T(8,128)S(1)}, f32[4,128,128]{2,1,0:T(8,128)S(1)}, u32[]{:S(2)}, u32[]{:S(2)}) collective-permute-start(f32[4,128,128]{2,1,0:T(8,128)S(1)} %get-tuple-element.170.refs_0_), channel_id=1, source_target_pairs={{0,2},{1,3},{2,0},{3,1},{4,6},{5,7},{6,4},{7,5},{8,10},{9,11},{10,... | collective-permute-start | bytes 786440 | tf_op jit(solution)/shard_map/ppermute | solution.py:349
  7.1 0.6 copy-done.6
  8.0 2.6 %collective-permute-done.refs_1_.refs_0_ = f32[4,128,128]{2,1,0:T(8,128)S(1)} collective-permute-done((f32[4,128,128]{2,1,0:T(8,128)}, f32[4,128,128]{2,1,0:T(8,128)S(1)}, u32[]{:S(2)}, u32[]{:S(2)}) %collective-permute-start) | collective-permute-done | bytes 262176 | tf_op jit(solution)/shard_map/ppermute | solution.py:349
  10.9 0.6 collective-permute-done.4.refs_1_.refs_0_
  11.6 1.3 %collective-permute-start.5 = (f32[4,128,128]{2,1,0:T(8,128)S(1)}, f32[4,128,128]{2,1,0:T(8,128)S(1)}, u32[]{:S(2)}, u32[]{:S(2)}) collective-permute-start(f32[4,128,128]{2,1,0:T(8,128)S(1)} %get-tuple-element.186), channel_id=1, source_target_pairs={{0,1},{1,0},{2,3},{3,2},{4,5},{5,4},{6,7},{7,6},{8,9},{9,8},{10,11... | collective-permute-start | bytes 786440 | tf_op jit(solution)/shard_map/ppermute | solution.py:349
  13.6 2.7 %collective-permute-done.3.refs_1_.refs_0_ = f32[4,128,128]{2,1,0:T(8,128)S(1)} collective-permute-done((f32[4,128,128]{2,1,0:T(8,128)S(1)}, f32[4,128,128]{2,1,0:T(8,128)S(1)}, u32[]{:S(2)}, u32[]{:S(2)}) %collective-permute-start.3) | collective-permute-done | bytes 262176 | tf_op jit(solution)/shard_map/ppermute | solution.py:349
  16.6 0.6 collective-permute-done.2.refs_1_.refs_0_
  17.2 0.7 collective-permute-start.7
  17.9 4.8 %collective-permute-done.1.refs_1_ = f32[4,128,128]{2,1,0:T(8,128)S(1)} collective-permute-done((f32[4,128,128]{2,1,0:T(8,128)S(1)}, f32[4,128,128]{2,1,0:T(8,128)S(1)}, u32[]{:S(2)}, u32[]{:S(2)}) %collective-permute-start.1) | collective-permute-done | bytes 262176 | tf_op jit(solution)/shard_map/ppermute | solution.py:349
  22.8 0.6 numer_0.1
  23.7 0.6 numer_1.1
  24.6 0.8 query_grad_0.1
  25.4 0.8 query_grad_1.1
  26.3 2.1 %collective-permute-done.6.refs_1_ = f32[4,128,128]{2,1,0:T(8,128)S(1)} collective-permute-done((f32[4,128,128]{2,1,0:T(8,128)S(1)}, f32[4,128,128]{2,1,0:T(8,128)S(1)}, u32[]{:S(2)}, u32[]{:S(2)}) %collective-permute-start.6) | collective-permute-done | bytes 262176 | tf_op jit(solution)/shard_map/ppermute | solution.py:349
  28.4 0.6 numer_2.1
  29.3 0.6 numer_3.1
  30.3 4.4 %collective-permute-start.8 = (f32[2,2,136,128]{3,2,1,0:T(8,128)S(1)}, f32[2,2,136,128]{3,2,1,0:T(8,128)S(1)}, u32[]{:S(2)}, u32[]{:S(2)}) collective-permute-start(f32[2,2,136,128]{3,2,1,0:T(8,128)S(1)} %get-tuple-element.225), channel_id=1, source_target_pairs={{0,4},{4,0},{8,12},{12,8},{16,20},{20,16},{24,28},{28,24},{1,5},{5... | collective-permute-start | bytes 835592 | tf_op jit(solution)/shard_map/ppermute | solution.py:349
  34.7 0.8 query_grad_2.1
  35.6 0.8 query_grad_3.1
  36.6 0.9 %collective-permute-start.11 = (f32[2,2,136,128]{3,2,1,0:T(8,128)S(1)}, f32[2,2,136,128]{3,2,1,0:T(8,128)S(1)}, u32[]{:S(2)}, u32[]{:S(2)}) collective-permute-start(f32[2,2,136,128]{3,2,1,0:T(8,128)S(1)} %get-tuple-element.234), channel_id=1, source_target_pairs={{0,4},{4,0},{8,12},{12,8},{16,20},{20,16},{24,28},{28,24},{1,5},{5... | collective-permute-start | bytes 835592 | tf_op jit(solution)/shard_map/ppermute | solution.py:349
  37.7 0.7 collective-permute-done.13.refs_1_.refs_0_
  38.5 1.4 %collective-permute-start.16 = (f32[4,128,128]{2,1,0:T(8,128)S(1)}, f32[4,128,128]{2,1,0:T(8,128)S(1)}, u32[]{:S(2)}, u32[]{:S(2)}) collective-permute-start(f32[4,128,128]{2,1,0:T(8,128)S(1)} %get-tuple-element.244), channel_id=1, source_target_pairs={{0,1},{1,0},{2,3},{3,2},{4,5},{5,4},{6,7},{7,6},{8,9},{9,8},{10,11... | collective-permute-start | bytes 786440 | tf_op jit(solution)/shard_map/ppermute | solution.py:349
  40.8 1.4 %collective-permute-start.14 = (f32[2,2,136,128]{3,2,1,0:T(8,128)S(1)}, f32[2,2,136,128]{3,2,1,0:T(8,128)S(1)}, u32[]{:S(2)}, u32[]{:S(2)}) collective-permute-start(f32[2,2,136,128]{3,2,1,0:T(8,128)S(1)} %get-tuple-element.241), channel_id=1, source_target_pairs={{0,8},{4,12},{8,0},{12,4},{16,24},{20,28},{24,16},{28,20},{1,9},{5... | collective-permute-start | bytes 835592 | tf_op jit(solution)/shard_map/ppermute | solution.py:349
  42.1 3.8 %collective-permute-done.17.refs_1_ = f32[4,128,128]{2,1,0:T(8,128)S(1)} collective-permute-done((f32[4,128,128]{2,1,0:T(8,128)S(1)}, f32[4,128,128]{2,1,0:T(8,128)S(1)}, u32[]{:S(2)}, u32[]{:S(2)}) %collective-permute-start.17) | collective-permute-done | bytes 262176 | tf_op jit(solution)/shard_map/ppermute | solution.py:349
  45.9 0.5 key_grad_0.1
  46.4 0.6 key_grad_1.1
  47.8 3.7 %collective-permute-done.15.refs_1_ = f32[4,128,128]{2,1,0:T(8,128)S(1)} collective-permute-done((f32[4,128,128]{2,1,0:T(8,128)S(1)}, f32[4,128,128]{2,1,0:T(8,128)S(1)}, u32[]{:S(2)}, u32[]{:S(2)}) %collective-permute-start.15) | collective-permute-done | bytes 262176 | tf_op jit(solution)/shard_map/ppermute | solution.py:349
  51.5 0.5 key_grad_2.1
  52.1 0.6 key_grad_3.1
  52.7 1.3 %collective-permute-start.21 = (f32[2,2,128,128]{3,2,1,0:T(8,128)S(1)}, f32[2,2,128,128]{3,2,1,0:T(8,128)S(1)}, u32[]{:S(2)}, u32[]{:S(2)}) collective-permute-start(f32[2,2,128,128]{3,2,1,0:T(8,128)S(1)} %get-tuple-element.274), channel_id=1, source_target_pairs={{0,4},{4,0},{8,12},{12,8},{16,20},{20,16},{24,28},{28,24},{1,5},{5... | collective-permute-start | bytes 786440 | tf_op jit(solution)/shard_map/ppermute | solution.py:349
  55.6 1.4 %collective-permute-start.24 = (f32[2,128,128]{2,1,0:T(8,128)S(1)}, f32[2,128,128]{2,1,0:T(8,128)S(1)}, u32[]{:S(2)}, u32[]{:S(2)}) collective-permute-start(f32[2,128,128]{2,1,0:T(8,128)S(1)} %get-tuple-element.300), channel_id=1, source_target_pairs={{0,8},{4,12},{8,0},{12,4},{16,24},{20,28},{24,16},{28,20},{1,9},{5... | collective-permute-start | bytes 393224 | tf_op jit(solution)/shard_map/ppermute | solution.py:349
  56.9 1.8 %collective-permute-start.25 = (f32[2,128,128]{2,1,0:T(8,128)S(1)}, f32[2,128,128]{2,1,0:T(8,128)S(1)}, u32[]{:S(2)}, u32[]{:S(2)}) collective-permute-start(f32[2,128,128]{2,1,0:T(8,128)S(1)} %get-tuple-element.301), channel_id=1, source_target_pairs={{0,16},{4,20},{8,24},{12,28},{16,0},{20,4},{24,8},{28,12},{1,17},{... | collective-permute-start | bytes 393224 | tf_op jit(solution)/shard_map/ppermute | solution.py:349
  58.7 1.2 %collective-permute-done.19.refs_1_ = f32[2,136,128]{2,1,0:T(8,128)S(1)} collective-permute-done((f32[2,136,128]{2,1,0:T(8,128)S(1)}, f32[2,136,128]{2,1,0:T(8,128)S(1)}, u32[]{:S(2)}, u32[]{:S(2)}) %collective-permute-start.19) | collective-permute-done | bytes 139296 | tf_op jit(solution)/shard_map/ppermute | solution.py:349
  59.9 1.1 %collective-permute-start.22 = (f32[136,128]{1,0:T(8,128)S(1)}, f32[136,128]{1,0:T(8,128)S(1)}, u32[]{:S(2)}, u32[]{:S(2)}) collective-permute-start(f32[136,128]{1,0:T(8,128)S(1)} %get-tuple-element.297.refs_0_), channel_id=1, source_target_pairs={{0,1},{1,0},{2,3},{3,2},{4,5},{5,4},{6,7},{7,6},{8,9},{9,8},{10,11... | collective-permute-start | bytes 208904 | tf_op jit(solution)/shard_map/ppermute | solution.py:349
  61.2 0.9 %lay_0.1 = (bf16[128,2048]{1,0:T(8,128)(2,1)}, f32[8,128]{1,0:T(8,128)S(1)}) custom-call(bf16[4,128,128]{2,1,0:T(8,128)(2,1)S(1)} %get-tuple-element.191.refs_0_, bf16[4,128,128]{2,1,0:T(8,128)(2,1)S(1)} %get-tuple-element.198.refs_1_, bf16[4,128,128]{2,1,0:T(8,128)(2,1)S(1)} %get-tuple-element.216.refs_2_, ...), custom_call_target="tpu_custom_call" | custom-call | flops 200000000 | tf_op jit(solution)/shard_map/lay_0/pallas_call | solution.py:312
  62.1 0.9 %lay_1.1 = (bf16[128,2048]{1,0:T(8,128)(2,1)}, f32[8,128]{1,0:T(8,128)S(1)}) custom-call(bf16[4,128,128]{2,1,0:T(8,128)(2,1)S(1)} %get-tuple-element.287.refs_0_, bf16[4,128,128]{2,1,0:T(8,128)(2,1)S(1)} %get-tuple-element.288.refs_1_, bf16[4,128,128]{2,1,0:T(8,128)(2,1)S(1)} %get-tuple-element.289.refs_2_, ...), custom_call_target="tpu_custom_call" | custom-call | flops 200000000 | tf_op jit(solution)/shard_map/lay_1/pallas_call | solution.py:312
  63.1 5.1 %collective-permute-done.25.refs_2_ = f32[2,128,128]{2,1,0:T(8,128)S(1)} collective-permute-done((f32[2,128,128]{2,1,0:T(8,128)S(1)}, f32[2,128,128]{2,1,0:T(8,128)S(1)}, u32[]{:S(2)}, u32[]{:S(2)}) %collective-permute-start.25) | collective-permute-done | bytes 131104 | tf_op jit(solution)/shard_map/ppermute | solution.py:349
  68.2 6.7 %collective-permute-done.26.refs_3_ = f32[2,128,128]{2,1,0:T(8,128)S(1)} collective-permute-done((f32[2,128,128]{2,1,0:T(8,128)S(1)}, f32[2,128,128]{2,1,0:T(8,128)S(1)}, u32[]{:S(2)}, u32[]{:S(2)}) %collective-permute-start.26) | collective-permute-done | bytes 131104 | tf_op jit(solution)/shard_map/ppermute | solution.py:349
  74.9 1.0 %collective-permute-start.31 = (f32[2,128,128]{2,1,0:T(8,128)S(1)}, f32[2,128,128]{2,1,0:T(8,128)S(1)}, u32[]{:S(2)}, u32[]{:S(2)}) collective-permute-start(f32[2,128,128]{2,1,0:T(8,128)S(1)} %get-tuple-element.309.refs_4_), channel_id=1, source_target_pairs={{0,3},{1,2},{2,1},{3,0},{4,7},{5,6},{6,5},{7,4},{8,11},{9,10},{10,... | collective-permute-start | bytes 393224 | tf_op jit(solution)/shard_map/ppermute | solution.py:349
  75.9 1.3 %collective-permute-start.30 = (f32[2,128,128]{2,1,0:T(8,128)S(1)}, f32[2,128,128]{2,1,0:T(8,128)S(1)}, u32[]{:S(2)}, u32[]{:S(2)}) collective-permute-start(f32[2,128,128]{2,1,0:T(8,128)S(1)} %get-tuple-element.309.refs_4_), channel_id=1, source_target_pairs={{0,2},{1,3},{2,0},{3,1},{4,6},{5,7},{6,4},{7,5},{8,10},{9,11},{10,... | collective-permute-start | bytes 393224 | tf_op jit(solution)/shard_map/ppermute | solution.py:349
  78.0 1.0 %collective-permute-start.28 = (f32[136,128]{1,0:T(8,128)S(1)}, f32[136,128]{1,0:T(8,128)S(1)}, u32[]{:S(2)}, u32[]{:S(2)}) collective-permute-start(f32[136,128]{1,0:T(8,128)S(1)} %get-tuple-element.308.refs_2_), channel_id=1, source_target_pairs={{0,1},{1,0},{2,3},{3,2},{4,5},{5,4},{6,7},{7,6},{8,9},{9,8},{10,11... | collective-permute-start | bytes 208904 | tf_op jit(solution)/shard_map/ppermute | solution.py:349
  79.0 0.9 %lay_2.1 = (bf16[128,2048]{1,0:T(8,128)(2,1)}, f32[8,128]{1,0:T(8,128)S(1)}) custom-call(bf16[4,128,128]{2,1,0:T(8,128)(2,1)S(1)} %get-tuple-element.293.refs_0_, bf16[4,128,128]{2,1,0:T(8,128)(2,1)S(1)} %get-tuple-element.294.refs_1_, bf16[4,128,128]{2,1,0:T(8,128)(2,1)S(1)} %get-tuple-element.295.refs_2_, ...), custom_call_target="tpu_custom_call" | custom-call | flops 200000000 | tf_op jit(solution)/shard_map/lay_2/pallas_call | solution.py:312
  79.9 0.6 collective-permute-done.31.refs_7_
  80.5 3.6 %collective-permute-done.30.refs_6_ = f32[2,128,128]{2,1,0:T(8,128)S(1)} collective-permute-done((f32[2,128,128]{2,1,0:T(8,128)S(1)}, f32[2,128,128]{2,1,0:T(8,128)S(1)}, u32[]{:S(2)}, u32[]{:S(2)}) %collective-permute-start.30) | collective-permute-done | bytes 131104 | tf_op jit(solution)/shard_map/ppermute | solution.py:349
  84.1 1.5 %collective-permute-done.27.refs_1_ = f32[136,128]{1,0:T(8,128)S(1)} collective-permute-done((f32[136,128]{1,0:T(8,128)S(1)}, f32[136,128]{1,0:T(8,128)S(1)}, u32[]{:S(2)}, u32[]{:S(2)}) %collective-permute-start.27) | collective-permute-done | bytes 69664 | tf_op jit(solution)/shard_map/ppermute | solution.py:349
  85.6 0.8 total.1
  (84 shorter events, 9.3 us)
Async XLA Ops:
  0.6 4.0 %copy-start = (bf16[1,128,2048]{2,1,0:T(8,128)(2,1)S(1)}, bf16[1,128,2048]{2,1,0:T(8,128)(2,1)}, u32[]{:S(2)}) copy-start(bf16[1,128,2048]{2,1,0:T(8,128)(2,1)} %param.9) | copy-start | bytes 1572868
  0.6 4.0 %copy-start.1 = (bf16[2048,128]{1,0:T(8,128)(2,1)S(1)}, bf16[2048,128]{1,0:T(8,128)(2,1)}, u32[]{:S(2)}) copy-start(bf16[2048,128]{1,0:T(8,128)(2,1)} %refs_6_.15) | copy-start | bytes 1572868
  0.7 4.0 %copy-start.4 = (bf16[1,128,2048]{2,1,0:T(8,128)(2,1)S(1)}, bf16[1,128,2048]{2,1,0:T(8,128)(2,1)}, u32[]{:S(2)}) copy-start(bf16[1,128,2048]{2,1,0:T(8,128)(2,1)} %param.8) | copy-start | bytes 1572868
  3.2 1.5 %copy-start.9 = (f32[8,128]{1,0:T(8,128)S(1)}, f32[8,128]{1,0:T(8,128)}, u32[]{:S(2)}) copy-start(f32[8,128]{1,0:T(8,128)} %get-tuple-element.163.refs_3_) | copy-start | bytes 12292
  3.2 7.5 %collective-permute-start = (f32[4,128,128]{2,1,0:T(8,128)}, f32[4,128,128]{2,1,0:T(8,128)S(1)}, u32[]{:S(2)}, u32[]{:S(2)}) collective-permute-start(f32[4,128,128]{2,1,0:T(8,128)} %get-tuple-element.160.refs_0_), channel_id=1, source_target_pairs={{0,1},{1,0},{2,3},{3,2},{4,5},{5,4},{6,7},{7,6},{8,9},{9,8},{10,11... | collective-permute-start | bytes 786440 | tf_op jit(solution)/shard_map/ppermute | solution.py:349
  4.4 7.1 %collective-permute-start.4 = (f32[4,128,128]{2,1,0:T(8,128)}, f32[4,128,128]{2,1,0:T(8,128)S(1)}, u32[]{:S(2)}, u32[]{:S(2)}) collective-permute-start(f32[4,128,128]{2,1,0:T(8,128)} %get-tuple-element.174.refs_0_), channel_id=1, source_target_pairs={{0,2},{1,3},{2,0},{3,1},{4,6},{5,7},{6,4},{7,5},{8,10},{9,11},{10,... | collective-permute-start | bytes 786440 | tf_op jit(solution)/shard_map/ppermute | solution.py:349
  4.7 2.1 %copy-start.2 = (bf16[1,128,2048]{2,1,0:T(8,128)(2,1)S(1)}, bf16[1,128,2048]{2,1,0:T(8,128)(2,1)}, u32[]{:S(2)}) copy-start(bf16[1,128,2048]{2,1,0:T(8,128)(2,1)} %param.7) | copy-start | bytes 1572868
  4.7 2.1 %copy-start.3 = (bf16[2048,128]{1,0:T(8,128)(2,1)S(1)}, bf16[2048,128]{1,0:T(8,128)(2,1)}, u32[]{:S(2)}) copy-start(bf16[2048,128]{1,0:T(8,128)(2,1)} %refs_7_.7) | copy-start | bytes 1572868
  4.7 2.1 %copy-start.7 = (bf16[4,128,128]{2,1,0:T(8,128)(2,1)S(1)}, bf16[4,128,128]{2,1,0:T(8,128)(2,1)}, u32[]{:S(2)}) copy-start(bf16[4,128,128]{2,1,0:T(8,128)(2,1)} %get-tuple-element.162.refs_2_.refs_4_) | copy-start | bytes 393220
  5.2 11.0 %collective-permute-start.3 = (f32[4,128,128]{2,1,0:T(8,128)S(1)}, f32[4,128,128]{2,1,0:T(8,128)S(1)}, u32[]{:S(2)}, u32[]{:S(2)}) collective-permute-start(f32[4,128,128]{2,1,0:T(8,128)S(1)} %get-tuple-element.171.refs_0_), channel_id=1, source_target_pairs={{0,1},{1,0},{2,3},{3,2},{4,5},{5,4},{6,7},{7,6},{8,9},{9,8},{10,11... | collective-permute-start | bytes 786440 | tf_op jit(solution)/shard_map/ppermute | solution.py:349
  5.6 11.5 %collective-permute-start.2 = (f32[4,128,128]{2,1,0:T(8,128)S(1)}, f32[4,128,128]{2,1,0:T(8,128)S(1)}, u32[]{:S(2)}, u32[]{:S(2)}) collective-permute-start(f32[4,128,128]{2,1,0:T(8,128)S(1)} %get-tuple-element.170.refs_0_), channel_id=1, source_target_pairs={{0,2},{1,3},{2,0},{3,1},{4,6},{5,7},{6,4},{7,5},{8,10},{9,11},{10,... | collective-permute-start | bytes 786440 | tf_op jit(solution)/shard_map/ppermute | solution.py:349
  6.8 0.9 %copy-start.6 = (bf16[4,128,128]{2,1,0:T(8,128)(2,1)S(1)}, bf16[4,128,128]{2,1,0:T(8,128)(2,1)}, u32[]{:S(2)}) copy-start(bf16[4,128,128]{2,1,0:T(8,128)(2,1)} %get-tuple-element.161.refs_2_.refs_4_) | copy-start | bytes 393220
  7.7 2.9 %copy-start.11 = (f32[4,128,128]{2,1,0:T(8,128)S(1)}, f32[4,128,128]{2,1,0:T(8,128)}, u32[]{:S(2)}) copy-start(f32[4,128,128]{2,1,0:T(8,128)} %get-tuple-element.160.refs_0_) | copy-start | bytes 786436
  10.6 1.0 %copy-start.10 = (f32[4,128,128]{2,1,0:T(8,128)S(1)}, f32[4,128,128]{2,1,0:T(8,128)}, u32[]{:S(2)}) copy-start(f32[4,128,128]{2,1,0:T(8,128)} %get-tuple-element.174.refs_0_) | copy-start | bytes 786436
  10.7 12.1 %collective-permute-start.1 = (f32[4,128,128]{2,1,0:T(8,128)S(1)}, f32[4,128,128]{2,1,0:T(8,128)S(1)}, u32[]{:S(2)}, u32[]{:S(2)}) collective-permute-start(f32[4,128,128]{2,1,0:T(8,128)S(1)} %get-tuple-element.167), channel_id=1, source_target_pairs={{0,2},{1,3},{2,0},{3,1},{4,6},{5,7},{6,4},{7,5},{8,10},{9,11},{10,... | collective-permute-start | bytes 786440 | tf_op jit(solution)/shard_map/ppermute | solution.py:349
  11.6 12.1 %collective-permute-start.5 = (f32[4,128,128]{2,1,0:T(8,128)S(1)}, f32[4,128,128]{2,1,0:T(8,128)S(1)}, u32[]{:S(2)}, u32[]{:S(2)}) collective-permute-start(f32[4,128,128]{2,1,0:T(8,128)S(1)} %get-tuple-element.186), channel_id=1, source_target_pairs={{0,1},{1,0},{2,3},{3,2},{4,5},{5,4},{6,7},{7,6},{8,9},{9,8},{10,11... | collective-permute-start | bytes 786440 | tf_op jit(solution)/shard_map/ppermute | solution.py:349
  16.3 6.5 %copy-start.5 = (bf16[1,128,2048]{2,1,0:T(8,128)(2,1)S(1)}, bf16[1,128,2048]{2,1,0:T(8,128)(2,1)}, u32[]{:S(2)}) copy-start(bf16[1,128,2048]{2,1,0:T(8,128)(2,1)} %param.10) | copy-start | bytes 1572868
  16.3 12.1 %collective-permute-start.6 = (f32[4,128,128]{2,1,0:T(8,128)S(1)}, f32[4,128,128]{2,1,0:T(8,128)S(1)}, u32[]{:S(2)}, u32[]{:S(2)}) collective-permute-start(f32[4,128,128]{2,1,0:T(8,128)S(1)} %get-tuple-element.199), channel_id=1, source_target_pairs={{0,2},{1,3},{2,0},{3,1},{4,6},{5,7},{6,4},{7,5},{8,10},{9,11},{10,... | collective-permute-start | bytes 786440 | tf_op jit(solution)/shard_map/ppermute | solution.py:349
  17.2 5.6 %copy-start.8 = (f32[2048]{0:T(1024)S(1)}, f32[2048]{0:T(1024)}, u32[]{:S(2)}) copy-start(f32[2048]{0:T(1024)} %param.13) | copy-start | bytes 24580
  17.2 12.1 %collective-permute-start.7 = (f32[4,128,128]{2,1,0:T(8,128)S(1)}, f32[4,128,128]{2,1,0:T(8,128)S(1)}, u32[]{:S(2)}, u32[]{:S(2)}) collective-permute-start(f32[4,128,128]{2,1,0:T(8,128)S(1)} %get-tuple-element.210), channel_id=1, source_target_pairs={{0,1},{1,0},{2,3},{3,2},{4,5},{5,4},{6,7},{7,6},{8,9},{9,8},{10,11... | collective-permute-start | bytes 786440 | tf_op jit(solution)/shard_map/ppermute | solution.py:349
  23.4 13.0 %collective-permute-start.10 = (f32[4,128,128]{2,1,0:T(8,128)S(1)}, f32[4,128,128]{2,1,0:T(8,128)S(1)}, u32[]{:S(2)}, u32[]{:S(2)}) collective-permute-start(f32[4,128,128]{2,1,0:T(8,128)S(1)} %get-tuple-element.229.refs_0_), channel_id=1, source_target_pairs={{0,1},{1,0},{2,3},{3,2},{4,5},{5,4},{6,7},{7,6},{8,9},{9,8},{10,11... | collective-permute-start | bytes 786440 | tf_op jit(solution)/shard_map/ppermute | solution.py:349
  24.3 12.1 %collective-permute-start.9 = (f32[4,128,128]{2,1,0:T(8,128)S(1)}, f32[4,128,128]{2,1,0:T(8,128)S(1)}, u32[]{:S(2)}, u32[]{:S(2)}) collective-permute-start(f32[4,128,128]{2,1,0:T(8,128)S(1)} %get-tuple-element.228.refs_0_), channel_id=1, source_target_pairs={{0,2},{1,3},{2,0},{3,1},{4,6},{5,7},{6,4},{7,5},{8,10},{9,11},{10,... | collective-permute-start | bytes 786440 | tf_op jit(solution)/shard_map/ppermute | solution.py:349
  29.0 9.5 %collective-permute-start.13 = (f32[4,128,128]{2,1,0:T(8,128)S(1)}, f32[4,128,128]{2,1,0:T(8,128)S(1)}, u32[]{:S(2)}, u32[]{:S(2)}) collective-permute-start(f32[4,128,128]{2,1,0:T(8,128)S(1)} %get-tuple-element.236.refs_0_), channel_id=1, source_target_pairs={{0,1},{1,0},{2,3},{3,2},{4,5},{5,4},{6,7},{7,6},{8,9},{9,8},{10,11... | collective-permute-start | bytes 786440 | tf_op jit(solution)/shard_map/ppermute | solution.py:349
  29.9 10.0 %collective-permute-start.12 = (f32[4,128,128]{2,1,0:T(8,128)S(1)}, f32[4,128,128]{2,1,0:T(8,128)S(1)}, u32[]{:S(2)}, u32[]{:S(2)}) collective-permute-start(f32[4,128,128]{2,1,0:T(8,128)S(1)} %get-tuple-element.235.refs_0_), channel_id=1, source_target_pairs={{0,2},{1,3},{2,0},{3,1},{4,6},{5,7},{6,4},{7,5},{8,10},{9,11},{10,... | collective-permute-start | bytes 786440 | tf_op jit(solution)/shard_map/ppermute | solution.py:349
  30.3 10.0 %collective-permute-start.8 = (f32[2,2,136,128]{3,2,1,0:T(8,128)S(1)}, f32[2,2,136,128]{3,2,1,0:T(8,128)S(1)}, u32[]{:S(2)}, u32[]{:S(2)}) collective-permute-start(f32[2,2,136,128]{3,2,1,0:T(8,128)S(1)} %get-tuple-element.225), channel_id=1, source_target_pairs={{0,4},{4,0},{8,12},{12,8},{16,20},{20,16},{24,28},{28,24},{1,5},{5... | collective-permute-start | bytes 835592 | tf_op jit(solution)/shard_map/ppermute | solution.py:349
  36.6 4.1 %collective-permute-start.11 = (f32[2,2,136,128]{3,2,1,0:T(8,128)S(1)}, f32[2,2,136,128]{3,2,1,0:T(8,128)S(1)}, u32[]{:S(2)}, u32[]{:S(2)}) collective-permute-start(f32[2,2,136,128]{3,2,1,0:T(8,128)S(1)} %get-tuple-element.234), channel_id=1, source_target_pairs={{0,4},{4,0},{8,12},{12,8},{16,20},{20,16},{24,28},{28,24},{1,5},{5... | collective-permute-start | bytes 835592 | tf_op jit(solution)/shard_map/ppermute | solution.py:349
  37.5 8.4 %collective-permute-start.17 = (f32[4,128,128]{2,1,0:T(8,128)S(1)}, f32[4,128,128]{2,1,0:T(8,128)S(1)}, u32[]{:S(2)}, u32[]{:S(2)}) collective-permute-start(f32[4,128,128]{2,1,0:T(8,128)S(1)} %get-tuple-element.246), channel_id=1, source_target_pairs={{0,2},{1,3},{2,0},{3,1},{4,6},{5,7},{6,4},{7,5},{8,10},{9,11},{10,... | collective-permute-start | bytes 786440 | tf_op jit(solution)/shard_map/ppermute | solution.py:349
  38.5 8.0 %collective-permute-start.16 = (f32[4,128,128]{2,1,0:T(8,128)S(1)}, f32[4,128,128]{2,1,0:T(8,128)S(1)}, u32[]{:S(2)}, u32[]{:S(2)}) collective-permute-start(f32[4,128,128]{2,1,0:T(8,128)S(1)} %get-tuple-element.244), channel_id=1, source_target_pairs={{0,1},{1,0},{2,3},{3,2},{4,5},{5,4},{6,7},{7,6},{8,9},{9,8},{10,11... | collective-permute-start | bytes 786440 | tf_op jit(solution)/shard_map/ppermute | solution.py:349
  40.0 11.6 %collective-permute-start.15 = (f32[4,128,128]{2,1,0:T(8,128)S(1)}, f32[4,128,128]{2,1,0:T(8,128)S(1)}, u32[]{:S(2)}, u32[]{:S(2)}) collective-permute-start(f32[4,128,128]{2,1,0:T(8,128)S(1)} %get-tuple-element.242), channel_id=1, source_target_pairs={{0,2},{1,3},{2,0},{3,1},{4,6},{5,7},{6,4},{7,5},{8,10},{9,11},{10,... | collective-permute-start | bytes 786440 | tf_op jit(solution)/shard_map/ppermute | solution.py:349
  40.3 11.7 %collective-permute-start.18 = (f32[4,128,128]{2,1,0:T(8,128)S(1)}, f32[4,128,128]{2,1,0:T(8,128)S(1)}, u32[]{:S(2)}, u32[]{:S(2)}) collective-permute-start(f32[4,128,128]{2,1,0:T(8,128)S(1)} %get-tuple-element.263), channel_id=1, source_target_pairs={{0,1},{1,0},{2,3},{3,2},{4,5},{5,4},{6,7},{7,6},{8,9},{9,8},{10,11... | collective-permute-start | bytes 786440 | tf_op jit(solution)/shard_map/ppermute | solution.py:349
  40.8 13.3 %collective-permute-start.14 = (f32[2,2,136,128]{3,2,1,0:T(8,128)S(1)}, f32[2,2,136,128]{3,2,1,0:T(8,128)S(1)}, u32[]{:S(2)}, u32[]{:S(2)}) collective-permute-start(f32[2,2,136,128]{3,2,1,0:T(8,128)S(1)} %get-tuple-element.241), channel_id=1, source_target_pairs={{0,8},{4,12},{8,0},{12,4},{16,24},{20,28},{24,16},{28,20},{1,9},{5... | collective-permute-start | bytes 835592 | tf_op jit(solution)/shard_map/ppermute | solution.py:349
  52.7 2.4 %collective-permute-start.21 = (f32[2,2,128,128]{3,2,1,0:T(8,128)S(1)}, f32[2,2,128,128]{3,2,1,0:T(8,128)S(1)}, u32[]{:S(2)}, u32[]{:S(2)}) collective-permute-start(f32[2,2,128,128]{3,2,1,0:T(8,128)S(1)} %get-tuple-element.274), channel_id=1, source_target_pairs={{0,4},{4,0},{8,12},{12,8},{16,20},{20,16},{24,28},{28,24},{1,5},{5... | collective-permute-start | bytes 786440 | tf_op jit(solution)/shard_map/ppermute | solution.py:349
  53.9 1.5 %collective-permute-start.20 = (f32[2,2,128,128]{3,2,1,0:T(8,128)S(1)}, f32[2,2,128,128]{3,2,1,0:T(8,128)S(1)}, u32[]{:S(2)}, u32[]{:S(2)}) collective-permute-start(f32[2,2,128,128]{3,2,1,0:T(8,128)S(1)} %get-tuple-element.272), channel_id=1, source_target_pairs={{0,4},{4,0},{8,12},{12,8},{16,20},{20,16},{24,28},{28,24},{1,5},{5... | collective-permute-start | bytes 786440 | tf_op jit(solution)/shard_map/ppermute | solution.py:349
  54.1 5.8 %collective-permute-start.19 = (f32[2,136,128]{2,1,0:T(8,128)S(1)}, f32[2,136,128]{2,1,0:T(8,128)S(1)}, u32[]{:S(2)}, u32[]{:S(2)}) collective-permute-start(f32[2,136,128]{2,1,0:T(8,128)S(1)} %get-tuple-element.270), channel_id=1, source_target_pairs={{0,16},{4,20},{8,24},{12,28},{16,0},{20,4},{24,8},{28,12},{1,17},{... | collective-permute-start | bytes 417800 | tf_op jit(solution)/shard_map/ppermute | solution.py:349
  55.6 7.5 %collective-permute-start.24 = (f32[2,128,128]{2,1,0:T(8,128)S(1)}, f32[2,128,128]{2,1,0:T(8,128)S(1)}, u32[]{:S(2)}, u32[]{:S(2)}) collective-permute-start(f32[2,128,128]{2,1,0:T(8,128)S(1)} %get-tuple-element.300), channel_id=1, source_target_pairs={{0,8},{4,12},{8,0},{12,4},{16,24},{20,28},{24,16},{28,20},{1,9},{5... | collective-permute-start | bytes 393224 | tf_op jit(solution)/shard_map/ppermute | solution.py:349
  56.9 11.3 %collective-permute-start.25 = (f32[2,128,128]{2,1,0:T(8,128)S(1)}, f32[2,128,128]{2,1,0:T(8,128)S(1)}, u32[]{:S(2)}, u32[]{:S(2)}) collective-permute-start(f32[2,128,128]{2,1,0:T(8,128)S(1)} %get-tuple-element.301), channel_id=1, source_target_pairs={{0,16},{4,20},{8,24},{12,28},{16,0},{20,4},{24,8},{28,12},{1,17},{... | collective-permute-start | bytes 393224 | tf_op jit(solution)/shard_map/ppermute | solution.py:349
  58.7 16.2 %collective-permute-start.26 = (f32[2,128,128]{2,1,0:T(8,128)S(1)}, f32[2,128,128]{2,1,0:T(8,128)S(1)}, u32[]{:S(2)}, u32[]{:S(2)}) collective-permute-start(f32[2,128,128]{2,1,0:T(8,128)S(1)} %get-tuple-element.302), channel_id=1, source_target_pairs={{0,24},{4,28},{8,16},{12,20},{16,8},{20,12},{24,0},{28,4},{1,25},{... | collective-permute-start | bytes 393224 | tf_op jit(solution)/shard_map/ppermute | solution.py:349
  59.9 17.7 %collective-permute-start.22 = (f32[136,128]{1,0:T(8,128)S(1)}, f32[136,128]{1,0:T(8,128)S(1)}, u32[]{:S(2)}, u32[]{:S(2)}) collective-permute-start(f32[136,128]{1,0:T(8,128)S(1)} %get-tuple-element.297.refs_0_), channel_id=1, source_target_pairs={{0,1},{1,0},{2,3},{3,2},{4,5},{5,4},{6,7},{7,6},{8,9},{9,8},{10,11... | collective-permute-start | bytes 208904 | tf_op jit(solution)/shard_map/ppermute | solution.py:349
  61.0 16.7 %collective-permute-start.23 = (f32[136,128]{1,0:T(8,128)S(1)}, f32[136,128]{1,0:T(8,128)S(1)}, u32[]{:S(2)}, u32[]{:S(2)}) collective-permute-start(f32[136,128]{1,0:T(8,128)S(1)} %get-tuple-element.298.refs_2_), channel_id=1, source_target_pairs={{0,2},{1,3},{2,0},{3,1},{4,6},{5,7},{6,4},{7,5},{8,10},{9,11},{10,... | collective-permute-start | bytes 208904 | tf_op jit(solution)/shard_map/ppermute | solution.py:349
  74.9 5.6 %collective-permute-start.31 = (f32[2,128,128]{2,1,0:T(8,128)S(1)}, f32[2,128,128]{2,1,0:T(8,128)S(1)}, u32[]{:S(2)}, u32[]{:S(2)}) collective-permute-start(f32[2,128,128]{2,1,0:T(8,128)S(1)} %get-tuple-element.309.refs_4_), channel_id=1, source_target_pairs={{0,3},{1,2},{2,1},{3,0},{4,7},{5,6},{6,5},{7,4},{8,11},{9,10},{10,... | collective-permute-start | bytes 393224 | tf_op jit(solution)/shard_map/ppermute | solution.py:349
  75.9 8.2 %collective-permute-start.30 = (f32[2,128,128]{2,1,0:T(8,128)S(1)}, f32[2,128,128]{2,1,0:T(8,128)S(1)}, u32[]{:S(2)}, u32[]{:S(2)}) collective-permute-start(f32[2,128,128]{2,1,0:T(8,128)S(1)} %get-tuple-element.309.refs_4_), channel_id=1, source_target_pairs={{0,2},{1,3},{2,0},{3,1},{4,6},{5,7},{6,4},{7,5},{8,10},{9,11},{10,... | collective-permute-start | bytes 393224 | tf_op jit(solution)/shard_map/ppermute | solution.py:349
  77.2 6.9 %collective-permute-start.29 = (f32[2,128,128]{2,1,0:T(8,128)S(1)}, f32[2,128,128]{2,1,0:T(8,128)S(1)}, u32[]{:S(2)}, u32[]{:S(2)}) collective-permute-start(f32[2,128,128]{2,1,0:T(8,128)S(1)} %get-tuple-element.309.refs_4_), channel_id=1, source_target_pairs={{0,1},{1,0},{2,3},{3,2},{4,5},{5,4},{6,7},{7,6},{8,9},{9,8},{10,11... | collective-permute-start | bytes 393224 | tf_op jit(solution)/shard_map/ppermute | solution.py:349
  77.7 7.9 %collective-permute-start.27 = (f32[136,128]{1,0:T(8,128)S(1)}, f32[136,128]{1,0:T(8,128)S(1)}, u32[]{:S(2)}, u32[]{:S(2)}) collective-permute-start(f32[136,128]{1,0:T(8,128)S(1)} %get-tuple-element.307.refs_0_), channel_id=1, source_target_pairs={{0,2},{1,3},{2,0},{3,1},{4,6},{5,7},{6,4},{7,5},{8,10},{9,11},{10,... | collective-permute-start | bytes 208904 | tf_op jit(solution)/shard_map/ppermute | solution.py:349
  78.0 7.7 %collective-permute-start.28 = (f32[136,128]{1,0:T(8,128)S(1)}, f32[136,128]{1,0:T(8,128)S(1)}, u32[]{:S(2)}, u32[]{:S(2)}) collective-permute-start(f32[136,128]{1,0:T(8,128)S(1)} %get-tuple-element.308.refs_2_), channel_id=1, source_target_pairs={{0,1},{1,0},{2,3},{3,2},{4,5},{5,4},{6,7},{7,6},{8,9},{9,8},{10,11... | collective-permute-start | bytes 208904 | tf_op jit(solution)/shard_map/ppermute | solution.py:349

commit v3 on v2

--- a/solution.py
+++ b/solution.py
@@ -9,7 +9,7 @@
 
 HEAD = 128
 GROUP = 4
-FIRST_VMEM = 64 * 1024 - 1600
+FIRST_VMEM = 64 * 1024 - 4000
 NORM_EPS = 1e-05
 F32 = jnp.float32
 BF16 = jnp.bfloat16
@@ -34,9 +34,8 @@
     )
 
 
-def columns(offset, i):
-    at = (2 * i + offset) * HEAD
-    return slice(at, at + HEAD)
+def columns(i):
+    return slice(i * HEAD, (i + 1) * HEAD)
 
 
 def place_in_square():
@@ -67,23 +66,19 @@
 
 
 def key_features(key, w_key):
-    return [
-        [feature(dot(key[:, c], w_key[c, :])).astype(BF16) for c in (columns(offset, i) for i in range(GROUP))]
-        for offset in range(2)
-    ]
-
-
-def key_states(low, value, outs):
-    for offset in range(2):
-        feat_key, state = outs[2 * offset : 2 * offset + 2]
-        states = [dot(low[offset][i], value[:, columns(offset, i)], 0, 0) for i in range(GROUP)]
+    return [feature(dot(key[:, c], w_key[c, :])).astype(BF16) for c in map(columns, range(2 * GROUP))]
+
+
+def key_states(low, value, *outs):
+    states = [dot(f, value[:, columns(i)], 0, 0) for i, f in enumerate(low)]
+    for g in range(2):
         for i in range(GROUP):
-            state[i] = states[i]
-            feat_key[i] = low[offset][i]
+            outs[2 * g][i] = low[g * GROUP + i]
+            outs[2 * g + 1][i] = states[g * GROUP + i]
 
 
 def key_kernel(key, value, w_key, *outs):
-    key_states(key_features(key, w_key), value, outs)
+    key_states(key_features(key, w_key), value, *outs)
 
 
 def first_kernel(key, value, w_key, *refs):
@@ -100,12 +95,12 @@
     copies[1].wait()
     low = key_features(key_buf, w_buf)
     copies[2].wait()
-    key_states(low, value_buf, outs)
-
-
-def query_kernel(offset, query, w_query, feat_key, feat_query, attn):
+    key_states(low, value_buf, *outs)
+
+
+def query_kernel(query, w_query, feat_key, feat_query, attn):
     causal = tril(query.shape[0])
-    at = [columns(offset, i) for i in range(GROUP)]
+    at = [columns(i) for i in range(GROUP)]
     low = [feature(dot(query[:, c], w_query[c, :])).astype(BF16) for c in at]
     scores = [dot(low[i], feat_key[i], 1, 1) for i in range(GROUP)]
     for i in range(GROUP):
@@ -113,9 +108,9 @@
         attn[i] = jnp.where(causal, scores[i], 0.0).astype(BF16)
 
 
-def numer_kernel(offset, order, first, second, feat_query, attn, value, grad, gain, adjoint, low_out, rest_out, ph_out, pl_out, gain_out):
+def numer_kernel(order, first, second, feat_query, attn, value, grad, gain, adjoint, low_out, rest_out, ph_out, pl_out, gain_out):
     every = range(GROUP)
-    at = [columns(offset, i) for i in every]
+    at = [columns(i) for i in every]
     inner = [dot(attn[i], value[:, at[i]]) for i in every]
     prior = summed(order, 0, first, second)
     parts = [split_low(p) for p in prior]
@@ -135,10 +130,10 @@
         gain_out[i] = jnp.broadcast_to(jnp.sum(normed[i] * grad_f[i], axis=0, keepdims=True), (8, HEAD))
 
 
-def query_grad_kernel(offset, numer_low, rest, high, low, feat_key, query, value, w_query, gain, mixed_out, grad_out, weight):
+def query_grad_kernel(numer_low, rest, high, low, feat_key, query, value, w_query, gain, mixed_out, grad_out, weight):
     causal = tril(query.shape[0])
     every = range(GROUP)
-    at = [columns(offset, i) for i in every]
+    at = [columns(i) for i in every]
     grad_low = [numer_low[i] for i in every]
     slope = [jnp.minimum(feature(dot(query[:, c], w_query[c, :])), 1.0) for c in at]
     raw = [dot(grad_low[i], value[:, at[i]], 1, 1) for i in every]
@@ -160,9 +155,9 @@
         weight[i, HEAD:, :] = gain[i]
 
 
-def key_grad_kernel(offset, order, first, second, mixed, feat_query, key, value, w_key, pre_out, lh_out, ll_out, weight):
+def key_grad_kernel(order, first, second, mixed, feat_query, key, value, w_key, pre_out, lh_out, ll_out, weight):
     every = range(GROUP)
-    at = [columns(offset, i) for i in every]
+    at = [columns(i) for i in every]
     slope = [jnp.minimum(feature(dot(key[:, c], w_key[c, :])), 1.0) for c in at]
     later = summed(order, 1, first, second)
     parts = [split_low(x) for x in later]
@@ -179,13 +174,13 @@
         lh_out[i], ll_out[i] = parts[i]
 
 
-def value_grad_kernel(offset, attn, numer_low, feat_key, high, low, pre, w_key, key_out, value_out):
+def value_grad_kernel(attn, numer_low, feat_key, high, low, pre, w_key, key_out, value_out):
     every = range(GROUP)
     feat = [feat_key[i] for i in every]
     grads = [
         dot(attn[i], numer_low[i], 0, 0) + dot(feat[i], high[i]) + dot(feat[i], low[i]) for i in every
     ]
-    back = [dot(pre[i], w_key[columns(offset, i), :], 1, 1) for i in every]
+    back = [dot(pre[i], w_key[columns(i), :], 1, 1) for i in every]
     for i in every:
         value_out[i] = grads[i].astype(BF16)
         key_out[i] = back[i].astype(BF16)
@@ -205,38 +200,46 @@
     out[...] = one[...] + two[...]
 
 
-def core_kernel(even, odd, kept, sent):
+def core_kernel(low, high, *refs):
+    if len(refs) == 5:
+        one, two, kept, *sent, total = refs
+        total[...] = one[...] + two[...]
+    else:
+        kept, *sent = refs
     first = bit_clear(1)
-    for m in range(2):
-        for b, part in enumerate((even, odd)):
-            one, two = part[2 * m], part[2 * m + 1]
+    for m, part in enumerate((low, high)):
+        for b in range(2):
+            one, two = part[b], part[2 + b]
             kept[m, b] = jnp.where(first, one, two)
-            sent[m, b] = jnp.where(first, two, one)
-
-
-def near_kernel(*refs):
-    parts, (kept, sent) = refs[:-2], refs[-2:]
+            out = jnp.where(first, two, one)
+            if len(sent) == 2:
+                sent[m][b] = out
+            else:
+                sent[0][m, b] = out
+
+
+def far_kernel(low, own, theirs, kept, sent):
+    first = bit_clear(4)
+    high = own[...] + theirs[...]
+    kept[...] = jnp.where(first, low[...], high)
+    sent[...] = jnp.where(first, high, low[...])
+
+
+def near_kernel(mine, theirs, kept, *sent):
     first = bit_clear(2)
-    for block in range(2):
-        own, theirs = parts[2 * block : 2 * block + 2]
-        one, two = own[0] + theirs[0], own[1] + theirs[1]
-        kept[block] = jnp.where(first, one, two)
-        sent[block] = jnp.where(first, two, one)
-
-
-def far_kernel(mine, theirs, kept, sent):
-    first = bit_clear(4)
     one, two = mine[0] + theirs[0], mine[1] + theirs[1]
     kept[...] = jnp.where(first, one, two)
-    sent[...] = jnp.where(first, two, one)
+    out = jnp.where(first, two, one)
+    for b in range(2):
+        sent[b][...] = out[b]
 
 
 def spread_kernel(*refs):
-    (low_own, low_theirs, high_own, high_theirs), outs = refs[:4], refs[4:]
+    parts, outs = refs[:6], refs[6:]
     near, far = bit_clear(2), bit_clear(4)
     for m in range(2):
-        low = low_own[m] + low_theirs[m]
-        high = high_own[m] + high_theirs[m]
+        low = parts[0][m] + parts[1 + m][...]
+        high = parts[3][m] + parts[4 + m][...]
         here, there = jnp.where(far, low, high), jnp.where(far, high, low)
         same = near if m == 0 else jnp.logical_not(near)
 
@@ -255,9 +258,9 @@
     out[...] = (own[...] + near[...]) + (far[...] + both[...])
 
 
-def halves_kernel(one, two, even, odd):
-    even[...] = one[0] + two[0]
-    odd[...] = one[1] + two[1]
+def halves_kernel(own, even_other, odd_other, even, odd):
+    even[...] = own[0] + even_other[...]
+    odd[...] = own[1] + odd_other[...]
 
 
 def both_pairs_kernel(even, even_other, odd, odd_other, even_out, odd_out):
@@ -275,12 +278,8 @@
         out_k[b * HEAD : (b + 1) * HEAD, :] = total_k[b]
 
 
-def head_of(g, i):
-    return (g // 2) * 2 * GROUP + 2 * i + g % 2
-
-
 def place(g, i):
-    at = head_of(g, i) * HEAD
+    at = (g * GROUP + i) * HEAD
     return slice(at, at + HEAD)
 
 
@@ -288,7 +287,7 @@
     def __init__(self):
         self.last = None
 
-    def __call__(self, body, ins, outs, name, scratch=(), to_hbm=False, chain=True, vmem=12 * 1024):
+    def __call__(self, body, ins, outs, name, scratch=(), to_hbm=False, to_vmem=False, chain=True, vmem=12 * 1024):
         at = len(ins)
         after = chain and self.last is not None
         if after:
@@ -306,7 +305,13 @@
             for shape, _ in outs
         ]
         out_shape = [jax.ShapeDtypeStruct(shape, kind) for shape, kind in outs]
-        if chain:
+        if to_vmem:
+            out_specs = [pl.BlockSpec(memory_space=pltpu.VMEM) for _ in outs]
+            out_shape = [pltpu.VMEM(shape, kind) for shape, kind in outs]
+        if chain and to_vmem:
+            out_specs.append(pl.BlockSpec(memory_space=pltpu.VMEM))
+            out_shape.append(pltpu.VMEM((8, HEAD), F32))
+        elif chain:
             out_specs.append(pl.BlockSpec((8, HEAD), lambda _: (0, 0)))
             out_shape.append(jax.ShapeDtypeStruct((8, HEAD), F32))
         result = pl.pallas_call(
@@ -356,13 +361,13 @@
     tuned = lax.axis_size("seq") == 4 and lax.axis_size("dp") == 8 and heads == 16
     query, key, value, grad = (x.reshape(rows, width) for x in (query_in, key_in, value_in, grad_out))
     gain = norm_gain.reshape(1, width)
-    wide = 2 * GROUP * HEAD
+    wide = GROUP * HEAD
 
     def cols(x, g):
-        return (x, pl.BlockSpec((x.shape[0], wide), lambda _: (0, g // 2)))
+        return (x, pl.BlockSpec((x.shape[0], wide), lambda _: (0, g)))
 
     def wrows(x, g):
-        return (x, pl.BlockSpec((wide, HEAD), lambda _: (g // 2, 0)))
+        return (x, pl.BlockSpec((wide, HEAD), lambda _: (g, 0)))
 
     def tok(kind):
         return ((GROUP, rows, HEAD), kind)
@@ -402,17 +407,20 @@
 
     def key_state(g):
         outs = [tok(BF16), sq(F32)] * 2
+        pair_wide = 2 * wide
         if g == 0:
             scratch = [
-                pltpu.VMEM((rows, wide), BF16),
-                pltpu.VMEM((rows, wide), BF16),
-                pltpu.VMEM((wide, HEAD), BF16),
+                pltpu.VMEM((rows, pair_wide), BF16),
+                pltpu.VMEM((rows, pair_wide), BF16),
+                pltpu.VMEM((pair_wide, HEAD), BF16),
                 pltpu.SemaphoreType.DMA((3,)),
             ]
             inputs = [in_hbm(key), in_hbm(value), in_hbm(w_key)]
-            result = call(first_kernel, inputs, outs, "key_state_0", scratch, vmem=FIRST_VMEM)
+            result = call(first_kernel, inputs, outs, "key_state_first", scratch, to_vmem=True, vmem=FIRST_VMEM)
         else:
-            result = call(key_kernel, [cols(key, g), cols(value, g), wrows(w_key, g)], outs, f"key_state_{g}")
+            by_cols = pl.BlockSpec((rows, pair_wide), lambda _: (0, g // 2))
+            by_rows = pl.BlockSpec((pair_wide, HEAD), lambda _: (g // 2, 0))
+            result = call(key_kernel, [(key, by_cols), (value, by_cols), (w_key, by_rows)], outs, f"key_state_{g}")
         feat_k[g], state[g], feat_k[g + 1], state[g + 1] = result
         for k in (g, g + 1):
             first[k] = hop_one(state[k], k, 0)
@@ -422,7 +430,7 @@
 
     def query_attn(g):
         feat_q[g], attn[g] = call(
-            functools.partial(query_kernel, g % 2),
+            query_kernel,
             [cols(query, g), wrows(w_query, g), whole(feat_k[g])],
             [tok(BF16), ((GROUP, rows, rows), BF16)],
             f"query_attn_{g}",
@@ -430,7 +438,7 @@
 
     def numer_state(g):
         numer[g] = call(
-            functools.partial(numer_kernel, g % 2, order_of(g)),
+            functools.partial(numer_kernel, order_of(g)),
             [whole(first[g]), whole(second[g]), whole(feat_q[g]), whole(attn[g]), cols(value, g), cols(grad, g), cols(gain, g)],
             [sq(F32), tok(BF16), tok(BF16), sq(BF16), sq(BF16), ((GROUP, 8, HEAD), F32)],
             f"numer_{g}",
@@ -443,7 +451,7 @@
     def query_grad(g):
         _, low, rest, ph, pl_, gains = numer[g]
         mixed[g], back_q[g], sum_q[g] = call(
-            functools.partial(query_grad_kernel, g % 2),
+            query_grad_kernel,
             [whole(x) for x in (low, rest, ph, pl_, feat_k[g])]
             + [cols(query, g), cols(value, g), wrows(w_query, g), whole(gains)],
             [((GROUP, rows, rows), BF16), tok(BF16), ((GROUP, HEAD + 8, HEAD), F32)],
@@ -452,7 +460,7 @@
 
     def key_grad(g):
         pre_k[g], late_h[g], late_l[g], sum_k[g] = call(
-            functools.partial(key_grad_kernel, g % 2, order_of(g)),
+            functools.partial(key_grad_kernel, order_of(g)),
             [whole(first_back[g]), whole(second_back[g]), whole(mixed[g]), whole(feat_q[g])]
             + [cols(key, g), cols(value, g), wrows(w_key, g)],
             [tok(BF16), sq(BF16), sq(BF16), sq(F32)],
@@ -461,7 +469,7 @@
 
     def value_grad(g):
         back_k[g], back_v[g] = call(
-            functools.partial(value_grad_kernel, g % 2),
+            value_grad_kernel,
             [whole(x) for x in (attn[g], numer[g][1], feat_k[g], late_h[g], late_l[g], pre_k[g])] + [wrows(w_key, g)],
             [tok(BF16), tok(BF16)],
             f"value_grad_{g}",
@@ -471,23 +479,32 @@
 
     def core_hop(b):
         parts = sum_q if b > 1 else sum_k
-        parts = [whole(parts[2 * (b % 2)]), whole(parts[2 * (b % 2) + 1])]
-        shape = (2, 2) + parts[0][0].shape[1:]
-        kept, sent = call(core_kernel, parts, [(shape, F32)] * 2, f"core_{b}")
-        hops[b] = (kept, swap(sent, "dp", 1))
-
-    def near_hop(b):
-        inputs = [whole(x) for x in hops[2] + hops[3]]
-        kept, sent = call(near_kernel, inputs, [(hops[2][0].shape, F32)] * 2, "near")
-        hops[2] = (kept, swap(sent, "dp", 2))
-
-    def far_hop(b):
-        kept, sent = call(far_kernel, [whole(x) for x in hops[2]], [(hops[2][0].shape[1:], F32)] * 2, "far")
+        inputs = [whole(parts[2 * (b % 2)]), whole(parts[2 * (b % 2) + 1])]
+        shape = (2,) + parts[0].shape[1:]
+        both = ((2,) + shape, F32)
+        if b == 2:
+            kept, sent = call(core_kernel, inputs, [both, both], "core_2")
+            hops[b] = (kept, swap(sent, "dp", 1))
+        elif b == 3:
+            kept, sent, total = call(core_kernel, inputs + [whole(x) for x in hops[2]], [both] * 3, "core_3")
+            hops[2] = (total, kept, swap(sent, "dp", 1))
+        else:
+            kept, *sent = call(core_kernel, inputs, [both, (shape, F32), (shape, F32)], f"core_{b}")
+            hops[b] = (kept,) + tuple(swap(x, "dp", 1) for x in sent)
+
+    def far_hop(_):
+        kept, sent = call(far_kernel, [whole(x) for x in hops[2]], [(hops[2][0].shape, F32)] * 2, "far")
         hops[2] = (kept, swap(sent, "dp", 4))
+
+    def near_hop(_):
+        shape = hops[2][0].shape[1:]
+        outs = [(shape, F32), (shape[1:], F32), (shape[1:], F32)]
+        kept, *sent = call(near_kernel, [whole(x) for x in hops[2]], outs, "near")
+        hops[2] = (kept,) + tuple(swap(x, "dp", 2) for x in sent)
 
     def z_hop(b):
         inputs = hops[0] + hops[1]
-        own, *sent = call(spread_kernel, [whole(x) for x in inputs], [(inputs[1].shape[1:], F32)] * 4, "spread")
+        own, *sent = call(spread_kernel, [whole(x) for x in inputs], [(inputs[1].shape, F32)] * 4, "spread")
         hops[0] = (own,) + tuple(swap(x, "dp", 2 * bits) for bits, x in enumerate(sent, 1))
 
     totals = {}
@@ -496,7 +513,7 @@
         return (part,) + tuple(swap(part, "seq", bits) for bits in (1, 2, 3))
 
     def query_first(_):
-        parts = call(halves_kernel, [whole(x) for x in hops[2]], [(hops[2][0].shape[1:], F32)] * 2, "query_sum")
+        parts = call(halves_kernel, [whole(x) for x in hops[2]], [(hops[2][1].shape, F32)] * 2, "query_sum")
         totals["query"] = [(x, swap(x, "seq", bit)) for bit, x in enumerate(parts, 1)]
 
     def query_second(_):
@@ -536,8 +553,8 @@
 
     if tuned:
         steps = (
-            "K0K2Q0Q1p0p1Q2Q3p2p3N0N1G0G1N2N3a2G2G3",
-            "l0l1a3l2l3B2H0H1a0V0V1H2H3a1c2V2V3Z0E0L0L1C0F0L2T0",
+            "K0K2Q0Q1p1p0Q2Q3p3p2N0N1G0G1N2N3a2G2G3",
+            "l0l1a3l2l3B2H0H1a0V0V1H2H3a1V2V3Z0c2L0L1E0C0F0L2T0",
         )
         steps = "".join(steps)
     else:
@@ -554,8 +571,8 @@
         "V": value_grad,
         "L": lay,
         "a": core_hop,
-        "B": near_hop,
-        "c": far_hop,
+        "B": far_hop,
+        "c": near_hop,
         "Z": z_hop,
         "E": query_first,
         "F": query_second,
@@ -569,11 +586,7 @@
     else:
 
         def in_order(parts):
-            spread = [None] * heads
-            for g in range(groups):
-                for i in range(GROUP):
-                    spread[head_of(g, i)] = parts[g][i]
-            return jnp.stack(spread)
+            return jnp.concatenate(listed(parts), axis=0)
 
         both = in_order(sum_q)
         owned = (

time: 86.6 us -> 83.5 us (0.964)
  the two profiles are of different devices: /device:TPU:21 before, /device:TPU:0 now
where the time goes in v3:
time: 83.5 us; the launch traced here: 83.3 us
  starting transfers between devices  36.2 us (43%)
  waiting for transfers between devices  28.6 us (34%)
  Pallas kernels  17.5 us (21%)
  between operations  1.03 us (1%)
    ppermute x35, starting transfers between devices, swap(): lax.ppermute(value, axis, [(i, i ^ bit) for i in range(lax.axis_size(axis...  36.2 us
    ppermute x35, waiting for transfers between devices, swap(): lax.ppermute(value, axis, [(i, i ^ bit) for i in range(lax.axis_size(axis...  28.6 us
    pallas_call x44, Pallas kernels, __call__(): pl.pallas_call(ordered, grid=(1,), in_specs=[spec for _, spec in ins], ou...  17.5 us
  transfers between devices with their start and end apart: 35, of which 17 were waited for; matrix products, arithmetic and copies ran while one was open for 0% of the time, Pallas kernels for 18%

profile of v3, /device:TPU:0, one launch (start us, length us, event | category | flops | bytes accessed | tf_op | source)
XLA Modules:
  0.0 83.3 jit_solution(11776673385868999337)
XLA Ops:
  0.7 1.7 %key_state_first.1 = (bf16[4,128,128]{2,1,0:T(8,128)(2,1)S(1)}, f32[4,128,128]{2,1,0:T(8,128)S(1)}, bf16[4,128,128]{2,1,0:T(8,128)(2,1)S(1)}, f32[4,128,128]{2,1,0:T(8,128)S(1)}, f32[8,128]{1,0:T(8,128)S(1)}) custom-call(bf16[128,2048]{1,0:T(8,128)(2,1)} %bitcast.31, bf16[128,2048]{1,0:T(8,128)(2,1)} %bitcast.9, bf16[2048,128]{1,0:T(8,128)(2,1)} %refs_6_.15), custom_call_target="tpu_custom_call" | custom-call | flops 200000000 | tf_op jit(solution)/shard_map/key_state_first/pallas_call | solution.py:317
  2.4 3.0 %collective-permute-start.1 = (f32[4,128,128]{2,1,0:T(8,128)S(1)}, f32[4,128,128]{2,1,0:T(8,128)S(1)}, u32[]{:S(2)}, u32[]{:S(2)}) collective-permute-start(f32[4,128,128]{2,1,0:T(8,128)S(1)} %get-tuple-element.165.refs_0_), channel_id=1, source_target_pairs={{0,2},{1,3},{2,0},{3,1},{4,6},{5,7},{6,4},{7,5},{8,10},{9,11},{10,... | collective-permute-start | bytes 786440 | tf_op jit(solution)/shard_map/ppermute | solution.py:354
  5.4 1.5 %collective-permute-start = (f32[4,128,128]{2,1,0:T(8,128)S(1)}, f32[4,128,128]{2,1,0:T(8,128)S(1)}, u32[]{:S(2)}, u32[]{:S(2)}) collective-permute-start(f32[4,128,128]{2,1,0:T(8,128)S(1)} %get-tuple-element.164.refs_0_), channel_id=1, source_target_pairs={{0,1},{1,0},{2,3},{3,2},{4,5},{5,4},{6,7},{7,6},{8,9},{9,8},{10,11... | collective-permute-start | bytes 786440 | tf_op jit(solution)/shard_map/ppermute | solution.py:354
  8.8 3.8 %collective-permute-done.1.refs_1_.refs_0_ = f32[4,128,128]{2,1,0:T(8,128)S(1)} collective-permute-done((f32[4,128,128]{2,1,0:T(8,128)S(1)}, f32[4,128,128]{2,1,0:T(8,128)S(1)}, u32[]{:S(2)}, u32[]{:S(2)}) %collective-permute-start.1) | collective-permute-done | bytes 262176 | tf_op jit(solution)/shard_map/ppermute | solution.py:354
  12.6 2.0 %collective-permute-done.refs_1_.refs_0_ = f32[4,128,128]{2,1,0:T(8,128)S(1)} collective-permute-done((f32[4,128,128]{2,1,0:T(8,128)S(1)}, f32[4,128,128]{2,1,0:T(8,128)S(1)}, u32[]{:S(2)}, u32[]{:S(2)}) %collective-permute-start) | collective-permute-done | bytes 262176 | tf_op jit(solution)/shard_map/ppermute | solution.py:354
  14.8 2.0 %collective-permute-start.5 = (f32[4,128,128]{2,1,0:T(8,128)S(1)}, f32[4,128,128]{2,1,0:T(8,128)S(1)}, u32[]{:S(2)}, u32[]{:S(2)}) collective-permute-start(f32[4,128,128]{2,1,0:T(8,128)S(1)} %get-tuple-element.190), channel_id=1, source_target_pairs={{0,1},{1,0},{2,3},{3,2},{4,5},{5,4},{6,7},{7,6},{8,9},{9,8},{10,11... | collective-permute-start | bytes 786440 | tf_op jit(solution)/shard_map/ppermute | solution.py:354
  17.4 0.7 collective-permute-done.4.refs_1_.refs_0_
  18.2 2.0 %collective-permute-done.3.refs_1_.refs_0_ = f32[4,128,128]{2,1,0:T(8,128)S(1)} collective-permute-done((f32[4,128,128]{2,1,0:T(8,128)S(1)}, f32[4,128,128]{2,1,0:T(8,128)S(1)}, u32[]{:S(2)}, u32[]{:S(2)}) %collective-permute-start.3) | collective-permute-done | bytes 262176 | tf_op jit(solution)/shard_map/ppermute | solution.py:354
  20.4 2.0 %collective-permute-start.7 = (f32[4,128,128]{2,1,0:T(8,128)S(1)}, f32[4,128,128]{2,1,0:T(8,128)S(1)}, u32[]{:S(2)}, u32[]{:S(2)}) collective-permute-start(f32[4,128,128]{2,1,0:T(8,128)S(1)} %get-tuple-element.214), channel_id=1, source_target_pairs={{0,1},{1,0},{2,3},{3,2},{4,5},{5,4},{6,7},{7,6},{8,9},{9,8},{10,11... | collective-permute-start | bytes 786440 | tf_op jit(solution)/shard_map/ppermute | solution.py:354
  22.4 1.6 %collective-permute-done.2.refs_1_ = f32[4,128,128]{2,1,0:T(8,128)S(1)} collective-permute-done((f32[4,128,128]{2,1,0:T(8,128)S(1)}, f32[4,128,128]{2,1,0:T(8,128)S(1)}, u32[]{:S(2)}, u32[]{:S(2)}) %collective-permute-start.2) | collective-permute-done | bytes 262176 | tf_op jit(solution)/shard_map/ppermute | solution.py:354
  24.0 0.6 numer_0.1
  24.6 1.9 %collective-permute-start.10 = (f32[4,128,128]{2,1,0:T(8,128)S(1)}, f32[4,128,128]{2,1,0:T(8,128)S(1)}, u32[]{:S(2)}, u32[]{:S(2)}) collective-permute-start(f32[4,128,128]{2,1,0:T(8,128)S(1)} %get-tuple-element.233.refs_0_), channel_id=1, source_target_pairs={{0,1},{1,0},{2,3},{3,2},{4,5},{5,4},{6,7},{7,6},{8,9},{9,8},{10,11... | collective-permute-start | bytes 786440 | tf_op jit(solution)/shard_map/ppermute | solution.py:354
  26.5 0.6 numer_1.1
  27.1 1.6 %collective-permute-start.9 = (f32[4,128,128]{2,1,0:T(8,128)S(1)}, f32[4,128,128]{2,1,0:T(8,128)S(1)}, u32[]{:S(2)}, u32[]{:S(2)}) collective-permute-start(f32[4,128,128]{2,1,0:T(8,128)S(1)} %get-tuple-element.232.refs_0_), channel_id=1, source_target_pairs={{0,2},{1,3},{2,0},{3,1},{4,6},{5,7},{6,4},{7,5},{8,10},{9,11},{10,... | collective-permute-start | bytes 786440 | tf_op jit(solution)/shard_map/ppermute | solution.py:354
  28.7 0.8 query_grad_0.1
  29.5 0.8 %query_grad_1.1 = (bf16[4,128,128]{2,1,0:T(8,128)(2,1)S(1)}, bf16[4,128,128]{2,1,0:T(8,128)(2,1)S(1)}, f32[4,136,128]{2,1,0:T(8,128)S(1)}, f32[8,128]{1,0:T(8,128)S(1)}) custom-call(bf16[4,128,128]{2,1,0:T(8,128)(2,1)S(1)} %get-tuple-element.196.refs_0_.refs_1_, bf16[4,128,128]{2,1,0:T(8,128)(2,1)S(1)} %get-tuple-element.197.refs_1_, ...), custom_call_target="tpu_custom_call" | custom-call | flops 200000000 | tf_op jit(solution)/shard_map/query_grad_1/pallas_call | solution.py:317
  30.4 0.6 numer_2.1
  31.5 0.6 numer_3.1
  32.3 1.5 %collective-permute-start.13 = (f32[4,128,128]{2,1,0:T(8,128)S(1)}, f32[4,128,128]{2,1,0:T(8,128)S(1)}, u32[]{:S(2)}, u32[]{:S(2)}) collective-permute-start(f32[4,128,128]{2,1,0:T(8,128)S(1)} %get-tuple-element.241.refs_0_), channel_id=1, source_target_pairs={{0,1},{1,0},{2,3},{3,2},{4,5},{5,4},{6,7},{7,6},{8,9},{9,8},{10,11... | collective-permute-start | bytes 786440 | tf_op jit(solution)/shard_map/ppermute | solution.py:354
  33.8 0.6 collective-permute-start.12
  34.4 0.8 %query_grad_2.1 = (bf16[4,128,128]{2,1,0:T(8,128)(2,1)S(1)}, bf16[4,128,128]{2,1,0:T(8,128)(2,1)S(1)}, f32[4,136,128]{2,1,0:T(8,128)S(1)}, f32[8,128]{1,0:T(8,128)S(1)}) custom-call(bf16[4,128,128]{2,1,0:T(8,128)(2,1)S(1)} %get-tuple-element.207.refs_0_.refs_1_, bf16[4,128,128]{2,1,0:T(8,128)(2,1)S(1)} %get-tuple-element.208.refs_1_, ...), custom_call_target="tpu_custom_call" | custom-call | flops 200000000 | tf_op jit(solution)/shard_map/query_grad_2/pallas_call | solution.py:317
  35.3 0.8 %query_grad_3.1 = (bf16[4,128,128]{2,1,0:T(8,128)(2,1)S(1)}, bf16[4,128,128]{2,1,0:T(8,128)(2,1)S(1)}, f32[4,136,128]{2,1,0:T(8,128)S(1)}, f32[8,128]{1,0:T(8,128)S(1)}) custom-call(bf16[4,128,128]{2,1,0:T(8,128)(2,1)S(1)} %get-tuple-element.221.refs_0_.refs_1_, bf16[4,128,128]{2,1,0:T(8,128)(2,1)S(1)} %get-tuple-element.222.refs_1_, ...), custom_call_target="tpu_custom_call" | custom-call | flops 200000000 | tf_op jit(solution)/shard_map/query_grad_3/pallas_call | solution.py:317
  36.4 1.5 %collective-permute-start.15 = (f32[4,128,128]{2,1,0:T(8,128)S(1)}, f32[4,128,128]{2,1,0:T(8,128)S(1)}, u32[]{:S(2)}, u32[]{:S(2)}) collective-permute-start(f32[4,128,128]{2,1,0:T(8,128)S(1)} %get-tuple-element.247), channel_id=1, source_target_pairs={{0,2},{1,3},{2,0},{3,1},{4,6},{5,7},{6,4},{7,5},{8,10},{9,11},{10,... | collective-permute-start | bytes 786440 | tf_op jit(solution)/shard_map/ppermute | solution.py:354
  38.4 3.1 %collective-permute-done.13.refs_1_.refs_0_ = f32[4,128,128]{2,1,0:T(8,128)S(1)} collective-permute-done((f32[4,128,128]{2,1,0:T(8,128)S(1)}, f32[4,128,128]{2,1,0:T(8,128)S(1)}, u32[]{:S(2)}, u32[]{:S(2)}) %collective-permute-start.13) | collective-permute-done | bytes 262176 | tf_op jit(solution)/shard_map/ppermute | solution.py:354
  42.0 0.9 %collective-permute-done.12.refs_1_.refs_0_ = f32[4,128,128]{2,1,0:T(8,128)S(1)} collective-permute-done((f32[4,128,128]{2,1,0:T(8,128)S(1)}, f32[4,128,128]{2,1,0:T(8,128)S(1)}, u32[]{:S(2)}, u32[]{:S(2)}) %collective-permute-start.12) | collective-permute-done | bytes 262176 | tf_op jit(solution)/shard_map/ppermute | solution.py:354
  43.0 0.8 collective-permute-start.20
  43.9 2.7 %collective-permute-start.14 = (f32[2,2,136,128]{3,2,1,0:T(8,128)S(1)}, f32[2,2,136,128]{3,2,1,0:T(8,128)S(1)}, u32[]{:S(2)}, u32[]{:S(2)}) collective-permute-start(f32[2,2,136,128]{3,2,1,0:T(8,128)S(1)} %get-tuple-element.246), channel_id=1, source_target_pairs={{0,16},{4,20},{8,24},{12,28},{16,0},{20,4},{24,8},{28,12},{1,17},{... | collective-permute-start | bytes 835592 | tf_op jit(solution)/shard_map/ppermute | solution.py:354
  46.5 2.0 %collective-permute-done.15.refs_1_ = f32[4,128,128]{2,1,0:T(8,128)S(1)} collective-permute-done((f32[4,128,128]{2,1,0:T(8,128)S(1)}, f32[4,128,128]{2,1,0:T(8,128)S(1)}, u32[]{:S(2)}, u32[]{:S(2)}) %collective-permute-start.15) | collective-permute-done | bytes 262176 | tf_op jit(solution)/shard_map/ppermute | solution.py:354
  50.5 2.9 %collective-permute-done.19.refs_1_ = f32[4,128,128]{2,1,0:T(8,128)S(1)} collective-permute-done((f32[4,128,128]{2,1,0:T(8,128)S(1)}, f32[4,128,128]{2,1,0:T(8,128)S(1)}, u32[]{:S(2)}, u32[]{:S(2)}) %collective-permute-start.19) | collective-permute-done | bytes 262176 | tf_op jit(solution)/shard_map/ppermute | solution.py:354
  56.8 1.7 %collective-permute-start.27 = (f32[2,128,128]{2,1,0:T(8,128)S(1)}, f32[2,128,128]{2,1,0:T(8,128)S(1)}, u32[]{:S(2)}, u32[]{:S(2)}) collective-permute-start(f32[2,128,128]{2,1,0:T(8,128)S(1)} %get-tuple-element.308), channel_id=1, source_target_pairs={{0,8},{4,12},{8,0},{12,4},{16,24},{20,28},{24,16},{28,20},{1,9},{5... | collective-permute-start | bytes 393224 | tf_op jit(solution)/shard_map/ppermute | solution.py:354
  58.5 2.6 %collective-permute-start.28 = (f32[2,128,128]{2,1,0:T(8,128)S(1)}, f32[2,128,128]{2,1,0:T(8,128)S(1)}, u32[]{:S(2)}, u32[]{:S(2)}) collective-permute-start(f32[2,128,128]{2,1,0:T(8,128)S(1)} %get-tuple-element.309), channel_id=1, source_target_pairs={{0,16},{4,20},{8,24},{12,28},{16,0},{20,4},{24,8},{28,12},{1,17},{... | collective-permute-start | bytes 393224 | tf_op jit(solution)/shard_map/ppermute | solution.py:354
  61.3 0.8 collective-permute-start.23
  62.1 1.3 %collective-permute-start.24 = (f32[136,128]{1,0:T(8,128)S(1)}, f32[136,128]{1,0:T(8,128)S(1)}, u32[]{:S(2)}, u32[]{:S(2)}) collective-permute-start(f32[136,128]{1,0:T(8,128)S(1)} %get-tuple-element.303), channel_id=1, source_target_pairs={{0,8},{4,12},{8,0},{12,4},{16,24},{20,28},{24,16},{28,20},{1,9},{5... | collective-permute-start | bytes 208904 | tf_op jit(solution)/shard_map/ppermute | solution.py:354
  63.4 0.9 %lay_0.1 = (bf16[128,2048]{1,0:T(8,128)(2,1)}, f32[8,128]{1,0:T(8,128)S(1)}) custom-call(bf16[4,128,128]{2,1,0:T(8,128)(2,1)S(1)} %get-tuple-element.195.refs_0_, bf16[4,128,128]{2,1,0:T(8,128)(2,1)S(1)} %get-tuple-element.202.refs_1_, bf16[4,128,128]{2,1,0:T(8,128)(2,1)S(1)} %get-tuple-element.220.refs_2_, ...), custom_call_target="tpu_custom_call" | custom-call | flops 200000000 | tf_op jit(solution)/shard_map/lay_0/pallas_call | solution.py:317
  64.4 0.9 %lay_1.1 = (bf16[128,2048]{1,0:T(8,128)(2,1)}, f32[8,128]{1,0:T(8,128)S(1)}) custom-call(bf16[4,128,128]{2,1,0:T(8,128)(2,1)S(1)} %get-tuple-element.291.refs_0_, bf16[4,128,128]{2,1,0:T(8,128)(2,1)S(1)} %get-tuple-element.292.refs_1_, bf16[4,128,128]{2,1,0:T(8,128)(2,1)S(1)} %get-tuple-element.293.refs_2_, ...), custom_call_target="tpu_custom_call" | custom-call | flops 200000000 | tf_op jit(solution)/shard_map/lay_1/pallas_call | solution.py:317
  65.3 4.1 %collective-permute-done.23.refs_1_ = f32[136,128]{1,0:T(8,128)S(1)} collective-permute-done((f32[136,128]{1,0:T(8,128)S(1)}, f32[136,128]{1,0:T(8,128)S(1)}, u32[]{:S(2)}, u32[]{:S(2)}) %collective-permute-start.23) | collective-permute-done | bytes 69664 | tf_op jit(solution)/shard_map/ppermute | solution.py:354
  69.4 1.6 %collective-permute-done.24.refs_2_ = f32[136,128]{1,0:T(8,128)S(1)} collective-permute-done((f32[136,128]{1,0:T(8,128)S(1)}, f32[136,128]{1,0:T(8,128)S(1)}, u32[]{:S(2)}, u32[]{:S(2)}) %collective-permute-start.24) | collective-permute-done | bytes 69664 | tf_op jit(solution)/shard_map/ppermute | solution.py:354
  71.0 0.7 collective-permute-start.25
  72.3 1.5 %collective-permute-start.32 = (f32[2,128,128]{2,1,0:T(8,128)S(1)}, f32[2,128,128]{2,1,0:T(8,128)S(1)}, u32[]{:S(2)}, u32[]{:S(2)}) collective-permute-start(f32[2,128,128]{2,1,0:T(8,128)S(1)} %get-tuple-element.317.refs_4_), channel_id=1, source_target_pairs={{0,1},{1,0},{2,3},{3,2},{4,5},{5,4},{6,7},{7,6},{8,9},{9,8},{10,11... | collective-permute-start | bytes 393224 | tf_op jit(solution)/shard_map/ppermute | solution.py:354
  73.9 1.4 %collective-permute-start.33 = (f32[2,128,128]{2,1,0:T(8,128)S(1)}, f32[2,128,128]{2,1,0:T(8,128)S(1)}, u32[]{:S(2)}, u32[]{:S(2)}) collective-permute-start(f32[2,128,128]{2,1,0:T(8,128)S(1)} %get-tuple-element.317.refs_4_), channel_id=1, source_target_pairs={{0,2},{1,3},{2,0},{3,1},{4,6},{5,7},{6,4},{7,5},{8,10},{9,11},{10,... | collective-permute-start | bytes 393224 | tf_op jit(solution)/shard_map/ppermute | solution.py:354
  75.3 0.6 collective-permute-start.34
  75.9 0.8 collective-permute-done.26.refs_3_
  76.7 0.7 collective-permute-start.30
  77.4 2.0 %collective-permute-start.31 = (f32[136,128]{1,0:T(8,128)S(1)}, f32[136,128]{1,0:T(8,128)S(1)}, u32[]{:S(2)}, u32[]{:S(2)}) collective-permute-start(f32[136,128]{1,0:T(8,128)S(1)} %get-tuple-element.316.refs_2_), channel_id=1, source_target_pairs={{0,1},{1,0},{2,3},{3,2},{4,5},{5,4},{6,7},{7,6},{8,9},{9,8},{10,11... | collective-permute-start | bytes 208904 | tf_op jit(solution)/shard_map/ppermute | solution.py:354
  79.4 0.9 %lay_2.1 = (bf16[128,2048]{1,0:T(8,128)(2,1)}, f32[8,128]{1,0:T(8,128)S(1)}) custom-call(bf16[4,128,128]{2,1,0:T(8,128)(2,1)S(1)} %get-tuple-element.297.refs_0_, bf16[4,128,128]{2,1,0:T(8,128)(2,1)S(1)} %get-tuple-element.298.refs_1_, bf16[4,128,128]{2,1,0:T(8,128)(2,1)S(1)} %get-tuple-element.299.refs_2_, ...), custom_call_target="tpu_custom_call" | custom-call | flops 200000000 | tf_op jit(solution)/shard_map/lay_2/pallas_call | solution.py:317
  80.3 1.5 %collective-permute-done.33.refs_6_ = f32[2,128,128]{2,1,0:T(8,128)S(1)} collective-permute-done((f32[2,128,128]{2,1,0:T(8,128)S(1)}, f32[2,128,128]{2,1,0:T(8,128)S(1)}, u32[]{:S(2)}, u32[]{:S(2)}) %collective-permute-start.33) | collective-permute-done | bytes 131104 | tf_op jit(solution)/shard_map/ppermute | solution.py:354
  81.8 0.7 collective-permute-done.30.refs_1_
  82.6 0.7 total.1
  (80 shorter events, 11.2 us)
Async XLA Ops:
  0.6 6.3 %copy-start = (bf16[1,128,2048]{2,1,0:T(8,128)(2,1)S(1)}, bf16[1,128,2048]{2,1,0:T(8,128)(2,1)}, u32[]{:S(2)}) copy-start(bf16[1,128,2048]{2,1,0:T(8,128)(2,1)} %param.9) | copy-start | bytes 1572868
  0.6 6.3 %copy-start.1 = (bf16[2048,128]{1,0:T(8,128)(2,1)S(1)}, bf16[2048,128]{1,0:T(8,128)(2,1)}, u32[]{:S(2)}) copy-start(bf16[2048,128]{1,0:T(8,128)(2,1)} %refs_6_.15) | copy-start | bytes 1572868
  0.7 6.3 %copy-start.4 = (bf16[1,128,2048]{2,1,0:T(8,128)(2,1)S(1)}, bf16[1,128,2048]{2,1,0:T(8,128)(2,1)}, u32[]{:S(2)}) copy-start(bf16[1,128,2048]{2,1,0:T(8,128)(2,1)} %param.8) | copy-start | bytes 1572868
  2.4 10.2 %collective-permute-start.1 = (f32[4,128,128]{2,1,0:T(8,128)S(1)}, f32[4,128,128]{2,1,0:T(8,128)S(1)}, u32[]{:S(2)}, u32[]{:S(2)}) collective-permute-start(f32[4,128,128]{2,1,0:T(8,128)S(1)} %get-tuple-element.165.refs_0_), channel_id=1, source_target_pairs={{0,2},{1,3},{2,0},{3,1},{4,6},{5,7},{6,4},{7,5},{8,10},{9,11},{10,... | collective-permute-start | bytes 786440 | tf_op jit(solution)/shard_map/ppermute | solution.py:354
  5.4 9.2 %collective-permute-start = (f32[4,128,128]{2,1,0:T(8,128)S(1)}, f32[4,128,128]{2,1,0:T(8,128)S(1)}, u32[]{:S(2)}, u32[]{:S(2)}) collective-permute-start(f32[4,128,128]{2,1,0:T(8,128)S(1)} %get-tuple-element.164.refs_0_), channel_id=1, source_target_pairs={{0,1},{1,0},{2,3},{3,2},{4,5},{5,4},{6,7},{7,6},{8,9},{9,8},{10,11... | collective-permute-start | bytes 786440 | tf_op jit(solution)/shard_map/ppermute | solution.py:354
  6.9 1.2 %copy-start.2 = (bf16[1,128,2048]{2,1,0:T(8,128)(2,1)S(1)}, bf16[1,128,2048]{2,1,0:T(8,128)(2,1)}, u32[]{:S(2)}) copy-start(bf16[1,128,2048]{2,1,0:T(8,128)(2,1)} %param.7) | copy-start | bytes 1572868
  6.9 1.2 %copy-start.3 = (bf16[2048,128]{1,0:T(8,128)(2,1)S(1)}, bf16[2048,128]{1,0:T(8,128)(2,1)}, u32[]{:S(2)}) copy-start(bf16[2048,128]{1,0:T(8,128)(2,1)} %refs_7_.7) | copy-start | bytes 1572868
  7.4 10.7 %collective-permute-start.4 = (f32[4,128,128]{2,1,0:T(8,128)S(1)}, f32[4,128,128]{2,1,0:T(8,128)S(1)}, u32[]{:S(2)}, u32[]{:S(2)}) collective-permute-start(f32[4,128,128]{2,1,0:T(8,128)S(1)} %get-tuple-element.177.refs_0_), channel_id=1, source_target_pairs={{0,2},{1,3},{2,0},{3,1},{4,6},{5,7},{6,4},{7,5},{8,10},{9,11},{10,... | collective-permute-start | bytes 786440 | tf_op jit(solution)/shard_map/ppermute | solution.py:354
  8.0 12.3 %collective-permute-start.3 = (f32[4,128,128]{2,1,0:T(8,128)S(1)}, f32[4,128,128]{2,1,0:T(8,128)S(1)}, u32[]{:S(2)}, u32[]{:S(2)}) collective-permute-start(f32[4,128,128]{2,1,0:T(8,128)S(1)} %get-tuple-element.176.refs_0_), channel_id=1, source_target_pairs={{0,1},{1,0},{2,3},{3,2},{4,5},{5,4},{6,7},{7,6},{8,9},{9,8},{10,11... | collective-permute-start | bytes 786440 | tf_op jit(solution)/shard_map/ppermute | solution.py:354
  14.7 9.3 %collective-permute-start.2 = (f32[4,128,128]{2,1,0:T(8,128)S(1)}, f32[4,128,128]{2,1,0:T(8,128)S(1)}, u32[]{:S(2)}, u32[]{:S(2)}) collective-permute-start(f32[4,128,128]{2,1,0:T(8,128)S(1)} %get-tuple-element.173), channel_id=1, source_target_pairs={{0,2},{1,3},{2,0},{3,1},{4,6},{5,7},{6,4},{7,5},{8,10},{9,11},{10,... | collective-permute-start | bytes 786440 | tf_op jit(solution)/shard_map/ppermute | solution.py:354
  14.8 11.7 %collective-permute-start.5 = (f32[4,128,128]{2,1,0:T(8,128)S(1)}, f32[4,128,128]{2,1,0:T(8,128)S(1)}, u32[]{:S(2)}, u32[]{:S(2)}) collective-permute-start(f32[4,128,128]{2,1,0:T(8,128)S(1)} %get-tuple-element.190), channel_id=1, source_target_pairs={{0,1},{1,0},{2,3},{3,2},{4,5},{5,4},{6,7},{7,6},{8,9},{9,8},{10,11... | collective-permute-start | bytes 786440 | tf_op jit(solution)/shard_map/ppermute | solution.py:354
  18.2 5.8 %copy-start.5 = (bf16[1,128,2048]{2,1,0:T(8,128)(2,1)S(1)}, bf16[1,128,2048]{2,1,0:T(8,128)(2,1)}, u32[]{:S(2)}) copy-start(bf16[1,128,2048]{2,1,0:T(8,128)(2,1)} %param.10) | copy-start | bytes 1572868
  20.3 3.7 %copy-start.6 = (f32[2048]{0:T(1024)S(1)}, f32[2048]{0:T(1024)}, u32[]{:S(2)}) copy-start(f32[2048]{0:T(1024)} %param.13) | copy-start | bytes 24580
  20.3 10.1 %collective-permute-start.6 = (f32[4,128,128]{2,1,0:T(8,128)S(1)}, f32[4,128,128]{2,1,0:T(8,128)S(1)}, u32[]{:S(2)}, u32[]{:S(2)}) collective-permute-start(f32[4,128,128]{2,1,0:T(8,128)S(1)} %get-tuple-element.203), channel_id=1, source_target_pairs={{0,2},{1,3},{2,0},{3,1},{4,6},{5,7},{6,4},{7,5},{8,10},{9,11},{10,... | collective-permute-start | bytes 786440 | tf_op jit(solution)/shard_map/ppermute | solution.py:354
  20.4 11.1 %collective-permute-start.7 = (f32[4,128,128]{2,1,0:T(8,128)S(1)}, f32[4,128,128]{2,1,0:T(8,128)S(1)}, u32[]{:S(2)}, u32[]{:S(2)}) collective-permute-start(f32[4,128,128]{2,1,0:T(8,128)S(1)} %get-tuple-element.214), channel_id=1, source_target_pairs={{0,1},{1,0},{2,3},{3,2},{4,5},{5,4},{6,7},{7,6},{8,9},{9,8},{10,11... | collective-permute-start | bytes 786440 | tf_op jit(solution)/shard_map/ppermute | solution.py:354
  24.6 11.5 %collective-permute-start.10 = (f32[4,128,128]{2,1,0:T(8,128)S(1)}, f32[4,128,128]{2,1,0:T(8,128)S(1)}, u32[]{:S(2)}, u32[]{:S(2)}) collective-permute-start(f32[4,128,128]{2,1,0:T(8,128)S(1)} %get-tuple-element.233.refs_0_), channel_id=1, source_target_pairs={{0,1},{1,0},{2,3},{3,2},{4,5},{5,4},{6,7},{7,6},{8,9},{9,8},{10,11... | collective-permute-start | bytes 786440 | tf_op jit(solution)/shard_map/ppermute | solution.py:354
  27.1 9.0 %collective-permute-start.9 = (f32[4,128,128]{2,1,0:T(8,128)S(1)}, f32[4,128,128]{2,1,0:T(8,128)S(1)}, u32[]{:S(2)}, u32[]{:S(2)}) collective-permute-start(f32[4,128,128]{2,1,0:T(8,128)S(1)} %get-tuple-element.232.refs_0_), channel_id=1, source_target_pairs={{0,2},{1,3},{2,0},{3,1},{4,6},{5,7},{6,4},{7,5},{8,10},{9,11},{10,... | collective-permute-start | bytes 786440 | tf_op jit(solution)/shard_map/ppermute | solution.py:354
  32.2 4.1 %collective-permute-start.8 = (f32[2,2,136,128]{3,2,1,0:T(8,128)S(1)}, f32[2,2,136,128]{3,2,1,0:T(8,128)S(1)}, u32[]{:S(2)}, u32[]{:S(2)}) collective-permute-start(f32[2,2,136,128]{3,2,1,0:T(8,128)S(1)} %get-tuple-element.231), channel_id=1, source_target_pairs={{0,4},{4,0},{8,12},{12,8},{16,20},{20,16},{24,28},{28,24},{1,5},{5... | collective-permute-start | bytes 835592 | tf_op jit(solution)/shard_map/ppermute | solution.py:354
  32.3 9.2 %collective-permute-start.13 = (f32[4,128,128]{2,1,0:T(8,128)S(1)}, f32[4,128,128]{2,1,0:T(8,128)S(1)}, u32[]{:S(2)}, u32[]{:S(2)}) collective-permute-start(f32[4,128,128]{2,1,0:T(8,128)S(1)} %get-tuple-element.241.refs_0_), channel_id=1, source_target_pairs={{0,1},{1,0},{2,3},{3,2},{4,5},{5,4},{6,7},{7,6},{8,9},{9,8},{10,11... | collective-permute-start | bytes 786440 | tf_op jit(solution)/shard_map/ppermute | solution.py:354
  33.8 9.2 %collective-permute-start.12 = (f32[4,128,128]{2,1,0:T(8,128)S(1)}, f32[4,128,128]{2,1,0:T(8,128)S(1)}, u32[]{:S(2)}, u32[]{:S(2)}) collective-permute-start(f32[4,128,128]{2,1,0:T(8,128)S(1)} %get-tuple-element.240.refs_0_), channel_id=1, source_target_pairs={{0,2},{1,3},{2,0},{3,1},{4,6},{5,7},{6,4},{7,5},{8,10},{9,11},{10,... | collective-permute-start | bytes 786440 | tf_op jit(solution)/shard_map/ppermute | solution.py:354
  36.3 7.5 %collective-permute-start.11 = (f32[2,2,136,128]{3,2,1,0:T(8,128)S(1)}, f32[2,2,136,128]{3,2,1,0:T(8,128)S(1)}, u32[]{:S(2)}, u32[]{:S(2)}) collective-permute-start(f32[2,2,136,128]{3,2,1,0:T(8,128)S(1)} %get-tuple-element.239), channel_id=1, source_target_pairs={{0,4},{4,0},{8,12},{12,8},{16,20},{20,16},{24,28},{28,24},{1,5},{5... | collective-permute-start | bytes 835592 | tf_op jit(solution)/shard_map/ppermute | solution.py:354
  36.4 12.2 %collective-permute-start.15 = (f32[4,128,128]{2,1,0:T(8,128)S(1)}, f32[4,128,128]{2,1,0:T(8,128)S(1)}, u32[]{:S(2)}, u32[]{:S(2)}) collective-permute-start(f32[4,128,128]{2,1,0:T(8,128)S(1)} %get-tuple-element.247), channel_id=1, source_target_pairs={{0,2},{1,3},{2,0},{3,1},{4,6},{5,7},{6,4},{7,5},{8,10},{9,11},{10,... | collective-permute-start | bytes 786440 | tf_op jit(solution)/shard_map/ppermute | solution.py:354
  37.9 11.3 %collective-permute-start.16 = (f32[4,128,128]{2,1,0:T(8,128)S(1)}, f32[4,128,128]{2,1,0:T(8,128)S(1)}, u32[]{:S(2)}, u32[]{:S(2)}) collective-permute-start(f32[4,128,128]{2,1,0:T(8,128)S(1)} %get-tuple-element.251), channel_id=1, source_target_pairs={{0,1},{1,0},{2,3},{3,2},{4,5},{5,4},{6,7},{7,6},{8,9},{9,8},{10,11... | collective-permute-start | bytes 786440 | tf_op jit(solution)/shard_map/ppermute | solution.py:354
  41.5 11.9 %collective-permute-start.19 = (f32[4,128,128]{2,1,0:T(8,128)S(1)}, f32[4,128,128]{2,1,0:T(8,128)S(1)}, u32[]{:S(2)}, u32[]{:S(2)}) collective-permute-start(f32[4,128,128]{2,1,0:T(8,128)S(1)} %get-tuple-element.259), channel_id=1, source_target_pairs={{0,2},{1,3},{2,0},{3,1},{4,6},{5,7},{6,4},{7,5},{8,10},{9,11},{10,... | collective-permute-start | bytes 786440 | tf_op jit(solution)/shard_map/ppermute | solution.py:354
  43.0 11.0 %collective-permute-start.20 = (f32[4,128,128]{2,1,0:T(8,128)S(1)}, f32[4,128,128]{2,1,0:T(8,128)S(1)}, u32[]{:S(2)}, u32[]{:S(2)}) collective-permute-start(f32[4,128,128]{2,1,0:T(8,128)S(1)} %get-tuple-element.271), channel_id=1, source_target_pairs={{0,1},{1,0},{2,3},{3,2},{4,5},{5,4},{6,7},{7,6},{8,9},{9,8},{10,11... | collective-permute-start | bytes 786440 | tf_op jit(solution)/shard_map/ppermute | solution.py:354
  43.9 17.4 %collective-permute-start.14 = (f32[2,2,136,128]{3,2,1,0:T(8,128)S(1)}, f32[2,2,136,128]{3,2,1,0:T(8,128)S(1)}, u32[]{:S(2)}, u32[]{:S(2)}) collective-permute-start(f32[2,2,136,128]{3,2,1,0:T(8,128)S(1)} %get-tuple-element.246), channel_id=1, source_target_pairs={{0,16},{4,20},{8,24},{12,28},{16,0},{20,4},{24,8},{28,12},{1,17},{... | collective-permute-start | bytes 835592 | tf_op jit(solution)/shard_map/ppermute | solution.py:354
  54.6 1.8 %collective-permute-start.21 = (f32[2,128,128]{2,1,0:T(8,128)S(1)}, f32[2,128,128]{2,1,0:T(8,128)S(1)}, u32[]{:S(2)}, u32[]{:S(2)}) collective-permute-start(f32[2,128,128]{2,1,0:T(8,128)S(1)} %get-tuple-element.277), channel_id=1, source_target_pairs={{0,4},{4,0},{8,12},{12,8},{16,20},{20,16},{24,28},{28,24},{1,5},{5... | collective-permute-start | bytes 393224 | tf_op jit(solution)/shard_map/ppermute | solution.py:354
  54.7 1.8 %collective-permute-start.22 = (f32[2,128,128]{2,1,0:T(8,128)S(1)}, f32[2,128,128]{2,1,0:T(8,128)S(1)}, u32[]{:S(2)}, u32[]{:S(2)}) collective-permute-start(f32[2,128,128]{2,1,0:T(8,128)S(1)} %get-tuple-element.278), channel_id=1, source_target_pairs={{0,4},{4,0},{8,12},{12,8},{16,20},{20,16},{24,28},{28,24},{1,5},{5... | collective-permute-start | bytes 393224 | tf_op jit(solution)/shard_map/ppermute | solution.py:354
  55.2 1.3 %collective-permute-start.17 = (f32[2,128,128]{2,1,0:T(8,128)S(1)}, f32[2,128,128]{2,1,0:T(8,128)S(1)}, u32[]{:S(2)}, u32[]{:S(2)}) collective-permute-start(f32[2,128,128]{2,1,0:T(8,128)S(1)} %get-tuple-element.257), channel_id=1, source_target_pairs={{0,4},{4,0},{8,12},{12,8},{16,20},{20,16},{24,28},{28,24},{1,5},{5... | collective-permute-start | bytes 393224 | tf_op jit(solution)/shard_map/ppermute | solution.py:354
  55.3 1.5 %collective-permute-start.18 = (f32[2,128,128]{2,1,0:T(8,128)S(1)}, f32[2,128,128]{2,1,0:T(8,128)S(1)}, u32[]{:S(2)}, u32[]{:S(2)}) collective-permute-start(f32[2,128,128]{2,1,0:T(8,128)S(1)} %get-tuple-element.258), channel_id=1, source_target_pairs={{0,4},{4,0},{8,12},{12,8},{16,20},{20,16},{24,28},{28,24},{1,5},{5... | collective-permute-start | bytes 393224 | tf_op jit(solution)/shard_map/ppermute | solution.py:354
  56.8 15.4 %collective-permute-start.27 = (f32[2,128,128]{2,1,0:T(8,128)S(1)}, f32[2,128,128]{2,1,0:T(8,128)S(1)}, u32[]{:S(2)}, u32[]{:S(2)}) collective-permute-start(f32[2,128,128]{2,1,0:T(8,128)S(1)} %get-tuple-element.308), channel_id=1, source_target_pairs={{0,8},{4,12},{8,0},{12,4},{16,24},{20,28},{24,16},{28,20},{1,9},{5... | collective-permute-start | bytes 393224 | tf_op jit(solution)/shard_map/ppermute | solution.py:354
  58.5 13.8 %collective-permute-start.28 = (f32[2,128,128]{2,1,0:T(8,128)S(1)}, f32[2,128,128]{2,1,0:T(8,128)S(1)}, u32[]{:S(2)}, u32[]{:S(2)}) collective-permute-start(f32[2,128,128]{2,1,0:T(8,128)S(1)} %get-tuple-element.309), channel_id=1, source_target_pairs={{0,16},{4,20},{8,24},{12,28},{16,0},{20,4},{24,8},{28,12},{1,17},{... | collective-permute-start | bytes 393224 | tf_op jit(solution)/shard_map/ppermute | solution.py:354
  61.1 11.2 %collective-permute-start.29 = (f32[2,128,128]{2,1,0:T(8,128)S(1)}, f32[2,128,128]{2,1,0:T(8,128)S(1)}, u32[]{:S(2)}, u32[]{:S(2)}) collective-permute-start(f32[2,128,128]{2,1,0:T(8,128)S(1)} %get-tuple-element.310), channel_id=1, source_target_pairs={{0,24},{4,28},{8,16},{12,20},{16,8},{20,12},{24,0},{28,4},{1,25},{... | collective-permute-start | bytes 393224 | tf_op jit(solution)/shard_map/ppermute | solution.py:354
  61.3 8.0 %collective-permute-start.23 = (f32[136,128]{1,0:T(8,128)S(1)}, f32[136,128]{1,0:T(8,128)S(1)}, u32[]{:S(2)}, u32[]{:S(2)}) collective-permute-start(f32[136,128]{1,0:T(8,128)S(1)} %get-tuple-element.302), channel_id=1, source_target_pairs={{0,8},{4,12},{8,0},{12,4},{16,24},{20,28},{24,16},{28,20},{1,9},{5... | collective-permute-start | bytes 208904 | tf_op jit(solution)/shard_map/ppermute | solution.py:354
  62.1 8.9 %collective-permute-start.24 = (f32[136,128]{1,0:T(8,128)S(1)}, f32[136,128]{1,0:T(8,128)S(1)}, u32[]{:S(2)}, u32[]{:S(2)}) collective-permute-start(f32[136,128]{1,0:T(8,128)S(1)} %get-tuple-element.303), channel_id=1, source_target_pairs={{0,8},{4,12},{8,0},{12,4},{16,24},{20,28},{24,16},{28,20},{1,9},{5... | collective-permute-start | bytes 208904 | tf_op jit(solution)/shard_map/ppermute | solution.py:354
  71.0 4.9 %collective-permute-start.25 = (f32[136,128]{1,0:T(8,128)S(1)}, f32[136,128]{1,0:T(8,128)S(1)}, u32[]{:S(2)}, u32[]{:S(2)}) collective-permute-start(f32[136,128]{1,0:T(8,128)S(1)} %get-tuple-element.305.refs_0_), channel_id=1, source_target_pairs={{0,1},{1,0},{2,3},{3,2},{4,5},{5,4},{6,7},{7,6},{8,9},{9,8},{10,11... | collective-permute-start | bytes 208904 | tf_op jit(solution)/shard_map/ppermute | solution.py:354
  71.7 5.0 %collective-permute-start.26 = (f32[136,128]{1,0:T(8,128)S(1)}, f32[136,128]{1,0:T(8,128)S(1)}, u32[]{:S(2)}, u32[]{:S(2)}) collective-permute-start(f32[136,128]{1,0:T(8,128)S(1)} %get-tuple-element.306.refs_2_), channel_id=1, source_target_pairs={{0,2},{1,3},{2,0},{3,1},{4,6},{5,7},{6,4},{7,5},{8,10},{9,11},{10,... | collective-permute-start | bytes 208904 | tf_op jit(solution)/shard_map/ppermute | solution.py:354
  72.3 8.0 %collective-permute-start.32 = (f32[2,128,128]{2,1,0:T(8,128)S(1)}, f32[2,128,128]{2,1,0:T(8,128)S(1)}, u32[]{:S(2)}, u32[]{:S(2)}) collective-permute-start(f32[2,128,128]{2,1,0:T(8,128)S(1)} %get-tuple-element.317.refs_4_), channel_id=1, source_target_pairs={{0,1},{1,0},{2,3},{3,2},{4,5},{5,4},{6,7},{7,6},{8,9},{9,8},{10,11... | collective-permute-start | bytes 393224 | tf_op jit(solution)/shard_map/ppermute | solution.py:354
  73.9 8.0 %collective-permute-start.33 = (f32[2,128,128]{2,1,0:T(8,128)S(1)}, f32[2,128,128]{2,1,0:T(8,128)S(1)}, u32[]{:S(2)}, u32[]{:S(2)}) collective-permute-start(f32[2,128,128]{2,1,0:T(8,128)S(1)} %get-tuple-element.317.refs_4_), channel_id=1, source_target_pairs={{0,2},{1,3},{2,0},{3,1},{4,6},{5,7},{6,4},{7,5},{8,10},{9,11},{10,... | collective-permute-start | bytes 393224 | tf_op jit(solution)/shard_map/ppermute | solution.py:354
  75.3 6.6 %collective-permute-start.34 = (f32[2,128,128]{2,1,0:T(8,128)S(1)}, f32[2,128,128]{2,1,0:T(8,128)S(1)}, u32[]{:S(2)}, u32[]{:S(2)}) collective-permute-start(f32[2,128,128]{2,1,0:T(8,128)S(1)} %get-tuple-element.317.refs_4_), channel_id=1, source_target_pairs={{0,3},{1,2},{2,1},{3,0},{4,7},{5,6},{6,5},{7,4},{8,11},{9,10},{10,... | collective-permute-start | bytes 393224 | tf_op jit(solution)/shard_map/ppermute | solution.py:354
  76.7 5.9 %collective-permute-start.30 = (f32[136,128]{1,0:T(8,128)S(1)}, f32[136,128]{1,0:T(8,128)S(1)}, u32[]{:S(2)}, u32[]{:S(2)}) collective-permute-start(f32[136,128]{1,0:T(8,128)S(1)} %get-tuple-element.315.refs_0_), channel_id=1, source_target_pairs={{0,2},{1,3},{2,0},{3,1},{4,6},{5,7},{6,4},{7,5},{8,10},{9,11},{10,... | collective-permute-start | bytes 208904 | tf_op jit(solution)/shard_map/ppermute | solution.py:354
  77.4 5.2 %collective-permute-start.31 = (f32[136,128]{1,0:T(8,128)S(1)}, f32[136,128]{1,0:T(8,128)S(1)}, u32[]{:S(2)}, u32[]{:S(2)}) collective-permute-start(f32[136,128]{1,0:T(8,128)S(1)} %get-tuple-element.316.refs_2_), channel_id=1, source_target_pairs={{0,1},{1,0},{2,3},{3,2},{4,5},{5,4},{6,7},{7,6},{8,9},{9,8},{10,11... | collective-permute-start | bytes 208904 | tf_op jit(solution)/shard_map/ppermute | solution.py:354

commit v4 on v3

--- a/solution.py
+++ b/solution.py
@@ -9,7 +9,7 @@
 
 HEAD = 128
 GROUP = 4
-FIRST_VMEM = 64 * 1024 - 4000
+KEY_VMEM = (64 * 1024 - 4000, 64 * 1024 - 10000)
 NORM_EPS = 1e-05
 F32 = jnp.float32
 BF16 = jnp.bfloat16
@@ -77,13 +77,9 @@
             outs[2 * g + 1][i] = states[g * GROUP + i]
 
 
-def key_kernel(key, value, w_key, *outs):
-    key_states(key_features(key, w_key), value, *outs)
-
-
-def first_kernel(key, value, w_key, *refs):
+def key_kernel(block, key, value, w_key, *refs):
     outs, (key_buf, value_buf, w_buf, sems) = refs[:4], refs[4:]
-    span = pl.ds(0, key_buf.shape[1])
+    span = pl.ds(block * key_buf.shape[1], key_buf.shape[1])
     copies = [
         pltpu.make_async_copy(key.at[:, span], key_buf, sems.at[0]),
         pltpu.make_async_copy(w_key.at[span, :], w_buf, sems.at[1]),
@@ -268,14 +264,17 @@
     odd_out[...] = odd[...] + odd_other[...]
 
 
-def total_kernel(*refs):
-    query, (key, key_x, key_y, key_d), (out_q, out_k, out_gain) = refs[:4], refs[4:8], refs[8:]
-    total_k = (key[...] + key_x[...]) + (key_y[...] + key_d[...])
+def key_total_kernel(key, key_x, key_y, key_d, out):
+    total = (key[...] + key_x[...]) + (key_y[...] + key_d[...])
     for b in range(2):
-        total_q = query[2 * b][...] + query[2 * b + 1][...]
-        out_q[b * HEAD : (b + 1) * HEAD, :] = total_q[:HEAD, :]
-        out_gain[b : b + 1, :] = total_q[HEAD : HEAD + 1, :]
-        out_k[b * HEAD : (b + 1) * HEAD, :] = total_k[b]
+        out[b * HEAD : (b + 1) * HEAD, :] = total[b]
+
+
+def query_total_kernel(even, even_other, odd, odd_other, out, out_gain):
+    for b, (one, two) in enumerate(((even, even_other), (odd, odd_other))):
+        total = one[...] + two[...]
+        out[b * HEAD : (b + 1) * HEAD, :] = total[:HEAD, :]
+        out_gain[b : b + 1, :] = total[HEAD : HEAD + 1, :]
 
 
 def place(g, i):
@@ -408,19 +407,15 @@
     def key_state(g):
         outs = [tok(BF16), sq(F32)] * 2
         pair_wide = 2 * wide
-        if g == 0:
-            scratch = [
-                pltpu.VMEM((rows, pair_wide), BF16),
-                pltpu.VMEM((rows, pair_wide), BF16),
-                pltpu.VMEM((pair_wide, HEAD), BF16),
-                pltpu.SemaphoreType.DMA((3,)),
-            ]
-            inputs = [in_hbm(key), in_hbm(value), in_hbm(w_key)]
-            result = call(first_kernel, inputs, outs, "key_state_first", scratch, to_vmem=True, vmem=FIRST_VMEM)
-        else:
-            by_cols = pl.BlockSpec((rows, pair_wide), lambda _: (0, g // 2))
-            by_rows = pl.BlockSpec((pair_wide, HEAD), lambda _: (g // 2, 0))
-            result = call(key_kernel, [(key, by_cols), (value, by_cols), (w_key, by_rows)], outs, f"key_state_{g}")
+        scratch = [
+            pltpu.VMEM((rows, pair_wide), BF16),
+            pltpu.VMEM((rows, pair_wide), BF16),
+            pltpu.VMEM((pair_wide, HEAD), BF16),
+            pltpu.SemaphoreType.DMA((3,)),
+        ]
+        inputs = [in_hbm(key), in_hbm(value), in_hbm(w_key)]
+        body = functools.partial(key_kernel, g // 2)
+        result = call(body, inputs, outs, f"key_state_{g}", scratch, to_vmem=True, vmem=KEY_VMEM[min(g // 2, 1)])
         feat_k[g], state[g], feat_k[g + 1], state[g + 1] = result
         for k in (g, g + 1):
             first[k] = hop_one(state[k], k, 0)
@@ -526,13 +521,14 @@
         (part,) = call(gather_kernel, [whole(x) for x in hops[0]], [(hops[0][0].shape, F32)], "key_sum")
         totals["key"] = square(part)
 
-    def total(_):
-        rows_out = ((2 * HEAD, HEAD), F32)
-        totals["q"], totals["k"], totals["gain"] = call(
-            total_kernel,
-            [whole(x) for x in sum(totals["query"], ()) + totals["key"]],
-            [rows_out, rows_out, ((2, HEAD), F32)],
-            "total",
+    rows_out = ((2 * HEAD, HEAD), F32)
+
+    def key_total(_):
+        (totals["k"],) = call(key_total_kernel, [whole(x) for x in totals["key"]], [rows_out], "key_total")
+
+    def query_total(_):
+        totals["q"], totals["gain"] = call(
+            query_total_kernel, [whole(x) for x in sum(totals["query"], ())], [rows_out, ((2, HEAD), F32)], "query_total"
         )
 
     def listed(by_group):
@@ -554,7 +550,7 @@
     if tuned:
         steps = (
             "K0K2Q0Q1p1p0Q2Q3p3p2N0N1G0G1N2N3a2G2G3",
-            "l0l1a3l2l3B2H0H1a0V0V1H2H3a1V2V3Z0c2L0L1E0C0F0L2T0",
+            "l0l1a3l2l3B2H0H1a0V0V1H2H3a1V2V3Z0c2L0L1E0C0F0L2T0U0",
         )
         steps = "".join(steps)
     else:
@@ -577,7 +573,8 @@
         "E": query_first,
         "F": query_second,
         "C": key_square,
-        "T": total,
+        "T": key_total,
+        "U": query_total,
     }
     for k in range(0, len(steps), 2):
         does[steps[k]](int(steps[k + 1]))

time: 83.5 us -> 83.3 us (level)
  waiting for transfers between devices: 28.6 us -> 26.8 us
  Pallas kernels: 17.5 us -> 19.2 us
    ppermute x35, waiting for transfers between devices: 28.6 us -> 26.8 us  [swap(): lax.ppermute(value, axis, [(i, i ^ bit) for i in range(lax.axis_size(axis...]
    pallas_call x44 -> x45, Pallas kernels: 17.5 us -> 19.2 us  [__call__(): pl.pallas_call(ordered, grid=(1,), in_specs=[spec for _, spec in ins], ou...]
  transfers between devices with their start and end apart: 35 -> 35, of which waited for: 17 -> 17; matrix products, arithmetic and copies ran while one was open for 0% -> 0% of each run, Pallas kernels for 18% -> 20%
where the time goes in v4:
time: 83.3 us; the launch traced here: 83.1 us
  starting transfers between devices  36.1 us (43%)
  waiting for transfers between devices  26.8 us (32%)
  Pallas kernels  19.2 us (23%)
  between operations  1.03 us (1%)
    ppermute x35, starting transfers between devices, swap(): lax.ppermute(value, axis, [(i, i ^ bit) for i in range(lax.axis_size(axis...  36.1 us
    ppermute x35, waiting for transfers between devices, swap(): lax.ppermute(value, axis, [(i, i ^ bit) for i in range(lax.axis_size(axis...  26.8 us
    pallas_call x45, Pallas kernels, __call__(): pl.pallas_call(ordered, grid=(1,), in_specs=[spec for _, spec in ins], ou...  19.2 us
  transfers between devices with their start and end apart: 35, of which 17 were waited for; matrix products, arithmetic and copies ran while one was open for 0% of the time, Pallas kernels for 20%

profile of v4, /device:TPU:0, one launch (start us, length us, event | category | flops | bytes accessed | tf_op | source)
XLA Modules:
  0.0 83.1 jit_solution(8451754381544971786)
XLA Ops:
  0.6 1.6 %key_state_0.1 = (bf16[4,128,128]{2,1,0:T(8,128)(2,1)S(1)}, f32[4,128,128]{2,1,0:T(8,128)S(1)}, bf16[4,128,128]{2,1,0:T(8,128)(2,1)S(1)}, f32[4,128,128]{2,1,0:T(8,128)S(1)}, f32[8,128]{1,0:T(8,128)S(1)}) custom-call(bf16[128,2048]{1,0:T(8,128)(2,1)} %bitcast.31, bf16[128,2048]{1,0:T(8,128)(2,1)} %bitcast.9, bf16[2048,128]{1,0:T(8,128)(2,1)} %refs_6_.15), custom_call_target="tpu_custom_call" | custom-call | flops 200000000 | tf_op jit(solution)/shard_map/key_state_0/pallas_call | solution.py:316
  2.2 3.0 %collective-permute-start.1 = (f32[4,128,128]{2,1,0:T(8,128)S(1)}, f32[4,128,128]{2,1,0:T(8,128)S(1)}, u32[]{:S(2)}, u32[]{:S(2)}) collective-permute-start(f32[4,128,128]{2,1,0:T(8,128)S(1)} %get-tuple-element.166.refs_0_), channel_id=1, source_target_pairs={{0,2},{1,3},{2,0},{3,1},{4,6},{5,7},{6,4},{7,5},{8,10},{9,11},{10,... | collective-permute-start | bytes 786440 | tf_op jit(solution)/shard_map/ppermute | solution.py:353
  5.3 1.5 %collective-permute-start = (f32[4,128,128]{2,1,0:T(8,128)S(1)}, f32[4,128,128]{2,1,0:T(8,128)S(1)}, u32[]{:S(2)}, u32[]{:S(2)}) collective-permute-start(f32[4,128,128]{2,1,0:T(8,128)S(1)} %get-tuple-element.165.refs_0_), channel_id=1, source_target_pairs={{0,1},{1,0},{2,3},{3,2},{4,5},{5,4},{6,7},{7,6},{8,9},{9,8},{10,11... | collective-permute-start | bytes 786440 | tf_op jit(solution)/shard_map/ppermute | solution.py:353
  6.8 1.7 %key_state_2.1 = (bf16[4,128,128]{2,1,0:T(8,128)(2,1)S(1)}, f32[4,128,128]{2,1,0:T(8,128)S(1)}, bf16[4,128,128]{2,1,0:T(8,128)(2,1)S(1)}, f32[4,128,128]{2,1,0:T(8,128)S(1)}, f32[8,128]{1,0:T(8,128)S(1)}) custom-call(bf16[128,2048]{1,0:T(8,128)(2,1)} %bitcast.32, bf16[128,2048]{1,0:T(8,128)(2,1)} %bitcast.10, bf16[2048,128]{1,0:T(8,128)(2,1)} %refs_6_.15, ...), custom_call_target="tpu_custom_call" | custom-call | flops 200000000 | tf_op jit(solution)/shard_map/key_state_2/pallas_call | solution.py:316
  9.8 2.6 %collective-permute-done.1.refs_1_.refs_0_ = f32[4,128,128]{2,1,0:T(8,128)S(1)} collective-permute-done((f32[4,128,128]{2,1,0:T(8,128)S(1)}, f32[4,128,128]{2,1,0:T(8,128)S(1)}, u32[]{:S(2)}, u32[]{:S(2)}) %collective-permute-start.1) | collective-permute-done | bytes 262176 | tf_op jit(solution)/shard_map/ppermute | solution.py:353
  12.5 2.0 %collective-permute-done.refs_1_.refs_0_ = f32[4,128,128]{2,1,0:T(8,128)S(1)} collective-permute-done((f32[4,128,128]{2,1,0:T(8,128)S(1)}, f32[4,128,128]{2,1,0:T(8,128)S(1)}, u32[]{:S(2)}, u32[]{:S(2)}) %collective-permute-start) | collective-permute-done | bytes 262176 | tf_op jit(solution)/shard_map/ppermute | solution.py:353
  14.6 2.0 %collective-permute-start.5 = (f32[4,128,128]{2,1,0:T(8,128)S(1)}, f32[4,128,128]{2,1,0:T(8,128)S(1)}, u32[]{:S(2)}, u32[]{:S(2)}) collective-permute-start(f32[4,128,128]{2,1,0:T(8,128)S(1)} %get-tuple-element.191), channel_id=1, source_target_pairs={{0,1},{1,0},{2,3},{3,2},{4,5},{5,4},{6,7},{7,6},{8,9},{9,8},{10,11... | collective-permute-start | bytes 786440 | tf_op jit(solution)/shard_map/ppermute | solution.py:353
  17.3 0.7 collective-permute-done.4.refs_1_.refs_0_
  18.1 2.0 %collective-permute-done.3.refs_1_.refs_0_ = f32[4,128,128]{2,1,0:T(8,128)S(1)} collective-permute-done((f32[4,128,128]{2,1,0:T(8,128)S(1)}, f32[4,128,128]{2,1,0:T(8,128)S(1)}, u32[]{:S(2)}, u32[]{:S(2)}) %collective-permute-start.3) | collective-permute-done | bytes 262176 | tf_op jit(solution)/shard_map/ppermute | solution.py:353
  20.3 2.0 %collective-permute-start.7 = (f32[4,128,128]{2,1,0:T(8,128)S(1)}, f32[4,128,128]{2,1,0:T(8,128)S(1)}, u32[]{:S(2)}, u32[]{:S(2)}) collective-permute-start(f32[4,128,128]{2,1,0:T(8,128)S(1)} %get-tuple-element.215), channel_id=1, source_target_pairs={{0,1},{1,0},{2,3},{3,2},{4,5},{5,4},{6,7},{7,6},{8,9},{9,8},{10,11... | collective-permute-start | bytes 786440 | tf_op jit(solution)/shard_map/ppermute | solution.py:353
  22.2 1.6 %collective-permute-done.2.refs_1_ = f32[4,128,128]{2,1,0:T(8,128)S(1)} collective-permute-done((f32[4,128,128]{2,1,0:T(8,128)S(1)}, f32[4,128,128]{2,1,0:T(8,128)S(1)}, u32[]{:S(2)}, u32[]{:S(2)}) %collective-permute-start.2) | collective-permute-done | bytes 262176 | tf_op jit(solution)/shard_map/ppermute | solution.py:353
  23.9 0.6 numer_0.1
  24.5 1.9 %collective-permute-start.10 = (f32[4,128,128]{2,1,0:T(8,128)S(1)}, f32[4,128,128]{2,1,0:T(8,128)S(1)}, u32[]{:S(2)}, u32[]{:S(2)}) collective-permute-start(f32[4,128,128]{2,1,0:T(8,128)S(1)} %get-tuple-element.234.refs_0_), channel_id=1, source_target_pairs={{0,1},{1,0},{2,3},{3,2},{4,5},{5,4},{6,7},{7,6},{8,9},{9,8},{10,11... | collective-permute-start | bytes 786440 | tf_op jit(solution)/shard_map/ppermute | solution.py:353
  26.4 0.6 numer_1.1
  27.0 1.6 %collective-permute-start.9 = (f32[4,128,128]{2,1,0:T(8,128)S(1)}, f32[4,128,128]{2,1,0:T(8,128)S(1)}, u32[]{:S(2)}, u32[]{:S(2)}) collective-permute-start(f32[4,128,128]{2,1,0:T(8,128)S(1)} %get-tuple-element.233.refs_0_), channel_id=1, source_target_pairs={{0,2},{1,3},{2,0},{3,1},{4,6},{5,7},{6,4},{7,5},{8,10},{9,11},{10,... | collective-permute-start | bytes 786440 | tf_op jit(solution)/shard_map/ppermute | solution.py:353
  28.6 0.8 %query_grad_0.1 = (bf16[4,128,128]{2,1,0:T(8,128)(2,1)S(1)}, bf16[4,128,128]{2,1,0:T(8,128)(2,1)S(1)}, f32[4,136,128]{2,1,0:T(8,128)S(1)}, f32[8,128]{1,0:T(8,128)S(1)}) custom-call(bf16[4,128,128]{2,1,0:T(8,128)(2,1)S(1)} %get-tuple-element.186.refs_0_.refs_1_, bf16[4,128,128]{2,1,0:T(8,128)(2,1)S(1)} %get-tuple-element.187.refs_1_, ...), custom_call_target="tpu_custom_call" | custom-call | flops 200000000 | tf_op jit(solution)/shard_map/query_grad_0/pallas_call | solution.py:316
  29.4 0.8 %query_grad_1.1 = (bf16[4,128,128]{2,1,0:T(8,128)(2,1)S(1)}, bf16[4,128,128]{2,1,0:T(8,128)(2,1)S(1)}, f32[4,136,128]{2,1,0:T(8,128)S(1)}, f32[8,128]{1,0:T(8,128)S(1)}) custom-call(bf16[4,128,128]{2,1,0:T(8,128)(2,1)S(1)} %get-tuple-element.197.refs_0_.refs_1_, bf16[4,128,128]{2,1,0:T(8,128)(2,1)S(1)} %get-tuple-element.198.refs_1_, ...), custom_call_target="tpu_custom_call" | custom-call | flops 200000000 | tf_op jit(solution)/shard_map/query_grad_1/pallas_call | solution.py:316
  30.3 0.6 numer_2.1
  31.4 0.6 numer_3.1
  32.1 1.6 %collective-permute-start.13 = (f32[4,128,128]{2,1,0:T(8,128)S(1)}, f32[4,128,128]{2,1,0:T(8,128)S(1)}, u32[]{:S(2)}, u32[]{:S(2)}) collective-permute-start(f32[4,128,128]{2,1,0:T(8,128)S(1)} %get-tuple-element.242.refs_0_), channel_id=1, source_target_pairs={{0,1},{1,0},{2,3},{3,2},{4,5},{5,4},{6,7},{7,6},{8,9},{9,8},{10,11... | collective-permute-start | bytes 786440 | tf_op jit(solution)/shard_map/ppermute | solution.py:353
  33.7 0.6 collective-permute-start.12
  34.3 0.8 %query_grad_2.1 = (bf16[4,128,128]{2,1,0:T(8,128)(2,1)S(1)}, bf16[4,128,128]{2,1,0:T(8,128)(2,1)S(1)}, f32[4,136,128]{2,1,0:T(8,128)S(1)}, f32[8,128]{1,0:T(8,128)S(1)}) custom-call(bf16[4,128,128]{2,1,0:T(8,128)(2,1)S(1)} %get-tuple-element.208.refs_0_.refs_1_, bf16[4,128,128]{2,1,0:T(8,128)(2,1)S(1)} %get-tuple-element.209.refs_1_, ...), custom_call_target="tpu_custom_call" | custom-call | flops 200000000 | tf_op jit(solution)/shard_map/query_grad_2/pallas_call | solution.py:316
  35.1 0.8 %query_grad_3.1 = (bf16[4,128,128]{2,1,0:T(8,128)(2,1)S(1)}, bf16[4,128,128]{2,1,0:T(8,128)(2,1)S(1)}, f32[4,136,128]{2,1,0:T(8,128)S(1)}, f32[8,128]{1,0:T(8,128)S(1)}) custom-call(bf16[4,128,128]{2,1,0:T(8,128)(2,1)S(1)} %get-tuple-element.222.refs_0_.refs_1_, bf16[4,128,128]{2,1,0:T(8,128)(2,1)S(1)} %get-tuple-element.223.refs_1_, ...), custom_call_target="tpu_custom_call" | custom-call | flops 200000000 | tf_op jit(solution)/shard_map/query_grad_3/pallas_call | solution.py:316
  36.3 1.5 %collective-permute-start.15 = (f32[4,128,128]{2,1,0:T(8,128)S(1)}, f32[4,128,128]{2,1,0:T(8,128)S(1)}, u32[]{:S(2)}, u32[]{:S(2)}) collective-permute-start(f32[4,128,128]{2,1,0:T(8,128)S(1)} %get-tuple-element.248), channel_id=1, source_target_pairs={{0,2},{1,3},{2,0},{3,1},{4,6},{5,7},{6,4},{7,5},{8,10},{9,11},{10,... | collective-permute-start | bytes 786440 | tf_op jit(solution)/shard_map/ppermute | solution.py:353
  38.3 3.1 %collective-permute-done.13.refs_1_.refs_0_ = f32[4,128,128]{2,1,0:T(8,128)S(1)} collective-permute-done((f32[4,128,128]{2,1,0:T(8,128)S(1)}, f32[4,128,128]{2,1,0:T(8,128)S(1)}, u32[]{:S(2)}, u32[]{:S(2)}) %collective-permute-start.13) | collective-permute-done | bytes 262176 | tf_op jit(solution)/shard_map/ppermute | solution.py:353
  41.9 1.0 %collective-permute-done.12.refs_1_.refs_0_ = f32[4,128,128]{2,1,0:T(8,128)S(1)} collective-permute-done((f32[4,128,128]{2,1,0:T(8,128)S(1)}, f32[4,128,128]{2,1,0:T(8,128)S(1)}, u32[]{:S(2)}, u32[]{:S(2)}) %collective-permute-start.12) | collective-permute-done | bytes 262176 | tf_op jit(solution)/shard_map/ppermute | solution.py:353
  42.9 0.8 collective-permute-start.20
  43.8 2.7 %collective-permute-start.14 = (f32[2,2,136,128]{3,2,1,0:T(8,128)S(1)}, f32[2,2,136,128]{3,2,1,0:T(8,128)S(1)}, u32[]{:S(2)}, u32[]{:S(2)}) collective-permute-start(f32[2,2,136,128]{3,2,1,0:T(8,128)S(1)} %get-tuple-element.247), channel_id=1, source_target_pairs={{0,16},{4,20},{8,24},{12,28},{16,0},{20,4},{24,8},{28,12},{1,17},{... | collective-permute-start | bytes 835592 | tf_op jit(solution)/shard_map/ppermute | solution.py:353
  46.4 2.0 %collective-permute-done.15.refs_1_ = f32[4,128,128]{2,1,0:T(8,128)S(1)} collective-permute-done((f32[4,128,128]{2,1,0:T(8,128)S(1)}, f32[4,128,128]{2,1,0:T(8,128)S(1)}, u32[]{:S(2)}, u32[]{:S(2)}) %collective-permute-start.15) | collective-permute-done | bytes 262176 | tf_op jit(solution)/shard_map/ppermute | solution.py:353
  50.4 2.9 %collective-permute-done.19.refs_1_ = f32[4,128,128]{2,1,0:T(8,128)S(1)} collective-permute-done((f32[4,128,128]{2,1,0:T(8,128)S(1)}, f32[4,128,128]{2,1,0:T(8,128)S(1)}, u32[]{:S(2)}, u32[]{:S(2)}) %collective-permute-start.19) | collective-permute-done | bytes 262176 | tf_op jit(solution)/shard_map/ppermute | solution.py:353
  56.7 1.6 %collective-permute-start.27 = (f32[2,128,128]{2,1,0:T(8,128)S(1)}, f32[2,128,128]{2,1,0:T(8,128)S(1)}, u32[]{:S(2)}, u32[]{:S(2)}) collective-permute-start(f32[2,128,128]{2,1,0:T(8,128)S(1)} %get-tuple-element.309), channel_id=1, source_target_pairs={{0,8},{4,12},{8,0},{12,4},{16,24},{20,28},{24,16},{28,20},{1,9},{5... | collective-permute-start | bytes 393224 | tf_op jit(solution)/shard_map/ppermute | solution.py:353
  58.4 2.6 %collective-permute-start.28 = (f32[2,128,128]{2,1,0:T(8,128)S(1)}, f32[2,128,128]{2,1,0:T(8,128)S(1)}, u32[]{:S(2)}, u32[]{:S(2)}) collective-permute-start(f32[2,128,128]{2,1,0:T(8,128)S(1)} %get-tuple-element.310), channel_id=1, source_target_pairs={{0,16},{4,20},{8,24},{12,28},{16,0},{20,4},{24,8},{28,12},{1,17},{... | collective-permute-start | bytes 393224 | tf_op jit(solution)/shard_map/ppermute | solution.py:353
  61.2 0.7 collective-permute-start.23
  62.0 1.3 %collective-permute-start.24 = (f32[136,128]{1,0:T(8,128)S(1)}, f32[136,128]{1,0:T(8,128)S(1)}, u32[]{:S(2)}, u32[]{:S(2)}) collective-permute-start(f32[136,128]{1,0:T(8,128)S(1)} %get-tuple-element.304), channel_id=1, source_target_pairs={{0,8},{4,12},{8,0},{12,4},{16,24},{20,28},{24,16},{28,20},{1,9},{5... | collective-permute-start | bytes 208904 | tf_op jit(solution)/shard_map/ppermute | solution.py:353
  63.3 0.9 %lay_0.1 = (bf16[128,2048]{1,0:T(8,128)(2,1)}, f32[8,128]{1,0:T(8,128)S(1)}) custom-call(bf16[4,128,128]{2,1,0:T(8,128)(2,1)S(1)} %get-tuple-element.196.refs_0_, bf16[4,128,128]{2,1,0:T(8,128)(2,1)S(1)} %get-tuple-element.203.refs_1_, bf16[4,128,128]{2,1,0:T(8,128)(2,1)S(1)} %get-tuple-element.221.refs_2_, ...), custom_call_target="tpu_custom_call" | custom-call | flops 200000000 | tf_op jit(solution)/shard_map/lay_0/pallas_call | solution.py:316
  64.3 0.9 %lay_1.1 = (bf16[128,2048]{1,0:T(8,128)(2,1)}, f32[8,128]{1,0:T(8,128)S(1)}) custom-call(bf16[4,128,128]{2,1,0:T(8,128)(2,1)S(1)} %get-tuple-element.292.refs_0_, bf16[4,128,128]{2,1,0:T(8,128)(2,1)S(1)} %get-tuple-element.293.refs_1_, bf16[4,128,128]{2,1,0:T(8,128)(2,1)S(1)} %get-tuple-element.294.refs_2_, ...), custom_call_target="tpu_custom_call" | custom-call | flops 200000000 | tf_op jit(solution)/shard_map/lay_1/pallas_call | solution.py:316
  65.2 4.0 %collective-permute-done.23.refs_1_ = f32[136,128]{1,0:T(8,128)S(1)} collective-permute-done((f32[136,128]{1,0:T(8,128)S(1)}, f32[136,128]{1,0:T(8,128)S(1)}, u32[]{:S(2)}, u32[]{:S(2)}) %collective-permute-start.23) | collective-permute-done | bytes 69664 | tf_op jit(solution)/shard_map/ppermute | solution.py:353
  69.3 1.6 %collective-permute-done.24.refs_2_ = f32[136,128]{1,0:T(8,128)S(1)} collective-permute-done((f32[136,128]{1,0:T(8,128)S(1)}, f32[136,128]{1,0:T(8,128)S(1)}, u32[]{:S(2)}, u32[]{:S(2)}) %collective-permute-start.24) | collective-permute-done | bytes 69664 | tf_op jit(solution)/shard_map/ppermute | solution.py:353
  70.9 0.6 collective-permute-start.25
  72.2 1.5 %collective-permute-start.32 = (f32[2,128,128]{2,1,0:T(8,128)S(1)}, f32[2,128,128]{2,1,0:T(8,128)S(1)}, u32[]{:S(2)}, u32[]{:S(2)}) collective-permute-start(f32[2,128,128]{2,1,0:T(8,128)S(1)} %get-tuple-element.318.refs_0_), channel_id=1, source_target_pairs={{0,1},{1,0},{2,3},{3,2},{4,5},{5,4},{6,7},{7,6},{8,9},{9,8},{10,11... | collective-permute-start | bytes 393224 | tf_op jit(solution)/shard_map/ppermute | solution.py:353
  73.7 1.4 %collective-permute-start.33 = (f32[2,128,128]{2,1,0:T(8,128)S(1)}, f32[2,128,128]{2,1,0:T(8,128)S(1)}, u32[]{:S(2)}, u32[]{:S(2)}) collective-permute-start(f32[2,128,128]{2,1,0:T(8,128)S(1)} %get-tuple-element.318.refs_0_), channel_id=1, source_target_pairs={{0,2},{1,3},{2,0},{3,1},{4,6},{5,7},{6,4},{7,5},{8,10},{9,11},{10,... | collective-permute-start | bytes 393224 | tf_op jit(solution)/shard_map/ppermute | solution.py:353
  75.7 0.8 collective-permute-done.26.refs_3_
  76.5 0.7 collective-permute-start.30
  77.3 1.9 %collective-permute-start.31 = (f32[136,128]{1,0:T(8,128)S(1)}, f32[136,128]{1,0:T(8,128)S(1)}, u32[]{:S(2)}, u32[]{:S(2)}) collective-permute-start(f32[136,128]{1,0:T(8,128)S(1)} %get-tuple-element.317.refs_2_), channel_id=1, source_target_pairs={{0,1},{1,0},{2,3},{3,2},{4,5},{5,4},{6,7},{7,6},{8,9},{9,8},{10,11... | collective-permute-start | bytes 208904 | tf_op jit(solution)/shard_map/ppermute | solution.py:353
  79.2 0.9 %lay_2.1 = (bf16[128,2048]{1,0:T(8,128)(2,1)}, f32[8,128]{1,0:T(8,128)S(1)}) custom-call(bf16[4,128,128]{2,1,0:T(8,128)(2,1)S(1)} %get-tuple-element.298.refs_0_, bf16[4,128,128]{2,1,0:T(8,128)(2,1)S(1)} %get-tuple-element.299.refs_1_, bf16[4,128,128]{2,1,0:T(8,128)(2,1)S(1)} %get-tuple-element.300.refs_2_, ...), custom_call_target="tpu_custom_call" | custom-call | flops 200000000 | tf_op jit(solution)/shard_map/lay_2/pallas_call | solution.py:316
  80.1 1.6 %collective-permute-done.33.refs_2_ = f32[2,128,128]{2,1,0:T(8,128)S(1)} collective-permute-done((f32[2,128,128]{2,1,0:T(8,128)S(1)}, f32[2,128,128]{2,1,0:T(8,128)S(1)}, u32[]{:S(2)}, u32[]{:S(2)}) %collective-permute-start.33) | collective-permute-done | bytes 131104 | tf_op jit(solution)/shard_map/ppermute | solution.py:353
  81.7 0.7 key_total.1
  82.4 0.7 query_total.1
  (83 shorter events, 11.3 us)
Async XLA Ops:
  2.2 4.5 %copy-start.7 = (f32[8,128]{1,0:T(8,128)}, f32[8,128]{1,0:T(8,128)S(1)}, u32[]{:S(2)}) copy-start(f32[8,128]{1,0:T(8,128)S(1)} %get-tuple-element.169.refs_3_) | copy-start | bytes 12292
  2.2 10.2 %collective-permute-start.1 = (f32[4,128,128]{2,1,0:T(8,128)S(1)}, f32[4,128,128]{2,1,0:T(8,128)S(1)}, u32[]{:S(2)}, u32[]{:S(2)}) collective-permute-start(f32[4,128,128]{2,1,0:T(8,128)S(1)} %get-tuple-element.166.refs_0_), channel_id=1, source_target_pairs={{0,2},{1,3},{2,0},{3,1},{4,6},{5,7},{6,4},{7,5},{8,10},{9,11},{10,... | collective-permute-start | bytes 786440 | tf_op jit(solution)/shard_map/ppermute | solution.py:353
  5.3 9.2 %collective-permute-start = (f32[4,128,128]{2,1,0:T(8,128)S(1)}, f32[4,128,128]{2,1,0:T(8,128)S(1)}, u32[]{:S(2)}, u32[]{:S(2)}) collective-permute-start(f32[4,128,128]{2,1,0:T(8,128)S(1)} %get-tuple-element.165.refs_0_), channel_id=1, source_target_pairs={{0,1},{1,0},{2,3},{3,2},{4,5},{5,4},{6,7},{7,6},{8,9},{9,8},{10,11... | collective-permute-start | bytes 786440 | tf_op jit(solution)/shard_map/ppermute | solution.py:353
  6.8 2.4 %copy-start.2 = (bf16[1,128,2048]{2,1,0:T(8,128)(2,1)S(1)}, bf16[1,128,2048]{2,1,0:T(8,128)(2,1)}, u32[]{:S(2)}) copy-start(bf16[1,128,2048]{2,1,0:T(8,128)(2,1)} %param.7) | copy-start | bytes 1572868
  6.8 2.4 %copy-start.3 = (bf16[2048,128]{1,0:T(8,128)(2,1)S(1)}, bf16[2048,128]{1,0:T(8,128)(2,1)}, u32[]{:S(2)}) copy-start(bf16[2048,128]{1,0:T(8,128)(2,1)} %refs_7_.7) | copy-start | bytes 1572868
  8.5 9.6 %collective-permute-start.4 = (f32[4,128,128]{2,1,0:T(8,128)S(1)}, f32[4,128,128]{2,1,0:T(8,128)S(1)}, u32[]{:S(2)}, u32[]{:S(2)}) collective-permute-start(f32[4,128,128]{2,1,0:T(8,128)S(1)} %get-tuple-element.178.refs_0_), channel_id=1, source_target_pairs={{0,2},{1,3},{2,0},{3,1},{4,6},{5,7},{6,4},{7,5},{8,10},{9,11},{10,... | collective-permute-start | bytes 786440 | tf_op jit(solution)/shard_map/ppermute | solution.py:353
  9.0 11.1 %collective-permute-start.3 = (f32[4,128,128]{2,1,0:T(8,128)S(1)}, f32[4,128,128]{2,1,0:T(8,128)S(1)}, u32[]{:S(2)}, u32[]{:S(2)}) collective-permute-start(f32[4,128,128]{2,1,0:T(8,128)S(1)} %get-tuple-element.177.refs_0_), channel_id=1, source_target_pairs={{0,1},{1,0},{2,3},{3,2},{4,5},{5,4},{6,7},{7,6},{8,9},{9,8},{10,11... | collective-permute-start | bytes 786440 | tf_op jit(solution)/shard_map/ppermute | solution.py:353
  14.5 9.3 %collective-permute-start.2 = (f32[4,128,128]{2,1,0:T(8,128)S(1)}, f32[4,128,128]{2,1,0:T(8,128)S(1)}, u32[]{:S(2)}, u32[]{:S(2)}) collective-permute-start(f32[4,128,128]{2,1,0:T(8,128)S(1)} %get-tuple-element.174), channel_id=1, source_target_pairs={{0,2},{1,3},{2,0},{3,1},{4,6},{5,7},{6,4},{7,5},{8,10},{9,11},{10,... | collective-permute-start | bytes 786440 | tf_op jit(solution)/shard_map/ppermute | solution.py:353
  14.6 11.7 %collective-permute-start.5 = (f32[4,128,128]{2,1,0:T(8,128)S(1)}, f32[4,128,128]{2,1,0:T(8,128)S(1)}, u32[]{:S(2)}, u32[]{:S(2)}) collective-permute-start(f32[4,128,128]{2,1,0:T(8,128)S(1)} %get-tuple-element.191), channel_id=1, source_target_pairs={{0,1},{1,0},{2,3},{3,2},{4,5},{5,4},{6,7},{7,6},{8,9},{9,8},{10,11... | collective-permute-start | bytes 786440 | tf_op jit(solution)/shard_map/ppermute | solution.py:353
  18.0 5.8 %copy-start.5 = (bf16[1,128,2048]{2,1,0:T(8,128)(2,1)S(1)}, bf16[1,128,2048]{2,1,0:T(8,128)(2,1)}, u32[]{:S(2)}) copy-start(bf16[1,128,2048]{2,1,0:T(8,128)(2,1)} %param.10) | copy-start | bytes 1572868
  18.1 5.8 %copy-start = (bf16[1,128,2048]{2,1,0:T(8,128)(2,1)S(1)}, bf16[1,128,2048]{2,1,0:T(8,128)(2,1)}, u32[]{:S(2)}) copy-start(bf16[1,128,2048]{2,1,0:T(8,128)(2,1)} %param.9) | copy-start | bytes 1572868
  20.2 3.7 %copy-start.6 = (f32[2048]{0:T(1024)S(1)}, f32[2048]{0:T(1024)}, u32[]{:S(2)}) copy-start(f32[2048]{0:T(1024)} %param.13) | copy-start | bytes 24580
  20.2 10.1 %collective-permute-start.6 = (f32[4,128,128]{2,1,0:T(8,128)S(1)}, f32[4,128,128]{2,1,0:T(8,128)S(1)}, u32[]{:S(2)}, u32[]{:S(2)}) collective-permute-start(f32[4,128,128]{2,1,0:T(8,128)S(1)} %get-tuple-element.204), channel_id=1, source_target_pairs={{0,2},{1,3},{2,0},{3,1},{4,6},{5,7},{6,4},{7,5},{8,10},{9,11},{10,... | collective-permute-start | bytes 786440 | tf_op jit(solution)/shard_map/ppermute | solution.py:353
  20.3 11.1 %collective-permute-start.7 = (f32[4,128,128]{2,1,0:T(8,128)S(1)}, f32[4,128,128]{2,1,0:T(8,128)S(1)}, u32[]{:S(2)}, u32[]{:S(2)}) collective-permute-start(f32[4,128,128]{2,1,0:T(8,128)S(1)} %get-tuple-element.215), channel_id=1, source_target_pairs={{0,1},{1,0},{2,3},{3,2},{4,5},{5,4},{6,7},{7,6},{8,9},{9,8},{10,11... | collective-permute-start | bytes 786440 | tf_op jit(solution)/shard_map/ppermute | solution.py:353
  24.5 11.5 %collective-permute-start.10 = (f32[4,128,128]{2,1,0:T(8,128)S(1)}, f32[4,128,128]{2,1,0:T(8,128)S(1)}, u32[]{:S(2)}, u32[]{:S(2)}) collective-permute-start(f32[4,128,128]{2,1,0:T(8,128)S(1)} %get-tuple-element.234.refs_0_), channel_id=1, source_target_pairs={{0,1},{1,0},{2,3},{3,2},{4,5},{5,4},{6,7},{7,6},{8,9},{9,8},{10,11... | collective-permute-start | bytes 786440 | tf_op jit(solution)/shard_map/ppermute | solution.py:353
  27.0 9.0 %collective-permute-start.9 = (f32[4,128,128]{2,1,0:T(8,128)S(1)}, f32[4,128,128]{2,1,0:T(8,128)S(1)}, u32[]{:S(2)}, u32[]{:S(2)}) collective-permute-start(f32[4,128,128]{2,1,0:T(8,128)S(1)} %get-tuple-element.233.refs_0_), channel_id=1, source_target_pairs={{0,2},{1,3},{2,0},{3,1},{4,6},{5,7},{6,4},{7,5},{8,10},{9,11},{10,... | collective-permute-start | bytes 786440 | tf_op jit(solution)/shard_map/ppermute | solution.py:353
  32.0 4.1 %collective-permute-start.8 = (f32[2,2,136,128]{3,2,1,0:T(8,128)S(1)}, f32[2,2,136,128]{3,2,1,0:T(8,128)S(1)}, u32[]{:S(2)}, u32[]{:S(2)}) collective-permute-start(f32[2,2,136,128]{3,2,1,0:T(8,128)S(1)} %get-tuple-element.232), channel_id=1, source_target_pairs={{0,4},{4,0},{8,12},{12,8},{16,20},{20,16},{24,28},{28,24},{1,5},{5... | collective-permute-start | bytes 835592 | tf_op jit(solution)/shard_map/ppermute | solution.py:353
  32.1 9.2 %collective-permute-start.13 = (f32[4,128,128]{2,1,0:T(8,128)S(1)}, f32[4,128,128]{2,1,0:T(8,128)S(1)}, u32[]{:S(2)}, u32[]{:S(2)}) collective-permute-start(f32[4,128,128]{2,1,0:T(8,128)S(1)} %get-tuple-element.242.refs_0_), channel_id=1, source_target_pairs={{0,1},{1,0},{2,3},{3,2},{4,5},{5,4},{6,7},{7,6},{8,9},{9,8},{10,11... | collective-permute-start | bytes 786440 | tf_op jit(solution)/shard_map/ppermute | solution.py:353
  33.7 9.2 %collective-permute-start.12 = (f32[4,128,128]{2,1,0:T(8,128)S(1)}, f32[4,128,128]{2,1,0:T(8,128)S(1)}, u32[]{:S(2)}, u32[]{:S(2)}) collective-permute-start(f32[4,128,128]{2,1,0:T(8,128)S(1)} %get-tuple-element.241.refs_0_), channel_id=1, source_target_pairs={{0,2},{1,3},{2,0},{3,1},{4,6},{5,7},{6,4},{7,5},{8,10},{9,11},{10,... | collective-permute-start | bytes 786440 | tf_op jit(solution)/shard_map/ppermute | solution.py:353
  36.2 7.5 %collective-permute-start.11 = (f32[2,2,136,128]{3,2,1,0:T(8,128)S(1)}, f32[2,2,136,128]{3,2,1,0:T(8,128)S(1)}, u32[]{:S(2)}, u32[]{:S(2)}) collective-permute-start(f32[2,2,136,128]{3,2,1,0:T(8,128)S(1)} %get-tuple-element.240), channel_id=1, source_target_pairs={{0,4},{4,0},{8,12},{12,8},{16,20},{20,16},{24,28},{28,24},{1,5},{5... | collective-permute-start | bytes 835592 | tf_op jit(solution)/shard_map/ppermute | solution.py:353
  36.3 12.2 %collective-permute-start.15 = (f32[4,128,128]{2,1,0:T(8,128)S(1)}, f32[4,128,128]{2,1,0:T(8,128)S(1)}, u32[]{:S(2)}, u32[]{:S(2)}) collective-permute-start(f32[4,128,128]{2,1,0:T(8,128)S(1)} %get-tuple-element.248), channel_id=1, source_target_pairs={{0,2},{1,3},{2,0},{3,1},{4,6},{5,7},{6,4},{7,5},{8,10},{9,11},{10,... | collective-permute-start | bytes 786440 | tf_op jit(solution)/shard_map/ppermute | solution.py:353
  37.8 11.3 %collective-permute-start.16 = (f32[4,128,128]{2,1,0:T(8,128)S(1)}, f32[4,128,128]{2,1,0:T(8,128)S(1)}, u32[]{:S(2)}, u32[]{:S(2)}) collective-permute-start(f32[4,128,128]{2,1,0:T(8,128)S(1)} %get-tuple-element.252), channel_id=1, source_target_pairs={{0,1},{1,0},{2,3},{3,2},{4,5},{5,4},{6,7},{7,6},{8,9},{9,8},{10,11... | collective-permute-start | bytes 786440 | tf_op jit(solution)/shard_map/ppermute | solution.py:353
  41.4 11.9 %collective-permute-start.19 = (f32[4,128,128]{2,1,0:T(8,128)S(1)}, f32[4,128,128]{2,1,0:T(8,128)S(1)}, u32[]{:S(2)}, u32[]{:S(2)}) collective-permute-start(f32[4,128,128]{2,1,0:T(8,128)S(1)} %get-tuple-element.260), channel_id=1, source_target_pairs={{0,2},{1,3},{2,0},{3,1},{4,6},{5,7},{6,4},{7,5},{8,10},{9,11},{10,... | collective-permute-start | bytes 786440 | tf_op jit(solution)/shard_map/ppermute | solution.py:353
  42.8 5.6 %copy-start.4 = (bf16[1,128,2048]{2,1,0:T(8,128)(2,1)S(1)}, bf16[1,128,2048]{2,1,0:T(8,128)(2,1)}, u32[]{:S(2)}) copy-start(bf16[1,128,2048]{2,1,0:T(8,128)(2,1)} %param.8) | copy-start | bytes 1572868
  42.9 5.6 %copy-start.1 = (bf16[2048,128]{1,0:T(8,128)(2,1)S(1)}, bf16[2048,128]{1,0:T(8,128)(2,1)}, u32[]{:S(2)}) copy-start(bf16[2048,128]{1,0:T(8,128)(2,1)} %refs_6_.15) | copy-start | bytes 1572868
  42.9 11.0 %collective-permute-start.20 = (f32[4,128,128]{2,1,0:T(8,128)S(1)}, f32[4,128,128]{2,1,0:T(8,128)S(1)}, u32[]{:S(2)}, u32[]{:S(2)}) collective-permute-start(f32[4,128,128]{2,1,0:T(8,128)S(1)} %get-tuple-element.272), channel_id=1, source_target_pairs={{0,1},{1,0},{2,3},{3,2},{4,5},{5,4},{6,7},{7,6},{8,9},{9,8},{10,11... | collective-permute-start | bytes 786440 | tf_op jit(solution)/shard_map/ppermute | solution.py:353
  43.8 17.4 %collective-permute-start.14 = (f32[2,2,136,128]{3,2,1,0:T(8,128)S(1)}, f32[2,2,136,128]{3,2,1,0:T(8,128)S(1)}, u32[]{:S(2)}, u32[]{:S(2)}) collective-permute-start(f32[2,2,136,128]{3,2,1,0:T(8,128)S(1)} %get-tuple-element.247), channel_id=1, source_target_pairs={{0,16},{4,20},{8,24},{12,28},{16,0},{20,4},{24,8},{28,12},{1,17},{... | collective-permute-start | bytes 835592 | tf_op jit(solution)/shard_map/ppermute | solution.py:353
  54.5 1.8 %collective-permute-start.21 = (f32[2,128,128]{2,1,0:T(8,128)S(1)}, f32[2,128,128]{2,1,0:T(8,128)S(1)}, u32[]{:S(2)}, u32[]{:S(2)}) collective-permute-start(f32[2,128,128]{2,1,0:T(8,128)S(1)} %get-tuple-element.278), channel_id=1, source_target_pairs={{0,4},{4,0},{8,12},{12,8},{16,20},{20,16},{24,28},{28,24},{1,5},{5... | collective-permute-start | bytes 393224 | tf_op jit(solution)/shard_map/ppermute | solution.py:353
  54.6 1.8 %collective-permute-start.22 = (f32[2,128,128]{2,1,0:T(8,128)S(1)}, f32[2,128,128]{2,1,0:T(8,128)S(1)}, u32[]{:S(2)}, u32[]{:S(2)}) collective-permute-start(f32[2,128,128]{2,1,0:T(8,128)S(1)} %get-tuple-element.279), channel_id=1, source_target_pairs={{0,4},{4,0},{8,12},{12,8},{16,20},{20,16},{24,28},{28,24},{1,5},{5... | collective-permute-start | bytes 393224 | tf_op jit(solution)/shard_map/ppermute | solution.py:353
  55.1 1.3 %collective-permute-start.17 = (f32[2,128,128]{2,1,0:T(8,128)S(1)}, f32[2,128,128]{2,1,0:T(8,128)S(1)}, u32[]{:S(2)}, u32[]{:S(2)}) collective-permute-start(f32[2,128,128]{2,1,0:T(8,128)S(1)} %get-tuple-element.258), channel_id=1, source_target_pairs={{0,4},{4,0},{8,12},{12,8},{16,20},{20,16},{24,28},{28,24},{1,5},{5... | collective-permute-start | bytes 393224 | tf_op jit(solution)/shard_map/ppermute | solution.py:353
  55.2 1.5 %collective-permute-start.18 = (f32[2,128,128]{2,1,0:T(8,128)S(1)}, f32[2,128,128]{2,1,0:T(8,128)S(1)}, u32[]{:S(2)}, u32[]{:S(2)}) collective-permute-start(f32[2,128,128]{2,1,0:T(8,128)S(1)} %get-tuple-element.259), channel_id=1, source_target_pairs={{0,4},{4,0},{8,12},{12,8},{16,20},{20,16},{24,28},{28,24},{1,5},{5... | collective-permute-start | bytes 393224 | tf_op jit(solution)/shard_map/ppermute | solution.py:353
  56.7 15.4 %collective-permute-start.27 = (f32[2,128,128]{2,1,0:T(8,128)S(1)}, f32[2,128,128]{2,1,0:T(8,128)S(1)}, u32[]{:S(2)}, u32[]{:S(2)}) collective-permute-start(f32[2,128,128]{2,1,0:T(8,128)S(1)} %get-tuple-element.309), channel_id=1, source_target_pairs={{0,8},{4,12},{8,0},{12,4},{16,24},{20,28},{24,16},{28,20},{1,9},{5... | collective-permute-start | bytes 393224 | tf_op jit(solution)/shard_map/ppermute | solution.py:353
  58.4 13.8 %collective-permute-start.28 = (f32[2,128,128]{2,1,0:T(8,128)S(1)}, f32[2,128,128]{2,1,0:T(8,128)S(1)}, u32[]{:S(2)}, u32[]{:S(2)}) collective-permute-start(f32[2,128,128]{2,1,0:T(8,128)S(1)} %get-tuple-element.310), channel_id=1, source_target_pairs={{0,16},{4,20},{8,24},{12,28},{16,0},{20,4},{24,8},{28,12},{1,17},{... | collective-permute-start | bytes 393224 | tf_op jit(solution)/shard_map/ppermute | solution.py:353
  61.0 11.2 %collective-permute-start.29 = (f32[2,128,128]{2,1,0:T(8,128)S(1)}, f32[2,128,128]{2,1,0:T(8,128)S(1)}, u32[]{:S(2)}, u32[]{:S(2)}) collective-permute-start(f32[2,128,128]{2,1,0:T(8,128)S(1)} %get-tuple-element.311), channel_id=1, source_target_pairs={{0,24},{4,28},{8,16},{12,20},{16,8},{20,12},{24,0},{28,4},{1,25},{... | collective-permute-start | bytes 393224 | tf_op jit(solution)/shard_map/ppermute | solution.py:353
  61.2 8.0 %collective-permute-start.23 = (f32[136,128]{1,0:T(8,128)S(1)}, f32[136,128]{1,0:T(8,128)S(1)}, u32[]{:S(2)}, u32[]{:S(2)}) collective-permute-start(f32[136,128]{1,0:T(8,128)S(1)} %get-tuple-element.303), channel_id=1, source_target_pairs={{0,8},{4,12},{8,0},{12,4},{16,24},{20,28},{24,16},{28,20},{1,9},{5... | collective-permute-start | bytes 208904 | tf_op jit(solution)/shard_map/ppermute | solution.py:353
  62.0 8.9 %collective-permute-start.24 = (f32[136,128]{1,0:T(8,128)S(1)}, f32[136,128]{1,0:T(8,128)S(1)}, u32[]{:S(2)}, u32[]{:S(2)}) collective-permute-start(f32[136,128]{1,0:T(8,128)S(1)} %get-tuple-element.304), channel_id=1, source_target_pairs={{0,8},{4,12},{8,0},{12,4},{16,24},{20,28},{24,16},{28,20},{1,9},{5... | collective-permute-start | bytes 208904 | tf_op jit(solution)/shard_map/ppermute | solution.py:353
  70.9 4.8 %collective-permute-start.25 = (f32[136,128]{1,0:T(8,128)S(1)}, f32[136,128]{1,0:T(8,128)S(1)}, u32[]{:S(2)}, u32[]{:S(2)}) collective-permute-start(f32[136,128]{1,0:T(8,128)S(1)} %get-tuple-element.306.refs_0_), channel_id=1, source_target_pairs={{0,1},{1,0},{2,3},{3,2},{4,5},{5,4},{6,7},{7,6},{8,9},{9,8},{10,11... | collective-permute-start | bytes 208904 | tf_op jit(solution)/shard_map/ppermute | solution.py:353
  71.5 5.0 %collective-permute-start.26 = (f32[136,128]{1,0:T(8,128)S(1)}, f32[136,128]{1,0:T(8,128)S(1)}, u32[]{:S(2)}, u32[]{:S(2)}) collective-permute-start(f32[136,128]{1,0:T(8,128)S(1)} %get-tuple-element.307.refs_2_), channel_id=1, source_target_pairs={{0,2},{1,3},{2,0},{3,1},{4,6},{5,7},{6,4},{7,5},{8,10},{9,11},{10,... | collective-permute-start | bytes 208904 | tf_op jit(solution)/shard_map/ppermute | solution.py:353
  72.2 7.9 %collective-permute-start.32 = (f32[2,128,128]{2,1,0:T(8,128)S(1)}, f32[2,128,128]{2,1,0:T(8,128)S(1)}, u32[]{:S(2)}, u32[]{:S(2)}) collective-permute-start(f32[2,128,128]{2,1,0:T(8,128)S(1)} %get-tuple-element.318.refs_0_), channel_id=1, source_target_pairs={{0,1},{1,0},{2,3},{3,2},{4,5},{5,4},{6,7},{7,6},{8,9},{9,8},{10,11... | collective-permute-start | bytes 393224 | tf_op jit(solution)/shard_map/ppermute | solution.py:353
  73.7 8.0 %collective-permute-start.33 = (f32[2,128,128]{2,1,0:T(8,128)S(1)}, f32[2,128,128]{2,1,0:T(8,128)S(1)}, u32[]{:S(2)}, u32[]{:S(2)}) collective-permute-start(f32[2,128,128]{2,1,0:T(8,128)S(1)} %get-tuple-element.318.refs_0_), channel_id=1, source_target_pairs={{0,2},{1,3},{2,0},{3,1},{4,6},{5,7},{6,4},{7,5},{8,10},{9,11},{10,... | collective-permute-start | bytes 393224 | tf_op jit(solution)/shard_map/ppermute | solution.py:353
  75.2 6.5 %collective-permute-start.34 = (f32[2,128,128]{2,1,0:T(8,128)S(1)}, f32[2,128,128]{2,1,0:T(8,128)S(1)}, u32[]{:S(2)}, u32[]{:S(2)}) collective-permute-start(f32[2,128,128]{2,1,0:T(8,128)S(1)} %get-tuple-element.318.refs_0_), channel_id=1, source_target_pairs={{0,3},{1,2},{2,1},{3,0},{4,7},{5,6},{6,5},{7,4},{8,11},{9,10},{10,... | collective-permute-start | bytes 393224 | tf_op jit(solution)/shard_map/ppermute | solution.py:353
  76.5 5.9 %collective-permute-start.30 = (f32[136,128]{1,0:T(8,128)S(1)}, f32[136,128]{1,0:T(8,128)S(1)}, u32[]{:S(2)}, u32[]{:S(2)}) collective-permute-start(f32[136,128]{1,0:T(8,128)S(1)} %get-tuple-element.316.refs_0_), channel_id=1, source_target_pairs={{0,2},{1,3},{2,0},{3,1},{4,6},{5,7},{6,4},{7,5},{8,10},{9,11},{10,... | collective-permute-start | bytes 208904 | tf_op jit(solution)/shard_map/ppermute | solution.py:353
  77.3 5.2 %collective-permute-start.31 = (f32[136,128]{1,0:T(8,128)S(1)}, f32[136,128]{1,0:T(8,128)S(1)}, u32[]{:S(2)}, u32[]{:S(2)}) collective-permute-start(f32[136,128]{1,0:T(8,128)S(1)} %get-tuple-element.317.refs_2_), channel_id=1, source_target_pairs={{0,1},{1,0},{2,3},{3,2},{4,5},{5,4},{6,7},{7,6},{8,9},{9,8},{10,11... | collective-permute-start | bytes 208904 | tf_op jit(solution)/shard_map/ppermute | solution.py:353

commit v5 on v4

--- a/solution.py
+++ b/solution.py
@@ -254,14 +254,8 @@
     out[...] = (own[...] + near[...]) + (far[...] + both[...])
 
 
-def halves_kernel(own, even_other, odd_other, even, odd):
-    even[...] = own[0] + even_other[...]
-    odd[...] = own[1] + odd_other[...]
-
-
-def both_pairs_kernel(even, even_other, odd, odd_other, even_out, odd_out):
-    even_out[...] = even[...] + even_other[...]
-    odd_out[...] = odd[...] + odd_other[...]
+def half_kernel(b, own, other, out):
+    out[...] = own[b] + other[...]
 
 
 def key_total_kernel(key, key_x, key_y, key_d, out):
@@ -507,15 +501,14 @@
     def square(part):
         return (part,) + tuple(swap(part, "seq", bits) for bits in (1, 2, 3))
 
-    def query_first(_):
-        parts = call(halves_kernel, [whole(x) for x in hops[2]], [(hops[2][1].shape, F32)] * 2, "query_sum")
-        totals["query"] = [(x, swap(x, "seq", bit)) for bit, x in enumerate(parts, 1)]
-
-    def query_second(_):
-        parts = call(
-            both_pairs_kernel, [whole(x) for x in sum(totals["query"], ())], [(totals["query"][0][0].shape, F32)] * 2, "query_turn"
-        )
-        totals["query"] = [(x, swap(x, "seq", 2 - bit)) for bit, x in enumerate(parts)]
+    def query_first(b):
+        own, other = hops[2][0], hops[2][1 + b]
+        (part,) = call(functools.partial(half_kernel, b), [whole(own), whole(other)], [(other.shape, F32)], f"query_sum_{b}")
+        totals["query", b] = (part, swap(part, "seq", 1 + b))
+
+    def query_second(b):
+        part = pair(*totals["query", b], f"query_turn_{b}")
+        totals["query", b] = (part, swap(part, "seq", 2 - b))
 
     def key_square(_):
         (part,) = call(gather_kernel, [whole(x) for x in hops[0]], [(hops[0][0].shape, F32)], "key_sum")
@@ -528,7 +521,7 @@
 
     def query_total(_):
         totals["q"], totals["gain"] = call(
-            query_total_kernel, [whole(x) for x in sum(totals["query"], ())], [rows_out, ((2, HEAD), F32)], "query_total"
+            query_total_kernel, [whole(x) for x in totals["query", 0] + totals["query", 1]], [rows_out, ((2, HEAD), F32)], "query_total"
         )
 
     def listed(by_group):
@@ -550,7 +543,7 @@
     if tuned:
         steps = (
             "K0K2Q0Q1p1p0Q2Q3p3p2N0N1G0G1N2N3a2G2G3",
-            "l0l1a3l2l3B2H0H1a0V0V1H2H3a1V2V3Z0c2L0L1E0C0F0L2T0U0",
+            "l0l1a3l2l3B2H0H1a0V0V1H2H3a1V2V3Z0c2L0L1E0E1C0F0F1L2T0U0",
         )
         steps = "".join(steps)
     else:

time: 83.3 us -> 82.1 us (0.986)
  starting transfers between devices: 36.1 us -> 34.3 us
    ppermute x35, starting transfers between devices: 36.1 us -> 34.3 us  [swap(): lax.ppermute(value, axis, [(i, i ^ bit) for i in range(lax.axis_size(axis...]
    pallas_call x45 -> x47, Pallas kernels: 19.2 us -> 19.2 us  [__call__(): pl.pallas_call(ordered, grid=(1,), in_specs=[spec for _, spec in ins], ou...]
  transfers between devices with their start and end apart: 35 -> 35, of which waited for: 17 -> 16; matrix products, arithmetic and copies ran while one was open for 0% -> 0% of each run, Pallas kernels for 20% -> 21%
where the time goes in v5:
time: 82.1 us; the launch traced here: 82 us
  starting transfers between devices  34.3 us (42%)
  waiting for transfers between devices  27.4 us (33%)
  Pallas kernels  19.2 us (23%)
  between operations  1.03 us (1%)
    ppermute x35, starting transfers between devices, swap(): lax.ppermute(value, axis, [(i, i ^ bit) for i in range(lax.axis_size(axis...  34.3 us
    ppermute x35, waiting for transfers between devices, swap(): lax.ppermute(value, axis, [(i, i ^ bit) for i in range(lax.axis_size(axis...  27.4 us
    pallas_call x47, Pallas kernels, __call__(): pl.pallas_call(ordered, grid=(1,), in_specs=[spec for _, spec in ins], ou...  19.2 us
  transfers between devices with their start and end apart: 35, of which 16 were waited for; matrix products, arithmetic and copies ran while one was open for 0% of the time, Pallas kernels for 21%

profile of v5, /device:TPU:0, one launch (start us, length us, event | category | flops | bytes accessed | tf_op | source)
XLA Modules:
  0.0 82.0 jit_solution(4394344434458318350)
XLA Ops:
  0.6 1.6 %key_state_0.1 = (bf16[4,128,128]{2,1,0:T(8,128)(2,1)S(1)}, f32[4,128,128]{2,1,0:T(8,128)S(1)}, bf16[4,128,128]{2,1,0:T(8,128)(2,1)S(1)}, f32[4,128,128]{2,1,0:T(8,128)S(1)}, f32[8,128]{1,0:T(8,128)S(1)}) custom-call(bf16[128,2048]{1,0:T(8,128)(2,1)} %bitcast.31, bf16[128,2048]{1,0:T(8,128)(2,1)} %bitcast.9, bf16[2048,128]{1,0:T(8,128)(2,1)} %refs_6_.15), custom_call_target="tpu_custom_call" | custom-call | flops 200000000 | tf_op jit(solution)/shard_map/key_state_0/pallas_call | solution.py:310
  2.2 3.0 %collective-permute-start.1 = (f32[4,128,128]{2,1,0:T(8,128)S(1)}, f32[4,128,128]{2,1,0:T(8,128)S(1)}, u32[]{:S(2)}, u32[]{:S(2)}) collective-permute-start(f32[4,128,128]{2,1,0:T(8,128)S(1)} %get-tuple-element.168.refs_0_), channel_id=1, source_target_pairs={{0,2},{1,3},{2,0},{3,1},{4,6},{5,7},{6,4},{7,5},{8,10},{9,11},{10,... | collective-permute-start | bytes 786440 | tf_op jit(solution)/shard_map/ppermute | solution.py:347
  5.3 1.5 %collective-permute-start = (f32[4,128,128]{2,1,0:T(8,128)S(1)}, f32[4,128,128]{2,1,0:T(8,128)S(1)}, u32[]{:S(2)}, u32[]{:S(2)}) collective-permute-start(f32[4,128,128]{2,1,0:T(8,128)S(1)} %get-tuple-element.167.refs_0_), channel_id=1, source_target_pairs={{0,1},{1,0},{2,3},{3,2},{4,5},{5,4},{6,7},{7,6},{8,9},{9,8},{10,11... | collective-permute-start | bytes 786440 | tf_op jit(solution)/shard_map/ppermute | solution.py:347
  6.8 1.7 %key_state_2.1 = (bf16[4,128,128]{2,1,0:T(8,128)(2,1)S(1)}, f32[4,128,128]{2,1,0:T(8,128)S(1)}, bf16[4,128,128]{2,1,0:T(8,128)(2,1)S(1)}, f32[4,128,128]{2,1,0:T(8,128)S(1)}, f32[8,128]{1,0:T(8,128)S(1)}) custom-call(bf16[128,2048]{1,0:T(8,128)(2,1)} %bitcast.32, bf16[128,2048]{1,0:T(8,128)(2,1)} %bitcast.10, bf16[2048,128]{1,0:T(8,128)(2,1)} %refs_6_.15, ...), custom_call_target="tpu_custom_call" | custom-call | flops 200000000 | tf_op jit(solution)/shard_map/key_state_2/pallas_call | solution.py:310
  9.8 2.6 %collective-permute-done.1.refs_1_.refs_0_ = f32[4,128,128]{2,1,0:T(8,128)S(1)} collective-permute-done((f32[4,128,128]{2,1,0:T(8,128)S(1)}, f32[4,128,128]{2,1,0:T(8,128)S(1)}, u32[]{:S(2)}, u32[]{:S(2)}) %collective-permute-start.1) | collective-permute-done | bytes 262176 | tf_op jit(solution)/shard_map/ppermute | solution.py:347
  12.5 2.0 %collective-permute-done.refs_1_.refs_0_ = f32[4,128,128]{2,1,0:T(8,128)S(1)} collective-permute-done((f32[4,128,128]{2,1,0:T(8,128)S(1)}, f32[4,128,128]{2,1,0:T(8,128)S(1)}, u32[]{:S(2)}, u32[]{:S(2)}) %collective-permute-start) | collective-permute-done | bytes 262176 | tf_op jit(solution)/shard_map/ppermute | solution.py:347
  14.6 2.0 %collective-permute-start.5 = (f32[4,128,128]{2,1,0:T(8,128)S(1)}, f32[4,128,128]{2,1,0:T(8,128)S(1)}, u32[]{:S(2)}, u32[]{:S(2)}) collective-permute-start(f32[4,128,128]{2,1,0:T(8,128)S(1)} %get-tuple-element.193), channel_id=1, source_target_pairs={{0,1},{1,0},{2,3},{3,2},{4,5},{5,4},{6,7},{7,6},{8,9},{9,8},{10,11... | collective-permute-start | bytes 786440 | tf_op jit(solution)/shard_map/ppermute | solution.py:347
  17.3 0.7 collective-permute-done.4.refs_1_.refs_0_
  18.1 2.0 %collective-permute-done.3.refs_1_.refs_0_ = f32[4,128,128]{2,1,0:T(8,128)S(1)} collective-permute-done((f32[4,128,128]{2,1,0:T(8,128)S(1)}, f32[4,128,128]{2,1,0:T(8,128)S(1)}, u32[]{:S(2)}, u32[]{:S(2)}) %collective-permute-start.3) | collective-permute-done | bytes 262176 | tf_op jit(solution)/shard_map/ppermute | solution.py:347
  20.3 2.0 %collective-permute-start.7 = (f32[4,128,128]{2,1,0:T(8,128)S(1)}, f32[4,128,128]{2,1,0:T(8,128)S(1)}, u32[]{:S(2)}, u32[]{:S(2)}) collective-permute-start(f32[4,128,128]{2,1,0:T(8,128)S(1)} %get-tuple-element.217), channel_id=1, source_target_pairs={{0,1},{1,0},{2,3},{3,2},{4,5},{5,4},{6,7},{7,6},{8,9},{9,8},{10,11... | collective-permute-start | bytes 786440 | tf_op jit(solution)/shard_map/ppermute | solution.py:347
  22.2 1.6 %collective-permute-done.2.refs_1_ = f32[4,128,128]{2,1,0:T(8,128)S(1)} collective-permute-done((f32[4,128,128]{2,1,0:T(8,128)S(1)}, f32[4,128,128]{2,1,0:T(8,128)S(1)}, u32[]{:S(2)}, u32[]{:S(2)}) %collective-permute-start.2) | collective-permute-done | bytes 262176 | tf_op jit(solution)/shard_map/ppermute | solution.py:347
  23.9 0.6 numer_0.1
  24.5 1.9 %collective-permute-start.10 = (f32[4,128,128]{2,1,0:T(8,128)S(1)}, f32[4,128,128]{2,1,0:T(8,128)S(1)}, u32[]{:S(2)}, u32[]{:S(2)}) collective-permute-start(f32[4,128,128]{2,1,0:T(8,128)S(1)} %get-tuple-element.236.refs_0_), channel_id=1, source_target_pairs={{0,1},{1,0},{2,3},{3,2},{4,5},{5,4},{6,7},{7,6},{8,9},{9,8},{10,11... | collective-permute-start | bytes 786440 | tf_op jit(solution)/shard_map/ppermute | solution.py:347
  26.4 0.6 numer_1.1
  27.0 1.6 %collective-permute-start.9 = (f32[4,128,128]{2,1,0:T(8,128)S(1)}, f32[4,128,128]{2,1,0:T(8,128)S(1)}, u32[]{:S(2)}, u32[]{:S(2)}) collective-permute-start(f32[4,128,128]{2,1,0:T(8,128)S(1)} %get-tuple-element.235.refs_0_), channel_id=1, source_target_pairs={{0,2},{1,3},{2,0},{3,1},{4,6},{5,7},{6,4},{7,5},{8,10},{9,11},{10,... | collective-permute-start | bytes 786440 | tf_op jit(solution)/shard_map/ppermute | solution.py:347
  28.6 0.8 %query_grad_0.1 = (bf16[4,128,128]{2,1,0:T(8,128)(2,1)S(1)}, bf16[4,128,128]{2,1,0:T(8,128)(2,1)S(1)}, f32[4,136,128]{2,1,0:T(8,128)S(1)}, f32[8,128]{1,0:T(8,128)S(1)}) custom-call(bf16[4,128,128]{2,1,0:T(8,128)(2,1)S(1)} %get-tuple-element.188.refs_0_.refs_1_, bf16[4,128,128]{2,1,0:T(8,128)(2,1)S(1)} %get-tuple-element.189.refs_1_, ...), custom_call_target="tpu_custom_call" | custom-call | flops 200000000 | tf_op jit(solution)/shard_map/query_grad_0/pallas_call | solution.py:310
  29.4 0.8 %query_grad_1.1 = (bf16[4,128,128]{2,1,0:T(8,128)(2,1)S(1)}, bf16[4,128,128]{2,1,0:T(8,128)(2,1)S(1)}, f32[4,136,128]{2,1,0:T(8,128)S(1)}, f32[8,128]{1,0:T(8,128)S(1)}) custom-call(bf16[4,128,128]{2,1,0:T(8,128)(2,1)S(1)} %get-tuple-element.199.refs_0_.refs_1_, bf16[4,128,128]{2,1,0:T(8,128)(2,1)S(1)} %get-tuple-element.200.refs_1_, ...), custom_call_target="tpu_custom_call" | custom-call | flops 200000000 | tf_op jit(solution)/shard_map/query_grad_1/pallas_call | solution.py:310
  30.3 0.6 numer_2.1
  31.4 0.6 numer_3.1
  32.1 1.6 %collective-permute-start.13 = (f32[4,128,128]{2,1,0:T(8,128)S(1)}, f32[4,128,128]{2,1,0:T(8,128)S(1)}, u32[]{:S(2)}, u32[]{:S(2)}) collective-permute-start(f32[4,128,128]{2,1,0:T(8,128)S(1)} %get-tuple-element.244.refs_0_), channel_id=1, source_target_pairs={{0,1},{1,0},{2,3},{3,2},{4,5},{5,4},{6,7},{7,6},{8,9},{9,8},{10,11... | collective-permute-start | bytes 786440 | tf_op jit(solution)/shard_map/ppermute | solution.py:347
  33.7 0.6 collective-permute-start.12
  34.3 0.8 %query_grad_2.1 = (bf16[4,128,128]{2,1,0:T(8,128)(2,1)S(1)}, bf16[4,128,128]{2,1,0:T(8,128)(2,1)S(1)}, f32[4,136,128]{2,1,0:T(8,128)S(1)}, f32[8,128]{1,0:T(8,128)S(1)}) custom-call(bf16[4,128,128]{2,1,0:T(8,128)(2,1)S(1)} %get-tuple-element.210.refs_0_.refs_1_, bf16[4,128,128]{2,1,0:T(8,128)(2,1)S(1)} %get-tuple-element.211.refs_1_, ...), custom_call_target="tpu_custom_call" | custom-call | flops 200000000 | tf_op jit(solution)/shard_map/query_grad_2/pallas_call | solution.py:310
  35.1 0.8 %query_grad_3.1 = (bf16[4,128,128]{2,1,0:T(8,128)(2,1)S(1)}, bf16[4,128,128]{2,1,0:T(8,128)(2,1)S(1)}, f32[4,136,128]{2,1,0:T(8,128)S(1)}, f32[8,128]{1,0:T(8,128)S(1)}) custom-call(bf16[4,128,128]{2,1,0:T(8,128)(2,1)S(1)} %get-tuple-element.224.refs_0_.refs_1_, bf16[4,128,128]{2,1,0:T(8,128)(2,1)S(1)} %get-tuple-element.225.refs_1_, ...), custom_call_target="tpu_custom_call" | custom-call | flops 200000000 | tf_op jit(solution)/shard_map/query_grad_3/pallas_call | solution.py:310
  36.3 1.5 %collective-permute-start.15 = (f32[4,128,128]{2,1,0:T(8,128)S(1)}, f32[4,128,128]{2,1,0:T(8,128)S(1)}, u32[]{:S(2)}, u32[]{:S(2)}) collective-permute-start(f32[4,128,128]{2,1,0:T(8,128)S(1)} %get-tuple-element.250), channel_id=1, source_target_pairs={{0,2},{1,3},{2,0},{3,1},{4,6},{5,7},{6,4},{7,5},{8,10},{9,11},{10,... | collective-permute-start | bytes 786440 | tf_op jit(solution)/shard_map/ppermute | solution.py:347
  38.3 3.1 %collective-permute-done.13.refs_1_.refs_0_ = f32[4,128,128]{2,1,0:T(8,128)S(1)} collective-permute-done((f32[4,128,128]{2,1,0:T(8,128)S(1)}, f32[4,128,128]{2,1,0:T(8,128)S(1)}, u32[]{:S(2)}, u32[]{:S(2)}) %collective-permute-start.13) | collective-permute-done | bytes 262176 | tf_op jit(solution)/shard_map/ppermute | solution.py:347
  41.9 1.0 %collective-permute-done.12.refs_1_.refs_0_ = f32[4,128,128]{2,1,0:T(8,128)S(1)} collective-permute-done((f32[4,128,128]{2,1,0:T(8,128)S(1)}, f32[4,128,128]{2,1,0:T(8,128)S(1)}, u32[]{:S(2)}, u32[]{:S(2)}) %collective-permute-start.12) | collective-permute-done | bytes 262176 | tf_op jit(solution)/shard_map/ppermute | solution.py:347
  42.9 0.8 collective-permute-start.20
  43.8 2.7 %collective-permute-start.14 = (f32[2,2,136,128]{3,2,1,0:T(8,128)S(1)}, f32[2,2,136,128]{3,2,1,0:T(8,128)S(1)}, u32[]{:S(2)}, u32[]{:S(2)}) collective-permute-start(f32[2,2,136,128]{3,2,1,0:T(8,128)S(1)} %get-tuple-element.249), channel_id=1, source_target_pairs={{0,16},{4,20},{8,24},{12,28},{16,0},{20,4},{24,8},{28,12},{1,17},{... | collective-permute-start | bytes 835592 | tf_op jit(solution)/shard_map/ppermute | solution.py:347
  46.4 2.0 %collective-permute-done.15.refs_1_ = f32[4,128,128]{2,1,0:T(8,128)S(1)} collective-permute-done((f32[4,128,128]{2,1,0:T(8,128)S(1)}, f32[4,128,128]{2,1,0:T(8,128)S(1)}, u32[]{:S(2)}, u32[]{:S(2)}) %collective-permute-start.15) | collective-permute-done | bytes 262176 | tf_op jit(solution)/shard_map/ppermute | solution.py:347
  50.4 2.9 %collective-permute-done.19.refs_1_ = f32[4,128,128]{2,1,0:T(8,128)S(1)} collective-permute-done((f32[4,128,128]{2,1,0:T(8,128)S(1)}, f32[4,128,128]{2,1,0:T(8,128)S(1)}, u32[]{:S(2)}, u32[]{:S(2)}) %collective-permute-start.19) | collective-permute-done | bytes 262176 | tf_op jit(solution)/shard_map/ppermute | solution.py:347
  56.7 1.6 %collective-permute-start.27 = (f32[2,128,128]{2,1,0:T(8,128)S(1)}, f32[2,128,128]{2,1,0:T(8,128)S(1)}, u32[]{:S(2)}, u32[]{:S(2)}) collective-permute-start(f32[2,128,128]{2,1,0:T(8,128)S(1)} %get-tuple-element.312), channel_id=1, source_target_pairs={{0,8},{4,12},{8,0},{12,4},{16,24},{20,28},{24,16},{28,20},{1,9},{5... | collective-permute-start | bytes 393224 | tf_op jit(solution)/shard_map/ppermute | solution.py:347
  58.4 2.6 %collective-permute-start.28 = (f32[2,128,128]{2,1,0:T(8,128)S(1)}, f32[2,128,128]{2,1,0:T(8,128)S(1)}, u32[]{:S(2)}, u32[]{:S(2)}) collective-permute-start(f32[2,128,128]{2,1,0:T(8,128)S(1)} %get-tuple-element.313), channel_id=1, source_target_pairs={{0,16},{4,20},{8,24},{12,28},{16,0},{20,4},{24,8},{28,12},{1,17},{... | collective-permute-start | bytes 393224 | tf_op jit(solution)/shard_map/ppermute | solution.py:347
  61.2 0.7 collective-permute-start.24
  62.0 1.3 %collective-permute-start.23 = (f32[136,128]{1,0:T(8,128)S(1)}, f32[136,128]{1,0:T(8,128)S(1)}, u32[]{:S(2)}, u32[]{:S(2)}) collective-permute-start(f32[136,128]{1,0:T(8,128)S(1)} %get-tuple-element.305), channel_id=1, source_target_pairs={{0,8},{4,12},{8,0},{12,4},{16,24},{20,28},{24,16},{28,20},{1,9},{5... | collective-permute-start | bytes 208904 | tf_op jit(solution)/shard_map/ppermute | solution.py:347
  63.3 0.9 %lay_0.1 = (bf16[128,2048]{1,0:T(8,128)(2,1)}, f32[8,128]{1,0:T(8,128)S(1)}) custom-call(bf16[4,128,128]{2,1,0:T(8,128)(2,1)S(1)} %get-tuple-element.198.refs_0_, bf16[4,128,128]{2,1,0:T(8,128)(2,1)S(1)} %get-tuple-element.205.refs_1_, bf16[4,128,128]{2,1,0:T(8,128)(2,1)S(1)} %get-tuple-element.223.refs_2_, ...), custom_call_target="tpu_custom_call" | custom-call | flops 200000000 | tf_op jit(solution)/shard_map/lay_0/pallas_call | solution.py:310
  64.3 0.9 %lay_1.1 = (bf16[128,2048]{1,0:T(8,128)(2,1)}, f32[8,128]{1,0:T(8,128)S(1)}) custom-call(bf16[4,128,128]{2,1,0:T(8,128)(2,1)S(1)} %get-tuple-element.294.refs_0_, bf16[4,128,128]{2,1,0:T(8,128)(2,1)S(1)} %get-tuple-element.295.refs_1_, bf16[4,128,128]{2,1,0:T(8,128)(2,1)S(1)} %get-tuple-element.296.refs_2_, ...), custom_call_target="tpu_custom_call" | custom-call | flops 200000000 | tf_op jit(solution)/shard_map/lay_1/pallas_call | solution.py:310
  65.2 4.0 %collective-permute-done.24.refs_1_ = f32[136,128]{1,0:T(8,128)S(1)} collective-permute-done((f32[136,128]{1,0:T(8,128)S(1)}, f32[136,128]{1,0:T(8,128)S(1)}, u32[]{:S(2)}, u32[]{:S(2)}) %collective-permute-start.24) | collective-permute-done | bytes 69664 | tf_op jit(solution)/shard_map/ppermute | solution.py:347
  69.9 1.0 %collective-permute-done.23.refs_1_ = f32[136,128]{1,0:T(8,128)S(1)} collective-permute-done((f32[136,128]{1,0:T(8,128)S(1)}, f32[136,128]{1,0:T(8,128)S(1)}, u32[]{:S(2)}, u32[]{:S(2)}) %collective-permute-start.23) | collective-permute-done | bytes 69664 | tf_op jit(solution)/shard_map/ppermute | solution.py:347
  70.9 0.6 collective-permute-start.25
  71.6 0.6 collective-permute-start.32
  72.2 1.4 %collective-permute-start.33 = (f32[2,128,128]{2,1,0:T(8,128)S(1)}, f32[2,128,128]{2,1,0:T(8,128)S(1)}, u32[]{:S(2)}, u32[]{:S(2)}) collective-permute-start(f32[2,128,128]{2,1,0:T(8,128)S(1)} %get-tuple-element.322.refs_0_), channel_id=1, source_target_pairs={{0,2},{1,3},{2,0},{3,1},{4,6},{5,7},{6,4},{7,5},{8,10},{9,11},{10,... | collective-permute-start | bytes 393224 | tf_op jit(solution)/shard_map/ppermute | solution.py:347
  73.7 1.5 %collective-permute-start.34 = (f32[2,128,128]{2,1,0:T(8,128)S(1)}, f32[2,128,128]{2,1,0:T(8,128)S(1)}, u32[]{:S(2)}, u32[]{:S(2)}) collective-permute-start(f32[2,128,128]{2,1,0:T(8,128)S(1)} %get-tuple-element.322.refs_0_), channel_id=1, source_target_pairs={{0,3},{1,2},{2,1},{3,0},{4,7},{5,6},{6,5},{7,4},{8,11},{9,10},{10,... | collective-permute-start | bytes 393224 | tf_op jit(solution)/shard_map/ppermute | solution.py:347
  75.2 1.3 %collective-permute-done.25.refs_1_ = f32[136,128]{1,0:T(8,128)S(1)} collective-permute-done((f32[136,128]{1,0:T(8,128)S(1)}, f32[136,128]{1,0:T(8,128)S(1)}, u32[]{:S(2)}, u32[]{:S(2)}) %collective-permute-start.25) | collective-permute-done | bytes 69664 | tf_op jit(solution)/shard_map/ppermute | solution.py:347
  76.7 0.6 collective-permute-start.30
  77.3 0.9 %lay_2.1 = (bf16[128,2048]{1,0:T(8,128)(2,1)}, f32[8,128]{1,0:T(8,128)S(1)}) custom-call(bf16[4,128,128]{2,1,0:T(8,128)(2,1)S(1)} %get-tuple-element.300.refs_0_, bf16[4,128,128]{2,1,0:T(8,128)(2,1)S(1)} %get-tuple-element.301.refs_1_, bf16[4,128,128]{2,1,0:T(8,128)(2,1)S(1)} %get-tuple-element.302.refs_2_, ...), custom_call_target="tpu_custom_call" | custom-call | flops 200000000 | tf_op jit(solution)/shard_map/lay_2/pallas_call | solution.py:310
  78.2 2.3 %collective-permute-done.33.refs_2_ = f32[2,128,128]{2,1,0:T(8,128)S(1)} collective-permute-done((f32[2,128,128]{2,1,0:T(8,128)S(1)}, f32[2,128,128]{2,1,0:T(8,128)S(1)}, u32[]{:S(2)}, u32[]{:S(2)}) %collective-permute-start.33) | collective-permute-done | bytes 131104 | tf_op jit(solution)/shard_map/ppermute | solution.py:347
  80.5 0.7 key_total.1
  81.3 0.7 query_total.1
  (85 shorter events, 10.9 us)
Async XLA Ops:
  2.2 4.5 %copy-start.7 = (f32[8,128]{1,0:T(8,128)}, f32[8,128]{1,0:T(8,128)S(1)}, u32[]{:S(2)}) copy-start(f32[8,128]{1,0:T(8,128)S(1)} %get-tuple-element.171.refs_3_) | copy-start | bytes 12292
  2.2 10.2 %collective-permute-start.1 = (f32[4,128,128]{2,1,0:T(8,128)S(1)}, f32[4,128,128]{2,1,0:T(8,128)S(1)}, u32[]{:S(2)}, u32[]{:S(2)}) collective-permute-start(f32[4,128,128]{2,1,0:T(8,128)S(1)} %get-tuple-element.168.refs_0_), channel_id=1, source_target_pairs={{0,2},{1,3},{2,0},{3,1},{4,6},{5,7},{6,4},{7,5},{8,10},{9,11},{10,... | collective-permute-start | bytes 786440 | tf_op jit(solution)/shard_map/ppermute | solution.py:347
  5.3 9.2 %collective-permute-start = (f32[4,128,128]{2,1,0:T(8,128)S(1)}, f32[4,128,128]{2,1,0:T(8,128)S(1)}, u32[]{:S(2)}, u32[]{:S(2)}) collective-permute-start(f32[4,128,128]{2,1,0:T(8,128)S(1)} %get-tuple-element.167.refs_0_), channel_id=1, source_target_pairs={{0,1},{1,0},{2,3},{3,2},{4,5},{5,4},{6,7},{7,6},{8,9},{9,8},{10,11... | collective-permute-start | bytes 786440 | tf_op jit(solution)/shard_map/ppermute | solution.py:347
  6.8 2.4 %copy-start.2 = (bf16[1,128,2048]{2,1,0:T(8,128)(2,1)S(1)}, bf16[1,128,2048]{2,1,0:T(8,128)(2,1)}, u32[]{:S(2)}) copy-start(bf16[1,128,2048]{2,1,0:T(8,128)(2,1)} %param.7) | copy-start | bytes 1572868
  6.8 2.4 %copy-start.3 = (bf16[2048,128]{1,0:T(8,128)(2,1)S(1)}, bf16[2048,128]{1,0:T(8,128)(2,1)}, u32[]{:S(2)}) copy-start(bf16[2048,128]{1,0:T(8,128)(2,1)} %refs_7_.7) | copy-start | bytes 1572868
  8.5 9.6 %collective-permute-start.4 = (f32[4,128,128]{2,1,0:T(8,128)S(1)}, f32[4,128,128]{2,1,0:T(8,128)S(1)}, u32[]{:S(2)}, u32[]{:S(2)}) collective-permute-start(f32[4,128,128]{2,1,0:T(8,128)S(1)} %get-tuple-element.180.refs_0_), channel_id=1, source_target_pairs={{0,2},{1,3},{2,0},{3,1},{4,6},{5,7},{6,4},{7,5},{8,10},{9,11},{10,... | collective-permute-start | bytes 786440 | tf_op jit(solution)/shard_map/ppermute | solution.py:347
  9.0 11.1 %collective-permute-start.3 = (f32[4,128,128]{2,1,0:T(8,128)S(1)}, f32[4,128,128]{2,1,0:T(8,128)S(1)}, u32[]{:S(2)}, u32[]{:S(2)}) collective-permute-start(f32[4,128,128]{2,1,0:T(8,128)S(1)} %get-tuple-element.179.refs_0_), channel_id=1, source_target_pairs={{0,1},{1,0},{2,3},{3,2},{4,5},{5,4},{6,7},{7,6},{8,9},{9,8},{10,11... | collective-permute-start | bytes 786440 | tf_op jit(solution)/shard_map/ppermute | solution.py:347
  14.5 9.3 %collective-permute-start.2 = (f32[4,128,128]{2,1,0:T(8,128)S(1)}, f32[4,128,128]{2,1,0:T(8,128)S(1)}, u32[]{:S(2)}, u32[]{:S(2)}) collective-permute-start(f32[4,128,128]{2,1,0:T(8,128)S(1)} %get-tuple-element.176), channel_id=1, source_target_pairs={{0,2},{1,3},{2,0},{3,1},{4,6},{5,7},{6,4},{7,5},{8,10},{9,11},{10,... | collective-permute-start | bytes 786440 | tf_op jit(solution)/shard_map/ppermute | solution.py:347
  14.6 11.7 %collective-permute-start.5 = (f32[4,128,128]{2,1,0:T(8,128)S(1)}, f32[4,128,128]{2,1,0:T(8,128)S(1)}, u32[]{:S(2)}, u32[]{:S(2)}) collective-permute-start(f32[4,128,128]{2,1,0:T(8,128)S(1)} %get-tuple-element.193), channel_id=1, source_target_pairs={{0,1},{1,0},{2,3},{3,2},{4,5},{5,4},{6,7},{7,6},{8,9},{9,8},{10,11... | collective-permute-start | bytes 786440 | tf_op jit(solution)/shard_map/ppermute | solution.py:347
  18.0 5.8 %copy-start.5 = (bf16[1,128,2048]{2,1,0:T(8,128)(2,1)S(1)}, bf16[1,128,2048]{2,1,0:T(8,128)(2,1)}, u32[]{:S(2)}) copy-start(bf16[1,128,2048]{2,1,0:T(8,128)(2,1)} %param.10) | copy-start | bytes 1572868
  18.1 5.8 %copy-start = (bf16[1,128,2048]{2,1,0:T(8,128)(2,1)S(1)}, bf16[1,128,2048]{2,1,0:T(8,128)(2,1)}, u32[]{:S(2)}) copy-start(bf16[1,128,2048]{2,1,0:T(8,128)(2,1)} %param.9) | copy-start | bytes 1572868
  20.2 3.7 %copy-start.6 = (f32[2048]{0:T(1024)S(1)}, f32[2048]{0:T(1024)}, u32[]{:S(2)}) copy-start(f32[2048]{0:T(1024)} %param.13) | copy-start | bytes 24580
  20.2 10.1 %collective-permute-start.6 = (f32[4,128,128]{2,1,0:T(8,128)S(1)}, f32[4,128,128]{2,1,0:T(8,128)S(1)}, u32[]{:S(2)}, u32[]{:S(2)}) collective-permute-start(f32[4,128,128]{2,1,0:T(8,128)S(1)} %get-tuple-element.206), channel_id=1, source_target_pairs={{0,2},{1,3},{2,0},{3,1},{4,6},{5,7},{6,4},{7,5},{8,10},{9,11},{10,... | collective-permute-start | bytes 786440 | tf_op jit(solution)/shard_map/ppermute | solution.py:347
  20.3 11.1 %collective-permute-start.7 = (f32[4,128,128]{2,1,0:T(8,128)S(1)}, f32[4,128,128]{2,1,0:T(8,128)S(1)}, u32[]{:S(2)}, u32[]{:S(2)}) collective-permute-start(f32[4,128,128]{2,1,0:T(8,128)S(1)} %get-tuple-element.217), channel_id=1, source_target_pairs={{0,1},{1,0},{2,3},{3,2},{4,5},{5,4},{6,7},{7,6},{8,9},{9,8},{10,11... | collective-permute-start | bytes 786440 | tf_op jit(solution)/shard_map/ppermute | solution.py:347
  24.5 11.5 %collective-permute-start.10 = (f32[4,128,128]{2,1,0:T(8,128)S(1)}, f32[4,128,128]{2,1,0:T(8,128)S(1)}, u32[]{:S(2)}, u32[]{:S(2)}) collective-permute-start(f32[4,128,128]{2,1,0:T(8,128)S(1)} %get-tuple-element.236.refs_0_), channel_id=1, source_target_pairs={{0,1},{1,0},{2,3},{3,2},{4,5},{5,4},{6,7},{7,6},{8,9},{9,8},{10,11... | collective-permute-start | bytes 786440 | tf_op jit(solution)/shard_map/ppermute | solution.py:347
  27.0 9.0 %collective-permute-start.9 = (f32[4,128,128]{2,1,0:T(8,128)S(1)}, f32[4,128,128]{2,1,0:T(8,128)S(1)}, u32[]{:S(2)}, u32[]{:S(2)}) collective-permute-start(f32[4,128,128]{2,1,0:T(8,128)S(1)} %get-tuple-element.235.refs_0_), channel_id=1, source_target_pairs={{0,2},{1,3},{2,0},{3,1},{4,6},{5,7},{6,4},{7,5},{8,10},{9,11},{10,... | collective-permute-start | bytes 786440 | tf_op jit(solution)/shard_map/ppermute | solution.py:347
  32.0 4.1 %collective-permute-start.8 = (f32[2,2,136,128]{3,2,1,0:T(8,128)S(1)}, f32[2,2,136,128]{3,2,1,0:T(8,128)S(1)}, u32[]{:S(2)}, u32[]{:S(2)}) collective-permute-start(f32[2,2,136,128]{3,2,1,0:T(8,128)S(1)} %get-tuple-element.234), channel_id=1, source_target_pairs={{0,4},{4,0},{8,12},{12,8},{16,20},{20,16},{24,28},{28,24},{1,5},{5... | collective-permute-start | bytes 835592 | tf_op jit(solution)/shard_map/ppermute | solution.py:347
  32.1 9.2 %collective-permute-start.13 = (f32[4,128,128]{2,1,0:T(8,128)S(1)}, f32[4,128,128]{2,1,0:T(8,128)S(1)}, u32[]{:S(2)}, u32[]{:S(2)}) collective-permute-start(f32[4,128,128]{2,1,0:T(8,128)S(1)} %get-tuple-element.244.refs_0_), channel_id=1, source_target_pairs={{0,1},{1,0},{2,3},{3,2},{4,5},{5,4},{6,7},{7,6},{8,9},{9,8},{10,11... | collective-permute-start | bytes 786440 | tf_op jit(solution)/shard_map/ppermute | solution.py:347
  33.7 9.2 %collective-permute-start.12 = (f32[4,128,128]{2,1,0:T(8,128)S(1)}, f32[4,128,128]{2,1,0:T(8,128)S(1)}, u32[]{:S(2)}, u32[]{:S(2)}) collective-permute-start(f32[4,128,128]{2,1,0:T(8,128)S(1)} %get-tuple-element.243.refs_0_), channel_id=1, source_target_pairs={{0,2},{1,3},{2,0},{3,1},{4,6},{5,7},{6,4},{7,5},{8,10},{9,11},{10,... | collective-permute-start | bytes 786440 | tf_op jit(solution)/shard_map/ppermute | solution.py:347
  36.2 7.5 %collective-permute-start.11 = (f32[2,2,136,128]{3,2,1,0:T(8,128)S(1)}, f32[2,2,136,128]{3,2,1,0:T(8,128)S(1)}, u32[]{:S(2)}, u32[]{:S(2)}) collective-permute-start(f32[2,2,136,128]{3,2,1,0:T(8,128)S(1)} %get-tuple-element.242), channel_id=1, source_target_pairs={{0,4},{4,0},{8,12},{12,8},{16,20},{20,16},{24,28},{28,24},{1,5},{5... | collective-permute-start | bytes 835592 | tf_op jit(solution)/shard_map/ppermute | solution.py:347
  36.3 12.2 %collective-permute-start.15 = (f32[4,128,128]{2,1,0:T(8,128)S(1)}, f32[4,128,128]{2,1,0:T(8,128)S(1)}, u32[]{:S(2)}, u32[]{:S(2)}) collective-permute-start(f32[4,128,128]{2,1,0:T(8,128)S(1)} %get-tuple-element.250), channel_id=1, source_target_pairs={{0,2},{1,3},{2,0},{3,1},{4,6},{5,7},{6,4},{7,5},{8,10},{9,11},{10,... | collective-permute-start | bytes 786440 | tf_op jit(solution)/shard_map/ppermute | solution.py:347
  37.8 11.3 %collective-permute-start.16 = (f32[4,128,128]{2,1,0:T(8,128)S(1)}, f32[4,128,128]{2,1,0:T(8,128)S(1)}, u32[]{:S(2)}, u32[]{:S(2)}) collective-permute-start(f32[4,128,128]{2,1,0:T(8,128)S(1)} %get-tuple-element.254), channel_id=1, source_target_pairs={{0,1},{1,0},{2,3},{3,2},{4,5},{5,4},{6,7},{7,6},{8,9},{9,8},{10,11... | collective-permute-start | bytes 786440 | tf_op jit(solution)/shard_map/ppermute | solution.py:347
  41.4 11.9 %collective-permute-start.19 = (f32[4,128,128]{2,1,0:T(8,128)S(1)}, f32[4,128,128]{2,1,0:T(8,128)S(1)}, u32[]{:S(2)}, u32[]{:S(2)}) collective-permute-start(f32[4,128,128]{2,1,0:T(8,128)S(1)} %get-tuple-element.262), channel_id=1, source_target_pairs={{0,2},{1,3},{2,0},{3,1},{4,6},{5,7},{6,4},{7,5},{8,10},{9,11},{10,... | collective-permute-start | bytes 786440 | tf_op jit(solution)/shard_map/ppermute | solution.py:347
  42.8 5.6 %copy-start.4 = (bf16[1,128,2048]{2,1,0:T(8,128)(2,1)S(1)}, bf16[1,128,2048]{2,1,0:T(8,128)(2,1)}, u32[]{:S(2)}) copy-start(bf16[1,128,2048]{2,1,0:T(8,128)(2,1)} %param.8) | copy-start | bytes 1572868
  42.9 5.6 %copy-start.1 = (bf16[2048,128]{1,0:T(8,128)(2,1)S(1)}, bf16[2048,128]{1,0:T(8,128)(2,1)}, u32[]{:S(2)}) copy-start(bf16[2048,128]{1,0:T(8,128)(2,1)} %refs_6_.15) | copy-start | bytes 1572868
  42.9 11.0 %collective-permute-start.20 = (f32[4,128,128]{2,1,0:T(8,128)S(1)}, f32[4,128,128]{2,1,0:T(8,128)S(1)}, u32[]{:S(2)}, u32[]{:S(2)}) collective-permute-start(f32[4,128,128]{2,1,0:T(8,128)S(1)} %get-tuple-element.274), channel_id=1, source_target_pairs={{0,1},{1,0},{2,3},{3,2},{4,5},{5,4},{6,7},{7,6},{8,9},{9,8},{10,11... | collective-permute-start | bytes 786440 | tf_op jit(solution)/shard_map/ppermute | solution.py:347
  43.8 17.4 %collective-permute-start.14 = (f32[2,2,136,128]{3,2,1,0:T(8,128)S(1)}, f32[2,2,136,128]{3,2,1,0:T(8,128)S(1)}, u32[]{:S(2)}, u32[]{:S(2)}) collective-permute-start(f32[2,2,136,128]{3,2,1,0:T(8,128)S(1)} %get-tuple-element.249), channel_id=1, source_target_pairs={{0,16},{4,20},{8,24},{12,28},{16,0},{20,4},{24,8},{28,12},{1,17},{... | collective-permute-start | bytes 835592 | tf_op jit(solution)/shard_map/ppermute | solution.py:347
  54.5 1.8 %collective-permute-start.21 = (f32[2,128,128]{2,1,0:T(8,128)S(1)}, f32[2,128,128]{2,1,0:T(8,128)S(1)}, u32[]{:S(2)}, u32[]{:S(2)}) collective-permute-start(f32[2,128,128]{2,1,0:T(8,128)S(1)} %get-tuple-element.280), channel_id=1, source_target_pairs={{0,4},{4,0},{8,12},{12,8},{16,20},{20,16},{24,28},{28,24},{1,5},{5... | collective-permute-start | bytes 393224 | tf_op jit(solution)/shard_map/ppermute | solution.py:347
  54.6 1.8 %collective-permute-start.22 = (f32[2,128,128]{2,1,0:T(8,128)S(1)}, f32[2,128,128]{2,1,0:T(8,128)S(1)}, u32[]{:S(2)}, u32[]{:S(2)}) collective-permute-start(f32[2,128,128]{2,1,0:T(8,128)S(1)} %get-tuple-element.281), channel_id=1, source_target_pairs={{0,4},{4,0},{8,12},{12,8},{16,20},{20,16},{24,28},{28,24},{1,5},{5... | collective-permute-start | bytes 393224 | tf_op jit(solution)/shard_map/ppermute | solution.py:347
  55.1 1.3 %collective-permute-start.17 = (f32[2,128,128]{2,1,0:T(8,128)S(1)}, f32[2,128,128]{2,1,0:T(8,128)S(1)}, u32[]{:S(2)}, u32[]{:S(2)}) collective-permute-start(f32[2,128,128]{2,1,0:T(8,128)S(1)} %get-tuple-element.260), channel_id=1, source_target_pairs={{0,4},{4,0},{8,12},{12,8},{16,20},{20,16},{24,28},{28,24},{1,5},{5... | collective-permute-start | bytes 393224 | tf_op jit(solution)/shard_map/ppermute | solution.py:347
  55.2 1.5 %collective-permute-start.18 = (f32[2,128,128]{2,1,0:T(8,128)S(1)}, f32[2,128,128]{2,1,0:T(8,128)S(1)}, u32[]{:S(2)}, u32[]{:S(2)}) collective-permute-start(f32[2,128,128]{2,1,0:T(8,128)S(1)} %get-tuple-element.261), channel_id=1, source_target_pairs={{0,4},{4,0},{8,12},{12,8},{16,20},{20,16},{24,28},{28,24},{1,5},{5... | collective-permute-start | bytes 393224 | tf_op jit(solution)/shard_map/ppermute | solution.py:347
  56.7 14.8 %collective-permute-start.27 = (f32[2,128,128]{2,1,0:T(8,128)S(1)}, f32[2,128,128]{2,1,0:T(8,128)S(1)}, u32[]{:S(2)}, u32[]{:S(2)}) collective-permute-start(f32[2,128,128]{2,1,0:T(8,128)S(1)} %get-tuple-element.312), channel_id=1, source_target_pairs={{0,8},{4,12},{8,0},{12,4},{16,24},{20,28},{24,16},{28,20},{1,9},{5... | collective-permute-start | bytes 393224 | tf_op jit(solution)/shard_map/ppermute | solution.py:347
  58.4 13.2 %collective-permute-start.28 = (f32[2,128,128]{2,1,0:T(8,128)S(1)}, f32[2,128,128]{2,1,0:T(8,128)S(1)}, u32[]{:S(2)}, u32[]{:S(2)}) collective-permute-start(f32[2,128,128]{2,1,0:T(8,128)S(1)} %get-tuple-element.313), channel_id=1, source_target_pairs={{0,16},{4,20},{8,24},{12,28},{16,0},{20,4},{24,8},{28,12},{1,17},{... | collective-permute-start | bytes 393224 | tf_op jit(solution)/shard_map/ppermute | solution.py:347
  61.0 10.6 %collective-permute-start.29 = (f32[2,128,128]{2,1,0:T(8,128)S(1)}, f32[2,128,128]{2,1,0:T(8,128)S(1)}, u32[]{:S(2)}, u32[]{:S(2)}) collective-permute-start(f32[2,128,128]{2,1,0:T(8,128)S(1)} %get-tuple-element.314), channel_id=1, source_target_pairs={{0,24},{4,28},{8,16},{12,20},{16,8},{20,12},{24,0},{28,4},{1,25},{... | collective-permute-start | bytes 393224 | tf_op jit(solution)/shard_map/ppermute | solution.py:347
  61.2 8.0 %collective-permute-start.24 = (f32[136,128]{1,0:T(8,128)S(1)}, f32[136,128]{1,0:T(8,128)S(1)}, u32[]{:S(2)}, u32[]{:S(2)}) collective-permute-start(f32[136,128]{1,0:T(8,128)S(1)} %get-tuple-element.306), channel_id=1, source_target_pairs={{0,8},{4,12},{8,0},{12,4},{16,24},{20,28},{24,16},{28,20},{1,9},{5... | collective-permute-start | bytes 208904 | tf_op jit(solution)/shard_map/ppermute | solution.py:347
  62.0 8.9 %collective-permute-start.23 = (f32[136,128]{1,0:T(8,128)S(1)}, f32[136,128]{1,0:T(8,128)S(1)}, u32[]{:S(2)}, u32[]{:S(2)}) collective-permute-start(f32[136,128]{1,0:T(8,128)S(1)} %get-tuple-element.305), channel_id=1, source_target_pairs={{0,8},{4,12},{8,0},{12,4},{16,24},{20,28},{24,16},{28,20},{1,9},{5... | collective-permute-start | bytes 208904 | tf_op jit(solution)/shard_map/ppermute | solution.py:347
  69.3 5.9 %collective-permute-start.26 = (f32[136,128]{1,0:T(8,128)S(1)}, f32[136,128]{1,0:T(8,128)S(1)}, u32[]{:S(2)}, u32[]{:S(2)}) collective-permute-start(f32[136,128]{1,0:T(8,128)S(1)} %get-tuple-element.310.refs_0_), channel_id=1, source_target_pairs={{0,1},{1,0},{2,3},{3,2},{4,5},{5,4},{6,7},{7,6},{8,9},{9,8},{10,11... | collective-permute-start | bytes 208904 | tf_op jit(solution)/shard_map/ppermute | solution.py:347
  70.9 5.5 %collective-permute-start.25 = (f32[136,128]{1,0:T(8,128)S(1)}, f32[136,128]{1,0:T(8,128)S(1)}, u32[]{:S(2)}, u32[]{:S(2)}) collective-permute-start(f32[136,128]{1,0:T(8,128)S(1)} %get-tuple-element.309.refs_0_), channel_id=1, source_target_pairs={{0,2},{1,3},{2,0},{3,1},{4,6},{5,7},{6,4},{7,5},{8,10},{9,11},{10,... | collective-permute-start | bytes 208904 | tf_op jit(solution)/shard_map/ppermute | solution.py:347
  71.6 6.6 %collective-permute-start.32 = (f32[2,128,128]{2,1,0:T(8,128)S(1)}, f32[2,128,128]{2,1,0:T(8,128)S(1)}, u32[]{:S(2)}, u32[]{:S(2)}) collective-permute-start(f32[2,128,128]{2,1,0:T(8,128)S(1)} %get-tuple-element.322.refs_0_), channel_id=1, source_target_pairs={{0,1},{1,0},{2,3},{3,2},{4,5},{5,4},{6,7},{7,6},{8,9},{9,8},{10,11... | collective-permute-start | bytes 393224 | tf_op jit(solution)/shard_map/ppermute | solution.py:347
  72.2 8.3 %collective-permute-start.33 = (f32[2,128,128]{2,1,0:T(8,128)S(1)}, f32[2,128,128]{2,1,0:T(8,128)S(1)}, u32[]{:S(2)}, u32[]{:S(2)}) collective-permute-start(f32[2,128,128]{2,1,0:T(8,128)S(1)} %get-tuple-element.322.refs_0_), channel_id=1, source_target_pairs={{0,2},{1,3},{2,0},{3,1},{4,6},{5,7},{6,4},{7,5},{8,10},{9,11},{10,... | collective-permute-start | bytes 393224 | tf_op jit(solution)/shard_map/ppermute | solution.py:347
  73.7 6.9 %collective-permute-start.34 = (f32[2,128,128]{2,1,0:T(8,128)S(1)}, f32[2,128,128]{2,1,0:T(8,128)S(1)}, u32[]{:S(2)}, u32[]{:S(2)}) collective-permute-start(f32[2,128,128]{2,1,0:T(8,128)S(1)} %get-tuple-element.322.refs_0_), channel_id=1, source_target_pairs={{0,3},{1,2},{2,1},{3,0},{4,7},{5,6},{6,5},{7,4},{8,11},{9,10},{10,... | collective-permute-start | bytes 393224 | tf_op jit(solution)/shard_map/ppermute | solution.py:347
  76.5 4.8 %collective-permute-start.31 = (f32[136,128]{1,0:T(8,128)S(1)}, f32[136,128]{1,0:T(8,128)S(1)}, u32[]{:S(2)}, u32[]{:S(2)}) collective-permute-start(f32[136,128]{1,0:T(8,128)S(1)} %get-tuple-element.321.refs_2_), channel_id=1, source_target_pairs={{0,1},{1,0},{2,3},{3,2},{4,5},{5,4},{6,7},{7,6},{8,9},{9,8},{10,11... | collective-permute-start | bytes 208904 | tf_op jit(solution)/shard_map/ppermute | solution.py:347
  76.7 4.6 %collective-permute-start.30 = (f32[136,128]{1,0:T(8,128)S(1)}, f32[136,128]{1,0:T(8,128)S(1)}, u32[]{:S(2)}, u32[]{:S(2)}) collective-permute-start(f32[136,128]{1,0:T(8,128)S(1)} %get-tuple-element.320.refs_0_), channel_id=1, source_target_pairs={{0,2},{1,3},{2,0},{3,1},{4,6},{5,7},{6,4},{7,5},{8,10},{9,11},{10,... | collective-permute-start | bytes 208904 | tf_op jit(solution)/shard_map/ppermute | solution.py:347

commit v6 on v5

--- a/solution.py
+++ b/solution.py
@@ -151,17 +151,22 @@
         weight[i, HEAD:, :] = gain[i]
 
 
-def key_grad_kernel(order, first, second, mixed, feat_query, key, value, w_key, pre_out, lh_out, ll_out, weight):
+def key_base_kernel(mixed, feat_query, key, w_key, base_out, slope_out):
     every = range(GROUP)
     at = [columns(i) for i in every]
     slope = [jnp.minimum(feature(dot(key[:, c], w_key[c, :])), 1.0) for c in at]
-    later = summed(order, 1, first, second)
-    parts = [split_low(x) for x in later]
+    base = [dot(mixed[i], feat_query[i], 0, 0) for i in every]
+    for i in every:
+        base_out[i] = base[i]
+        slope_out[i] = slope[i]
+
+
+def key_grad_kernel(order, first, second, base, slope, key, value, pre_out, lh_out, ll_out, weight):
+    every = range(GROUP)
+    at = [columns(i) for i in every]
+    parts = [split_low(x) for x in summed(order, 1, first, second)]
     val = [value[:, c] for c in at]
-    grad_fk = [
-        dot(mixed[i], feat_query[i], 0, 0) + dot(val[i], parts[i][0], 1, 1) + dot(val[i], parts[i][1], 1, 1)
-        for i in every
-    ]
+    grad_fk = [base[i] + dot(val[i], parts[i][0], 1, 1) + dot(val[i], parts[i][1], 1, 1) for i in every]
     pre = [(grad_fk[i] * slope[i]).astype(BF16) for i in every]
     sums = [dot(key[:, at[i]], pre[i], 0, 0) for i in every]
     for i in every:
@@ -447,11 +452,17 @@
             f"query_grad_{g}",
         )
 
+    bases = {}
+
+    def key_base(g):
+        inputs = [whole(mixed[g]), whole(feat_q[g]), cols(key, g), wrows(w_key, g)]
+        bases[g] = call(key_base_kernel, inputs, [tok(F32), tok(F32)], f"key_base_{g}")
+
     def key_grad(g):
         pre_k[g], late_h[g], late_l[g], sum_k[g] = call(
             functools.partial(key_grad_kernel, order_of(g)),
-            [whole(first_back[g]), whole(second_back[g]), whole(mixed[g]), whole(feat_q[g])]
-            + [cols(key, g), cols(value, g), wrows(w_key, g)],
+            [whole(first_back[g]), whole(second_back[g]), whole(bases[g][0]), whole(bases[g][1])]
+            + [cols(key, g), cols(value, g)],
             [tok(BF16), sq(BF16), sq(BF16), sq(F32)],
             f"key_grad_{g}",
         )
@@ -543,12 +554,12 @@
     if tuned:
         steps = (
             "K0K2Q0Q1p1p0Q2Q3p3p2N0N1G0G1N2N3a2G2G3",
-            "l0l1a3l2l3B2H0H1a0V0V1H2H3a1V2V3Z0c2L0L1E0E1C0F0F1L2T0U0",
+            "l0l1a3l2l3B2P0P1H0H1a0V0V1P2P3H2H3a1V2V3Z0c2L0L1E0E1C0F0F1L2T0U0",
         )
         steps = "".join(steps)
     else:
         steps = "".join(f"K{g}" for g in range(0, groups, 2))
-        steps += "".join(f"{kind}{g}" for kind in "pQNlGHV" for g in range(groups)) + "L0L1L2"
+        steps += "".join(f"{kind}{g}" for kind in "pQNlGPHV" for g in range(groups)) + "L0L1L2"
     does = {
         "K": key_state,
         "p": prior_hop,
@@ -556,6 +567,7 @@
         "N": numer_state,
         "l": later_hop,
         "G": query_grad,
+        "P": key_base,
         "H": key_grad,
         "V": value_grad,
         "L": lay,

time: 82.1 us -> 82.2 us (level)
  waiting for transfers between devices: 27.4 us -> 24.8 us
  starting transfers between devices: 34.3 us -> 36.4 us
    ppermute x35, waiting for transfers between devices: 27.4 us -> 24.8 us  [swap(): lax.ppermute(value, axis, [(i, i ^ bit) for i in range(lax.axis_size(axis...]
    ppermute x35, starting transfers between devices: 34.3 us -> 36.4 us  [swap(): lax.ppermute(value, axis, [(i, i ^ bit) for i in range(lax.axis_size(axis...]
    pallas_call x47 -> x51, Pallas kernels: 19.2 us -> 19.8 us  [__call__(): pl.pallas_call(ordered, grid=(1,), in_specs=[spec for _, spec in ins], ou...]
where the time goes in v6:
time: 82.2 us; the launch traced here: 82.1 us
  starting transfers between devices  36.4 us (44%)
  waiting for transfers between devices  24.8 us (30%)
  Pallas kernels  19.8 us (24%)
  between operations  1.05 us (1%)
    ppermute x35, starting transfers between devices, swap(): lax.ppermute(value, axis, [(i, i ^ bit) for i in range(lax.axis_size(axis...  36.4 us
    ppermute x35, waiting for transfers between devices, swap(): lax.ppermute(value, axis, [(i, i ^ bit) for i in range(lax.axis_size(axis...  24.8 us
    pallas_call x51, Pallas kernels, __call__(): pl.pallas_call(ordered, grid=(1,), in_specs=[spec for _, spec in ins], ou...  19.8 us
  transfers between devices with their start and end apart: 35, of which 16 were waited for; matrix products, arithmetic and copies ran while one was open for 0% of the time, Pallas kernels for 21%

profile of v6, /device:TPU:0, one launch (start us, length us, event | category | flops | bytes accessed | tf_op | source)
XLA Modules:
  0.0 82.1 jit_solution(4674525339876891182)
XLA Ops:
  0.6 1.6 %key_state_0.1 = (bf16[4,128,128]{2,1,0:T(8,128)(2,1)S(1)}, f32[4,128,128]{2,1,0:T(8,128)S(1)}, bf16[4,128,128]{2,1,0:T(8,128)(2,1)S(1)}, f32[4,128,128]{2,1,0:T(8,128)S(1)}, f32[8,128]{1,0:T(8,128)S(1)}) custom-call(bf16[128,2048]{1,0:T(8,128)(2,1)} %bitcast.23, bf16[128,2048]{1,0:T(8,128)(2,1)} %bitcast.9, bf16[2048,128]{1,0:T(8,128)(2,1)} %refs_6_.7), custom_call_target="tpu_custom_call" | custom-call | flops 200000000 | tf_op jit(solution)/shard_map/key_state_0/pallas_call | solution.py:315
  2.2 3.0 %collective-permute-start.1 = (f32[4,128,128]{2,1,0:T(8,128)S(1)}, f32[4,128,128]{2,1,0:T(8,128)S(1)}, u32[]{:S(2)}, u32[]{:S(2)}) collective-permute-start(f32[4,128,128]{2,1,0:T(8,128)S(1)} %get-tuple-element.180.refs_0_), channel_id=1, source_target_pairs={{0,2},{1,3},{2,0},{3,1},{4,6},{5,7},{6,4},{7,5},{8,10},{9,11},{10,... | collective-permute-start | bytes 786440 | tf_op jit(solution)/shard_map/ppermute | solution.py:352
  5.3 1.5 %collective-permute-start = (f32[4,128,128]{2,1,0:T(8,128)S(1)}, f32[4,128,128]{2,1,0:T(8,128)S(1)}, u32[]{:S(2)}, u32[]{:S(2)}) collective-permute-start(f32[4,128,128]{2,1,0:T(8,128)S(1)} %get-tuple-element.179.refs_0_), channel_id=1, source_target_pairs={{0,1},{1,0},{2,3},{3,2},{4,5},{5,4},{6,7},{7,6},{8,9},{9,8},{10,11... | collective-permute-start | bytes 786440 | tf_op jit(solution)/shard_map/ppermute | solution.py:352
  6.8 1.7 %key_state_2.1 = (bf16[4,128,128]{2,1,0:T(8,128)(2,1)S(1)}, f32[4,128,128]{2,1,0:T(8,128)S(1)}, bf16[4,128,128]{2,1,0:T(8,128)(2,1)S(1)}, f32[4,128,128]{2,1,0:T(8,128)S(1)}, f32[8,128]{1,0:T(8,128)S(1)}) custom-call(bf16[128,2048]{1,0:T(8,128)(2,1)} %bitcast.24, bf16[128,2048]{1,0:T(8,128)(2,1)} %bitcast.10, bf16[2048,128]{1,0:T(8,128)(2,1)} %refs_6_.7, ...), custom_call_target="tpu_custom_call" | custom-call | flops 200000000 | tf_op jit(solution)/shard_map/key_state_2/pallas_call | solution.py:315
  9.8 2.6 %collective-permute-done.1.refs_1_.refs_0_ = f32[4,128,128]{2,1,0:T(8,128)S(1)} collective-permute-done((f32[4,128,128]{2,1,0:T(8,128)S(1)}, f32[4,128,128]{2,1,0:T(8,128)S(1)}, u32[]{:S(2)}, u32[]{:S(2)}) %collective-permute-start.1) | collective-permute-done | bytes 262176 | tf_op jit(solution)/shard_map/ppermute | solution.py:352
  12.5 2.0 %collective-permute-done.refs_1_.refs_0_ = f32[4,128,128]{2,1,0:T(8,128)S(1)} collective-permute-done((f32[4,128,128]{2,1,0:T(8,128)S(1)}, f32[4,128,128]{2,1,0:T(8,128)S(1)}, u32[]{:S(2)}, u32[]{:S(2)}) %collective-permute-start) | collective-permute-done | bytes 262176 | tf_op jit(solution)/shard_map/ppermute | solution.py:352
  14.6 2.0 %collective-permute-start.5 = (f32[4,128,128]{2,1,0:T(8,128)S(1)}, f32[4,128,128]{2,1,0:T(8,128)S(1)}, u32[]{:S(2)}, u32[]{:S(2)}) collective-permute-start(f32[4,128,128]{2,1,0:T(8,128)S(1)} %get-tuple-element.205), channel_id=1, source_target_pairs={{0,1},{1,0},{2,3},{3,2},{4,5},{5,4},{6,7},{7,6},{8,9},{9,8},{10,11... | collective-permute-start | bytes 786440 | tf_op jit(solution)/shard_map/ppermute | solution.py:352
  17.3 0.7 collective-permute-done.4.refs_1_.refs_0_
  18.1 2.0 %collective-permute-done.3.refs_1_.refs_0_ = f32[4,128,128]{2,1,0:T(8,128)S(1)} collective-permute-done((f32[4,128,128]{2,1,0:T(8,128)S(1)}, f32[4,128,128]{2,1,0:T(8,128)S(1)}, u32[]{:S(2)}, u32[]{:S(2)}) %collective-permute-start.3) | collective-permute-done | bytes 262176 | tf_op jit(solution)/shard_map/ppermute | solution.py:352
  20.3 2.0 %collective-permute-start.7 = (f32[4,128,128]{2,1,0:T(8,128)S(1)}, f32[4,128,128]{2,1,0:T(8,128)S(1)}, u32[]{:S(2)}, u32[]{:S(2)}) collective-permute-start(f32[4,128,128]{2,1,0:T(8,128)S(1)} %get-tuple-element.229), channel_id=1, source_target_pairs={{0,1},{1,0},{2,3},{3,2},{4,5},{5,4},{6,7},{7,6},{8,9},{9,8},{10,11... | collective-permute-start | bytes 786440 | tf_op jit(solution)/shard_map/ppermute | solution.py:352
  22.2 1.6 %collective-permute-done.2.refs_1_ = f32[4,128,128]{2,1,0:T(8,128)S(1)} collective-permute-done((f32[4,128,128]{2,1,0:T(8,128)S(1)}, f32[4,128,128]{2,1,0:T(8,128)S(1)}, u32[]{:S(2)}, u32[]{:S(2)}) %collective-permute-start.2) | collective-permute-done | bytes 262176 | tf_op jit(solution)/shard_map/ppermute | solution.py:352
  23.9 0.6 numer_0.1
  24.5 1.3 %collective-permute-done.5.refs_1_ = f32[4,128,128]{2,1,0:T(8,128)S(1)} collective-permute-done((f32[4,128,128]{2,1,0:T(8,128)S(1)}, f32[4,128,128]{2,1,0:T(8,128)S(1)}, u32[]{:S(2)}, u32[]{:S(2)}) %collective-permute-start.5) | collective-permute-done | bytes 262176 | tf_op jit(solution)/shard_map/ppermute | solution.py:352
  25.7 0.6 numer_1.1
  26.4 0.7 collective-permute-start.9
  27.0 1.5 %collective-permute-start.10 = (f32[4,128,128]{2,1,0:T(8,128)S(1)}, f32[4,128,128]{2,1,0:T(8,128)S(1)}, u32[]{:S(2)}, u32[]{:S(2)}) collective-permute-start(f32[4,128,128]{2,1,0:T(8,128)S(1)} %get-tuple-element.248.refs_0_), channel_id=1, source_target_pairs={{0,1},{1,0},{2,3},{3,2},{4,5},{5,4},{6,7},{7,6},{8,9},{9,8},{10,11... | collective-permute-start | bytes 786440 | tf_op jit(solution)/shard_map/ppermute | solution.py:352
  28.6 0.8 %query_grad_0.1 = (bf16[4,128,128]{2,1,0:T(8,128)(2,1)S(1)}, bf16[4,128,128]{2,1,0:T(8,128)(2,1)S(1)}, f32[4,136,128]{2,1,0:T(8,128)S(1)}, f32[8,128]{1,0:T(8,128)S(1)}) custom-call(bf16[4,128,128]{2,1,0:T(8,128)(2,1)S(1)} %get-tuple-element.200.refs_0_.refs_1_, bf16[4,128,128]{2,1,0:T(8,128)(2,1)S(1)} %get-tuple-element.201.refs_1_, ...), custom_call_target="tpu_custom_call" | custom-call | flops 200000000 | tf_op jit(solution)/shard_map/query_grad_0/pallas_call | solution.py:315
  29.4 0.8 %query_grad_1.1 = (bf16[4,128,128]{2,1,0:T(8,128)(2,1)S(1)}, bf16[4,128,128]{2,1,0:T(8,128)(2,1)S(1)}, f32[4,136,128]{2,1,0:T(8,128)S(1)}, f32[8,128]{1,0:T(8,128)S(1)}) custom-call(bf16[4,128,128]{2,1,0:T(8,128)(2,1)S(1)} %get-tuple-element.211.refs_0_.refs_1_, bf16[4,128,128]{2,1,0:T(8,128)(2,1)S(1)} %get-tuple-element.212.refs_1_, ...), custom_call_target="tpu_custom_call" | custom-call | flops 200000000 | tf_op jit(solution)/shard_map/query_grad_1/pallas_call | solution.py:315
  30.3 0.6 numer_2.1
  31.4 0.6 numer_3.1
  32.1 1.0 %collective-permute-start.12 = (f32[4,128,128]{2,1,0:T(8,128)S(1)}, f32[4,128,128]{2,1,0:T(8,128)S(1)}, u32[]{:S(2)}, u32[]{:S(2)}) collective-permute-start(f32[4,128,128]{2,1,0:T(8,128)S(1)} %get-tuple-element.255.refs_0_), channel_id=1, source_target_pairs={{0,2},{1,3},{2,0},{3,1},{4,6},{5,7},{6,4},{7,5},{8,10},{9,11},{10,... | collective-permute-start | bytes 786440 | tf_op jit(solution)/shard_map/ppermute | solution.py:352
  33.1 1.1 %collective-permute-start.13 = (f32[4,128,128]{2,1,0:T(8,128)S(1)}, f32[4,128,128]{2,1,0:T(8,128)S(1)}, u32[]{:S(2)}, u32[]{:S(2)}) collective-permute-start(f32[4,128,128]{2,1,0:T(8,128)S(1)} %get-tuple-element.256.refs_0_), channel_id=1, source_target_pairs={{0,1},{1,0},{2,3},{3,2},{4,5},{5,4},{6,7},{7,6},{8,9},{9,8},{10,11... | collective-permute-start | bytes 786440 | tf_op jit(solution)/shard_map/ppermute | solution.py:352
  34.3 0.8 %query_grad_2.1 = (bf16[4,128,128]{2,1,0:T(8,128)(2,1)S(1)}, bf16[4,128,128]{2,1,0:T(8,128)(2,1)S(1)}, f32[4,136,128]{2,1,0:T(8,128)S(1)}, f32[8,128]{1,0:T(8,128)S(1)}) custom-call(bf16[4,128,128]{2,1,0:T(8,128)(2,1)S(1)} %get-tuple-element.222.refs_0_.refs_1_, bf16[4,128,128]{2,1,0:T(8,128)(2,1)S(1)} %get-tuple-element.223.refs_1_, ...), custom_call_target="tpu_custom_call" | custom-call | flops 200000000 | tf_op jit(solution)/shard_map/query_grad_2/pallas_call | solution.py:315
  35.1 0.8 %query_grad_3.1 = (bf16[4,128,128]{2,1,0:T(8,128)(2,1)S(1)}, bf16[4,128,128]{2,1,0:T(8,128)(2,1)S(1)}, f32[4,136,128]{2,1,0:T(8,128)S(1)}, f32[8,128]{1,0:T(8,128)S(1)}) custom-call(bf16[4,128,128]{2,1,0:T(8,128)(2,1)S(1)} %get-tuple-element.236.refs_0_.refs_1_, bf16[4,128,128]{2,1,0:T(8,128)(2,1)S(1)} %get-tuple-element.237.refs_1_, ...), custom_call_target="tpu_custom_call" | custom-call | flops 200000000 | tf_op jit(solution)/shard_map/query_grad_3/pallas_call | solution.py:315
  36.3 1.5 %collective-permute-start.15 = (f32[4,128,128]{2,1,0:T(8,128)S(1)}, f32[4,128,128]{2,1,0:T(8,128)S(1)}, u32[]{:S(2)}, u32[]{:S(2)}) collective-permute-start(f32[4,128,128]{2,1,0:T(8,128)S(1)} %get-tuple-element.262), channel_id=1, source_target_pairs={{0,2},{1,3},{2,0},{3,1},{4,6},{5,7},{6,4},{7,5},{8,10},{9,11},{10,... | collective-permute-start | bytes 786440 | tf_op jit(solution)/shard_map/ppermute | solution.py:352
  38.3 4.0 %collective-permute-done.13.refs_1_.refs_0_ = f32[4,128,128]{2,1,0:T(8,128)S(1)} collective-permute-done((f32[4,128,128]{2,1,0:T(8,128)S(1)}, f32[4,128,128]{2,1,0:T(8,128)S(1)}, u32[]{:S(2)}, u32[]{:S(2)}) %collective-permute-start.13) | collective-permute-done | bytes 262176 | tf_op jit(solution)/shard_map/ppermute | solution.py:352
  42.3 1.1 %collective-permute-start.19 = (f32[4,128,128]{2,1,0:T(8,128)S(1)}, f32[4,128,128]{2,1,0:T(8,128)S(1)}, u32[]{:S(2)}, u32[]{:S(2)}) collective-permute-start(f32[4,128,128]{2,1,0:T(8,128)S(1)} %get-tuple-element.280), channel_id=1, source_target_pairs={{0,2},{1,3},{2,0},{3,1},{4,6},{5,7},{6,4},{7,5},{8,10},{9,11},{10,... | collective-permute-start | bytes 786440 | tf_op jit(solution)/shard_map/ppermute | solution.py:352
  43.5 1.6 %collective-permute-start.20 = (f32[4,128,128]{2,1,0:T(8,128)S(1)}, f32[4,128,128]{2,1,0:T(8,128)S(1)}, u32[]{:S(2)}, u32[]{:S(2)}) collective-permute-start(f32[4,128,128]{2,1,0:T(8,128)S(1)} %get-tuple-element.297), channel_id=1, source_target_pairs={{0,1},{1,0},{2,3},{3,2},{4,5},{5,4},{6,7},{7,6},{8,9},{9,8},{10,11... | collective-permute-start | bytes 786440 | tf_op jit(solution)/shard_map/ppermute | solution.py:352
  45.2 2.7 %collective-permute-start.14 = (f32[2,2,136,128]{3,2,1,0:T(8,128)S(1)}, f32[2,2,136,128]{3,2,1,0:T(8,128)S(1)}, u32[]{:S(2)}, u32[]{:S(2)}) collective-permute-start(f32[2,2,136,128]{3,2,1,0:T(8,128)S(1)} %get-tuple-element.261), channel_id=1, source_target_pairs={{0,16},{4,20},{8,24},{12,28},{16,0},{20,4},{24,8},{28,12},{1,17},{... | collective-permute-start | bytes 835592 | tf_op jit(solution)/shard_map/ppermute | solution.py:352
  51.1 0.9 %collective-permute-done.19.refs_1_ = f32[4,128,128]{2,1,0:T(8,128)S(1)} collective-permute-done((f32[4,128,128]{2,1,0:T(8,128)S(1)}, f32[4,128,128]{2,1,0:T(8,128)S(1)}, u32[]{:S(2)}, u32[]{:S(2)}) %collective-permute-start.19) | collective-permute-done | bytes 262176 | tf_op jit(solution)/shard_map/ppermute | solution.py:352
  55.0 1.6 %collective-permute-start.27 = (f32[2,128,128]{2,1,0:T(8,128)S(1)}, f32[2,128,128]{2,1,0:T(8,128)S(1)}, u32[]{:S(2)}, u32[]{:S(2)}) collective-permute-start(f32[2,128,128]{2,1,0:T(8,128)S(1)} %get-tuple-element.336), channel_id=1, source_target_pairs={{0,8},{4,12},{8,0},{12,4},{16,24},{20,28},{24,16},{28,20},{1,9},{5... | collective-permute-start | bytes 393224 | tf_op jit(solution)/shard_map/ppermute | solution.py:352
  56.6 2.6 %collective-permute-start.28 = (f32[2,128,128]{2,1,0:T(8,128)S(1)}, f32[2,128,128]{2,1,0:T(8,128)S(1)}, u32[]{:S(2)}, u32[]{:S(2)}) collective-permute-start(f32[2,128,128]{2,1,0:T(8,128)S(1)} %get-tuple-element.337), channel_id=1, source_target_pairs={{0,16},{4,20},{8,24},{12,28},{16,0},{20,4},{24,8},{28,12},{1,17},{... | collective-permute-start | bytes 393224 | tf_op jit(solution)/shard_map/ppermute | solution.py:352
  59.5 0.7 collective-permute-start.24
  60.2 1.4 %collective-permute-start.23 = (f32[136,128]{1,0:T(8,128)S(1)}, f32[136,128]{1,0:T(8,128)S(1)}, u32[]{:S(2)}, u32[]{:S(2)}) collective-permute-start(f32[136,128]{1,0:T(8,128)S(1)} %get-tuple-element.329), channel_id=1, source_target_pairs={{0,8},{4,12},{8,0},{12,4},{16,24},{20,28},{24,16},{28,20},{1,9},{5... | collective-permute-start | bytes 208904 | tf_op jit(solution)/shard_map/ppermute | solution.py:352
  61.6 0.9 %lay_0.1 = (bf16[128,2048]{1,0:T(8,128)(2,1)}, f32[8,128]{1,0:T(8,128)S(1)}) custom-call(bf16[4,128,128]{2,1,0:T(8,128)(2,1)S(1)} %get-tuple-element.210.refs_0_, bf16[4,128,128]{2,1,0:T(8,128)(2,1)S(1)} %get-tuple-element.217.refs_1_, bf16[4,128,128]{2,1,0:T(8,128)(2,1)S(1)} %get-tuple-element.235.refs_2_, ...), custom_call_target="tpu_custom_call" | custom-call | flops 200000000 | tf_op jit(solution)/shard_map/lay_0/pallas_call | solution.py:315
  62.5 0.9 %lay_1.1 = (bf16[128,2048]{1,0:T(8,128)(2,1)}, f32[8,128]{1,0:T(8,128)S(1)}) custom-call(bf16[4,128,128]{2,1,0:T(8,128)(2,1)S(1)} %get-tuple-element.318.refs_0_, bf16[4,128,128]{2,1,0:T(8,128)(2,1)S(1)} %get-tuple-element.319.refs_1_, bf16[4,128,128]{2,1,0:T(8,128)(2,1)S(1)} %get-tuple-element.320.refs_2_, ...), custom_call_target="tpu_custom_call" | custom-call | flops 200000000 | tf_op jit(solution)/shard_map/lay_1/pallas_call | solution.py:315
  63.5 4.0 %collective-permute-done.24.refs_1_ = f32[136,128]{1,0:T(8,128)S(1)} collective-permute-done((f32[136,128]{1,0:T(8,128)S(1)}, f32[136,128]{1,0:T(8,128)S(1)}, u32[]{:S(2)}, u32[]{:S(2)}) %collective-permute-start.24) | collective-permute-done | bytes 69664 | tf_op jit(solution)/shard_map/ppermute | solution.py:352
  67.5 1.4 %collective-permute-start.26 = (f32[136,128]{1,0:T(8,128)S(1)}, f32[136,128]{1,0:T(8,128)S(1)}, u32[]{:S(2)}, u32[]{:S(2)}) collective-permute-start(f32[136,128]{1,0:T(8,128)S(1)} %get-tuple-element.334.refs_0_), channel_id=1, source_target_pairs={{0,1},{1,0},{2,3},{3,2},{4,5},{5,4},{6,7},{7,6},{8,9},{9,8},{10,11... | collective-permute-start | bytes 208904 | tf_op jit(solution)/shard_map/ppermute | solution.py:352
  68.9 1.2 %collective-permute-done.23.refs_1_ = f32[136,128]{1,0:T(8,128)S(1)} collective-permute-done((f32[136,128]{1,0:T(8,128)S(1)}, f32[136,128]{1,0:T(8,128)S(1)}, u32[]{:S(2)}, u32[]{:S(2)}) %collective-permute-start.23) | collective-permute-done | bytes 69664 | tf_op jit(solution)/shard_map/ppermute | solution.py:352
  70.1 0.7 collective-permute-start.25
  70.8 1.1 %collective-permute-start.32 = (f32[2,128,128]{2,1,0:T(8,128)S(1)}, f32[2,128,128]{2,1,0:T(8,128)S(1)}, u32[]{:S(2)}, u32[]{:S(2)}) collective-permute-start(f32[2,128,128]{2,1,0:T(8,128)S(1)} %get-tuple-element.346.refs_0_), channel_id=1, source_target_pairs={{0,1},{1,0},{2,3},{3,2},{4,5},{5,4},{6,7},{7,6},{8,9},{9,8},{10,11... | collective-permute-start | bytes 393224 | tf_op jit(solution)/shard_map/ppermute | solution.py:352
  71.9 0.8 collective-permute-start.33
  72.7 1.7 %collective-permute-start.34 = (f32[2,128,128]{2,1,0:T(8,128)S(1)}, f32[2,128,128]{2,1,0:T(8,128)S(1)}, u32[]{:S(2)}, u32[]{:S(2)}) collective-permute-start(f32[2,128,128]{2,1,0:T(8,128)S(1)} %get-tuple-element.346.refs_0_), channel_id=1, source_target_pairs={{0,3},{1,2},{2,1},{3,0},{4,7},{5,6},{6,5},{7,4},{8,11},{9,10},{10,... | collective-permute-start | bytes 393224 | tf_op jit(solution)/shard_map/ppermute | solution.py:352
  74.4 1.5 %collective-permute-start.30 = (f32[136,128]{1,0:T(8,128)S(1)}, f32[136,128]{1,0:T(8,128)S(1)}, u32[]{:S(2)}, u32[]{:S(2)}) collective-permute-start(f32[136,128]{1,0:T(8,128)S(1)} %get-tuple-element.344.refs_0_), channel_id=1, source_target_pairs={{0,2},{1,3},{2,0},{3,1},{4,6},{5,7},{6,4},{7,5},{8,10},{9,11},{10,... | collective-permute-start | bytes 208904 | tf_op jit(solution)/shard_map/ppermute | solution.py:352
  76.3 0.9 %lay_2.1 = (bf16[128,2048]{1,0:T(8,128)(2,1)}, f32[8,128]{1,0:T(8,128)S(1)}) custom-call(bf16[4,128,128]{2,1,0:T(8,128)(2,1)S(1)} %get-tuple-element.324.refs_0_, bf16[4,128,128]{2,1,0:T(8,128)(2,1)S(1)} %get-tuple-element.325.refs_1_, bf16[4,128,128]{2,1,0:T(8,128)(2,1)S(1)} %get-tuple-element.326.refs_2_, ...), custom_call_target="tpu_custom_call" | custom-call | flops 200000000 | tf_op jit(solution)/shard_map/lay_2/pallas_call | solution.py:315
  77.3 3.4 %collective-permute-done.33.refs_2_ = f32[2,128,128]{2,1,0:T(8,128)S(1)} collective-permute-done((f32[2,128,128]{2,1,0:T(8,128)S(1)}, f32[2,128,128]{2,1,0:T(8,128)S(1)}, u32[]{:S(2)}, u32[]{:S(2)}) %collective-permute-start.33) | collective-permute-done | bytes 131104 | tf_op jit(solution)/shard_map/ppermute | solution.py:352
  80.7 0.7 key_total.1
  81.4 0.7 query_total.1
  (89 shorter events, 11.0 us)
Async XLA Ops:
  2.2 4.5 %copy-start.7 = (f32[8,128]{1,0:T(8,128)}, f32[8,128]{1,0:T(8,128)S(1)}, u32[]{:S(2)}) copy-start(f32[8,128]{1,0:T(8,128)S(1)} %get-tuple-element.183.refs_3_) | copy-start | bytes 12292
  2.2 10.2 %collective-permute-start.1 = (f32[4,128,128]{2,1,0:T(8,128)S(1)}, f32[4,128,128]{2,1,0:T(8,128)S(1)}, u32[]{:S(2)}, u32[]{:S(2)}) collective-permute-start(f32[4,128,128]{2,1,0:T(8,128)S(1)} %get-tuple-element.180.refs_0_), channel_id=1, source_target_pairs={{0,2},{1,3},{2,0},{3,1},{4,6},{5,7},{6,4},{7,5},{8,10},{9,11},{10,... | collective-permute-start | bytes 786440 | tf_op jit(solution)/shard_map/ppermute | solution.py:352
  5.3 9.2 %collective-permute-start = (f32[4,128,128]{2,1,0:T(8,128)S(1)}, f32[4,128,128]{2,1,0:T(8,128)S(1)}, u32[]{:S(2)}, u32[]{:S(2)}) collective-permute-start(f32[4,128,128]{2,1,0:T(8,128)S(1)} %get-tuple-element.179.refs_0_), channel_id=1, source_target_pairs={{0,1},{1,0},{2,3},{3,2},{4,5},{5,4},{6,7},{7,6},{8,9},{9,8},{10,11... | collective-permute-start | bytes 786440 | tf_op jit(solution)/shard_map/ppermute | solution.py:352
  6.8 2.4 %copy-start.3 = (bf16[1,128,2048]{2,1,0:T(8,128)(2,1)S(1)}, bf16[1,128,2048]{2,1,0:T(8,128)(2,1)}, u32[]{:S(2)}) copy-start(bf16[1,128,2048]{2,1,0:T(8,128)(2,1)} %param.7) | copy-start | bytes 1572868
  6.8 2.4 %copy-start.4 = (bf16[2048,128]{1,0:T(8,128)(2,1)S(1)}, bf16[2048,128]{1,0:T(8,128)(2,1)}, u32[]{:S(2)}) copy-start(bf16[2048,128]{1,0:T(8,128)(2,1)} %refs_7_.7) | copy-start | bytes 1572868
  8.5 9.6 %collective-permute-start.4 = (f32[4,128,128]{2,1,0:T(8,128)S(1)}, f32[4,128,128]{2,1,0:T(8,128)S(1)}, u32[]{:S(2)}, u32[]{:S(2)}) collective-permute-start(f32[4,128,128]{2,1,0:T(8,128)S(1)} %get-tuple-element.192.refs_0_), channel_id=1, source_target_pairs={{0,2},{1,3},{2,0},{3,1},{4,6},{5,7},{6,4},{7,5},{8,10},{9,11},{10,... | collective-permute-start | bytes 786440 | tf_op jit(solution)/shard_map/ppermute | solution.py:352
  9.0 11.1 %collective-permute-start.3 = (f32[4,128,128]{2,1,0:T(8,128)S(1)}, f32[4,128,128]{2,1,0:T(8,128)S(1)}, u32[]{:S(2)}, u32[]{:S(2)}) collective-permute-start(f32[4,128,128]{2,1,0:T(8,128)S(1)} %get-tuple-element.191.refs_0_), channel_id=1, source_target_pairs={{0,1},{1,0},{2,3},{3,2},{4,5},{5,4},{6,7},{7,6},{8,9},{9,8},{10,11... | collective-permute-start | bytes 786440 | tf_op jit(solution)/shard_map/ppermute | solution.py:352
  14.5 9.3 %collective-permute-start.2 = (f32[4,128,128]{2,1,0:T(8,128)S(1)}, f32[4,128,128]{2,1,0:T(8,128)S(1)}, u32[]{:S(2)}, u32[]{:S(2)}) collective-permute-start(f32[4,128,128]{2,1,0:T(8,128)S(1)} %get-tuple-element.188), channel_id=1, source_target_pairs={{0,2},{1,3},{2,0},{3,1},{4,6},{5,7},{6,4},{7,5},{8,10},{9,11},{10,... | collective-permute-start | bytes 786440 | tf_op jit(solution)/shard_map/ppermute | solution.py:352
  14.6 11.1 %collective-permute-start.5 = (f32[4,128,128]{2,1,0:T(8,128)S(1)}, f32[4,128,128]{2,1,0:T(8,128)S(1)}, u32[]{:S(2)}, u32[]{:S(2)}) collective-permute-start(f32[4,128,128]{2,1,0:T(8,128)S(1)} %get-tuple-element.205), channel_id=1, source_target_pairs={{0,1},{1,0},{2,3},{3,2},{4,5},{5,4},{6,7},{7,6},{8,9},{9,8},{10,11... | collective-permute-start | bytes 786440 | tf_op jit(solution)/shard_map/ppermute | solution.py:352
  18.0 5.8 %copy-start.5 = (bf16[1,128,2048]{2,1,0:T(8,128)(2,1)S(1)}, bf16[1,128,2048]{2,1,0:T(8,128)(2,1)}, u32[]{:S(2)}) copy-start(bf16[1,128,2048]{2,1,0:T(8,128)(2,1)} %param.10) | copy-start | bytes 1572868
  18.1 5.8 %copy-start = (bf16[1,128,2048]{2,1,0:T(8,128)(2,1)S(1)}, bf16[1,128,2048]{2,1,0:T(8,128)(2,1)}, u32[]{:S(2)}) copy-start(bf16[1,128,2048]{2,1,0:T(8,128)(2,1)} %param.9) | copy-start | bytes 1572868
  20.2 3.7 %copy-start.6 = (f32[2048]{0:T(1024)S(1)}, f32[2048]{0:T(1024)}, u32[]{:S(2)}) copy-start(f32[2048]{0:T(1024)} %param.13) | copy-start | bytes 24580
  20.2 10.1 %collective-permute-start.6 = (f32[4,128,128]{2,1,0:T(8,128)S(1)}, f32[4,128,128]{2,1,0:T(8,128)S(1)}, u32[]{:S(2)}, u32[]{:S(2)}) collective-permute-start(f32[4,128,128]{2,1,0:T(8,128)S(1)} %get-tuple-element.218), channel_id=1, source_target_pairs={{0,2},{1,3},{2,0},{3,1},{4,6},{5,7},{6,4},{7,5},{8,10},{9,11},{10,... | collective-permute-start | bytes 786440 | tf_op jit(solution)/shard_map/ppermute | solution.py:352
  20.3 11.1 %collective-permute-start.7 = (f32[4,128,128]{2,1,0:T(8,128)S(1)}, f32[4,128,128]{2,1,0:T(8,128)S(1)}, u32[]{:S(2)}, u32[]{:S(2)}) collective-permute-start(f32[4,128,128]{2,1,0:T(8,128)S(1)} %get-tuple-element.229), channel_id=1, source_target_pairs={{0,1},{1,0},{2,3},{3,2},{4,5},{5,4},{6,7},{7,6},{8,9},{9,8},{10,11... | collective-permute-start | bytes 786440 | tf_op jit(solution)/shard_map/ppermute | solution.py:352
  26.4 9.7 %collective-permute-start.9 = (f32[4,128,128]{2,1,0:T(8,128)S(1)}, f32[4,128,128]{2,1,0:T(8,128)S(1)}, u32[]{:S(2)}, u32[]{:S(2)}) collective-permute-start(f32[4,128,128]{2,1,0:T(8,128)S(1)} %get-tuple-element.247.refs_0_), channel_id=1, source_target_pairs={{0,2},{1,3},{2,0},{3,1},{4,6},{5,7},{6,4},{7,5},{8,10},{9,11},{10,... | collective-permute-start | bytes 786440 | tf_op jit(solution)/shard_map/ppermute | solution.py:352
  27.0 8.9 %collective-permute-start.10 = (f32[4,128,128]{2,1,0:T(8,128)S(1)}, f32[4,128,128]{2,1,0:T(8,128)S(1)}, u32[]{:S(2)}, u32[]{:S(2)}) collective-permute-start(f32[4,128,128]{2,1,0:T(8,128)S(1)} %get-tuple-element.248.refs_0_), channel_id=1, source_target_pairs={{0,1},{1,0},{2,3},{3,2},{4,5},{5,4},{6,7},{7,6},{8,9},{9,8},{10,11... | collective-permute-start | bytes 786440 | tf_op jit(solution)/shard_map/ppermute | solution.py:352
  32.0 4.1 %collective-permute-start.8 = (f32[2,2,136,128]{3,2,1,0:T(8,128)S(1)}, f32[2,2,136,128]{3,2,1,0:T(8,128)S(1)}, u32[]{:S(2)}, u32[]{:S(2)}) collective-permute-start(f32[2,2,136,128]{3,2,1,0:T(8,128)S(1)} %get-tuple-element.246), channel_id=1, source_target_pairs={{0,4},{4,0},{8,12},{12,8},{16,20},{20,16},{24,28},{28,24},{1,5},{5... | collective-permute-start | bytes 835592 | tf_op jit(solution)/shard_map/ppermute | solution.py:352
  32.1 11.3 %collective-permute-start.12 = (f32[4,128,128]{2,1,0:T(8,128)S(1)}, f32[4,128,128]{2,1,0:T(8,128)S(1)}, u32[]{:S(2)}, u32[]{:S(2)}) collective-permute-start(f32[4,128,128]{2,1,0:T(8,128)S(1)} %get-tuple-element.255.refs_0_), channel_id=1, source_target_pairs={{0,2},{1,3},{2,0},{3,1},{4,6},{5,7},{6,4},{7,5},{8,10},{9,11},{10,... | collective-permute-start | bytes 786440 | tf_op jit(solution)/shard_map/ppermute | solution.py:352
  33.1 9.2 %collective-permute-start.13 = (f32[4,128,128]{2,1,0:T(8,128)S(1)}, f32[4,128,128]{2,1,0:T(8,128)S(1)}, u32[]{:S(2)}, u32[]{:S(2)}) collective-permute-start(f32[4,128,128]{2,1,0:T(8,128)S(1)} %get-tuple-element.256.refs_0_), channel_id=1, source_target_pairs={{0,1},{1,0},{2,3},{3,2},{4,5},{5,4},{6,7},{7,6},{8,9},{9,8},{10,11... | collective-permute-start | bytes 786440 | tf_op jit(solution)/shard_map/ppermute | solution.py:352
  36.2 8.9 %collective-permute-start.11 = (f32[2,2,136,128]{3,2,1,0:T(8,128)S(1)}, f32[2,2,136,128]{3,2,1,0:T(8,128)S(1)}, u32[]{:S(2)}, u32[]{:S(2)}) collective-permute-start(f32[2,2,136,128]{3,2,1,0:T(8,128)S(1)} %get-tuple-element.254), channel_id=1, source_target_pairs={{0,4},{4,0},{8,12},{12,8},{16,20},{20,16},{24,28},{28,24},{1,5},{5... | collective-permute-start | bytes 835592 | tf_op jit(solution)/shard_map/ppermute | solution.py:352
  36.3 12.0 %collective-permute-start.15 = (f32[4,128,128]{2,1,0:T(8,128)S(1)}, f32[4,128,128]{2,1,0:T(8,128)S(1)}, u32[]{:S(2)}, u32[]{:S(2)}) collective-permute-start(f32[4,128,128]{2,1,0:T(8,128)S(1)} %get-tuple-element.262), channel_id=1, source_target_pairs={{0,2},{1,3},{2,0},{3,1},{4,6},{5,7},{6,4},{7,5},{8,10},{9,11},{10,... | collective-permute-start | bytes 786440 | tf_op jit(solution)/shard_map/ppermute | solution.py:352
  37.8 11.0 %collective-permute-start.16 = (f32[4,128,128]{2,1,0:T(8,128)S(1)}, f32[4,128,128]{2,1,0:T(8,128)S(1)}, u32[]{:S(2)}, u32[]{:S(2)}) collective-permute-start(f32[4,128,128]{2,1,0:T(8,128)S(1)} %get-tuple-element.271), channel_id=1, source_target_pairs={{0,1},{1,0},{2,3},{3,2},{4,5},{5,4},{6,7},{7,6},{8,9},{9,8},{10,11... | collective-permute-start | bytes 786440 | tf_op jit(solution)/shard_map/ppermute | solution.py:352
  42.3 9.8 %collective-permute-start.19 = (f32[4,128,128]{2,1,0:T(8,128)S(1)}, f32[4,128,128]{2,1,0:T(8,128)S(1)}, u32[]{:S(2)}, u32[]{:S(2)}) collective-permute-start(f32[4,128,128]{2,1,0:T(8,128)S(1)} %get-tuple-element.280), channel_id=1, source_target_pairs={{0,2},{1,3},{2,0},{3,1},{4,6},{5,7},{6,4},{7,5},{8,10},{9,11},{10,... | collective-permute-start | bytes 786440 | tf_op jit(solution)/shard_map/ppermute | solution.py:352
  43.5 4.4 %copy-start.2 = (bf16[1,128,2048]{2,1,0:T(8,128)(2,1)S(1)}, bf16[1,128,2048]{2,1,0:T(8,128)(2,1)}, u32[]{:S(2)}) copy-start(bf16[1,128,2048]{2,1,0:T(8,128)(2,1)} %param.8) | copy-start | bytes 1572868
  43.5 4.3 %copy-start.1 = (bf16[2048,128]{1,0:T(8,128)(2,1)S(1)}, bf16[2048,128]{1,0:T(8,128)(2,1)}, u32[]{:S(2)}) copy-start(bf16[2048,128]{1,0:T(8,128)(2,1)} %refs_6_.7) | copy-start | bytes 1572868
  43.5 9.2 %collective-permute-start.20 = (f32[4,128,128]{2,1,0:T(8,128)S(1)}, f32[4,128,128]{2,1,0:T(8,128)S(1)}, u32[]{:S(2)}, u32[]{:S(2)}) collective-permute-start(f32[4,128,128]{2,1,0:T(8,128)S(1)} %get-tuple-element.297), channel_id=1, source_target_pairs={{0,1},{1,0},{2,3},{3,2},{4,5},{5,4},{6,7},{7,6},{8,9},{9,8},{10,11... | collective-permute-start | bytes 786440 | tf_op jit(solution)/shard_map/ppermute | solution.py:352
  45.2 14.3 %collective-permute-start.14 = (f32[2,2,136,128]{3,2,1,0:T(8,128)S(1)}, f32[2,2,136,128]{3,2,1,0:T(8,128)S(1)}, u32[]{:S(2)}, u32[]{:S(2)}) collective-permute-start(f32[2,2,136,128]{3,2,1,0:T(8,128)S(1)} %get-tuple-element.261), channel_id=1, source_target_pairs={{0,16},{4,20},{8,24},{12,28},{16,0},{20,4},{24,8},{28,12},{1,17},{... | collective-permute-start | bytes 835592 | tf_op jit(solution)/shard_map/ppermute | solution.py:352
  49.3 5.2 %collective-permute-start.17 = (f32[2,128,128]{2,1,0:T(8,128)S(1)}, f32[2,128,128]{2,1,0:T(8,128)S(1)}, u32[]{:S(2)}, u32[]{:S(2)}) collective-permute-start(f32[2,128,128]{2,1,0:T(8,128)S(1)} %get-tuple-element.278), channel_id=1, source_target_pairs={{0,4},{4,0},{8,12},{12,8},{16,20},{20,16},{24,28},{28,24},{1,5},{5... | collective-permute-start | bytes 393224 | tf_op jit(solution)/shard_map/ppermute | solution.py:352
  49.4 5.2 %collective-permute-start.18 = (f32[2,128,128]{2,1,0:T(8,128)S(1)}, f32[2,128,128]{2,1,0:T(8,128)S(1)}, u32[]{:S(2)}, u32[]{:S(2)}) collective-permute-start(f32[2,128,128]{2,1,0:T(8,128)S(1)} %get-tuple-element.279), channel_id=1, source_target_pairs={{0,4},{4,0},{8,12},{12,8},{16,20},{20,16},{24,28},{28,24},{1,5},{5... | collective-permute-start | bytes 393224 | tf_op jit(solution)/shard_map/ppermute | solution.py:352
  53.3 1.4 %collective-permute-start.21 = (f32[2,128,128]{2,1,0:T(8,128)S(1)}, f32[2,128,128]{2,1,0:T(8,128)S(1)}, u32[]{:S(2)}, u32[]{:S(2)}) collective-permute-start(f32[2,128,128]{2,1,0:T(8,128)S(1)} %get-tuple-element.304), channel_id=1, source_target_pairs={{0,4},{4,0},{8,12},{12,8},{16,20},{20,16},{24,28},{28,24},{1,5},{5... | collective-permute-start | bytes 393224 | tf_op jit(solution)/shard_map/ppermute | solution.py:352
  53.3 1.5 %collective-permute-start.22 = (f32[2,128,128]{2,1,0:T(8,128)S(1)}, f32[2,128,128]{2,1,0:T(8,128)S(1)}, u32[]{:S(2)}, u32[]{:S(2)}) collective-permute-start(f32[2,128,128]{2,1,0:T(8,128)S(1)} %get-tuple-element.305), channel_id=1, source_target_pairs={{0,4},{4,0},{8,12},{12,8},{16,20},{20,16},{24,28},{28,24},{1,5},{5... | collective-permute-start | bytes 393224 | tf_op jit(solution)/shard_map/ppermute | solution.py:352
  55.0 15.8 %collective-permute-start.27 = (f32[2,128,128]{2,1,0:T(8,128)S(1)}, f32[2,128,128]{2,1,0:T(8,128)S(1)}, u32[]{:S(2)}, u32[]{:S(2)}) collective-permute-start(f32[2,128,128]{2,1,0:T(8,128)S(1)} %get-tuple-element.336), channel_id=1, source_target_pairs={{0,8},{4,12},{8,0},{12,4},{16,24},{20,28},{24,16},{28,20},{1,9},{5... | collective-permute-start | bytes 393224 | tf_op jit(solution)/shard_map/ppermute | solution.py:352
  56.6 14.1 %collective-permute-start.28 = (f32[2,128,128]{2,1,0:T(8,128)S(1)}, f32[2,128,128]{2,1,0:T(8,128)S(1)}, u32[]{:S(2)}, u32[]{:S(2)}) collective-permute-start(f32[2,128,128]{2,1,0:T(8,128)S(1)} %get-tuple-element.337), channel_id=1, source_target_pairs={{0,16},{4,20},{8,24},{12,28},{16,0},{20,4},{24,8},{28,12},{1,17},{... | collective-permute-start | bytes 393224 | tf_op jit(solution)/shard_map/ppermute | solution.py:352
  59.2 11.6 %collective-permute-start.29 = (f32[2,128,128]{2,1,0:T(8,128)S(1)}, f32[2,128,128]{2,1,0:T(8,128)S(1)}, u32[]{:S(2)}, u32[]{:S(2)}) collective-permute-start(f32[2,128,128]{2,1,0:T(8,128)S(1)} %get-tuple-element.338), channel_id=1, source_target_pairs={{0,24},{4,28},{8,16},{12,20},{16,8},{20,12},{24,0},{28,4},{1,25},{... | collective-permute-start | bytes 393224 | tf_op jit(solution)/shard_map/ppermute | solution.py:352
  59.5 8.0 %collective-permute-start.24 = (f32[136,128]{1,0:T(8,128)S(1)}, f32[136,128]{1,0:T(8,128)S(1)}, u32[]{:S(2)}, u32[]{:S(2)}) collective-permute-start(f32[136,128]{1,0:T(8,128)S(1)} %get-tuple-element.330), channel_id=1, source_target_pairs={{0,8},{4,12},{8,0},{12,4},{16,24},{20,28},{24,16},{28,20},{1,9},{5... | collective-permute-start | bytes 208904 | tf_op jit(solution)/shard_map/ppermute | solution.py:352
  60.2 9.8 %collective-permute-start.23 = (f32[136,128]{1,0:T(8,128)S(1)}, f32[136,128]{1,0:T(8,128)S(1)}, u32[]{:S(2)}, u32[]{:S(2)}) collective-permute-start(f32[136,128]{1,0:T(8,128)S(1)} %get-tuple-element.329), channel_id=1, source_target_pairs={{0,8},{4,12},{8,0},{12,4},{16,24},{20,28},{24,16},{28,20},{1,9},{5... | collective-permute-start | bytes 208904 | tf_op jit(solution)/shard_map/ppermute | solution.py:352
  67.5 6.9 %collective-permute-start.26 = (f32[136,128]{1,0:T(8,128)S(1)}, f32[136,128]{1,0:T(8,128)S(1)}, u32[]{:S(2)}, u32[]{:S(2)}) collective-permute-start(f32[136,128]{1,0:T(8,128)S(1)} %get-tuple-element.334.refs_0_), channel_id=1, source_target_pairs={{0,1},{1,0},{2,3},{3,2},{4,5},{5,4},{6,7},{7,6},{8,9},{9,8},{10,11... | collective-permute-start | bytes 208904 | tf_op jit(solution)/shard_map/ppermute | solution.py:352
  70.1 5.8 %collective-permute-start.25 = (f32[136,128]{1,0:T(8,128)S(1)}, f32[136,128]{1,0:T(8,128)S(1)}, u32[]{:S(2)}, u32[]{:S(2)}) collective-permute-start(f32[136,128]{1,0:T(8,128)S(1)} %get-tuple-element.333.refs_0_), channel_id=1, source_target_pairs={{0,2},{1,3},{2,0},{3,1},{4,6},{5,7},{6,4},{7,5},{8,10},{9,11},{10,... | collective-permute-start | bytes 208904 | tf_op jit(solution)/shard_map/ppermute | solution.py:352
  70.8 6.5 %collective-permute-start.32 = (f32[2,128,128]{2,1,0:T(8,128)S(1)}, f32[2,128,128]{2,1,0:T(8,128)S(1)}, u32[]{:S(2)}, u32[]{:S(2)}) collective-permute-start(f32[2,128,128]{2,1,0:T(8,128)S(1)} %get-tuple-element.346.refs_0_), channel_id=1, source_target_pairs={{0,1},{1,0},{2,3},{3,2},{4,5},{5,4},{6,7},{7,6},{8,9},{9,8},{10,11... | collective-permute-start | bytes 393224 | tf_op jit(solution)/shard_map/ppermute | solution.py:352
  71.9 8.7 %collective-permute-start.33 = (f32[2,128,128]{2,1,0:T(8,128)S(1)}, f32[2,128,128]{2,1,0:T(8,128)S(1)}, u32[]{:S(2)}, u32[]{:S(2)}) collective-permute-start(f32[2,128,128]{2,1,0:T(8,128)S(1)} %get-tuple-element.346.refs_0_), channel_id=1, source_target_pairs={{0,2},{1,3},{2,0},{3,1},{4,6},{5,7},{6,4},{7,5},{8,10},{9,11},{10,... | collective-permute-start | bytes 393224 | tf_op jit(solution)/shard_map/ppermute | solution.py:352
  72.7 8.0 %collective-permute-start.34 = (f32[2,128,128]{2,1,0:T(8,128)S(1)}, f32[2,128,128]{2,1,0:T(8,128)S(1)}, u32[]{:S(2)}, u32[]{:S(2)}) collective-permute-start(f32[2,128,128]{2,1,0:T(8,128)S(1)} %get-tuple-element.346.refs_0_), channel_id=1, source_target_pairs={{0,3},{1,2},{2,1},{3,0},{4,7},{5,6},{6,5},{7,4},{8,11},{9,10},{10,... | collective-permute-start | bytes 393224 | tf_op jit(solution)/shard_map/ppermute | solution.py:352
  74.4 7.0 %collective-permute-start.30 = (f32[136,128]{1,0:T(8,128)S(1)}, f32[136,128]{1,0:T(8,128)S(1)}, u32[]{:S(2)}, u32[]{:S(2)}) collective-permute-start(f32[136,128]{1,0:T(8,128)S(1)} %get-tuple-element.344.refs_0_), channel_id=1, source_target_pairs={{0,2},{1,3},{2,0},{3,1},{4,6},{5,7},{6,4},{7,5},{8,10},{9,11},{10,... | collective-permute-start | bytes 208904 | tf_op jit(solution)/shard_map/ppermute | solution.py:352
  75.9 5.5 %collective-permute-start.31 = (f32[136,128]{1,0:T(8,128)S(1)}, f32[136,128]{1,0:T(8,128)S(1)}, u32[]{:S(2)}, u32[]{:S(2)}) collective-permute-start(f32[136,128]{1,0:T(8,128)S(1)} %get-tuple-element.345.refs_2_), channel_id=1, source_target_pairs={{0,1},{1,0},{2,3},{3,2},{4,5},{5,4},{6,7},{7,6},{8,9},{9,8},{10,11... | collective-permute-start | bytes 208904 | tf_op jit(solution)/shard_map/ppermute | solution.py:352

commit v7 on v6

--- a/solution.py
+++ b/solution.py
@@ -554,7 +554,7 @@
     if tuned:
         steps = (
             "K0K2Q0Q1p1p0Q2Q3p3p2N0N1G0G1N2N3a2G2G3",
-            "l0l1a3l2l3B2P0P1H0H1a0V0V1P2P3H2H3a1V2V3Z0c2L0L1E0E1C0F0F1L2T0U0",
+            "l0l1a3P0P1P2P3l2l3B2H0H1a0V0V1H2H3a1V2V3Z0c2L0L1E0E1C0F0F1L2T0U0",
         )
         steps = "".join(steps)
     else:

time: 82.2 us -> 83.3 us (1.013)
  waiting for transfers between devices: 24.8 us -> 27.8 us
  starting transfers between devices: 36.4 us -> 34.5 us
    ppermute x35, waiting for transfers between devices: 24.8 us -> 27.8 us  [swap(): lax.ppermute(value, axis, [(i, i ^ bit) for i in range(lax.axis_size(axis...]
    ppermute x35, starting transfers between devices: 36.4 us -> 34.5 us  [swap(): lax.ppermute(value, axis, [(i, i ^ bit) for i in range(lax.axis_size(axis...]
  transfers between devices with their start and end apart: 35 -> 35, of which waited for: 16 -> 18; matrix products, arithmetic and copies ran while one was open for 0% -> 0% of each run, Pallas kernels for 21% -> 21%
where the time goes in v7:
time: 83.3 us; the launch traced here: 83.1 us
  starting transfers between devices  34.5 us (41%)
  waiting for transfers between devices  27.8 us (33%)
  Pallas kernels  19.7 us (24%)
  between operations  1.05 us (1%)
    ppermute x35, starting transfers between devices, swap(): lax.ppermute(value, axis, [(i, i ^ bit) for i in range(lax.axis_size(axis...  34.5 us
    ppermute x35, waiting for transfers between devices, swap(): lax.ppermute(value, axis, [(i, i ^ bit) for i in range(lax.axis_size(axis...  27.8 us
    pallas_call x51, Pallas kernels, __call__(): pl.pallas_call(ordered, grid=(1,), in_specs=[spec for _, spec in ins], ou...  19.7 us
  transfers between devices with their start and end apart: 35, of which 18 were waited for; matrix products, arithmetic and copies ran while one was open for 0% of the time, Pallas kernels for 21%

profile of v7, /device:TPU:0, one launch (start us, length us, event | category | flops | bytes accessed | tf_op | source)
XLA Modules:
  0.0 83.1 jit_solution(10742556920190537876)
XLA Ops:
  0.6 1.6 %key_state_0.1 = (bf16[4,128,128]{2,1,0:T(8,128)(2,1)S(1)}, f32[4,128,128]{2,1,0:T(8,128)S(1)}, bf16[4,128,128]{2,1,0:T(8,128)(2,1)S(1)}, f32[4,128,128]{2,1,0:T(8,128)S(1)}, f32[8,128]{1,0:T(8,128)S(1)}) custom-call(bf16[128,2048]{1,0:T(8,128)(2,1)} %bitcast.23, bf16[128,2048]{1,0:T(8,128)(2,1)} %bitcast.9, bf16[2048,128]{1,0:T(8,128)(2,1)} %refs_6_.7), custom_call_target="tpu_custom_call" | custom-call | flops 200000000 | tf_op jit(solution)/shard_map/key_state_0/pallas_call | solution.py:315
  2.2 3.0 %collective-permute-start.1 = (f32[4,128,128]{2,1,0:T(8,128)S(1)}, f32[4,128,128]{2,1,0:T(8,128)S(1)}, u32[]{:S(2)}, u32[]{:S(2)}) collective-permute-start(f32[4,128,128]{2,1,0:T(8,128)S(1)} %get-tuple-element.180.refs_0_), channel_id=1, source_target_pairs={{0,2},{1,3},{2,0},{3,1},{4,6},{5,7},{6,4},{7,5},{8,10},{9,11},{10,... | collective-permute-start | bytes 786440 | tf_op jit(solution)/shard_map/ppermute | solution.py:352
  5.3 1.5 %collective-permute-start = (f32[4,128,128]{2,1,0:T(8,128)S(1)}, f32[4,128,128]{2,1,0:T(8,128)S(1)}, u32[]{:S(2)}, u32[]{:S(2)}) collective-permute-start(f32[4,128,128]{2,1,0:T(8,128)S(1)} %get-tuple-element.179.refs_0_), channel_id=1, source_target_pairs={{0,1},{1,0},{2,3},{3,2},{4,5},{5,4},{6,7},{7,6},{8,9},{9,8},{10,11... | collective-permute-start | bytes 786440 | tf_op jit(solution)/shard_map/ppermute | solution.py:352
  6.8 1.7 %key_state_2.1 = (bf16[4,128,128]{2,1,0:T(8,128)(2,1)S(1)}, f32[4,128,128]{2,1,0:T(8,128)S(1)}, bf16[4,128,128]{2,1,0:T(8,128)(2,1)S(1)}, f32[4,128,128]{2,1,0:T(8,128)S(1)}, f32[8,128]{1,0:T(8,128)S(1)}) custom-call(bf16[128,2048]{1,0:T(8,128)(2,1)} %bitcast.24, bf16[128,2048]{1,0:T(8,128)(2,1)} %bitcast.10, bf16[2048,128]{1,0:T(8,128)(2,1)} %refs_6_.7, ...), custom_call_target="tpu_custom_call" | custom-call | flops 200000000 | tf_op jit(solution)/shard_map/key_state_2/pallas_call | solution.py:315
  9.8 2.6 %collective-permute-done.1.refs_1_.refs_0_ = f32[4,128,128]{2,1,0:T(8,128)S(1)} collective-permute-done((f32[4,128,128]{2,1,0:T(8,128)S(1)}, f32[4,128,128]{2,1,0:T(8,128)S(1)}, u32[]{:S(2)}, u32[]{:S(2)}) %collective-permute-start.1) | collective-permute-done | bytes 262176 | tf_op jit(solution)/shard_map/ppermute | solution.py:352
  12.5 2.0 %collective-permute-done.refs_1_.refs_0_ = f32[4,128,128]{2,1,0:T(8,128)S(1)} collective-permute-done((f32[4,128,128]{2,1,0:T(8,128)S(1)}, f32[4,128,128]{2,1,0:T(8,128)S(1)}, u32[]{:S(2)}, u32[]{:S(2)}) %collective-permute-start) | collective-permute-done | bytes 262176 | tf_op jit(solution)/shard_map/ppermute | solution.py:352
  14.6 2.0 %collective-permute-start.5 = (f32[4,128,128]{2,1,0:T(8,128)S(1)}, f32[4,128,128]{2,1,0:T(8,128)S(1)}, u32[]{:S(2)}, u32[]{:S(2)}) collective-permute-start(f32[4,128,128]{2,1,0:T(8,128)S(1)} %get-tuple-element.205), channel_id=1, source_target_pairs={{0,1},{1,0},{2,3},{3,2},{4,5},{5,4},{6,7},{7,6},{8,9},{9,8},{10,11... | collective-permute-start | bytes 786440 | tf_op jit(solution)/shard_map/ppermute | solution.py:352
  17.3 0.7 collective-permute-done.4.refs_1_.refs_0_
  18.1 2.0 %collective-permute-done.3.refs_1_.refs_0_ = f32[4,128,128]{2,1,0:T(8,128)S(1)} collective-permute-done((f32[4,128,128]{2,1,0:T(8,128)S(1)}, f32[4,128,128]{2,1,0:T(8,128)S(1)}, u32[]{:S(2)}, u32[]{:S(2)}) %collective-permute-start.3) | collective-permute-done | bytes 262176 | tf_op jit(solution)/shard_map/ppermute | solution.py:352
  20.3 2.0 %collective-permute-start.7 = (f32[4,128,128]{2,1,0:T(8,128)S(1)}, f32[4,128,128]{2,1,0:T(8,128)S(1)}, u32[]{:S(2)}, u32[]{:S(2)}) collective-permute-start(f32[4,128,128]{2,1,0:T(8,128)S(1)} %get-tuple-element.229), channel_id=1, source_target_pairs={{0,1},{1,0},{2,3},{3,2},{4,5},{5,4},{6,7},{7,6},{8,9},{9,8},{10,11... | collective-permute-start | bytes 786440 | tf_op jit(solution)/shard_map/ppermute | solution.py:352
  22.2 1.6 %collective-permute-done.2.refs_1_ = f32[4,128,128]{2,1,0:T(8,128)S(1)} collective-permute-done((f32[4,128,128]{2,1,0:T(8,128)S(1)}, f32[4,128,128]{2,1,0:T(8,128)S(1)}, u32[]{:S(2)}, u32[]{:S(2)}) %collective-permute-start.2) | collective-permute-done | bytes 262176 | tf_op jit(solution)/shard_map/ppermute | solution.py:352
  23.9 0.6 numer_0.1
  24.5 1.9 %collective-permute-start.10 = (f32[4,128,128]{2,1,0:T(8,128)S(1)}, f32[4,128,128]{2,1,0:T(8,128)S(1)}, u32[]{:S(2)}, u32[]{:S(2)}) collective-permute-start(f32[4,128,128]{2,1,0:T(8,128)S(1)} %get-tuple-element.248.refs_0_), channel_id=1, source_target_pairs={{0,1},{1,0},{2,3},{3,2},{4,5},{5,4},{6,7},{7,6},{8,9},{9,8},{10,11... | collective-permute-start | bytes 786440 | tf_op jit(solution)/shard_map/ppermute | solution.py:352
  26.4 0.6 numer_1.1
  27.0 1.6 %collective-permute-start.9 = (f32[4,128,128]{2,1,0:T(8,128)S(1)}, f32[4,128,128]{2,1,0:T(8,128)S(1)}, u32[]{:S(2)}, u32[]{:S(2)}) collective-permute-start(f32[4,128,128]{2,1,0:T(8,128)S(1)} %get-tuple-element.247.refs_0_), channel_id=1, source_target_pairs={{0,2},{1,3},{2,0},{3,1},{4,6},{5,7},{6,4},{7,5},{8,10},{9,11},{10,... | collective-permute-start | bytes 786440 | tf_op jit(solution)/shard_map/ppermute | solution.py:352
  28.6 0.8 %query_grad_0.1 = (bf16[4,128,128]{2,1,0:T(8,128)(2,1)S(1)}, bf16[4,128,128]{2,1,0:T(8,128)(2,1)S(1)}, f32[4,136,128]{2,1,0:T(8,128)S(1)}, f32[8,128]{1,0:T(8,128)S(1)}) custom-call(bf16[4,128,128]{2,1,0:T(8,128)(2,1)S(1)} %get-tuple-element.200.refs_0_.refs_1_, bf16[4,128,128]{2,1,0:T(8,128)(2,1)S(1)} %get-tuple-element.201.refs_1_, ...), custom_call_target="tpu_custom_call" | custom-call | flops 200000000 | tf_op jit(solution)/shard_map/query_grad_0/pallas_call | solution.py:315
  29.4 0.8 %query_grad_1.1 = (bf16[4,128,128]{2,1,0:T(8,128)(2,1)S(1)}, bf16[4,128,128]{2,1,0:T(8,128)(2,1)S(1)}, f32[4,136,128]{2,1,0:T(8,128)S(1)}, f32[8,128]{1,0:T(8,128)S(1)}) custom-call(bf16[4,128,128]{2,1,0:T(8,128)(2,1)S(1)} %get-tuple-element.211.refs_0_.refs_1_, bf16[4,128,128]{2,1,0:T(8,128)(2,1)S(1)} %get-tuple-element.212.refs_1_, ...), custom_call_target="tpu_custom_call" | custom-call | flops 200000000 | tf_op jit(solution)/shard_map/query_grad_1/pallas_call | solution.py:315
  30.3 0.6 numer_2.1
  32.1 1.6 %collective-permute-start.13 = (f32[4,128,128]{2,1,0:T(8,128)S(1)}, f32[4,128,128]{2,1,0:T(8,128)S(1)}, u32[]{:S(2)}, u32[]{:S(2)}) collective-permute-start(f32[4,128,128]{2,1,0:T(8,128)S(1)} %get-tuple-element.256.refs_0_), channel_id=1, source_target_pairs={{0,1},{1,0},{2,3},{3,2},{4,5},{5,4},{6,7},{7,6},{8,9},{9,8},{10,11... | collective-permute-start | bytes 786440 | tf_op jit(solution)/shard_map/ppermute | solution.py:352
  33.7 0.6 collective-permute-start.12
  34.3 0.8 %query_grad_2.1 = (bf16[4,128,128]{2,1,0:T(8,128)(2,1)S(1)}, bf16[4,128,128]{2,1,0:T(8,128)(2,1)S(1)}, f32[4,136,128]{2,1,0:T(8,128)S(1)}, f32[8,128]{1,0:T(8,128)S(1)}) custom-call(bf16[4,128,128]{2,1,0:T(8,128)(2,1)S(1)} %get-tuple-element.222.refs_0_.refs_1_, bf16[4,128,128]{2,1,0:T(8,128)(2,1)S(1)} %get-tuple-element.223.refs_1_, ...), custom_call_target="tpu_custom_call" | custom-call | flops 200000000 | tf_op jit(solution)/shard_map/query_grad_2/pallas_call | solution.py:315
  35.1 0.8 %query_grad_3.1 = (bf16[4,128,128]{2,1,0:T(8,128)(2,1)S(1)}, bf16[4,128,128]{2,1,0:T(8,128)(2,1)S(1)}, f32[4,136,128]{2,1,0:T(8,128)S(1)}, f32[8,128]{1,0:T(8,128)S(1)}) custom-call(bf16[4,128,128]{2,1,0:T(8,128)(2,1)S(1)} %get-tuple-element.236.refs_0_.refs_1_, bf16[4,128,128]{2,1,0:T(8,128)(2,1)S(1)} %get-tuple-element.237.refs_1_, ...), custom_call_target="tpu_custom_call" | custom-call | flops 200000000 | tf_op jit(solution)/shard_map/query_grad_3/pallas_call | solution.py:315
  36.3 1.5 %collective-permute-start.15 = (f32[4,128,128]{2,1,0:T(8,128)S(1)}, f32[4,128,128]{2,1,0:T(8,128)S(1)}, u32[]{:S(2)}, u32[]{:S(2)}) collective-permute-start(f32[4,128,128]{2,1,0:T(8,128)S(1)} %get-tuple-element.270), channel_id=1, source_target_pairs={{0,2},{1,3},{2,0},{3,1},{4,6},{5,7},{6,4},{7,5},{8,10},{9,11},{10,... | collective-permute-start | bytes 786440 | tf_op jit(solution)/shard_map/ppermute | solution.py:352
  39.3 2.1 %collective-permute-done.13.refs_1_.refs_0_ = f32[4,128,128]{2,1,0:T(8,128)S(1)} collective-permute-done((f32[4,128,128]{2,1,0:T(8,128)S(1)}, f32[4,128,128]{2,1,0:T(8,128)S(1)}, u32[]{:S(2)}, u32[]{:S(2)}) %collective-permute-start.13) | collective-permute-done | bytes 262176 | tf_op jit(solution)/shard_map/ppermute | solution.py:352
  41.8 1.0 %collective-permute-done.12.refs_1_.refs_0_ = f32[4,128,128]{2,1,0:T(8,128)S(1)} collective-permute-done((f32[4,128,128]{2,1,0:T(8,128)S(1)}, f32[4,128,128]{2,1,0:T(8,128)S(1)}, u32[]{:S(2)}, u32[]{:S(2)}) %collective-permute-start.12) | collective-permute-done | bytes 262176 | tf_op jit(solution)/shard_map/ppermute | solution.py:352
  42.9 0.7 collective-permute-start.20
  43.7 2.7 %collective-permute-start.14 = (f32[2,2,136,128]{3,2,1,0:T(8,128)S(1)}, f32[2,2,136,128]{3,2,1,0:T(8,128)S(1)}, u32[]{:S(2)}, u32[]{:S(2)}) collective-permute-start(f32[2,2,136,128]{3,2,1,0:T(8,128)S(1)} %get-tuple-element.269), channel_id=1, source_target_pairs={{0,16},{4,20},{8,24},{12,28},{16,0},{20,4},{24,8},{28,12},{1,17},{... | collective-permute-start | bytes 835592 | tf_op jit(solution)/shard_map/ppermute | solution.py:352
  46.4 2.1 %collective-permute-done.15.refs_1_ = f32[4,128,128]{2,1,0:T(8,128)S(1)} collective-permute-done((f32[4,128,128]{2,1,0:T(8,128)S(1)}, f32[4,128,128]{2,1,0:T(8,128)S(1)}, u32[]{:S(2)}, u32[]{:S(2)}) %collective-permute-start.15) | collective-permute-done | bytes 262176 | tf_op jit(solution)/shard_map/ppermute | solution.py:352
  50.2 3.1 %collective-permute-done.19.refs_1_ = f32[4,128,128]{2,1,0:T(8,128)S(1)} collective-permute-done((f32[4,128,128]{2,1,0:T(8,128)S(1)}, f32[4,128,128]{2,1,0:T(8,128)S(1)}, u32[]{:S(2)}, u32[]{:S(2)}) %collective-permute-start.19) | collective-permute-done | bytes 262176 | tf_op jit(solution)/shard_map/ppermute | solution.py:352
  56.5 1.7 %collective-permute-start.27 = (f32[2,128,128]{2,1,0:T(8,128)S(1)}, f32[2,128,128]{2,1,0:T(8,128)S(1)}, u32[]{:S(2)}, u32[]{:S(2)}) collective-permute-start(f32[2,128,128]{2,1,0:T(8,128)S(1)} %get-tuple-element.336), channel_id=1, source_target_pairs={{0,8},{4,12},{8,0},{12,4},{16,24},{20,28},{24,16},{28,20},{1,9},{5... | collective-permute-start | bytes 393224 | tf_op jit(solution)/shard_map/ppermute | solution.py:352
  58.2 2.6 %collective-permute-start.28 = (f32[2,128,128]{2,1,0:T(8,128)S(1)}, f32[2,128,128]{2,1,0:T(8,128)S(1)}, u32[]{:S(2)}, u32[]{:S(2)}) collective-permute-start(f32[2,128,128]{2,1,0:T(8,128)S(1)} %get-tuple-element.337), channel_id=1, source_target_pairs={{0,16},{4,20},{8,24},{12,28},{16,0},{20,4},{24,8},{28,12},{1,17},{... | collective-permute-start | bytes 393224 | tf_op jit(solution)/shard_map/ppermute | solution.py:352
  61.0 0.8 collective-permute-start.24
  61.8 1.3 %collective-permute-start.23 = (f32[136,128]{1,0:T(8,128)S(1)}, f32[136,128]{1,0:T(8,128)S(1)}, u32[]{:S(2)}, u32[]{:S(2)}) collective-permute-start(f32[136,128]{1,0:T(8,128)S(1)} %get-tuple-element.329), channel_id=1, source_target_pairs={{0,8},{4,12},{8,0},{12,4},{16,24},{20,28},{24,16},{28,20},{1,9},{5... | collective-permute-start | bytes 208904 | tf_op jit(solution)/shard_map/ppermute | solution.py:352
  63.1 0.9 %lay_0.1 = (bf16[128,2048]{1,0:T(8,128)(2,1)}, f32[8,128]{1,0:T(8,128)S(1)}) custom-call(bf16[4,128,128]{2,1,0:T(8,128)(2,1)S(1)} %get-tuple-element.210.refs_0_, bf16[4,128,128]{2,1,0:T(8,128)(2,1)S(1)} %get-tuple-element.217.refs_1_, bf16[4,128,128]{2,1,0:T(8,128)(2,1)S(1)} %get-tuple-element.235.refs_2_, ...), custom_call_target="tpu_custom_call" | custom-call | flops 200000000 | tf_op jit(solution)/shard_map/lay_0/pallas_call | solution.py:315
  64.1 0.9 %lay_1.1 = (bf16[128,2048]{1,0:T(8,128)(2,1)}, f32[8,128]{1,0:T(8,128)S(1)}) custom-call(bf16[4,128,128]{2,1,0:T(8,128)(2,1)S(1)} %get-tuple-element.318.refs_0_, bf16[4,128,128]{2,1,0:T(8,128)(2,1)S(1)} %get-tuple-element.319.refs_1_, bf16[4,128,128]{2,1,0:T(8,128)(2,1)S(1)} %get-tuple-element.320.refs_2_, ...), custom_call_target="tpu_custom_call" | custom-call | flops 200000000 | tf_op jit(solution)/shard_map/lay_1/pallas_call | solution.py:315
  65.0 4.0 %collective-permute-done.24.refs_1_ = f32[136,128]{1,0:T(8,128)S(1)} collective-permute-done((f32[136,128]{1,0:T(8,128)S(1)}, f32[136,128]{1,0:T(8,128)S(1)}, u32[]{:S(2)}, u32[]{:S(2)}) %collective-permute-start.24) | collective-permute-done | bytes 69664 | tf_op jit(solution)/shard_map/ppermute | solution.py:352
  69.0 0.6 collective-permute-start.26
  69.7 1.0 %collective-permute-done.23.refs_1_ = f32[136,128]{1,0:T(8,128)S(1)} collective-permute-done((f32[136,128]{1,0:T(8,128)S(1)}, f32[136,128]{1,0:T(8,128)S(1)}, u32[]{:S(2)}, u32[]{:S(2)}) %collective-permute-start.23) | collective-permute-done | bytes 69664 | tf_op jit(solution)/shard_map/ppermute | solution.py:352
  70.7 0.7 collective-permute-start.25
  71.4 1.4 %collective-permute-start.34 = (f32[2,128,128]{2,1,0:T(8,128)S(1)}, f32[2,128,128]{2,1,0:T(8,128)S(1)}, u32[]{:S(2)}, u32[]{:S(2)}) collective-permute-start(f32[2,128,128]{2,1,0:T(8,128)S(1)} %get-tuple-element.346.refs_0_), channel_id=1, source_target_pairs={{0,3},{1,2},{2,1},{3,0},{4,7},{5,6},{6,5},{7,4},{8,11},{9,10},{10,... | collective-permute-start | bytes 393224 | tf_op jit(solution)/shard_map/ppermute | solution.py:352
  73.5 1.5 %collective-permute-start.32 = (f32[2,128,128]{2,1,0:T(8,128)S(1)}, f32[2,128,128]{2,1,0:T(8,128)S(1)}, u32[]{:S(2)}, u32[]{:S(2)}) collective-permute-start(f32[2,128,128]{2,1,0:T(8,128)S(1)} %get-tuple-element.346.refs_0_), channel_id=1, source_target_pairs={{0,1},{1,0},{2,3},{3,2},{4,5},{5,4},{6,7},{7,6},{8,9},{9,8},{10,11... | collective-permute-start | bytes 393224 | tf_op jit(solution)/shard_map/ppermute | solution.py:352
  75.0 2.4 %collective-permute-done.25.refs_1_ = f32[136,128]{1,0:T(8,128)S(1)} collective-permute-done((f32[136,128]{1,0:T(8,128)S(1)}, f32[136,128]{1,0:T(8,128)S(1)}, u32[]{:S(2)}, u32[]{:S(2)}) %collective-permute-start.25) | collective-permute-done | bytes 69664 | tf_op jit(solution)/shard_map/ppermute | solution.py:352
  77.4 0.8 collective-permute-start.31
  78.4 0.9 %lay_2.1 = (bf16[128,2048]{1,0:T(8,128)(2,1)}, f32[8,128]{1,0:T(8,128)S(1)}) custom-call(bf16[4,128,128]{2,1,0:T(8,128)(2,1)S(1)} %get-tuple-element.324.refs_0_, bf16[4,128,128]{2,1,0:T(8,128)(2,1)S(1)} %get-tuple-element.325.refs_1_, bf16[4,128,128]{2,1,0:T(8,128)(2,1)S(1)} %get-tuple-element.326.refs_2_, ...), custom_call_target="tpu_custom_call" | custom-call | flops 200000000 | tf_op jit(solution)/shard_map/lay_2/pallas_call | solution.py:315
  79.4 1.5 %collective-permute-done.33.refs_2_ = f32[2,128,128]{2,1,0:T(8,128)S(1)} collective-permute-done((f32[2,128,128]{2,1,0:T(8,128)S(1)}, f32[2,128,128]{2,1,0:T(8,128)S(1)}, u32[]{:S(2)}, u32[]{:S(2)}) %collective-permute-start.33) | collective-permute-done | bytes 131104 | tf_op jit(solution)/shard_map/ppermute | solution.py:352
  80.9 0.7 key_total.1
  81.8 0.7 collective-permute-done.30.refs_1_
  82.5 0.7 query_total.1
  (89 shorter events, 12.2 us)
Async XLA Ops:
  2.2 4.5 %copy-start.7 = (f32[8,128]{1,0:T(8,128)}, f32[8,128]{1,0:T(8,128)S(1)}, u32[]{:S(2)}) copy-start(f32[8,128]{1,0:T(8,128)S(1)} %get-tuple-element.183.refs_3_) | copy-start | bytes 12292
  2.2 10.2 %collective-permute-start.1 = (f32[4,128,128]{2,1,0:T(8,128)S(1)}, f32[4,128,128]{2,1,0:T(8,128)S(1)}, u32[]{:S(2)}, u32[]{:S(2)}) collective-permute-start(f32[4,128,128]{2,1,0:T(8,128)S(1)} %get-tuple-element.180.refs_0_), channel_id=1, source_target_pairs={{0,2},{1,3},{2,0},{3,1},{4,6},{5,7},{6,4},{7,5},{8,10},{9,11},{10,... | collective-permute-start | bytes 786440 | tf_op jit(solution)/shard_map/ppermute | solution.py:352
  5.3 9.2 %collective-permute-start = (f32[4,128,128]{2,1,0:T(8,128)S(1)}, f32[4,128,128]{2,1,0:T(8,128)S(1)}, u32[]{:S(2)}, u32[]{:S(2)}) collective-permute-start(f32[4,128,128]{2,1,0:T(8,128)S(1)} %get-tuple-element.179.refs_0_), channel_id=1, source_target_pairs={{0,1},{1,0},{2,3},{3,2},{4,5},{5,4},{6,7},{7,6},{8,9},{9,8},{10,11... | collective-permute-start | bytes 786440 | tf_op jit(solution)/shard_map/ppermute | solution.py:352
  6.8 2.4 %copy-start.3 = (bf16[1,128,2048]{2,1,0:T(8,128)(2,1)S(1)}, bf16[1,128,2048]{2,1,0:T(8,128)(2,1)}, u32[]{:S(2)}) copy-start(bf16[1,128,2048]{2,1,0:T(8,128)(2,1)} %param.7) | copy-start | bytes 1572868
  6.8 2.4 %copy-start.4 = (bf16[2048,128]{1,0:T(8,128)(2,1)S(1)}, bf16[2048,128]{1,0:T(8,128)(2,1)}, u32[]{:S(2)}) copy-start(bf16[2048,128]{1,0:T(8,128)(2,1)} %refs_7_.7) | copy-start | bytes 1572868
  8.5 9.6 %collective-permute-start.4 = (f32[4,128,128]{2,1,0:T(8,128)S(1)}, f32[4,128,128]{2,1,0:T(8,128)S(1)}, u32[]{:S(2)}, u32[]{:S(2)}) collective-permute-start(f32[4,128,128]{2,1,0:T(8,128)S(1)} %get-tuple-element.192.refs_0_), channel_id=1, source_target_pairs={{0,2},{1,3},{2,0},{3,1},{4,6},{5,7},{6,4},{7,5},{8,10},{9,11},{10,... | collective-permute-start | bytes 786440 | tf_op jit(solution)/shard_map/ppermute | solution.py:352
  9.0 11.1 %collective-permute-start.3 = (f32[4,128,128]{2,1,0:T(8,128)S(1)}, f32[4,128,128]{2,1,0:T(8,128)S(1)}, u32[]{:S(2)}, u32[]{:S(2)}) collective-permute-start(f32[4,128,128]{2,1,0:T(8,128)S(1)} %get-tuple-element.191.refs_0_), channel_id=1, source_target_pairs={{0,1},{1,0},{2,3},{3,2},{4,5},{5,4},{6,7},{7,6},{8,9},{9,8},{10,11... | collective-permute-start | bytes 786440 | tf_op jit(solution)/shard_map/ppermute | solution.py:352
  14.5 9.3 %collective-permute-start.2 = (f32[4,128,128]{2,1,0:T(8,128)S(1)}, f32[4,128,128]{2,1,0:T(8,128)S(1)}, u32[]{:S(2)}, u32[]{:S(2)}) collective-permute-start(f32[4,128,128]{2,1,0:T(8,128)S(1)} %get-tuple-element.188), channel_id=1, source_target_pairs={{0,2},{1,3},{2,0},{3,1},{4,6},{5,7},{6,4},{7,5},{8,10},{9,11},{10,... | collective-permute-start | bytes 786440 | tf_op jit(solution)/shard_map/ppermute | solution.py:352
  14.6 11.7 %collective-permute-start.5 = (f32[4,128,128]{2,1,0:T(8,128)S(1)}, f32[4,128,128]{2,1,0:T(8,128)S(1)}, u32[]{:S(2)}, u32[]{:S(2)}) collective-permute-start(f32[4,128,128]{2,1,0:T(8,128)S(1)} %get-tuple-element.205), channel_id=1, source_target_pairs={{0,1},{1,0},{2,3},{3,2},{4,5},{5,4},{6,7},{7,6},{8,9},{9,8},{10,11... | collective-permute-start | bytes 786440 | tf_op jit(solution)/shard_map/ppermute | solution.py:352
  18.0 5.8 %copy-start.5 = (bf16[1,128,2048]{2,1,0:T(8,128)(2,1)S(1)}, bf16[1,128,2048]{2,1,0:T(8,128)(2,1)}, u32[]{:S(2)}) copy-start(bf16[1,128,2048]{2,1,0:T(8,128)(2,1)} %param.10) | copy-start | bytes 1572868
  18.1 5.8 %copy-start = (bf16[1,128,2048]{2,1,0:T(8,128)(2,1)S(1)}, bf16[1,128,2048]{2,1,0:T(8,128)(2,1)}, u32[]{:S(2)}) copy-start(bf16[1,128,2048]{2,1,0:T(8,128)(2,1)} %param.9) | copy-start | bytes 1572868
  20.2 3.7 %copy-start.6 = (f32[2048]{0:T(1024)S(1)}, f32[2048]{0:T(1024)}, u32[]{:S(2)}) copy-start(f32[2048]{0:T(1024)} %param.13) | copy-start | bytes 24580
  20.2 10.1 %collective-permute-start.6 = (f32[4,128,128]{2,1,0:T(8,128)S(1)}, f32[4,128,128]{2,1,0:T(8,128)S(1)}, u32[]{:S(2)}, u32[]{:S(2)}) collective-permute-start(f32[4,128,128]{2,1,0:T(8,128)S(1)} %get-tuple-element.218), channel_id=1, source_target_pairs={{0,2},{1,3},{2,0},{3,1},{4,6},{5,7},{6,4},{7,5},{8,10},{9,11},{10,... | collective-permute-start | bytes 786440 | tf_op jit(solution)/shard_map/ppermute | solution.py:352
  20.3 11.1 %collective-permute-start.7 = (f32[4,128,128]{2,1,0:T(8,128)S(1)}, f32[4,128,128]{2,1,0:T(8,128)S(1)}, u32[]{:S(2)}, u32[]{:S(2)}) collective-permute-start(f32[4,128,128]{2,1,0:T(8,128)S(1)} %get-tuple-element.229), channel_id=1, source_target_pairs={{0,1},{1,0},{2,3},{3,2},{4,5},{5,4},{6,7},{7,6},{8,9},{9,8},{10,11... | collective-permute-start | bytes 786440 | tf_op jit(solution)/shard_map/ppermute | solution.py:352
  24.5 11.5 %collective-permute-start.10 = (f32[4,128,128]{2,1,0:T(8,128)S(1)}, f32[4,128,128]{2,1,0:T(8,128)S(1)}, u32[]{:S(2)}, u32[]{:S(2)}) collective-permute-start(f32[4,128,128]{2,1,0:T(8,128)S(1)} %get-tuple-element.248.refs_0_), channel_id=1, source_target_pairs={{0,1},{1,0},{2,3},{3,2},{4,5},{5,4},{6,7},{7,6},{8,9},{9,8},{10,11... | collective-permute-start | bytes 786440 | tf_op jit(solution)/shard_map/ppermute | solution.py:352
  27.0 9.0 %collective-permute-start.9 = (f32[4,128,128]{2,1,0:T(8,128)S(1)}, f32[4,128,128]{2,1,0:T(8,128)S(1)}, u32[]{:S(2)}, u32[]{:S(2)}) collective-permute-start(f32[4,128,128]{2,1,0:T(8,128)S(1)} %get-tuple-element.247.refs_0_), channel_id=1, source_target_pairs={{0,2},{1,3},{2,0},{3,1},{4,6},{5,7},{6,4},{7,5},{8,10},{9,11},{10,... | collective-permute-start | bytes 786440 | tf_op jit(solution)/shard_map/ppermute | solution.py:352
  32.0 4.1 %collective-permute-start.8 = (f32[2,2,136,128]{3,2,1,0:T(8,128)S(1)}, f32[2,2,136,128]{3,2,1,0:T(8,128)S(1)}, u32[]{:S(2)}, u32[]{:S(2)}) collective-permute-start(f32[2,2,136,128]{3,2,1,0:T(8,128)S(1)} %get-tuple-element.246), channel_id=1, source_target_pairs={{0,4},{4,0},{8,12},{12,8},{16,20},{20,16},{24,28},{28,24},{1,5},{5... | collective-permute-start | bytes 835592 | tf_op jit(solution)/shard_map/ppermute | solution.py:352
  32.1 9.2 %collective-permute-start.13 = (f32[4,128,128]{2,1,0:T(8,128)S(1)}, f32[4,128,128]{2,1,0:T(8,128)S(1)}, u32[]{:S(2)}, u32[]{:S(2)}) collective-permute-start(f32[4,128,128]{2,1,0:T(8,128)S(1)} %get-tuple-element.256.refs_0_), channel_id=1, source_target_pairs={{0,1},{1,0},{2,3},{3,2},{4,5},{5,4},{6,7},{7,6},{8,9},{9,8},{10,11... | collective-permute-start | bytes 786440 | tf_op jit(solution)/shard_map/ppermute | solution.py:352
  33.7 9.2 %collective-permute-start.12 = (f32[4,128,128]{2,1,0:T(8,128)S(1)}, f32[4,128,128]{2,1,0:T(8,128)S(1)}, u32[]{:S(2)}, u32[]{:S(2)}) collective-permute-start(f32[4,128,128]{2,1,0:T(8,128)S(1)} %get-tuple-element.255.refs_0_), channel_id=1, source_target_pairs={{0,2},{1,3},{2,0},{3,1},{4,6},{5,7},{6,4},{7,5},{8,10},{9,11},{10,... | collective-permute-start | bytes 786440 | tf_op jit(solution)/shard_map/ppermute | solution.py:352
  36.1 2.2 %copy-start.1 = (bf16[2048,128]{1,0:T(8,128)(2,1)S(1)}, bf16[2048,128]{1,0:T(8,128)(2,1)}, u32[]{:S(2)}) copy-start(bf16[2048,128]{1,0:T(8,128)(2,1)} %refs_6_.7) | copy-start | bytes 1572868
  36.1 2.2 %copy-start.2 = (bf16[1,128,2048]{2,1,0:T(8,128)(2,1)S(1)}, bf16[1,128,2048]{2,1,0:T(8,128)(2,1)}, u32[]{:S(2)}) copy-start(bf16[1,128,2048]{2,1,0:T(8,128)(2,1)} %param.8) | copy-start | bytes 1572868
  36.2 7.4 %collective-permute-start.11 = (f32[2,2,136,128]{3,2,1,0:T(8,128)S(1)}, f32[2,2,136,128]{3,2,1,0:T(8,128)S(1)}, u32[]{:S(2)}, u32[]{:S(2)}) collective-permute-start(f32[2,2,136,128]{3,2,1,0:T(8,128)S(1)} %get-tuple-element.254), channel_id=1, source_target_pairs={{0,4},{4,0},{8,12},{12,8},{16,20},{20,16},{24,28},{28,24},{1,5},{5... | collective-permute-start | bytes 835592 | tf_op jit(solution)/shard_map/ppermute | solution.py:352
  36.3 12.1 %collective-permute-start.15 = (f32[4,128,128]{2,1,0:T(8,128)S(1)}, f32[4,128,128]{2,1,0:T(8,128)S(1)}, u32[]{:S(2)}, u32[]{:S(2)}) collective-permute-start(f32[4,128,128]{2,1,0:T(8,128)S(1)} %get-tuple-element.270), channel_id=1, source_target_pairs={{0,2},{1,3},{2,0},{3,1},{4,6},{5,7},{6,4},{7,5},{8,10},{9,11},{10,... | collective-permute-start | bytes 786440 | tf_op jit(solution)/shard_map/ppermute | solution.py:352
  37.8 11.1 %collective-permute-start.16 = (f32[4,128,128]{2,1,0:T(8,128)S(1)}, f32[4,128,128]{2,1,0:T(8,128)S(1)}, u32[]{:S(2)}, u32[]{:S(2)}) collective-permute-start(f32[4,128,128]{2,1,0:T(8,128)S(1)} %get-tuple-element.275), channel_id=1, source_target_pairs={{0,1},{1,0},{2,3},{3,2},{4,5},{5,4},{6,7},{7,6},{8,9},{9,8},{10,11... | collective-permute-start | bytes 786440 | tf_op jit(solution)/shard_map/ppermute | solution.py:352
  41.4 11.9 %collective-permute-start.19 = (f32[4,128,128]{2,1,0:T(8,128)S(1)}, f32[4,128,128]{2,1,0:T(8,128)S(1)}, u32[]{:S(2)}, u32[]{:S(2)}) collective-permute-start(f32[4,128,128]{2,1,0:T(8,128)S(1)} %get-tuple-element.284), channel_id=1, source_target_pairs={{0,2},{1,3},{2,0},{3,1},{4,6},{5,7},{6,4},{7,5},{8,10},{9,11},{10,... | collective-permute-start | bytes 786440 | tf_op jit(solution)/shard_map/ppermute | solution.py:352
  42.9 10.9 %collective-permute-start.20 = (f32[4,128,128]{2,1,0:T(8,128)S(1)}, f32[4,128,128]{2,1,0:T(8,128)S(1)}, u32[]{:S(2)}, u32[]{:S(2)}) collective-permute-start(f32[4,128,128]{2,1,0:T(8,128)S(1)} %get-tuple-element.297), channel_id=1, source_target_pairs={{0,1},{1,0},{2,3},{3,2},{4,5},{5,4},{6,7},{7,6},{8,9},{9,8},{10,11... | collective-permute-start | bytes 786440 | tf_op jit(solution)/shard_map/ppermute | solution.py:352
  43.7 17.3 %collective-permute-start.14 = (f32[2,2,136,128]{3,2,1,0:T(8,128)S(1)}, f32[2,2,136,128]{3,2,1,0:T(8,128)S(1)}, u32[]{:S(2)}, u32[]{:S(2)}) collective-permute-start(f32[2,2,136,128]{3,2,1,0:T(8,128)S(1)} %get-tuple-element.269), channel_id=1, source_target_pairs={{0,16},{4,20},{8,24},{12,28},{16,0},{20,4},{24,8},{28,12},{1,17},{... | collective-permute-start | bytes 835592 | tf_op jit(solution)/shard_map/ppermute | solution.py:352
  54.3 1.8 %collective-permute-start.21 = (f32[2,128,128]{2,1,0:T(8,128)S(1)}, f32[2,128,128]{2,1,0:T(8,128)S(1)}, u32[]{:S(2)}, u32[]{:S(2)}) collective-permute-start(f32[2,128,128]{2,1,0:T(8,128)S(1)} %get-tuple-element.304), channel_id=1, source_target_pairs={{0,4},{4,0},{8,12},{12,8},{16,20},{20,16},{24,28},{28,24},{1,5},{5... | collective-permute-start | bytes 393224 | tf_op jit(solution)/shard_map/ppermute | solution.py:352
  54.4 1.8 %collective-permute-start.22 = (f32[2,128,128]{2,1,0:T(8,128)S(1)}, f32[2,128,128]{2,1,0:T(8,128)S(1)}, u32[]{:S(2)}, u32[]{:S(2)}) collective-permute-start(f32[2,128,128]{2,1,0:T(8,128)S(1)} %get-tuple-element.305), channel_id=1, source_target_pairs={{0,4},{4,0},{8,12},{12,8},{16,20},{20,16},{24,28},{28,24},{1,5},{5... | collective-permute-start | bytes 393224 | tf_op jit(solution)/shard_map/ppermute | solution.py:352
  54.9 1.3 %collective-permute-start.17 = (f32[2,128,128]{2,1,0:T(8,128)S(1)}, f32[2,128,128]{2,1,0:T(8,128)S(1)}, u32[]{:S(2)}, u32[]{:S(2)}) collective-permute-start(f32[2,128,128]{2,1,0:T(8,128)S(1)} %get-tuple-element.282), channel_id=1, source_target_pairs={{0,4},{4,0},{8,12},{12,8},{16,20},{20,16},{24,28},{28,24},{1,5},{5... | collective-permute-start | bytes 393224 | tf_op jit(solution)/shard_map/ppermute | solution.py:352
  54.9 1.5 %collective-permute-start.18 = (f32[2,128,128]{2,1,0:T(8,128)S(1)}, f32[2,128,128]{2,1,0:T(8,128)S(1)}, u32[]{:S(2)}, u32[]{:S(2)}) collective-permute-start(f32[2,128,128]{2,1,0:T(8,128)S(1)} %get-tuple-element.283), channel_id=1, source_target_pairs={{0,4},{4,0},{8,12},{12,8},{16,20},{20,16},{24,28},{28,24},{1,5},{5... | collective-permute-start | bytes 393224 | tf_op jit(solution)/shard_map/ppermute | solution.py:352
  56.5 14.9 %collective-permute-start.27 = (f32[2,128,128]{2,1,0:T(8,128)S(1)}, f32[2,128,128]{2,1,0:T(8,128)S(1)}, u32[]{:S(2)}, u32[]{:S(2)}) collective-permute-start(f32[2,128,128]{2,1,0:T(8,128)S(1)} %get-tuple-element.336), channel_id=1, source_target_pairs={{0,8},{4,12},{8,0},{12,4},{16,24},{20,28},{24,16},{28,20},{1,9},{5... | collective-permute-start | bytes 393224 | tf_op jit(solution)/shard_map/ppermute | solution.py:352
  58.2 13.2 %collective-permute-start.28 = (f32[2,128,128]{2,1,0:T(8,128)S(1)}, f32[2,128,128]{2,1,0:T(8,128)S(1)}, u32[]{:S(2)}, u32[]{:S(2)}) collective-permute-start(f32[2,128,128]{2,1,0:T(8,128)S(1)} %get-tuple-element.337), channel_id=1, source_target_pairs={{0,16},{4,20},{8,24},{12,28},{16,0},{20,4},{24,8},{28,12},{1,17},{... | collective-permute-start | bytes 393224 | tf_op jit(solution)/shard_map/ppermute | solution.py:352
  60.8 10.6 %collective-permute-start.29 = (f32[2,128,128]{2,1,0:T(8,128)S(1)}, f32[2,128,128]{2,1,0:T(8,128)S(1)}, u32[]{:S(2)}, u32[]{:S(2)}) collective-permute-start(f32[2,128,128]{2,1,0:T(8,128)S(1)} %get-tuple-element.338), channel_id=1, source_target_pairs={{0,24},{4,28},{8,16},{12,20},{16,8},{20,12},{24,0},{28,4},{1,25},{... | collective-permute-start | bytes 393224 | tf_op jit(solution)/shard_map/ppermute | solution.py:352
  61.0 8.0 %collective-permute-start.24 = (f32[136,128]{1,0:T(8,128)S(1)}, f32[136,128]{1,0:T(8,128)S(1)}, u32[]{:S(2)}, u32[]{:S(2)}) collective-permute-start(f32[136,128]{1,0:T(8,128)S(1)} %get-tuple-element.330), channel_id=1, source_target_pairs={{0,8},{4,12},{8,0},{12,4},{16,24},{20,28},{24,16},{28,20},{1,9},{5... | collective-permute-start | bytes 208904 | tf_op jit(solution)/shard_map/ppermute | solution.py:352
  61.8 8.9 %collective-permute-start.23 = (f32[136,128]{1,0:T(8,128)S(1)}, f32[136,128]{1,0:T(8,128)S(1)}, u32[]{:S(2)}, u32[]{:S(2)}) collective-permute-start(f32[136,128]{1,0:T(8,128)S(1)} %get-tuple-element.329), channel_id=1, source_target_pairs={{0,8},{4,12},{8,0},{12,4},{16,24},{20,28},{24,16},{28,20},{1,9},{5... | collective-permute-start | bytes 208904 | tf_op jit(solution)/shard_map/ppermute | solution.py:352
  69.0 6.0 %collective-permute-start.26 = (f32[136,128]{1,0:T(8,128)S(1)}, f32[136,128]{1,0:T(8,128)S(1)}, u32[]{:S(2)}, u32[]{:S(2)}) collective-permute-start(f32[136,128]{1,0:T(8,128)S(1)} %get-tuple-element.334.refs_0_), channel_id=1, source_target_pairs={{0,1},{1,0},{2,3},{3,2},{4,5},{5,4},{6,7},{7,6},{8,9},{9,8},{10,11... | collective-permute-start | bytes 208904 | tf_op jit(solution)/shard_map/ppermute | solution.py:352
  70.7 6.7 %collective-permute-start.25 = (f32[136,128]{1,0:T(8,128)S(1)}, f32[136,128]{1,0:T(8,128)S(1)}, u32[]{:S(2)}, u32[]{:S(2)}) collective-permute-start(f32[136,128]{1,0:T(8,128)S(1)} %get-tuple-element.333.refs_0_), channel_id=1, source_target_pairs={{0,2},{1,3},{2,0},{3,1},{4,6},{5,7},{6,4},{7,5},{8,10},{9,11},{10,... | collective-permute-start | bytes 208904 | tf_op jit(solution)/shard_map/ppermute | solution.py:352
  71.4 7.9 %collective-permute-start.34 = (f32[2,128,128]{2,1,0:T(8,128)S(1)}, f32[2,128,128]{2,1,0:T(8,128)S(1)}, u32[]{:S(2)}, u32[]{:S(2)}) collective-permute-start(f32[2,128,128]{2,1,0:T(8,128)S(1)} %get-tuple-element.346.refs_0_), channel_id=1, source_target_pairs={{0,3},{1,2},{2,1},{3,0},{4,7},{5,6},{6,5},{7,4},{8,11},{9,10},{10,... | collective-permute-start | bytes 393224 | tf_op jit(solution)/shard_map/ppermute | solution.py:352
  72.9 8.0 %collective-permute-start.33 = (f32[2,128,128]{2,1,0:T(8,128)S(1)}, f32[2,128,128]{2,1,0:T(8,128)S(1)}, u32[]{:S(2)}, u32[]{:S(2)}) collective-permute-start(f32[2,128,128]{2,1,0:T(8,128)S(1)} %get-tuple-element.346.refs_0_), channel_id=1, source_target_pairs={{0,2},{1,3},{2,0},{3,1},{4,6},{5,7},{6,4},{7,5},{8,10},{9,11},{10,... | collective-permute-start | bytes 393224 | tf_op jit(solution)/shard_map/ppermute | solution.py:352
  73.5 7.4 %collective-permute-start.32 = (f32[2,128,128]{2,1,0:T(8,128)S(1)}, f32[2,128,128]{2,1,0:T(8,128)S(1)}, u32[]{:S(2)}, u32[]{:S(2)}) collective-permute-start(f32[2,128,128]{2,1,0:T(8,128)S(1)} %get-tuple-element.346.refs_0_), channel_id=1, source_target_pairs={{0,1},{1,0},{2,3},{3,2},{4,5},{5,4},{6,7},{7,6},{8,9},{9,8},{10,11... | collective-permute-start | bytes 393224 | tf_op jit(solution)/shard_map/ppermute | solution.py:352
  77.4 4.4 %collective-permute-start.31 = (f32[136,128]{1,0:T(8,128)S(1)}, f32[136,128]{1,0:T(8,128)S(1)}, u32[]{:S(2)}, u32[]{:S(2)}) collective-permute-start(f32[136,128]{1,0:T(8,128)S(1)} %get-tuple-element.345.refs_2_), channel_id=1, source_target_pairs={{0,1},{1,0},{2,3},{3,2},{4,5},{5,4},{6,7},{7,6},{8,9},{9,8},{10,11... | collective-permute-start | bytes 208904 | tf_op jit(solution)/shard_map/ppermute | solution.py:352
  78.1 4.3 %collective-permute-start.30 = (f32[136,128]{1,0:T(8,128)S(1)}, f32[136,128]{1,0:T(8,128)S(1)}, u32[]{:S(2)}, u32[]{:S(2)}) collective-permute-start(f32[136,128]{1,0:T(8,128)S(1)} %get-tuple-element.344.refs_0_), channel_id=1, source_target_pairs={{0,2},{1,3},{2,0},{3,1},{4,6},{5,7},{6,4},{7,5},{8,10},{9,11},{10,... | collective-permute-start | bytes 208904 | tf_op jit(solution)/shard_map/ppermute | solution.py:352
